TPU v7x, 32 devices: a whole 2x2x4 slice. The times are simulated.
32 devices in a mesh: gene: 4 (over z), cell: 8 (over y, x, core).
Axes of the slice: x: 2, y: 2, z: 4, core: 2. Of those that a mesh axis runs over, the one named last changes fastest.
Arguments:
- counts: int32 [16384, 4096], P('gene', 'cell'), may hold values from 0 to 2047, as said below
- w1: bfloat16 [16384, 512], P(('gene', 'cell')), may hold values from 0.099609375 to 2
- h1: float32 [512, 4096], P(None, 'cell'), may hold values from 0.1 to 2
- w2: float32 [512, 64], replicated, may hold values from 0.1 to 2
- h2: float32 [64, 4096], P(None, 'cell'), may hold values from 0.005 to 0.1
Outputs:
- w1_new: bfloat16 [16384, 512], P(('gene', 'cell'))
- h1_new: float32 [512, 4096], P(None, 'cell')
- w2_new: float32 [512, 64], replicated
- h2_new: float32 [64, 4096], P(None, 'cell')
Inputs may be any that keep to these rules, and one draw needn't show every extreme that they name: `counts`: counts are whole numbers; a gene's and a cell's typical depth vary, and cells later in the order run deeper.
All inputs are finite; a program needn't handle non-finite values.
Results may differ from a plain program's by a relative error of at most 0.0013.
The roundings to bfloat16 on the way count: a program that leaves them out, or rounds other values in their place, can miss the bound.
Values may be sent and summed in bfloat16 or wider, within the bound.
No kernel may reach another device: no remote copies, remote signals or barrier semaphores. Data moves between devices by JAX's collectives and lax.ppermute only.
A program may use at most 64 MiB of HBM per device.

v0:
```python
import jax
import jax.numpy as jnp
from jax import lax
from jax.sharding import PartitionSpec as P


def layer_two(h1_new, w2, h2):
    hi = lax.Precision.HIGHEST
    ratio3 = h1_new / jnp.dot(w2, h2, precision=hi)
    h2_new = h2 * jnp.dot(w2.T, ratio3, precision=hi) / jnp.sum(w2, axis=0)[:, None]
    ratio4 = h1_new / jnp.dot(w2, h2_new, precision=hi)
    w2_part = jnp.dot(ratio4, h2_new.T, precision=hi)
    h2_part = jnp.sum(h2_new, axis=1)
    return (h2_new, w2_part, h2_part)


def on_device(counts, w1, h1, w2, h2):
    w1_block = lax.all_gather(w1, "cell", axis=0, tiled=True)
    values = counts.astype(jnp.float32)
    h1_low = h1.astype(jnp.bfloat16)
    approx = jnp.dot(w1_block, h1_low, preferred_element_type=jnp.float32)
    ratio = (values / approx).astype(jnp.bfloat16)
    partial_num = lax.dot_general(
        w1_block, ratio, (((0,), (0,)), ((), ())), preferred_element_type=jnp.float32
    )
    partial_col = jnp.sum(w1_block.astype(jnp.float32), axis=0)
    h1_num, colsum = lax.psum((partial_num, partial_col), "gene")
    h1_new = h1 * h1_num / colsum[:, None]
    h1_low2 = h1_new.astype(jnp.bfloat16)
    approx2 = jnp.dot(w1_block, h1_low2, preferred_element_type=jnp.float32)
    ratio2 = (values / approx2).astype(jnp.bfloat16)
    local_rows = jnp.sum(h1_new, axis=1)
    rowsum = lax.psum(local_rows, "cell")
    w1_num = lax.psum_scatter(
        lax.dot_general(
            ratio2, h1_low2, (((1,), (1,)), ((), ())), preferred_element_type=jnp.float32
        ),
        "cell",
        scatter_dimension=0,
        tiled=True,
    )
    w1_new = (w1.astype(jnp.float32) * w1_num / rowsum[None, :]).astype(jnp.bfloat16)
    h2_new, w2_part, h2_part = layer_two(h1_new, w2, h2)
    w2_num, h2_rows = lax.psum((w2_part, h2_part), "cell")
    w2_new = w2 * w2_num / h2_rows[None, :]
    return (w1_new, h1_new, w2_new, h2_new)


def solution(mesh):
    placed = (P("gene", "cell"), P(("gene", "cell"), None), P(None, "cell"), P(), P(None, "cell"))
    return jax.shard_map(
        on_device,
        mesh=mesh,
        in_specs=placed,
        out_specs=(P(("gene", "cell"), None), P(None, "cell"), P(), P(None, "cell")),
        check_vma=False,
    )
```

profile of v0, /device:TPU:0, one launch (start us, length us, event | category | flops | bytes accessed | tf_op | source)
XLA Modules:
  0.0 255.0 jit_solution(3091493164891977610)
XLA Ops:
  7.2 0.0 all-gather.2.cloned.1.call-start
  7.2 0.7 all-gather.2.cloned.1.call-update
  7.9 0.0 copy-start.2
  7.9 0.0 copy-start.1
  7.9 0.0 all-reduce.4.cloned.1.call-start
  8.0 41.4 %all-gather.2.cloned.1.call-done = bf16[4096,512]{1,0:T(8,128)(2,1)} async-done(((bf16[512,512]{1,0:T(8,128)(2,1)}), bf16[4096,512]{1,0:T(8,128)(2,1)}) %all-gather.2.cloned.1.call-update) | async-done | bytes 4194320 | tf_op jit(solution)/shard_map/all_gather | solution.py:18
  49.3 11.9 %fusion.8 = f32[512,512]{0,1:T(8,128)} fusion(bf16[4096,512]{1,0:T(8,128)(2,1)} %all-gather.2.cloned.1.call-done, s32[4096,512]{1,0:T(8,128)} %param.5, f32[512,512]{1,0:T(8,128)} %param.7), kind=kOutput, calls=%fused_computation.12 | convolution fusion | flops 4301520896 | bytes 14680064 | tf_op jit(solution)/shard_map/dot_general | solution.py:23
  61.3 0.0 all-reduce.4.cloned.1.call-update
  61.3 0.0 all-reduce.6.cloned.1.call-start
  61.3 0.3 copy.9
  61.7 0.0 copy-done.1
  61.7 0.1 reduce_sum.38
  61.8 2.8 %convert_reduce_fusion = f32[512]{0:T(512)S(1)} fusion(bf16[4096,512]{1,0:T(8,128)(2,1)} %all-gather.2.cloned.1.call-done), kind=kLoop, calls=%fused_computation.2 | loop fusion | flops 4193792 | bytes 4196352 | tf_op jit(solution)/shard_map/reduce_sum | solution.py:26
  64.6 11.9 %psum.36 = f32[512]{0:T(512)S(1)} all-reduce(f32[512]{0:T(512)S(1)} %convert_reduce_fusion), channel_id=1, replica_groups=mesh['gene'=4,'cell'=8] {'gene'}, use_global_device_ids=true, to_apply=%region_2.0 | all-reduce | flops 512 | bytes 4096 | tf_op jit(solution)/shard_map/psum | solution.py:27
  76.5 36.9 %all-reduce.4.cloned.1.call-done = f32[512,512]{0,1:T(8,128)} async-done(((f32[512,512]{0,1:T(8,128)}), f32[512,512]{0,1:T(8,128)}) %all-reduce.4.cloned.1.call-update) | async-done | bytes 1048592 | tf_op jit(solution)/shard_map/psum | solution.py:27
  113.4 0.0 copy-done.5
  113.5 2.5 fusion.6
  115.9 1.2 fusion.16
  117.2 0.0 copy-start.4
  117.2 1.2 fusion.7
  118.4 1.5 fusion.17
  119.8 0.0 all-reduce.6.cloned.1.call-update
  119.8 0.2 reduce-scatter.2.cloned.1.call-start
  120.1 0.3 fusion.15
  120.4 12.5 %fusion.4 = f32[4096,512]{1,0:T(8,128)} fusion(s32[4096,512]{1,0:T(8,128)} %param.5, bf16[4096,512]{1,0:T(8,128)(2,1)} %all-gather.2.cloned.1.call-done, f32[512,512]{0,1:T(8,128)S(1)} %get-tuple-element.11), kind=kOutput, calls=%fused_computation.6 | convolution fusion | flops 4301783040 | bytes 22020096 | tf_op jit(solution)/shard_map/dot_general | solution.py:35
  132.9 0.0 reduce-scatter.2.cloned.1.call-update
  132.9 1.3 copy.10
  134.2 13.8 %all-reduce = (f32[512]{0:T(512)S(1)}, f32[64]{0:T(128)S(1)}) all-reduce(f32[512]{0:T(512)S(1)} %get-tuple-element.10, f32[64]{0:T(128)S(1)} %get-tuple-element.12), channel_id=1, replica_groups=mesh['gene'=4,'cell'=8] {'cell'}, use_global_device_ids=true, to_apply=%region_5.0 | all-reduce | flops 576 | bytes 4608 | tf_op jit(solution)/shard_map/psum | solution.py:33
  148.0 24.3 %all-reduce.6.cloned.1.call-done = f32[512,64]{0,1:T(8,128)} async-done(((f32[512,64]{0,1:T(8,128)}), f32[512,64]{0,1:T(8,128)}) %all-reduce.6.cloned.1.call-update) | async-done | bytes 131088 | tf_op jit(solution)/shard_map/psum | solution.py:44
  172.3 1.6 multiply_divide_fusion
  173.9 72.3 %reduce-scatter.2.cloned.1.call-done = f32[512,512]{1,0:T(8,128)} async-done(((f32[4096,512]{1,0:T(8,128)}), f32[512,512]{1,0:T(8,128)}) %reduce-scatter.2.cloned.1.call-update) | async-done | bytes 1048592 | tf_op jit(solution)/shard_map/reduce_scatter | solution.py:34
  246.3 2.2 divide_convert_fusion.4
  (7 shorter events, 0.0 us)
Async XLA Ops:
  7.2 42.2 %all-gather.2.cloned.1.call-start = ((), (), s32[]{:S(2)}) async-start(), calls=%async_computation.1 | async-start | bytes 4718592 | tf_op jit(solution)/shard_map/all_gather | solution.py:18
  7.9 53.4 %copy-start.2 = (f32[512,512]{1,0:T(8,128)S(1)}, f32[512,512]{1,0:T(8,128)}, u32[]{:S(2)}) copy-start(f32[512,512]{1,0:T(8,128)} %param.7) | copy-start | bytes 3145732
  7.9 53.8 %copy-start.1 = (f32[512,64]{0,1:T(8,128)S(1)}, f32[512,64]{0,1:T(8,128)}, u32[]{:S(2)}) copy-start(f32[512,64]{0,1:T(8,128)} %param.8) | copy-start | bytes 393220
  7.9 105.5 %all-reduce.4.cloned.1.call-start = ((), (), s32[]{:S(2)}) async-start(), calls=%async_computation.2 | async-start | bytes 2097152 | tf_op jit(solution)/shard_map/psum | solution.py:27
  61.3 52.2 %copy-start.5 = (f32[64,512]{1,0:T(8,128)S(1)}, f32[64,512]{1,0:T(8,128)}, u32[]{:S(2)}) copy-start(f32[64,512]{1,0:T(8,128)} %param.9) | copy-start | bytes 393220
  61.3 111.0 %all-reduce.6.cloned.1.call-start = ((), (), s32[]{:S(2)}) async-start(), calls=%async_computation.4 | async-start | bytes 262144 | tf_op jit(solution)/shard_map/psum | solution.py:44
  113.5 3.7 %copy-start.3 = (f32[512,512]{0,1:T(8,128)S(1)}, f32[512,512]{0,1:T(8,128)}, u32[]{:S(2)}) copy-start(f32[512,512]{0,1:T(8,128)} %all-reduce.4.cloned.1.call-done) | copy-start | bytes 3145732
  117.2 3.2 %copy-start.4 = (f32[64,512]{1,0:T(8,128)}, f32[64,512]{1,0:T(8,128)S(1)}, u32[]{:S(2)}) copy-start(f32[64,512]{1,0:T(8,128)S(1)} %get-tuple-element.13) | copy-start | bytes 393220
  119.8 126.4 %reduce-scatter.2.cloned.1.call-start = ((), (), s32[]{:S(2)}) async-start(), calls=%async_computation.3 | async-start | bytes 9437184 | tf_op jit(solution)/shard_map/reduce_scatter | solution.py:34
  132.9 113.4 %copy-start = (bf16[512,512]{1,0:T(8,128)(2,1)S(1)}, bf16[512,512]{1,0:T(8,128)(2,1)}, u32[]{:S(2)}) copy-start(bf16[512,512]{1,0:T(8,128)(2,1)} %param.6) | copy-start | bytes 1572868
Sparse Core Ops, SparseCore 0:
  9.9 39.4 all-gather.1
  61.4 51.9 all-reduce.3
  120.0 52.2 all-reduce.5
  175.6 70.6 reduce-scatter.1
where the time goes:
time: 255 us
  waiting for transfers between devices  176 us (69%)
  matrix products  30.7 us (12%)
  blocking collectives  25.7 us (10%)
  between operations  13.8 us (5%)
  other arithmetic  7.07 us (3%)
    reduce_scatter x1, waiting for transfers between devices, on_device(): lax.psum_scatter(lax.dot_general(ratio2, h1_low2, (((1,), (1,)), ((), ())...  72.3 us
    all_gather x1, waiting for transfers between devices, on_device(): w1_block = lax.all_gather(w1, 'cell', axis=0, tiled=True)  41.4 us
    psum x1, waiting for transfers between devices, on_device(): h1_num, colsum = lax.psum((partial_num, partial_col), 'gene')  36.9 us
    psum x1, waiting for transfers between devices, on_device(): w2_num, h2_rows = lax.psum((w2_part, h2_part), 'cell')  24.3 us
    psum x1, blocking collectives, on_device(): rowsum = lax.psum(local_rows, 'cell')  13.8 us
    dot_general x1, matrix products, on_device(): lax.dot_general(ratio2, h1_low2, (((1,), (1,)), ((), ())), preferred_elem...  12.5 us
    psum x1, blocking collectives, on_device(): h1_num, colsum = lax.psum((partial_num, partial_col), 'gene')  11.9 us
    dot_general x1, matrix products, on_device(): lax.dot_general(w1_block, ratio, (((0,), (0,)), ((), ())), preferred_elem...  11.9 us
  transfers between devices with their start and end apart: 4, of which 4 were waited for; matrix products, arithmetic and copies ran while one was open for 7% of the time, Pallas kernels for 0%

commit v1 on v0

v1 whole, which is shorter than its diff:
```python
import functools

import jax
import jax.numpy as jnp
from jax import lax
from jax.experimental import pallas as pl
from jax.experimental.pallas import tpu as pltpu
from jax.sharding import PartitionSpec as P

F32 = jnp.float32
BF16 = jnp.bfloat16
PAD = 16
VMEM_LIMIT = 56 * 1024 * 1024


def params():
    return pltpu.CompilerParams(vmem_limit_bytes=VMEM_LIMIT)


def mm(a, b, dims):
    return lax.dot_general(a, b, ((dims[:1], dims[1:]), ((), ())), preferred_element_type=F32)


def encode(x, out_ref):
    rows = x.shape[0]
    top = jnp.maximum(jnp.max(x, axis=0, keepdims=True), 1e-30)
    power = jnp.ceil(jnp.log2(top))
    q = jnp.minimum(x * (jnp.exp2(-power) * 65535.0) + 0.5, 65535.0)
    out_ref[:rows, :] = (q.astype(jnp.int32) - 32768).astype(jnp.int16)
    out_ref[rows:, :] = jnp.broadcast_to(power, (PAD, x.shape[1])).astype(jnp.int32).astype(jnp.int16)


def decode(ref):
    rows = ref.shape[0] - PAD
    power = ref[rows:, :].astype(jnp.int32).astype(F32)[:1]
    unit = jnp.exp2(power) * (1.0 / 65535.0)
    return (ref[:rows, :].astype(jnp.int32) + 32768).astype(F32) * unit


def coded(rows, cols):
    return jax.ShapeDtypeStruct((rows + PAD, cols), jnp.int16)


def whole_spec(shape):
    return pl.BlockSpec(shape, lambda *_: (0,) * len(shape))


def pick(pieces, scratch):
    for k, piece in enumerate(pieces):
        @pl.when(pl.program_id(0) == k)
        def _():
            scratch[...] = piece[...]


def quotient(v_ref, approx):
    return (v_ref[...].astype(jnp.int32).astype(F32) / approx).astype(BF16)


def first_body(n, has_acc, *refs):
    _, _, *pieces = refs[: n + 2]
    ha, hb, va, vb, *rest = refs[n + 2 :]
    if has_acc:
        acc_a_in, acc_b_in, acc_a, acc_b, scratch = rest
    else:
        acc_a, acc_b, scratch = rest
    pick(pieces, scratch)

    @pl.when(pl.program_id(0) == 0)
    def _():
        if has_acc:
            acc_a[...] = acc_a_in[...]
            acc_b[...] = acc_b_in[...]
        else:
            acc_a[...] = jnp.zeros_like(acc_a)
            acc_b[...] = jnp.zeros_like(acc_b)

    w = scratch[...]
    for h, v, acc in ((ha, va, acc_a), (hb, vb, acc_b)):
        ratio = quotient(v, mm(w, h[...], (1, 0)))
        acc[...] += mm(w, ratio, (0, 0))


def first(pieces, at_a, at_b, ha, hb, va, vb, acc=None):
    n, (t, k) = len(pieces), pieces[0].shape
    cells = va.shape[1]
    num = jax.ShapeDtypeStruct((k, cells), F32)
    in_specs = [whole_spec((t, k))] * n + [whole_spec((k, cells))] * 2
    in_specs += [
        pl.BlockSpec((t, cells), lambda i, a, b: (a[i], 0)),
        pl.BlockSpec((t, cells), lambda i, a, b: (b[i], 0)),
    ]
    args = [*pieces, ha, hb, va, vb]
    aliases = {}
    if acc is not None:
        aliases = {2 + len(args): 0, 3 + len(args): 1}
        args += list(acc)
        in_specs += [whole_spec((k, cells))] * 2
    return pl.pallas_call(
        functools.partial(first_body, n, acc is not None),
        out_shape=(num, num),
        grid_spec=pltpu.PrefetchScalarGridSpec(
            num_scalar_prefetch=2,
            grid=(n,),
            in_specs=in_specs,
            out_specs=[whole_spec((k, cells))] * 2,
            scratch_shapes=[pltpu.VMEM((t, k), BF16)],
        ),
        input_output_aliases=aliases,
        compiler_params=params(),
        cost_estimate=pl.CostEstimate(
            flops=8 * n * t * k * cells, bytes_accessed=n * t * cells * 6, transcendentals=0
        ),
        name="first_products",
    )(at_a, at_b, *args)


def second_body(n, code, *refs):
    _, _, *pieces = refs[: n + 2]
    ha, hb, va, vb, *rest = refs[n + 2 :]
    outs, scratch = rest[:n], rest[n]
    pick(pieces, scratch)
    w = scratch[...]
    total = 0.0
    for h, v in ((ha, va), (hb, vb)):
        low = h[...]
        total += mm(quotient(v, mm(w, low, (1, 0))), low, (1, 1))
    for k, out in enumerate(outs):
        @pl.when(pl.program_id(0) == k)
        def _():
            if code:
                encode(total, out)
            else:
                out[...] = total


def second(pieces, at_a, at_b, ha, hb, va, vb, code):
    n, (t, k) = len(pieces), pieces[0].shape
    cells = va.shape[1]
    out = coded(t, k) if code else jax.ShapeDtypeStruct((t, k), F32)
    in_specs = [whole_spec((t, k))] * n + [whole_spec((k, cells))] * 2
    in_specs += [
        pl.BlockSpec((t, cells), lambda i, a, b: (a[i], 0)),
        pl.BlockSpec((t, cells), lambda i, a, b: (b[i], 0)),
    ]
    return pl.pallas_call(
        functools.partial(second_body, n, code),
        out_shape=(out,) * n,
        grid_spec=pltpu.PrefetchScalarGridSpec(
            num_scalar_prefetch=2,
            grid=(n,),
            in_specs=in_specs,
            out_specs=[whole_spec(out.shape)] * n,
            scratch_shapes=[pltpu.VMEM((t, k), BF16)],
        ),
        compiler_params=params(),
        cost_estimate=pl.CostEstimate(
            flops=8 * n * t * k * cells, bytes_accessed=n * t * cells * 6, transcendentals=0
        ),
        name="second_products",
    )(at_a, at_b, *pieces, ha, hb, va, vb)


def plain(body, outs, *args, name):
    return pl.pallas_call(body, out_shape=outs, compiler_params=params(), name=name)(*args)


def flip(x, axis, size, bit):
    return lax.ppermute(x, axis, [(i, i ^ bit) for i in range(size)])


def add_core_and_encode(a_ref, b_ref, lo_ref, hi_ref):
    half = a_ref.shape[0] // 2
    encode(a_ref[:half, :] + b_ref[:half, :], lo_ref)
    encode(a_ref[half:, :] + b_ref[half:, :], hi_ref)


def add_and_encode(lo, lo_in, hi, hi_in, lo_ref, hi_ref):
    encode(decode(lo) + decode(lo_in), lo_ref)
    encode(decode(hi) + decode(hi_in), hi_ref)


def h1_update(lo, lo_in, hi, hi_in, h1_ref, col_ref, new_ref, low_ref):
    half = h1_ref.shape[0] // 2
    for at, one, other in ((0, lo, lo_in), (half, hi, hi_in)):
        rows = pl.ds(at, half)
        new = h1_ref[rows, :] * (decode(one) + decode(other)) / col_ref[rows, :1]
        new_ref[rows, :] = new
        low_ref[rows, :] = new.astype(BF16)


def h1_update_plain(num, h1_ref, col_ref, new_ref, low_ref):
    new = h1_ref[...] * num[...] / col_ref[:, :1]
    new_ref[...] = new
    low_ref[...] = new.astype(BF16)


def relay_add(x, x_in, y, y_in, x_ref, y_ref):
    encode(x[...] + decode(x_in), x_ref)
    encode(y[...] + decode(y_in), y_ref)


def w1_update(own0, own1, x0, x1, y0, y1, w_ref, row_ref, out_ref):
    t = own0.shape[0]
    row = row_ref[:1, :]
    for at, parts in ((0, (own0, x0, y0)), (t, (own1, x1, y1))):
        total = parts[0][...] + decode(parts[1]) + decode(parts[2])
        w = w_ref[pl.ds(at, t), :].astype(F32)
        out_ref[pl.ds(at, t), :] = (w * total / row).astype(BF16)


def layer_two(h1_new, w2, h2):
    hi = lax.Precision.HIGHEST
    ratio3 = h1_new / jnp.dot(w2, h2, precision=hi)
    h2_new = h2 * jnp.dot(w2.T, ratio3, precision=hi) / jnp.sum(w2, axis=0)[:, None]
    ratio4 = h1_new / jnp.dot(w2, h2_new, precision=hi)
    w2_part = lax.dot_general(h2_new, ratio4, (((1,), (1,)), ((), ())), precision=hi)
    return h2_new, w2_part, jnp.sum(h2_new, axis=1)


def on_device(n_gene, n_cell, counts, w1, h1, w2, h2):
    genes, cells = counts.shape
    rows, k1 = w1.shape
    k2 = w2.shape[1]
    chips = n_cell // 2
    me = lax.axis_index("cell")
    core, chip = me % 2, me // 2
    rings = n_cell == 8 and n_gene == 4
    cell = functools.partial(flip, axis="cell", size=n_cell)
    gene = functools.partial(flip, axis="gene", size=n_gene)

    col = jnp.sum(w1.astype(F32), axis=0)[None, :]
    if rings:
        col = jnp.broadcast_to(col, (8, k1))
        for bit in (1, 2, 4):
            col = col + cell(col, bit=bit)
        for bit in (1, 3):
            col = col + gene(col, bit=bit)
        col = col[0]
    else:
        col = lax.psum(col, ("gene", "cell"))[0]
    col = jnp.broadcast_to(col[:, None], (k1, 128))

    h1_low = h1.astype(BF16)
    pairs = counts.reshape(chips, 2, rows, cells)
    theirs = lax.dynamic_index_in_dim(pairs, 1 - core, axis=1, keepdims=False)
    v_other = cell(theirs.astype(jnp.int16), bit=1).reshape(chips * rows, cells)
    h1_low_other = cell(h1_low, bit=1)

    if rings:
        t = rows // 2
        w_lo, w_hi = w1[:t], w1[t:]
        x_hi, y_lo = cell(w_hi, bit=2), cell(w_lo, bit=4)
        x_lo, y_hi = cell(w_lo, bit=2), cell(w_hi, bit=4)
        d_lo, d_hi = cell(y_lo, bit=2), cell(x_hi, bit=4)

        def places(*which):
            chip_at = jnp.stack([chip ^ d for d, _ in which])
            half = jnp.array([h for _, h in which], jnp.int32)
            return (chip_at * 2 + core) * 2 + half, chip_at * 2 + half

        own, near = places((0, 0), (0, 1)), places((1, 0), (1, 1), (2, 0), (2, 1))
        far = places((3, 0), (3, 1))
        data = (h1_low, h1_low_other, counts, v_other)
        acc = first((w_lo, w_hi), *own, *data)
        acc = first((x_lo, x_hi, y_lo, y_hi), *near, *data, acc)
        num, num_other = first((d_lo, d_hi), *far, *data, acc)
        num_in = cell(num_other, bit=1)
        half = coded(k1 // 2, cells)
        lo, hi = plain(add_core_and_encode, (half, half), num, num_in, name="encode_h1_num")
        lo_in, hi_in = gene(lo, bit=1), gene(hi, bit=3)
        lo, hi = plain(add_and_encode, (half, half), lo, lo_in, hi, hi_in, name="add_h1_num")
        lo_in, hi_in = gene(lo, bit=3), gene(hi, bit=1)
        h1_new, h1_low2 = plain(
            h1_update,
            (jax.ShapeDtypeStruct((k1, cells), F32), jax.ShapeDtypeStruct((k1, cells), BF16)),
            lo, lo_in, hi, hi_in, h1, col, name="h1_update",
        )
        h1_low2_other = cell(h1_low2, bit=1)

        data = (h1_low2, h1_low2_other, counts, v_other)
        d_lo, d_hi = second((d_lo, d_hi), *far, *data, True)
        y_in, x_in = cell(d_lo, bit=2), cell(d_hi, bit=4)
        x_lo2, y_hi2 = second((x_lo, y_hi), *places((1, 0), (2, 1)), *data, True)
        x_lo_in, y_hi_in = cell(x_lo2, bit=2), cell(y_hi2, bit=4)
        x_hi2, y_lo2 = second((x_hi, y_lo), *places((1, 1), (2, 0)), *data, False)
        piece = coded(t, k1)
        x_hi2, y_lo2 = plain(relay_add, (piece, piece), x_hi2, x_in, y_lo2, y_in, name="relay_add")
        x_hi_in, y_lo_in = cell(x_hi2, bit=2), cell(y_lo2, bit=4)
        own0, own1 = second((w_lo, w_hi), *own, *data, False)
    else:
        groups = [list(range(c, n_cell, 2)) for c in (0, 1)]
        w_all = lax.all_gather(w1, "cell", axis=0, tiled=True, axis_index_groups=groups)
        pieces = [w_all[i * rows : (i + 1) * rows] for i in range(chips)]
        at = jnp.arange(chips, dtype=jnp.int32)
        at = (at * 2 + core, at)
        num, num_other = first(pieces, *at, h1_low, h1_low_other, counts, v_other)
        num = lax.psum(num + cell(num_other, bit=1), "gene")
        h1_new, h1_low2 = plain(
            h1_update_plain,
            (jax.ShapeDtypeStruct((k1, cells), F32), jax.ShapeDtypeStruct((k1, cells), BF16)),
            num, h1, col, name="h1_update",
        )
        h1_low2_other = cell(h1_low2, bit=1)
        parts = second(pieces, *at, h1_low2, h1_low2_other, counts, v_other, False)
        w1_num = lax.psum_scatter(
            jnp.concatenate(parts), "cell", scatter_dimension=0, tiled=True, axis_index_groups=groups
        )

    h2_new, w2_part, h2_part = layer_two(h1_new, w2, h2)
    small = jnp.concatenate(
        [w2_part, jnp.sum(h1_new, axis=1)[None, :], jnp.pad(h2_part, (0, k1 - k2))[None, :], jnp.zeros((6, k1), F32)]
    )
    if rings:
        for bit in (1, 2, 4):
            small = small + cell(small, bit=bit)
    else:
        small = lax.psum(small, "cell")
    w2_num, rowsum, h2_rows = small[:k2], small[k2 : k2 + 1], small[k2 + 1, :k2]
    w2_new = w2 * w2_num.T / h2_rows[None, :]
    if rings:
        w1_new = plain(
            w1_update, jax.ShapeDtypeStruct((rows, k1), BF16),
            own0, own1, x_lo_in, x_hi_in, y_lo_in, y_hi_in, w1, rowsum, name="w1_update",
        )
    else:
        w1_new = (w1.astype(F32) * w1_num / rowsum).astype(BF16)
    return (w1_new, h1_new, w2_new, h2_new)


def solution(mesh):
    placed = (P("gene", "cell"), P(("gene", "cell"), None), P(None, "cell"), P(), P(None, "cell"))
    return jax.shard_map(
        functools.partial(on_device, mesh.shape["gene"], mesh.shape["cell"]),
        mesh=mesh,
        in_specs=placed,
        out_specs=(P(("gene", "cell"), None), P(None, "cell"), P(), P(None, "cell")),
        check_vma=False,
    )
```

time: 255 us -> 155 us (0.61)
  waiting for transfers between devices: 176 us -> 45.2 us
  Pallas kernels: 0 us -> 54.9 us
  starting transfers between devices: 0.34 us -> 29.6 us
  blocking collectives: 25.7 us -> 0 us
  matrix products: 30.7 us -> 5.37 us
  between operations: 13.8 us -> 1.01 us
  local copies, waits for them, and re-layouts: 1.66 us -> 8.73 us
  other arithmetic: 7.07 us -> 10.2 us
    reduce_scatter x1 -> x0, waiting for transfers between devices: 72.3 us -> none  [on_device(): lax.psum_scatter(lax.dot_general(ratio2, h1_low2, (((1,), (1,)), ((), ())...]
    psum x2 -> x0, waiting for transfers between devices: 61.2 us -> none  [the longest x1 36.9 us: on_device(): h1_num, colsum = lax.psum((partial_num, partial_col), 'gene')]
    pallas_call x0 -> x12, Pallas kernels: none -> 54.9 us  [the longest x4 20.5 us: second(): pl.pallas_call(functools.partial(second_body, n, code), out_shape=(out,)...]
    ppermute x0 -> x28, waiting for transfers between devices: none -> 45.2 us  [flip(): return lax.ppermute(x, axis, [(i, i ^ bit) for i in range(size)])]
    all_gather x1 -> x0, waiting for transfers between devices: 41.4 us -> none  [on_device(): w1_block = lax.all_gather(w1, 'cell', axis=0, tiled=True)]
    ppermute x0 -> x28, starting transfers between devices: none -> 29.6 us  [flip(): return lax.ppermute(x, axis, [(i, i ^ bit) for i in range(size)])]
    psum x2 -> x0, blocking collectives: 25.7 us -> none  [the longest x1 13.8 us: on_device(): rowsum = lax.psum(local_rows, 'cell')]
    dot_general x3 -> x1, matrix products: 25.9 us -> 1.12 us  [layer_two(): lax.dot_general(h2_new, ratio4, (((1,), (1,)), ((), ())), precision=hi)]
  transfers between devices with their start and end apart: 4 -> 28, of which waited for: 4 -> 12; matrix products, arithmetic and copies ran while one was open for 7% -> 4% of each run, Pallas kernels for 0% -> 22%
where the time goes in v1:
time: 155 us
  Pallas kernels  54.9 us (35%)
  waiting for transfers between devices  45.2 us (29%)
  starting transfers between devices  29.6 us (19%)
  other arithmetic  10.2 us (7%)
  local copies, waits for them, and re-layouts  8.73 us (6%)
  matrix products  5.37 us (3%)
    ppermute x28, waiting for transfers between devices, flip(): return lax.ppermute(x, axis, [(i, i ^ bit) for i in range(size)])  45.2 us
    ppermute x28, starting transfers between devices, flip(): return lax.ppermute(x, axis, [(i, i ^ bit) for i in range(size)])  29.6 us
    pallas_call x4, Pallas kernels, second(): pl.pallas_call(functools.partial(second_body, n, code), out_shape=(out,)...  20.5 us
    pallas_call x3, Pallas kernels, first(): pl.pallas_call(functools.partial(first_body, n, acc is not None), out_sha...  20.4 us
    pallas_call x5, Pallas kernels, plain(): pl.pallas_call(body, out_shape=outs, compiler_params=params(), name=name)  14.1 us
    unnamed x52, local copies, waits for them, and re-layouts  6.42 us
    convert_element_type x1, other arithmetic, on_device(): v_other = cell(theirs.astype(jnp.int16), bit=1).reshape(chips * rows, cells)  3.86 us
    add x6, other arithmetic, places(): return ((chip_at * 2 + core) * 2 + half, chip_at * 2 + half)  3.58 us
  transfers between devices with their start and end apart: 28, of which 12 were waited for; matrix products, arithmetic and copies ran while one was open for 4% of the time, Pallas kernels for 22%

profile of v1, /device:TPU:0, one launch (start us, length us, event | category | flops | bytes accessed | tf_op | source)
XLA Modules:
  0.0 154.9 jit_solution(2608862788401154157)
XLA Ops:
  0.7 3.9 %fusion = s16[4,512,512]{2,1,0:T(8,128)(2,1)} fusion(s32[4,2,512,512]{3,2,1,0:T(8,128)} %bitcast.41, s32[]{:T(128)S(6)} %select_n.17), kind=kLoop, calls=%fused_computation.1 | loop fusion | flops 1048576 | bytes 6291460 | tf_op jit(solution)/shard_map/convert_element_type | solution.py:246
  5.8 2.5 %collective-permute-start = (bf16[256,512]{1,0:T(8,128)(2,1)}, bf16[256,512]{1,0:T(8,128)(2,1)}, u32[]{:S(2)}, u32[]{:S(2)}) collective-permute-start(bf16[256,512]{1,0:T(8,128)(2,1)} %get-tuple-element.53.refs_2_), channel_id=1, source_target_pairs={{0,4},{1,5},{2,6},{3,7},{4,0},{5,1},{6,2},{7,3},{8,12},{9,13},{10,... | collective-permute-start | bytes 786440 | tf_op jit(solution)/shard_map/ppermute | solution.py:168
  11.7 3.9 %collective-permute-done.refs_4_.refs_3_ = bf16[256,512]{1,0:T(8,128)(2,1)} collective-permute-done((bf16[256,512]{1,0:T(8,128)(2,1)}, bf16[256,512]{1,0:T(8,128)(2,1)}, u32[]{:S(2)}, u32[]{:S(2)}) %collective-permute-start) | collective-permute-done | bytes 262176 | tf_op jit(solution)/shard_map/ppermute | solution.py:168
  15.6 1.7 %collective-permute-start.7 = (bf16[256,512]{1,0:T(8,128)(2,1)S(1)}, bf16[256,512]{1,0:T(8,128)(2,1)}, u32[]{:S(2)}, u32[]{:S(2)}) collective-permute-start(bf16[256,512]{1,0:T(8,128)(2,1)S(1)} %get-tuple-element.52.refs_3_), channel_id=1, source_target_pairs={{0,4},{1,5},{2,6},{3,7},{4,0},{5,1},{6,2},{7,3},{8,12},{9,13},{10,... | collective-permute-start | bytes 786440 | tf_op jit(solution)/shard_map/ppermute | solution.py:168
  18.5 4.1 %collective-permute-done.2.refs_3_.refs_2_ = bf16[256,512]{1,0:T(8,128)(2,1)} collective-permute-done((bf16[256,512]{1,0:T(8,128)(2,1)S(1)}, bf16[256,512]{1,0:T(8,128)(2,1)}, u32[]{:S(2)}, u32[]{:S(2)}) %collective-permute-start.2) | collective-permute-done | bytes 262176 | tf_op jit(solution)/shard_map/ppermute | solution.py:168
  25.9 5.5 %first_products.3 = (f32[512,512]{1,0:T(8,128)}, f32[512,512]{1,0:T(8,128)}) custom-call(s32[2]{0:T(128)} %get-tuple-element.60.refs_0_, s32[2]{0:T(128)} %get-tuple-element.59.refs_1_, bf16[256,512]{1,0:T(8,128)(2,1)} %get-tuple-element.53.refs_2_, bf16[256,512]{1,0:T(8,128)(2,1)} %copy-done.6, bf16[512,512]{1,0:T(8,128)(2,1)} %copy-done.3, ...), custom_call_target="tpu_custom_call" | custom-call | flops 1073741824 | bytes 1572864 | tf_op jit(solution)/shard_map/first_products/pallas_call | solution.py:98
  31.5 8.5 %first_products.4 = (f32[512,512]{1,0:T(8,128)}, f32[512,512]{1,0:T(8,128)}) custom-call(s32[4]{0:T(128)} %multiply_add_fusion.refs_0_, s32[4]{0:T(128)} %get-tuple-element.50.refs_1_, bf16[256,512]{1,0:T(8,128)(2,1)} %collective-permute-done.6.refs_2_, ...), custom_call_target="tpu_custom_call", output_to_operand_aliasing={{0}: (10, {}), {1}: (11, {})} | custom-call | flops 2147483648 | bytes 3145728 | tf_op jit(solution)/shard_map/first_products/pallas_call | solution.py:98
  40.8 6.3 %first_products.5 = (f32[512,512]{1,0:T(8,128)}, f32[512,512]{1,0:T(8,128)}) custom-call(s32[2]{0:T(128)} %get-tuple-element.62.refs_0_, s32[2]{0:T(128)} %get-tuple-element.61.refs_1_, bf16[256,512]{1,0:T(8,128)(2,1)} %copy-done.8, bf16[256,512]{1,0:T(8,128)(2,1)} %copy-done.9, ...), custom_call_target="tpu_custom_call", output_to_operand_aliasing={{0}: (8, {}), {1}: (9, {})} | custom-call | flops 1073741824 | bytes 1572864 | tf_op jit(solution)/shard_map/first_products/pallas_call | solution.py:98
  47.1 2.9 %collective-permute-done.8.b_ref = f32[512,512]{1,0:T(8,128)S(1)} collective-permute-done((f32[512,512]{1,0:T(8,128)}, f32[512,512]{1,0:T(8,128)S(1)}, u32[]{:S(2)}, u32[]{:S(2)}) %collective-permute-start.8) | collective-permute-done | bytes 1048608 | tf_op jit(solution)/shard_map/ppermute | solution.py:168
  51.0 2.7 %encode_h1_num.1 = (s16[272,512]{1,0:T(8,128)(2,1)}, s16[272,512]{1,0:T(8,128)(2,1)}) custom-call(f32[512,512]{1,0:T(8,128)} %get-tuple-element.30.a_ref, f32[512,512]{1,0:T(8,128)} %copy-done.11), custom_call_target="tpu_custom_call" | custom-call | tf_op jit(solution)/shard_map/encode_h1_num/pallas_call | solution.py:164
  53.7 3.6 %collective-permute-start.10 = (s16[272,512]{1,0:T(8,128)(2,1)}, s16[272,512]{1,0:T(8,128)(2,1)S(1)}, u32[]{:S(2)}, u32[]{:S(2)}) collective-permute-start(s16[272,512]{1,0:T(8,128)(2,1)} %get-tuple-element.33.hi), channel_id=1, source_target_pairs={{0,24},{8,16},{16,8},{24,0},{1,25},{9,17},{17,9},{25,1},{2,26},{10... | collective-permute-start | bytes 835592 | tf_op jit(solution)/shard_map/ppermute | solution.py:168
  59.2 6.1 %collective-permute-done.10.hi_in = s16[272,512]{1,0:T(8,128)(2,1)S(1)} collective-permute-done((s16[272,512]{1,0:T(8,128)(2,1)}, s16[272,512]{1,0:T(8,128)(2,1)S(1)}, u32[]{:S(2)}, u32[]{:S(2)}) %collective-permute-start.10) | collective-permute-done | bytes 278560 | tf_op jit(solution)/shard_map/ppermute | solution.py:168
  65.3 5.2 %collective-permute-done.9.lo_in = s16[272,512]{1,0:T(8,128)(2,1)S(1)} collective-permute-done((s16[272,512]{1,0:T(8,128)(2,1)}, s16[272,512]{1,0:T(8,128)(2,1)S(1)}, u32[]{:S(2)}, u32[]{:S(2)}) %collective-permute-start.9) | collective-permute-done | bytes 278560 | tf_op jit(solution)/shard_map/ppermute | solution.py:168
  71.2 2.6 %add_h1_num.1 = (s16[272,512]{1,0:T(8,128)(2,1)}, s16[272,512]{1,0:T(8,128)(2,1)}) custom-call(s16[272,512]{1,0:T(8,128)(2,1)} %get-tuple-element.32.lo, s16[272,512]{1,0:T(8,128)(2,1)} %copy-done.18, s16[272,512]{1,0:T(8,128)(2,1)} %get-tuple-element.33.hi, s16[272,512]{1,0:T(8,128)(2,1)} %copy-done.17), custom_call_target="tpu_custom_call" | custom-call | tf_op jit(solution)/shard_map/add_h1_num/pallas_call | solution.py:164
  73.9 1.6 %collective-permute-start.11 = (s16[272,512]{1,0:T(8,128)(2,1)}, s16[272,512]{1,0:T(8,128)(2,1)S(1)}, u32[]{:S(2)}, u32[]{:S(2)}) collective-permute-start(s16[272,512]{1,0:T(8,128)(2,1)} %get-tuple-element.34.lo), channel_id=1, source_target_pairs={{0,24},{8,16},{16,8},{24,0},{1,25},{9,17},{17,9},{25,1},{2,26},{10... | collective-permute-start | bytes 835592 | tf_op jit(solution)/shard_map/ppermute | solution.py:168
  75.8 1.6 %collective-permute-start.15 = (f32[8,512]{1,0:T(8,128)S(1)}, f32[8,512]{1,0:T(8,128)S(1)}, u32[]{:S(2)}, u32[]{:S(2)}) collective-permute-start(f32[8,512]{1,0:T(8,128)S(1)} %fusion.21), channel_id=1, source_target_pairs={{0,4},{1,5},{2,6},{3,7},{4,0},{5,1},{6,2},{7,3},{8,12},{9,13},{10,... | collective-permute-start | bytes 49160 | tf_op jit(solution)/shard_map/ppermute | solution.py:168
  77.4 2.2 %collective-permute-done.15 = f32[8,512]{1,0:T(8,128)S(1)} collective-permute-done((f32[8,512]{1,0:T(8,128)S(1)}, f32[8,512]{1,0:T(8,128)S(1)}, u32[]{:S(2)}, u32[]{:S(2)}) %collective-permute-start.15) | collective-permute-done | bytes 16416 | tf_op jit(solution)/shard_map/ppermute | solution.py:168
  79.6 1.8 %collective-permute-start.16 = (f32[8,512]{1,0:T(8,128)S(1)}, f32[8,512]{1,0:T(8,128)S(1)}, u32[]{:S(2)}, u32[]{:S(2)}) collective-permute-start(f32[8,512]{1,0:T(8,128)S(1)} %add.103), channel_id=1, source_target_pairs={{0,8},{8,0},{16,24},{24,16},{1,9},{9,1},{17,25},{25,17},{2,10},{10... | collective-permute-start | bytes 49160 | tf_op jit(solution)/shard_map/ppermute | solution.py:168
  81.3 8.0 %collective-permute-done.16 = f32[8,512]{1,0:T(8,128)S(1)} collective-permute-done((f32[8,512]{1,0:T(8,128)S(1)}, f32[8,512]{1,0:T(8,128)S(1)}, u32[]{:S(2)}, u32[]{:S(2)}) %collective-permute-start.16) | collective-permute-done | bytes 16416 | tf_op jit(solution)/shard_map/ppermute | solution.py:168
  89.4 2.2 %collective-permute-start.17 = (f32[8,512]{1,0:T(8,128)S(1)}, f32[8,512]{1,0:T(8,128)S(1)}, u32[]{:S(2)}, u32[]{:S(2)}) collective-permute-start(f32[8,512]{1,0:T(8,128)S(1)} %add.104), channel_id=1, source_target_pairs={{0,24},{8,16},{16,8},{24,0},{1,25},{9,17},{17,9},{25,1},{2,26},{10... | collective-permute-start | bytes 49160 | tf_op jit(solution)/shard_map/ppermute | solution.py:168
  91.7 3.2 %collective-permute-done.17 = f32[8,512]{1,0:T(8,128)S(1)} collective-permute-done((f32[8,512]{1,0:T(8,128)S(1)}, f32[8,512]{1,0:T(8,128)S(1)}, u32[]{:S(2)}, u32[]{:S(2)}) %collective-permute-start.17) | collective-permute-done | bytes 16416 | tf_op jit(solution)/shard_map/ppermute | solution.py:168
  95.8 3.2 %h1_update.1 = (f32[512,512]{1,0:T(8,128)}, bf16[512,512]{1,0:T(8,128)(2,1)}) custom-call(s16[272,512]{1,0:T(8,128)(2,1)} %get-tuple-element.34.lo, s16[272,512]{1,0:T(8,128)(2,1)} %copy-done.13, s16[272,512]{1,0:T(8,128)(2,1)} %get-tuple-element.35.hi, s16[272,512]{1,0:T(8,128)(2,1)} %copy-done.14, f32[512,512]{1,0:T(8,128)} %h1_ref.1, ...), custom_call_target="tpu_custom_call" | custom-call | tf_op jit(solution)/shard_map/h1_update/pallas_call | solution.py:164
  100.5 2.3 %convolution_divide_fusion = f32[512,512]{1,0:T(8,128)S(1)} fusion(f32[512,512]{1,0:T(8,128)} %get-tuple-element.23, f32[512,64]{0,1:T(8,128)S(1)} %copy-done.7, f32[64,512]{1,0:T(8,128)S(1)} %copy-done.23), kind=kOutput, calls=%fused_computation.4 | convolution fusion | flops 201588736 | bytes 2359296 | tf_op jit(solution)/shard_map/dot_general | solution.py:213
  109.0 4.5 %collective-permute-done.26 = f32[72,512]{1,0:T(8,128)S(1)} collective-permute-done((f32[72,512]{1,0:T(8,128)S(1)}, f32[72,512]{1,0:T(8,128)S(1)}, u32[]{:S(2)}, u32[]{:S(2)}) %collective-permute-start.26) | collective-permute-done | bytes 147488 | tf_op jit(solution)/shard_map/ppermute | solution.py:168
  113.5 1.6 %collective-permute-start.27 = (f32[72,512]{1,0:T(8,128)S(1)}, f32[72,512]{1,0:T(8,128)S(1)}, u32[]{:S(2)}, u32[]{:S(2)}) collective-permute-start(f32[72,512]{1,0:T(8,128)S(1)} %add.112), channel_id=1, source_target_pairs={{0,4},{1,5},{2,6},{3,7},{4,0},{5,1},{6,2},{7,3},{8,12},{9,13},{10,... | collective-permute-start | bytes 442376 | tf_op jit(solution)/shard_map/ppermute | solution.py:168
  115.7 3.0 %collective-permute-done.27 = f32[72,512]{1,0:T(8,128)S(1)} collective-permute-done((f32[72,512]{1,0:T(8,128)S(1)}, f32[72,512]{1,0:T(8,128)S(1)}, u32[]{:S(2)}, u32[]{:S(2)}) %collective-permute-start.27) | collective-permute-done | bytes 147488 | tf_op jit(solution)/shard_map/ppermute | solution.py:168
  119.6 5.1 %second_products.7 = (s16[272,512]{1,0:T(8,128)(2,1)}, s16[272,512]{1,0:T(8,128)(2,1)}) custom-call(s32[2]{0:T(128)} %get-tuple-element.62.refs_0_, s32[2]{0:T(128)} %get-tuple-element.61.refs_1_, bf16[256,512]{1,0:T(8,128)(2,1)} %copy-done.8, bf16[256,512]{1,0:T(8,128)(2,1)} %copy-done.9, bf16[512,512]{1,0:T(8,128)(2,1)} %get-tuple-element.36.refs_4_, ...), custom_call_target="tpu_custom_call" | custom-call | flops 1073741824 | bytes 1572864 | tf_op jit(solution)/shard_map/second_products/pallas_call | solution.py:145
  127.3 5.1 %second_products.5 = (s16[272,512]{1,0:T(8,128)(2,1)}, s16[272,512]{1,0:T(8,128)(2,1)}) custom-call(s32[2]{0:T(128)} %get-tuple-element.56.refs_0_, s32[2]{0:T(128)} %get-tuple-element.55.refs_1_, bf16[256,512]{1,0:T(8,128)(2,1)} %collective-permute-done.6.refs_2_, bf16[256,512]{1,0:T(8,128)(2,1)} %collective-permute-done.7.refs_5_.refs_3_, ...), custom_call_target="tpu_custom_call" | custom-call | flops 1073741824 | bytes 1572864 | tf_op jit(solution)/shard_map/second_products/pallas_call | solution.py:145
  134.5 5.2 %second_products.6 = (f32[256,512]{1,0:T(8,128)}, f32[256,512]{1,0:T(8,128)}) custom-call(s32[2]{0:T(128)} %get-tuple-element.54.refs_0_, s32[2]{0:T(128)} %get-tuple-element.48.refs_1_, bf16[256,512]{1,0:T(8,128)(2,1)} %collective-permute-done.2.refs_3_.refs_2_, bf16[256,512]{1,0:T(8,128)(2,1)} %collective-permute-done.refs_4_.refs_3_, ...), custom_call_target="tpu_custom_call" | custom-call | flops 1073741824 | bytes 1572864 | tf_op jit(solution)/shard_map/second_products/pallas_call | solution.py:145
  140.5 2.6 %relay_add.1 = (s16[272,512]{1,0:T(8,128)(2,1)}, s16[272,512]{1,0:T(8,128)(2,1)}) custom-call(f32[256,512]{1,0:T(8,128)} %get-tuple-element.40.x, s16[272,512]{1,0:T(8,128)(2,1)} %copy-done.15, f32[256,512]{1,0:T(8,128)} %get-tuple-element.42.y, s16[272,512]{1,0:T(8,128)(2,1)} %copy-done.16), custom_call_target="tpu_custom_call" | custom-call | tf_op jit(solution)/shard_map/relay_add/pallas_call | solution.py:164
  145.9 5.0 %second_products.4 = (f32[256,512]{1,0:T(8,128)}, f32[256,512]{1,0:T(8,128)}) custom-call(s32[2]{0:T(128)} %get-tuple-element.60.refs_0_, s32[2]{0:T(128)} %get-tuple-element.59.refs_1_, bf16[256,512]{1,0:T(8,128)(2,1)} %get-tuple-element.53.refs_2_, bf16[256,512]{1,0:T(8,128)(2,1)} %copy-done.6, bf16[512,512]{1,0:T(8,128)(2,1)} %get-tuple-element.36.refs_4_, ...), custom_call_target="tpu_custom_call" | custom-call | flops 1073741824 | bytes 1572864 | tf_op jit(solution)/shard_map/second_products/pallas_call | solution.py:145
  152.0 3.0 %w1_update.1 = bf16[512,512]{1,0:T(8,128)(2,1)} custom-call(f32[256,512]{1,0:T(8,128)} %get-tuple-element.37.own0, f32[256,512]{1,0:T(8,128)} %get-tuple-element.38.own1, s16[272,512]{1,0:T(8,128)(2,1)} %copy-done.19, s16[272,512]{1,0:T(8,128)(2,1)} %copy-done.21, s16[272,512]{1,0:T(8,128)(2,1)} %copy-done.22, s16[272,512]{1,0:T(8,128)(2,1)} %copy-done.20, ...), custom_call_target="tpu_custom_call" | custom-call | tf_op jit(solution)/shard_map/w1_update/pallas_call | solution.py:164
  (121 shorter events, 33.1 us)
Async XLA Ops:
  4.6 20.1 %collective-permute-start.5 = (s16[4,512,512]{2,1,0:T(8,128)(2,1)}, s16[4,512,512]{2,1,0:T(8,128)(2,1)S(1)}, u32[]{:S(2)}, u32[]{:S(2)}) collective-permute-start(s16[4,512,512]{2,1,0:T(8,128)(2,1)} %fusion), channel_id=1, source_target_pairs={{0,1},{1,0},{2,3},{3,2},{4,5},{5,4},{6,7},{7,6},{8,9},{9,8},{10,11... | collective-permute-start | bytes 6291464 | tf_op jit(solution)/shard_map/ppermute | solution.py:168
  5.8 18.9 %copy-start.6 = (bf16[256,512]{1,0:T(8,128)(2,1)}, bf16[256,512]{1,0:T(8,128)(2,1)S(1)}, u32[]{:S(2)}) copy-start(bf16[256,512]{1,0:T(8,128)(2,1)S(1)} %get-tuple-element.52.refs_3_) | copy-start | bytes 786436
  5.8 9.8 %collective-permute-start = (bf16[256,512]{1,0:T(8,128)(2,1)}, bf16[256,512]{1,0:T(8,128)(2,1)}, u32[]{:S(2)}, u32[]{:S(2)}) collective-permute-start(bf16[256,512]{1,0:T(8,128)(2,1)} %get-tuple-element.53.refs_2_), channel_id=1, source_target_pairs={{0,4},{1,5},{2,6},{3,7},{4,0},{5,1},{6,2},{7,3},{8,12},{9,13},{10,... | collective-permute-start | bytes 786440 | tf_op jit(solution)/shard_map/ppermute | solution.py:168
  8.3 23.2 %collective-permute-start.6 = (bf16[256,512]{1,0:T(8,128)(2,1)}, bf16[256,512]{1,0:T(8,128)(2,1)}, u32[]{:S(2)}, u32[]{:S(2)}) collective-permute-start(bf16[256,512]{1,0:T(8,128)(2,1)} %get-tuple-element.53.refs_2_), channel_id=1, source_target_pairs={{0,2},{1,3},{2,0},{3,1},{4,6},{5,7},{6,4},{7,5},{8,10},{9,11},{10,... | collective-permute-start | bytes 786440 | tf_op jit(solution)/shard_map/ppermute | solution.py:168
  9.9 14.3 %collective-permute-start.4 = (bf16[512,512]{1,0:T(8,128)(2,1)S(1)}, bf16[512,512]{1,0:T(8,128)(2,1)}, u32[]{:S(2)}, u32[]{:S(2)}) collective-permute-start(bf16[512,512]{1,0:T(8,128)(2,1)S(1)} %convert_element_type.14.refs_4_.refs_6_), channel_id=1, source_target_pairs={{0,1},{1,0},{2,3},{3,2},{4,5},{5,4},{6,7},{7,6},{8,9},{9,8},{10,11... | collective-permute-start | bytes 1572872 | tf_op jit(solution)/shard_map/ppermute | solution.py:168
  9.9 12.7 %collective-permute-start.2 = (bf16[256,512]{1,0:T(8,128)(2,1)S(1)}, bf16[256,512]{1,0:T(8,128)(2,1)}, u32[]{:S(2)}, u32[]{:S(2)}) collective-permute-start(bf16[256,512]{1,0:T(8,128)(2,1)S(1)} %get-tuple-element.52.refs_3_), channel_id=1, source_target_pairs={{0,2},{1,3},{2,0},{3,1},{4,6},{5,7},{6,4},{7,5},{8,10},{9,11},{10,... | collective-permute-start | bytes 786440 | tf_op jit(solution)/shard_map/ppermute | solution.py:168
  15.6 15.9 %collective-permute-start.7 = (bf16[256,512]{1,0:T(8,128)(2,1)S(1)}, bf16[256,512]{1,0:T(8,128)(2,1)}, u32[]{:S(2)}, u32[]{:S(2)}) collective-permute-start(bf16[256,512]{1,0:T(8,128)(2,1)S(1)} %get-tuple-element.52.refs_3_), channel_id=1, source_target_pairs={{0,4},{1,5},{2,6},{3,7},{4,0},{5,1},{6,2},{7,3},{8,12},{9,13},{10,... | collective-permute-start | bytes 786440 | tf_op jit(solution)/shard_map/ppermute | solution.py:168
  22.6 17.4 %collective-permute-start.1 = (bf16[256,512]{1,0:T(8,128)(2,1)}, bf16[256,512]{1,0:T(8,128)(2,1)S(1)}, u32[]{:S(2)}, u32[]{:S(2)}) collective-permute-start(bf16[256,512]{1,0:T(8,128)(2,1)} %collective-permute-done.refs_4_.refs_3_), channel_id=1, source_target_pairs={{0,2},{1,3},{2,0},{3,1},{4,6},{5,7},{6,4},{7,5},{8,10},{9,11},{10,... | collective-permute-start | bytes 786440 | tf_op jit(solution)/shard_map/ppermute | solution.py:168
  24.1 15.9 %collective-permute-start.3 = (bf16[256,512]{1,0:T(8,128)(2,1)}, bf16[256,512]{1,0:T(8,128)(2,1)S(1)}, u32[]{:S(2)}, u32[]{:S(2)}) collective-permute-start(bf16[256,512]{1,0:T(8,128)(2,1)} %collective-permute-done.2.refs_3_.refs_2_), channel_id=1, source_target_pairs={{0,4},{1,5},{2,6},{3,7},{4,0},{5,1},{6,2},{7,3},{8,12},{9,13},{10,... | collective-permute-start | bytes 786440 | tf_op jit(solution)/shard_map/ppermute | solution.py:168
  40.8 50.7 %copy-start.7 = (f32[512,64]{0,1:T(8,128)S(1)}, f32[512,64]{0,1:T(8,128)}, u32[]{:S(2)}) copy-start(f32[512,64]{0,1:T(8,128)} %param.13) | copy-start | bytes 393220
  47.1 53.3 %copy-start.23 = (f32[64,512]{1,0:T(8,128)S(1)}, f32[64,512]{1,0:T(8,128)}, u32[]{:S(2)}) copy-start(f32[64,512]{1,0:T(8,128)} %param.14) | copy-start | bytes 393220
  47.1 2.9 %collective-permute-start.8 = (f32[512,512]{1,0:T(8,128)}, f32[512,512]{1,0:T(8,128)S(1)}, u32[]{:S(2)}, u32[]{:S(2)}) collective-permute-start(f32[512,512]{1,0:T(8,128)} %get-tuple-element.31), channel_id=1, source_target_pairs={{0,1},{1,0},{2,3},{3,2},{4,5},{5,4},{6,7},{7,6},{8,9},{9,8},{10,11... | collective-permute-start | bytes 3145736 | tf_op jit(solution)/shard_map/ppermute | solution.py:168
  53.7 11.6 %collective-permute-start.10 = (s16[272,512]{1,0:T(8,128)(2,1)}, s16[272,512]{1,0:T(8,128)(2,1)S(1)}, u32[]{:S(2)}, u32[]{:S(2)}) collective-permute-start(s16[272,512]{1,0:T(8,128)(2,1)} %get-tuple-element.33.hi), channel_id=1, source_target_pairs={{0,24},{8,16},{16,8},{24,0},{1,25},{9,17},{17,9},{25,1},{2,26},{10... | collective-permute-start | bytes 835592 | tf_op jit(solution)/shard_map/ppermute | solution.py:168
  57.3 13.2 %collective-permute-start.9 = (s16[272,512]{1,0:T(8,128)(2,1)}, s16[272,512]{1,0:T(8,128)(2,1)S(1)}, u32[]{:S(2)}, u32[]{:S(2)}) collective-permute-start(s16[272,512]{1,0:T(8,128)(2,1)} %get-tuple-element.32.lo), channel_id=1, source_target_pairs={{0,8},{8,0},{16,24},{24,16},{1,9},{9,1},{17,25},{25,17},{2,10},{10... | collective-permute-start | bytes 835592 | tf_op jit(solution)/shard_map/ppermute | solution.py:168
  57.4 1.2 collective-permute-start.13
  58.6 17.1 %collective-permute-start.14 = (f32[8,512]{1,0:T(8,128)S(1)}, f32[8,512]{1,0:T(8,128)S(1)}, u32[]{:S(2)}, u32[]{:S(2)}) collective-permute-start(f32[8,512]{1,0:T(8,128)S(1)} %broadcast_add_fusion), channel_id=1, source_target_pairs={{0,2},{1,3},{2,0},{3,1},{4,6},{5,7},{6,4},{7,5},{8,10},{9,11},{10,... | collective-permute-start | bytes 49160 | tf_op jit(solution)/shard_map/ppermute | solution.py:168
  73.9 21.1 %collective-permute-start.11 = (s16[272,512]{1,0:T(8,128)(2,1)}, s16[272,512]{1,0:T(8,128)(2,1)S(1)}, u32[]{:S(2)}, u32[]{:S(2)}) collective-permute-start(s16[272,512]{1,0:T(8,128)(2,1)} %get-tuple-element.34.lo), channel_id=1, source_target_pairs={{0,24},{8,16},{16,8},{24,0},{1,25},{9,17},{17,9},{25,1},{2,26},{10... | collective-permute-start | bytes 835592 | tf_op jit(solution)/shard_map/ppermute | solution.py:168
  75.5 19.4 %collective-permute-start.12 = (s16[272,512]{1,0:T(8,128)(2,1)}, s16[272,512]{1,0:T(8,128)(2,1)S(1)}, u32[]{:S(2)}, u32[]{:S(2)}) collective-permute-start(s16[272,512]{1,0:T(8,128)(2,1)} %get-tuple-element.35.hi), channel_id=1, source_target_pairs={{0,8},{8,0},{16,24},{24,16},{1,9},{9,1},{17,25},{25,17},{2,10},{10... | collective-permute-start | bytes 835592 | tf_op jit(solution)/shard_map/ppermute | solution.py:168
  75.8 3.8 %collective-permute-start.15 = (f32[8,512]{1,0:T(8,128)S(1)}, f32[8,512]{1,0:T(8,128)S(1)}, u32[]{:S(2)}, u32[]{:S(2)}) collective-permute-start(f32[8,512]{1,0:T(8,128)S(1)} %fusion.21), channel_id=1, source_target_pairs={{0,4},{1,5},{2,6},{3,7},{4,0},{5,1},{6,2},{7,3},{8,12},{9,13},{10,... | collective-permute-start | bytes 49160 | tf_op jit(solution)/shard_map/ppermute | solution.py:168
  79.6 9.8 %collective-permute-start.16 = (f32[8,512]{1,0:T(8,128)S(1)}, f32[8,512]{1,0:T(8,128)S(1)}, u32[]{:S(2)}, u32[]{:S(2)}) collective-permute-start(f32[8,512]{1,0:T(8,128)S(1)} %add.103), channel_id=1, source_target_pairs={{0,8},{8,0},{16,24},{24,16},{1,9},{9,1},{17,25},{25,17},{2,10},{10... | collective-permute-start | bytes 49160 | tf_op jit(solution)/shard_map/ppermute | solution.py:168
  89.4 5.5 %collective-permute-start.17 = (f32[8,512]{1,0:T(8,128)S(1)}, f32[8,512]{1,0:T(8,128)S(1)}, u32[]{:S(2)}, u32[]{:S(2)}) collective-permute-start(f32[8,512]{1,0:T(8,128)S(1)} %add.104), channel_id=1, source_target_pairs={{0,24},{8,16},{16,8},{24,0},{1,25},{9,17},{17,9},{25,1},{2,26},{10... | collective-permute-start | bytes 49160 | tf_op jit(solution)/shard_map/ppermute | solution.py:168
  103.7 21.0 %copy-start.12 = (f32[64,512]{1,0:T(8,128)}, f32[64,512]{1,0:T(8,128)S(1)}, u32[]{:S(2)}) copy-start(f32[64,512]{1,0:T(8,128)S(1)} %get-tuple-element.58) | copy-start | bytes 393220
  106.0 1.4 collective-permute-start.25
  106.1 12.7 %collective-permute-start.18 = (bf16[512,512]{1,0:T(8,128)(2,1)S(1)}, bf16[512,512]{1,0:T(8,128)(2,1)S(1)}, u32[]{:S(2)}, u32[]{:S(2)}) collective-permute-start(bf16[512,512]{1,0:T(8,128)(2,1)S(1)} %copy-done.1), channel_id=1, source_target_pairs={{0,1},{1,0},{2,3},{3,2},{4,5},{5,4},{6,7},{7,6},{8,9},{9,8},{10,11... | collective-permute-start | bytes 1572872 | tf_op jit(solution)/shard_map/ppermute | solution.py:168
  107.5 6.0 %collective-permute-start.26 = (f32[72,512]{1,0:T(8,128)S(1)}, f32[72,512]{1,0:T(8,128)S(1)}, u32[]{:S(2)}, u32[]{:S(2)}) collective-permute-start(f32[72,512]{1,0:T(8,128)S(1)} %fusion.7), channel_id=1, source_target_pairs={{0,2},{1,3},{2,0},{3,1},{4,6},{5,7},{6,4},{7,5},{8,10},{9,11},{10,... | collective-permute-start | bytes 442376 | tf_op jit(solution)/shard_map/ppermute | solution.py:168
  113.5 5.2 %collective-permute-start.27 = (f32[72,512]{1,0:T(8,128)S(1)}, f32[72,512]{1,0:T(8,128)S(1)}, u32[]{:S(2)}, u32[]{:S(2)}) collective-permute-start(f32[72,512]{1,0:T(8,128)S(1)} %add.112), channel_id=1, source_target_pairs={{0,4},{1,5},{2,6},{3,7},{4,0},{5,1},{6,2},{7,3},{8,12},{9,13},{10,... | collective-permute-start | bytes 442376 | tf_op jit(solution)/shard_map/ppermute | solution.py:168
  124.7 15.0 %collective-permute-start.20 = (s16[272,512]{1,0:T(8,128)(2,1)}, s16[272,512]{1,0:T(8,128)(2,1)S(1)}, u32[]{:S(2)}, u32[]{:S(2)}) collective-permute-start(s16[272,512]{1,0:T(8,128)(2,1)} %get-tuple-element.41), channel_id=1, source_target_pairs={{0,4},{1,5},{2,6},{3,7},{4,0},{5,1},{6,2},{7,3},{8,12},{9,13},{10,... | collective-permute-start | bytes 835592 | tf_op jit(solution)/shard_map/ppermute | solution.py:168
  126.2 13.5 %collective-permute-start.21 = (s16[272,512]{1,0:T(8,128)(2,1)}, s16[272,512]{1,0:T(8,128)(2,1)S(1)}, u32[]{:S(2)}, u32[]{:S(2)}) collective-permute-start(s16[272,512]{1,0:T(8,128)(2,1)} %get-tuple-element.43), channel_id=1, source_target_pairs={{0,2},{1,3},{2,0},{3,1},{4,6},{5,7},{6,4},{7,5},{8,10},{9,11},{10,... | collective-permute-start | bytes 835592 | tf_op jit(solution)/shard_map/ppermute | solution.py:168
  132.5 18.5 %collective-permute-start.19 = (s16[272,512]{1,0:T(8,128)(2,1)}, s16[272,512]{1,0:T(8,128)(2,1)S(1)}, u32[]{:S(2)}, u32[]{:S(2)}) collective-permute-start(s16[272,512]{1,0:T(8,128)(2,1)} %get-tuple-element.39), channel_id=1, source_target_pairs={{0,2},{1,3},{2,0},{3,1},{4,6},{5,7},{6,4},{7,5},{8,10},{9,11},{10,... | collective-permute-start | bytes 835592 | tf_op jit(solution)/shard_map/ppermute | solution.py:168
  134.0 16.9 %collective-permute-start.24 = (s16[272,512]{1,0:T(8,128)(2,1)}, s16[272,512]{1,0:T(8,128)(2,1)S(1)}, u32[]{:S(2)}, u32[]{:S(2)}) collective-permute-start(s16[272,512]{1,0:T(8,128)(2,1)} %get-tuple-element.46), channel_id=1, source_target_pairs={{0,4},{1,5},{2,6},{3,7},{4,0},{5,1},{6,2},{7,3},{8,12},{9,13},{10,... | collective-permute-start | bytes 835592 | tf_op jit(solution)/shard_map/ppermute | solution.py:168
  143.1 7.8 %collective-permute-start.22 = (s16[272,512]{1,0:T(8,128)(2,1)}, s16[272,512]{1,0:T(8,128)(2,1)S(1)}, u32[]{:S(2)}, u32[]{:S(2)}) collective-permute-start(s16[272,512]{1,0:T(8,128)(2,1)} %get-tuple-element.44), channel_id=1, source_target_pairs={{0,2},{1,3},{2,0},{3,1},{4,6},{5,7},{6,4},{7,5},{8,10},{9,11},{10,... | collective-permute-start | bytes 835592 | tf_op jit(solution)/shard_map/ppermute | solution.py:168
  143.9 7.1 %collective-permute-start.23 = (s16[272,512]{1,0:T(8,128)(2,1)}, s16[272,512]{1,0:T(8,128)(2,1)S(1)}, u32[]{:S(2)}, u32[]{:S(2)}) collective-permute-start(s16[272,512]{1,0:T(8,128)(2,1)} %get-tuple-element.45), channel_id=1, source_target_pairs={{0,4},{1,5},{2,6},{3,7},{4,0},{5,1},{6,2},{7,3},{8,12},{9,13},{10,... | collective-permute-start | bytes 835592 | tf_op jit(solution)/shard_map/ppermute | solution.py:168
  (22 other events, 71.3 us)

commit v2 on v0

v2 whole, which is shorter than its diff:
```python
import functools

import jax
import jax.numpy as jnp
from jax import lax
from jax.experimental import pallas as pl
from jax.experimental.pallas import tpu as pltpu
from jax.sharding import PartitionSpec as P

F32 = jnp.float32
BF16 = jnp.bfloat16
PAD = 16
CHUNKS = 2


def params(mib=16):
    return pltpu.CompilerParams(vmem_limit_bytes=mib * 1024 * 1024)


def mm(a, b, dims):
    return lax.dot_general(a, b, ((dims[:1], dims[1:]), ((), ())), preferred_element_type=F32)


def encode(x, out_ref, extra=None):
    rows, cols = x.shape
    top = jnp.maximum(jnp.max(x, axis=0, keepdims=True), 1e-30)
    power = jnp.ceil(jnp.log2(top))
    q = jnp.minimum(x * (jnp.exp2(-power) * 65535.0) + 0.5, 65535.0)
    out_ref[:rows, :] = (q.astype(jnp.int32) - 32768).astype(jnp.int16)
    lines = [power]
    if extra is not None:
        whole = jnp.floor(extra)
        for y in (whole, jnp.floor((extra - whole) * 32768.0 + 0.25)):
            lines += [y[:, i : i + cols] for i in range(0, y.shape[1], cols)]
    lines.append(jnp.zeros((PAD - len(lines), cols), F32))
    out_ref[rows:, :] = jnp.concatenate(lines, axis=0).astype(jnp.int32).astype(jnp.int16)


def decode_extra(ref, width):
    rows, cols = ref.shape[0] - PAD, ref.shape[1]
    n = width // cols
    lines = ref[rows:, :].astype(jnp.int32).astype(F32)
    lines = [lines[1 + i : 2 + i] for i in range(2 * n)]
    return jnp.concatenate(lines[:n], axis=1) + jnp.concatenate(lines[n:], axis=1) * (1.0 / 32768.0)


def decode(ref):
    rows = ref.shape[0] - PAD
    power = ref[rows:, :].astype(jnp.int32).astype(F32)[:1]
    unit = jnp.exp2(power) * (1.0 / 65535.0)
    return (ref[:rows, :].astype(jnp.int32) + 32768).astype(F32) * unit


def coded(rows, cols):
    return jax.ShapeDtypeStruct((rows + PAD, cols), jnp.int16)


def quotient(v, approx):
    return (v.astype(jnp.int32).astype(F32) / approx).astype(BF16)


def counts_body(chips, rows, at, v, *refs):
    outs, held, low, sems = refs[: 2 * chips], *refs[2 * chips :]
    copies = []
    for q in range(chips):
        start = pl.multiple_of((at[0] ^ q) * 2 * rows, 2 * rows)
        both = pl.ds(q * 2 * rows, 2 * rows)
        copies.append(pltpu.make_async_copy(v.at[pl.ds(start, 2 * rows), :], held.at[both, :], sems.at[q]))
        copies[-1].start()
    for q in range(chips):
        copies[q].wait()
        for slot, core in ((q, at[1]), (chips + q, 1 - at[1])):
            some = held[pl.ds(pl.multiple_of((2 * q + core) * rows, rows), rows), :]
            low[slot] = some.astype(jnp.int16)
            copies.append(pltpu.make_async_copy(low.at[slot], outs[slot], sems.at[chips + slot]))
            copies[-1].start()
    for copy in copies[chips:]:
        copy.wait()


def split_counts(at, counts, chips, rows):
    cells = counts.shape[1]
    out = pltpu.HBM((rows, cells), jnp.int16)
    smem, hbm = pl.BlockSpec(memory_space=pltpu.SMEM), pl.BlockSpec(memory_space=pltpu.HBM)
    outs = pl.pallas_call(
        functools.partial(counts_body, chips, rows),
        out_shape=(out,) * (2 * chips),
        in_specs=[smem, hbm],
        out_specs=[hbm] * (2 * chips),
        scratch_shapes=[
            pltpu.VMEM(counts.shape, counts.dtype),
            pltpu.VMEM((2 * chips, rows, cells), jnp.int16),
            pltpu.SemaphoreType.DMA((3 * chips,)),
        ],
        compiler_params=params(),
        name="split_counts",
    )(at, pltpu.with_memory_space_constraint(counts, pltpu.HBM))
    return outs[:chips], outs[chips:]


class Later:
    def __init__(self, array):
        self.array = array


def fetching(refs, later, scratch):
    sems, slots, found = scratch[-1] if later else None, iter(scratch), []
    for i, ref in enumerate(refs):
        copy = None
        if i in later:
            slot = next(slots)
            copy = pltpu.make_async_copy(ref, slot, sems.at[later.index(i)])
            copy.start()
            ref = slot
        found.append((ref, copy))
    return found


def ready(operand):
    ref, copy = operand
    if copy is not None:
        copy.wait()
    return ref[...]


def joined(operands):
    return jnp.concatenate([ready(x) for x in operands], axis=0) if len(operands) > 1 else ready(operands[0])


def ahead(sources, outs, sems):
    copies = [pltpu.make_async_copy(x, out, sems.at[i]) for i, (x, out) in enumerate(zip(sources, outs))]
    for copy in copies:
        copy.start()
    return copies


def fetch_body(n, *refs):
    for copy in ahead(refs[:n], refs[n : 2 * n], refs[-1]):
        copy.wait()


def plain_fetch(arrays):
    n = len(arrays)
    vmem, hbm = pl.BlockSpec(memory_space=pltpu.VMEM), pl.BlockSpec(memory_space=pltpu.HBM)
    return pl.pallas_call(
        functools.partial(fetch_body, n),
        out_shape=[jax.ShapeDtypeStruct(x.shape, x.dtype) for x in arrays],
        in_specs=[hbm] * n,
        out_specs=[vmem] * n,
        scratch_shapes=[pltpu.SemaphoreType.DMA((n,))],
        compiler_params=params(),
        name="fetch",
    )(*(pltpu.with_memory_space_constraint(x, pltpu.HBM) for x in arrays))


def first_body(groups, later, n_ahead, has_acc, h, *refs):
    n, n_later = sum(groups) + len(groups), len(later)
    refs, sems = (refs[:-1], refs[-1:]) if n_ahead else (refs, ())
    refs, scratch = (refs[:-n_later - 1] + sems, refs[-n_later - 1 :]) if later else (refs + sems, ())
    operands = fetching(refs[:n], later, scratch)
    copies, refs = (), refs[n:]
    if n_ahead:
        copies, refs = ahead(refs[:n_ahead], refs[-1 - n_ahead : -1], refs[-1]), refs[n_ahead : -1 - n_ahead]
    num_ref, col_ref = refs[-2:]
    total, col = (refs[0][...], refs[1][...]) if has_acc else (0.0, 0.0)
    for n in groups:
        w, v = joined(operands[:n]), operands[n]
        operands = operands[n + 1 :]
        approx = mm(w, h[...], (1, 0))
        total += mm(w, quotient(ready(v), approx), (0, 0))
        col += jnp.sum(w.astype(F32), axis=0, keepdims=True)
    num_ref[...] = total
    col_ref[...] = jnp.broadcast_to(col, col_ref.shape)
    for copy in copies:
        copy.wait()


def second_body(groups, later, n_ahead, code, ha, hb, *refs):
    n, n_later = sum(groups) + 2 * len(groups), len(later)
    refs, scratch = (refs[:-n_later - 1], refs[-n_later - 1 :]) if later else (refs, ())
    operands, outs = fetching(refs[:n], later, scratch), refs[n:]
    for n in groups:
        pieces, v, operands = operands[:n], operands[n : n + 2], operands[n + 2 :]
        w, t = joined(pieces), pieces[0][0].shape[0]
        total = 0.0
        for h, some in ((hb, v[1]), (ha, v[0])):
            low = h[...]
            approx = mm(w, low, (1, 0))
            total += mm(quotient(ready(some), approx), low, (1, 1))
        for k in range(n):
            out, outs = outs[0], outs[1:]
            part = total[k * t : (k + 1) * t]
            if code:
                encode(part, out)
            else:
                out[...] = part


def products(body, flag, outs, groups, h, acc, name, fetch=()):
    n_h = len(h)
    sizes = tuple(len(g) - n_h for g in groups)
    flat = [x for g in groups for x in g]
    later = tuple(i for i, x in enumerate(flat) if isinstance(x, Later))
    vmem, hbm = pl.BlockSpec(memory_space=pltpu.VMEM), pl.BlockSpec(memory_space=pltpu.HBM)
    specs = [hbm if i in later else vmem for i in range(len(flat))]
    flat = [pltpu.with_memory_space_constraint(x.array, pltpu.HBM) if isinstance(x, Later) else x for x in flat]
    scratch = [pltpu.VMEM(flat[i].shape, flat[i].dtype) for i in later]
    if later:
        scratch.append(pltpu.SemaphoreType.DMA((len(later),)))
    fetch = [pltpu.with_memory_space_constraint(x, pltpu.HBM) for x in fetch]
    if fetch:
        scratch.append(pltpu.SemaphoreType.DMA((len(fetch),)))
    outs = (*outs, *(jax.ShapeDtypeStruct(x.shape, x.dtype) for x in fetch))
    args = [*h, *flat, *fetch, *acc]
    work = 2 * sum(x.shape[0] for x in flat) * h[0].shape[1]
    return pl.pallas_call(
        functools.partial(body, sizes, later, len(fetch), flag),
        out_shape=outs,
        in_specs=[vmem] * n_h + specs + [hbm] * len(fetch) + [vmem] * len(acc),
        out_specs=[vmem] * len(outs),
        scratch_shapes=scratch,
        input_output_aliases={len(args) - len(acc) + i: i for i in range(len(acc))},
        compiler_params=params(),
        cost_estimate=pl.CostEstimate(flops=2 * work * h[0].shape[0], bytes_accessed=work, transcendentals=0),
        name=name,
    )(*args)


def first(groups, h, acc=(), fetch=()):
    k1, cells = h.shape
    outs = (jax.ShapeDtypeStruct((k1, cells), F32), jax.ShapeDtypeStruct((8, k1), F32))
    return products(first_body, bool(acc), outs, groups, (h,), acc, "first_products", fetch)


def second(groups, t, h, code):
    k1 = h[0].shape[0]
    out = coded(t, k1) if code else jax.ShapeDtypeStruct((t, k1), F32)
    outs = (out,) * sum(len(g) - 2 for g in groups)
    return products(second_body, code, outs, groups, h, (), "second_products")


def plain(body, outs, *args, name, flag=None):
    vmem = pl.BlockSpec(memory_space=pltpu.VMEM)
    specs = [vmem] * len(args)
    if flag is not None:
        specs, args = [pl.BlockSpec(memory_space=pltpu.SMEM)] + specs, (flag, *args)
    out_specs = (vmem,) * len(outs) if isinstance(outs, tuple) else vmem
    return pl.pallas_call(
        body, out_shape=outs, in_specs=specs, out_specs=out_specs, compiler_params=params(), name=name
    )(*args)


def flip(x, axis, size, bit):
    return lax.ppermute(x, axis, [(i, i ^ bit) for i in range(size)])


def split_num(flag, num, col, keep_ref, *sends):
    inner = flag[0] == 1
    half = num.shape[1] // 2
    keep_ref[...] = jnp.where(inner, num[:, half:], num[:, :half])
    width = half // len(sends)
    for i, send in enumerate(sends):
        lo = num[:, i * width : (i + 1) * width]
        hi = num[:, half + i * width : half + (i + 1) * width]
        encode(jnp.where(inner, lo, hi), send, None if i else col[:1, :])


def add_kept(i, keep, other, *refs):
    width, k1 = other.shape[1], keep.shape[0]
    extra = None if i else decode_extra(refs[0], k1) + decode_extra(other, k1)
    encode(keep[:, i * width : (i + 1) * width] + decode(other), refs[-1], extra)


def add_coded(one, other, out_ref, *col_ref):
    encode(decode(one) + decode(other), out_ref)
    for ref in col_ref:
        k1 = ref.shape[1]
        ref[...] = jnp.broadcast_to(decode_extra(one, k1) + decode_extra(other, k1), ref.shape)


def h1_update(n, flag, *refs):
    mine, theirs, (h1_ref, col_ref, new_ref, low_ref, late_ref) = refs[:n], refs[n : 2 * n], refs[2 * n :]
    inner = flag[0] == 1
    half = h1_ref.shape[1] // 2
    width = half // n
    col = col_ref[...].T[:, :1]
    for i in range(n):
        a, b = decode(mine[i]), decode(theirs[i])
        for at, num in ((i * width, jnp.where(inner, b, a)), (half + i * width, jnp.where(inner, a, b))):
            new = h1_ref[:, at : at + width] * num / col
            new_ref[:, at : at + width] = new
            late_ref[:, at : at + width] = new
            low_ref[:, at : at + width] = new.astype(BF16)


def h1_update_plain(num, h1_ref, col_ref, new_ref, low_ref):
    new = h1_ref[...] * num[...] / col_ref[:, :1]
    new_ref[...] = new
    low_ref[...] = new.astype(BF16)


def relay_add(x, x_in, y, y_in, x_ref, y_ref):
    half = x.shape[0] // 2
    encode(jnp.concatenate([x[:half, :], x[half:, :] + decode(x_in)], axis=0), x_ref)
    encode(jnp.concatenate([y[:half, :] + decode(y_in), y[half:, :]], axis=0), y_ref)


def half_sum(core, a_ref, b_ref, out_ref):
    half = out_ref.shape[0]
    total = a_ref[...] + b_ref[...]
    out_ref[...] = jnp.where(core[0] == 0, total[:half], total[half:])


def add_two(a_ref, b_ref, out_ref):
    out_ref[...] = a_ref[...] + b_ref[...]


def w1_update(own, x, y, w_ref, row_ref, out_ref):
    total = own[...] + decode(x) + decode(y)
    out_ref[...] = (w_ref[...].astype(F32) * total / row_ref[:1, :]).astype(BF16)


def parts(x):
    hi = x.astype(BF16)
    return hi, (x - hi.astype(F32)).astype(BF16)


def mm3(a, b, dims):
    (ah, al), (bh, bl) = a, b
    return mm(ah, bh, dims) + (mm(ah, bl, dims) + mm(al, bh, dims))


def layer_two(h1_ref, w2t_ref, h2_ref, v, new_ref, sums_ref, v_out, sem):
    copy = pltpu.make_async_copy(v, v_out, sem)
    copy.start()
    h1, w2t, h2 = h1_ref[...], w2t_ref[...], h2_ref[...]
    k2, k1 = w2t.shape
    w2p = parts(w2t)
    ratio3 = h1 / mm3(w2p, parts(h2), (0, 0))
    h2_new = h2 * mm3(w2p, parts(ratio3), (1, 0)) / jnp.sum(w2t, axis=1, keepdims=True)
    new_ref[...] = h2_new
    h2p = parts(h2_new)
    ratio4 = h1 / mm3(w2p, h2p, (0, 0))
    sums_ref[:k2, :] = mm3(h2p, parts(ratio4), (1, 1))
    cells = h1.shape[1]
    row = (jnp.ones((8, cells), BF16), jnp.zeros((8, cells), BF16))
    sums_ref[k2 : k2 + 8, :] = mm3(row, parts(h1), (1, 1))
    sums_ref[k2 + 8 :, :] = jnp.zeros((8, k1), F32)
    sums_ref[k2 + 8 :, :k2] = mm3(row, h2p, (1, 1))
    copy.wait()


def on_device(n_gene, n_cell, counts, w1, h1, w2, h2):
    genes, cells = counts.shape
    rows, k1 = w1.shape
    k2 = w2.shape[1]
    chips = n_cell // 2
    me = lax.axis_index("cell")
    core, chip = me % 2, me // 2
    line = n_cell == 8 and n_gene == 4 and genes * 4 < 32768
    cell = functools.partial(flip, axis="cell", size=n_cell)
    gene = functools.partial(flip, axis="gene", size=n_gene)
    after = lax.optimization_barrier
    at = jnp.stack([chip, core]).astype(jnp.int32)

    h1_low = h1.astype(BF16)
    new_shapes = (jax.ShapeDtypeStruct((k1, cells), F32), jax.ShapeDtypeStruct((k1, cells), BF16))
    if line:
        t = rows // 2
        w_x, w_y = cell(w1, bit=2), cell(w1, bit=4)
        w_0 = cell(w1, bit=1)

        v_mine, v_theirs = split_counts(at, counts, chips, rows)
        v_other = [cell(v, bit=1) for v in v_theirs]
        on_mine, on_theirs = ([Later(v) for v in some] for some in (v_mine, v_theirs))
        acc = first(((Later(w1), on_mine[0]), (w_0, on_theirs[0])), h1_low)
        w_x, w_y, *acc = after((w_x, w_y, *acc))
        d_lo, d_hi = cell(w_y[:t], bit=2), cell(w_x[t:], bit=4)
        x_0, y_0 = cell(w_x, bit=1), cell(w_y, bit=1)
        near = ((Later(w_x), on_mine[1]), (Later(w_y), on_mine[2]), (x_0, on_theirs[1]), (y_0, on_theirs[2]))
        acc = first(near, h1_low, acc)
        d_lo, d_hi, *acc = after((d_lo, d_hi, *acc))
        v_far = after((v_mine[3], v_theirs[3], *acc))[:2]
        v_far = plain_fetch(v_far)
        far = cell(d_lo, bit=1), cell(d_hi, bit=1)
        acc = first(((d_lo, d_hi, v_far[0]),), h1_low, acc)
        num, col = first(((*far, v_far[1]),), h1_low, acc)

        z = lax.axis_index("gene")
        inner = jnp.where((z == 1) | (z == 2), 1, 0).astype(jnp.int32)[None]
        chunks = tuple(range(CHUNKS))
        piece = coded(k1, cells // 2 // CHUNKS)
        keep, *sent = plain(
            split_num, (jax.ShapeDtypeStruct((k1, cells // 2), F32),) + (piece,) * CHUNKS,
            num, col, flag=inner, name="split_num",
        )

        pair = []
        for i, x in enumerate(sent):
            got = gene(after((x, *pair))[0], bit=1)
            extra = () if i else (x,)
            pair.append(plain(functools.partial(add_kept, i), piece, keep, got, *extra, name="add_pair"))
        mine = []
        for i, x in enumerate(pair):
            outs = piece if i else (piece, jax.ShapeDtypeStruct((8, k1), F32))
            mine.append(plain(add_coded, outs, x, gene(x, bit=3), name="add_cross"))
        (first_mine, col), *mine = mine
        mine = [first_mine, *mine]
        theirs = [gene(x, bit=1) for x in mine]
        h1_new, h1_low2, h1_late = plain(
            functools.partial(h1_update, CHUNKS), new_shapes + new_shapes[:1], *mine, *theirs, h1, col,
            flag=inner, name="h1_update",
        )
        h1_low2_other = cell(h1_low2, bit=1)
    else:
        col = None
        groups = [list(range(c, n_cell, 2)) for c in (0, 1)]
        w_half = lax.all_gather(w1, "cell", axis=0, tiled=True, axis_index_groups=groups)
        v_mine, v_theirs = split_counts(at * jnp.array([0, 1], jnp.int32), counts, chips, rows)
        v_other = [cell(v, bit=1) for v in v_theirs]
        halves = [[w[j * rows : (j + 1) * rows] for j in range(chips)] for w in (w_half, cell(w_half, bit=1))]
        each = min(chips, max(1, 512 // rows))
        acc = ()
        for i in range(0, chips, each):
            for w, v in zip(halves, (v_mine, v_theirs)):
                acc = first(tuple((w[j], v[j]) for j in range(i, i + each)), h1_low, acc)
        num, col = lax.psum(tuple(acc), "gene")
        col = jnp.broadcast_to(col[0][:, None], (k1, 128))
        h1_new, h1_low2 = plain(h1_update_plain, new_shapes, num, h1, col, name="h1_update")
        h1_low2_other, h1_late = cell(h1_low2, bit=1), h1_new

    w2t = w2.T
    vmem, hbm = pl.BlockSpec(memory_space=pltpu.VMEM), pl.BlockSpec(memory_space=pltpu.HBM)
    h2_new, sums, v_far = pl.pallas_call(
        layer_two,
        out_shape=(
            jax.ShapeDtypeStruct((k2, cells), F32),
            jax.ShapeDtypeStruct((k2 + 16, k1), F32),
            jax.ShapeDtypeStruct(v_mine[-1].shape, jnp.int16),
        ),
        in_specs=[vmem] * 3 + [hbm],
        out_specs=[vmem] * 3,
        scratch_shapes=[pltpu.SemaphoreType.DMA(())],
        compiler_params=params(),
        name="layer_two",
    )(h1_late, w2t, h2, pltpu.with_memory_space_constraint(v_mine[-1], pltpu.HBM))
    low2 = (h1_low2, h1_low2_other)
    if line:
        sums_in = cell(sums, bit=1)
        d_lo, d_hi = second(((d_lo, d_hi, v_far, v_other[3]),), t, low2, True)
        half = jax.ShapeDtypeStruct(((k2 + 16) // 2, k1), F32)
        sums, sums_in, d_lo = after((sums, sums_in, d_lo))
        part = plain(half_sum, half, sums, sums_in, flag=core.astype(jnp.int32)[None], name="half_sum")
        part, d_lo, d_hi = after((part, d_lo, d_hi))
        part_in = cell(part, bit=2)
        y_in, x_in = cell(d_lo, bit=2), cell(d_hi, bit=4)
        part = plain(add_two, half, part, part_in, name="add_two")
        w_x, part = after((w_x, part))
        part_in = cell(part, bit=4)
        near = ((Later(w_x), on_mine[1], v_other[1]), (Later(w_y), on_mine[2], v_other[2]))
        x_num, y_num = second(near, rows, low2, False)
        part, x_num = after((part, x_num))
        w1_late, part = after((w1, part))
        (own,) = second(((Later(w1_late), on_mine[0], v_other[0]),), rows, low2, False)
        piece = coded(rows, k1)
        x_num, part_in, own = after((x_num, part_in, own))
        x_num, y_num = plain(relay_add, (piece, piece), x_num, x_in, y_num, y_in, name="relay_add")
        x_num_in, y_num_in = cell(x_num, bit=2), cell(y_num, bit=4)
        part = plain(add_two, half, part, part_in, name="add_two")
        rest = cell(part, bit=1)
        sums = jnp.where(core == 0, jnp.concatenate([part, rest]), jnp.concatenate([rest, part]))
    else:
        found = []
        for i in range(0, chips, each):
            some = tuple((halves[0][j], v_mine[j], v_other[j]) for j in range(i, i + each))
            found += second(some, rows, low2, False)
        w1_num = lax.psum_scatter(
            jnp.concatenate(found), "cell", scatter_dimension=0, tiled=True, axis_index_groups=groups
        )
        sums = lax.psum(sums, "cell")
    w2_num, rowsum, h2_rows = sums[:k2], sums[k2 : k2 + 8], sums[k2 + 8, :k2]
    w2_new = (w2t * w2_num / h2_rows[:, None]).T
    if line:
        w1_new = plain(
            w1_update, jax.ShapeDtypeStruct((rows, k1), BF16), own, x_num_in, y_num_in, w1, rowsum, name="w1_update"
        )
    else:
        w1_new = (w1.astype(F32) * w1_num / rowsum[:1]).astype(BF16)
    return (w1_new, h1_new, w2_new, h2_new)


def solution(mesh):
    placed = (P("gene", "cell"), P(("gene", "cell"), None), P(None, "cell"), P(), P(None, "cell"))
    return jax.shard_map(
        functools.partial(on_device, mesh.shape["gene"], mesh.shape["cell"]),
        mesh=mesh,
        in_specs=placed,
        out_specs=(P(("gene", "cell"), None), P(None, "cell"), P(), P(None, "cell")),
        check_vma=False,
    )
```

time: 255 us -> 104 us (0.41)
  waiting for transfers between devices: 176 us -> 32.1 us
  Pallas kernels: 0 us -> 35.1 us
  matrix products: 30.7 us -> 0 us
  starting transfers between devices: 0.34 us -> 30.9 us
  blocking collectives: 25.7 us -> 0 us
  between operations: 13.8 us -> 0.97 us
  other arithmetic: 7.07 us -> 2.12 us
    reduce_scatter x1 -> x0, waiting for transfers between devices: 72.3 us -> none  [on_device(): lax.psum_scatter(lax.dot_general(ratio2, h1_low2, (((1,), (1,)), ((), ())...]
    psum x2 -> x0, waiting for transfers between devices: 61.2 us -> none  [the longest x1 36.9 us: on_device(): h1_num, colsum = lax.psum((partial_num, partial_col), 'gene')]
    all_gather x1 -> x0, waiting for transfers between devices: 41.4 us -> none  [on_device(): w1_block = lax.all_gather(w1, 'cell', axis=0, tiled=True)]
    pallas_call x0 -> x21, Pallas kernels: none -> 35.1 us  [the longest x7 19.3 us: products(): pl.pallas_call(functools.partial(body, sizes, later, len(fetch), flag), o...]
    ppermute x0 -> x28, waiting for transfers between devices: none -> 32.1 us  [flip(): return lax.ppermute(x, axis, [(i, i ^ bit) for i in range(size)])]
    ppermute x0 -> x28, starting transfers between devices: none -> 30.9 us  [flip(): return lax.ppermute(x, axis, [(i, i ^ bit) for i in range(size)])]
    dot_general x6 -> x0, matrix products: 30.7 us -> none  [the longest x1 12.5 us: on_device(): lax.dot_general(ratio2, h1_low2, (((1,), (1,)), ((), ())), preferred_elem...]
    psum x2 -> x0, blocking collectives: 25.7 us -> none  [the longest x1 13.8 us: on_device(): rowsum = lax.psum(local_rows, 'cell')]
  transfers between devices with their start and end apart: 4 -> 28, of which waited for: 4 -> 12; matrix products, arithmetic and copies ran while one was open for 7% -> 3% of each run, Pallas kernels for 0% -> 31%
where the time goes in v2:
time: 104 us; the launch traced here: 103 us
  Pallas kernels  35.1 us (34%)
  waiting for transfers between devices  32.1 us (31%)
  starting transfers between devices  30.9 us (30%)
  other arithmetic  2.12 us (2%)
  local copies, waits for them, and re-layouts  2.07 us (2%)
    ppermute x28, waiting for transfers between devices, flip(): return lax.ppermute(x, axis, [(i, i ^ bit) for i in range(size)])  32.1 us
    ppermute x28, starting transfers between devices, flip(): return lax.ppermute(x, axis, [(i, i ^ bit) for i in range(size)])  30.9 us
    pallas_call x7, Pallas kernels, products(): pl.pallas_call(functools.partial(body, sizes, later, len(fetch), flag), o...  19.3 us
    pallas_call x1, Pallas kernels, split_counts(): pl.pallas_call(functools.partial(counts_body, chips, rows), out_shape=(ou...  5.89 us
    pallas_call x11, Pallas kernels, plain(): pl.pallas_call(body, out_shape=outs, in_specs=specs, out_specs=out_specs,...  5.48 us
    pallas_call x1, Pallas kernels, on_device(): pl.pallas_call(layer_two, out_shape=(jax.ShapeDtypeStruct((k2, cells), F3...  3.07 us
  transfers between devices with their start and end apart: 28, of which 12 were waited for; matrix products, arithmetic and copies ran while one was open for 3% of the time, Pallas kernels for 31%

profile of v2, /device:TPU:0, one launch (start us, length us, event | category | flops | bytes accessed | tf_op | source)
XLA Modules:
  0.0 103.2 jit_solution(4753800911060344731)
XLA Ops:
  1.1 2.6 %collective-permute-start = (bf16[512,512]{1,0:T(8,128)(2,1)}, bf16[512,512]{1,0:T(8,128)(2,1)S(1)}, u32[]{:S(2)}, u32[]{:S(2)}) collective-permute-start(bf16[512,512]{1,0:T(8,128)(2,1)} %w_ref.1), channel_id=1, source_target_pairs={{0,2},{1,3},{2,0},{3,1},{4,6},{5,7},{6,4},{7,5},{8,10},{9,11},{10,... | collective-permute-start | bytes 1572872 | tf_op jit(solution)/shard_map/ppermute | solution.py:254
  3.7 1.5 %collective-permute-start.1 = (bf16[512,512]{1,0:T(8,128)(2,1)}, bf16[512,512]{1,0:T(8,128)(2,1)}, u32[]{:S(2)}, u32[]{:S(2)}) collective-permute-start(bf16[512,512]{1,0:T(8,128)(2,1)} %w_ref.1), channel_id=1, source_target_pairs={{0,4},{1,5},{2,6},{3,7},{4,0},{5,1},{6,2},{7,3},{8,12},{9,13},{10,... | collective-permute-start | bytes 1572872 | tf_op jit(solution)/shard_map/ppermute | solution.py:254
  5.2 1.3 %convert_element_type.3.h = bf16[512,512]{1,0:T(8,128)(2,1)S(1)} convert(f32[512,512]{1,0:T(8,128)} %refs_4_.1) | non-fusion elementwise | flops 262144 | bytes 1572864 | tf_op jit(solution)/shard_map/convert_element_type | solution.py:366
  6.6 5.9 %split_counts.1 = (s16[512,512]{1,0:T(8,128)(2,1)}, s16[512,512]{1,0:T(8,128)(2,1)}, s16[512,512]{1,0:T(8,128)(2,1)}, s16[512,512]{1,0:T(8,128)(2,1)}, s16[512,5...) custom-call(s32[2]{0:T(128)S(1)} %pad_add_fusion.at, s32[4096,512]{1,0:T(8,128)} %v.1), custom_call_target="tpu_custom_call" | custom-call | tf_op jit(solution)/shard_map/split_counts/pallas_call | solution.py:85
  12.5 2.9 %first_products.4 = (f32[512,512]{1,0:T(8,128)S(1)}, f32[8,512]{1,0:T(8,128)S(1)}) custom-call(bf16[512,512]{1,0:T(8,128)(2,1)S(1)} %convert_element_type.3.h, bf16[512,512]{1,0:T(8,128)(2,1)} %w_ref.1, s16[512,512]{1,0:T(8,128)(2,1)} %get-tuple-element.65.refs_1_, bf16[512,512]{1,0:T(8,128)(2,1)S(1)} %collective-permute-done.2.refs_2_, ...), custom_call_target="tpu_custom_call" | custom-call | flops 2147483648 | bytes 2097152 | tf_op jit(solution)/shard_map/first_products/pallas_call | solution.py:216
  16.4 1.6 %collective-permute-done.1.refs_2_.refs_3_ = bf16[512,512]{1,0:T(8,128)(2,1)} collective-permute-done((bf16[512,512]{1,0:T(8,128)(2,1)}, bf16[512,512]{1,0:T(8,128)(2,1)}, u32[]{:S(2)}, u32[]{:S(2)}) %collective-permute-start.1) | collective-permute-done | bytes 524320 | tf_op jit(solution)/shard_map/ppermute | solution.py:254
  19.9 1.7 %collective-permute-start.4 = (bf16[256,512]{1,0:T(8,128)(2,1)S(1)}, bf16[256,512]{1,0:T(8,128)(2,1)S(1)}, u32[]{:S(2)}, u32[]{:S(2)}) collective-permute-start(bf16[256,512]{1,0:T(8,128)(2,1)S(1)} %slice.16), channel_id=1, source_target_pairs={{0,4},{1,5},{2,6},{3,7},{4,0},{5,1},{6,2},{7,3},{8,12},{9,13},{10,... | collective-permute-start | bytes 786440 | tf_op jit(solution)/shard_map/ppermute | solution.py:254
  21.7 4.5 %first_products.5 = (f32[512,512]{1,0:T(8,128)S(1)}, f32[8,512]{1,0:T(8,128)S(1)}) custom-call(bf16[512,512]{1,0:T(8,128)(2,1)S(1)} %convert_element_type.3.h, bf16[512,512]{1,0:T(8,128)(2,1)} %copy-done.5, s16[512,512]{1,0:T(8,128)(2,1)} %get-tuple-element.71.refs_1_, ...), custom_call_target="tpu_custom_call", output_to_operand_aliasing={{0}: (9, {}), {1}: (10, {})} | custom-call | flops 4294967296 | bytes 4194304 | tf_op jit(solution)/shard_map/first_products/pallas_call | solution.py:216
  26.2 1.6 %collective-permute-done.3.refs_0_ = bf16[256,512]{1,0:T(8,128)(2,1)S(1)} collective-permute-done((bf16[256,512]{1,0:T(8,128)(2,1)S(1)}, bf16[256,512]{1,0:T(8,128)(2,1)S(1)}, u32[]{:S(2)}, u32[]{:S(2)}) %collective-permute-start.3) | collective-permute-done | bytes 262176 | tf_op jit(solution)/shard_map/ppermute | solution.py:254
  28.4 1.4 %fetch.1 = (s16[512,512]{1,0:T(8,128)(2,1)S(1)}, s16[512,512]{1,0:T(8,128)(2,1)S(1)}) custom-call(s16[512,512]{1,0:T(8,128)(2,1)} %get-tuple-element.85.refs_0_.v, s16[512,512]{1,0:T(8,128)(2,1)} %get-tuple-element.86.refs_1_), custom_call_target="tpu_custom_call" | custom-call | tf_op jit(solution)/shard_map/fetch/pallas_call | solution.py:145
  30.6 1.9 %first_products.7 = (f32[512,512]{1,0:T(8,128)S(1)}, f32[8,512]{1,0:T(8,128)S(1)}) custom-call(bf16[512,512]{1,0:T(8,128)(2,1)S(1)} %convert_element_type.3.h, bf16[256,512]{1,0:T(8,128)(2,1)} %collective-permute-done.7.refs_0_, bf16[256,512]{1,0:T(8,128)(2,1)} %collective-permute-done.8.refs_1_, ...), custom_call_target="tpu_custom_call", output_to_operand_aliasing={{0}: (4, {}), {1}: (5, {})} | custom-call | flops 1073741824 | bytes 1048576 | tf_op jit(solution)/shard_map/first_products/pallas_call | solution.py:216
  32.8 1.8 %collective-permute-start.9 = (s16[528,128]{1,0:T(8,128)(2,1)S(1)}, s16[528,128]{1,0:T(8,128)(2,1)S(1)}, u32[]{:S(2)}, u32[]{:S(2)}) collective-permute-start(s16[528,128]{1,0:T(8,128)(2,1)S(1)} %get-tuple-element.94.refs_0_), channel_id=1, source_target_pairs={{0,8},{8,0},{16,24},{24,16},{1,9},{9,1},{17,25},{25,17},{2,10},{10... | collective-permute-start | bytes 405512 | tf_op jit(solution)/shard_map/ppermute | solution.py:254
  34.6 3.8 %collective-permute-done.9.other = s16[528,128]{1,0:T(8,128)(2,1)S(1)} collective-permute-done((s16[528,128]{1,0:T(8,128)(2,1)S(1)}, s16[528,128]{1,0:T(8,128)(2,1)S(1)}, u32[]{:S(2)}, u32[]{:S(2)}) %collective-permute-start.9) | collective-permute-done | bytes 135200 | tf_op jit(solution)/shard_map/ppermute | solution.py:254
  38.5 1.8 %collective-permute-start.11 = (s16[528,128]{1,0:T(8,128)(2,1)S(1)}, s16[528,128]{1,0:T(8,128)(2,1)S(1)}, u32[]{:S(2)}, u32[]{:S(2)}) collective-permute-start(s16[528,128]{1,0:T(8,128)(2,1)S(1)} %get-tuple-element.97), channel_id=1, source_target_pairs={{0,8},{8,0},{16,24},{24,16},{1,9},{9,1},{17,25},{25,17},{2,10},{10... | collective-permute-start | bytes 405512 | tf_op jit(solution)/shard_map/ppermute | solution.py:254
  40.3 2.5 %collective-permute-start.10 = (s16[528,128]{1,0:T(8,128)(2,1)S(1)}, s16[528,128]{1,0:T(8,128)(2,1)S(1)}, u32[]{:S(2)}, u32[]{:S(2)}) collective-permute-start(s16[528,128]{1,0:T(8,128)(2,1)S(1)} %add_pair.2.one), channel_id=1, source_target_pairs={{0,24},{8,16},{16,8},{24,0},{1,25},{9,17},{17,9},{25,1},{2,26},{10... | collective-permute-start | bytes 405512 | tf_op jit(solution)/shard_map/ppermute | solution.py:254
  44.2 7.7 %collective-permute-start.12 = (s16[528,128]{1,0:T(8,128)(2,1)S(1)}, s16[528,128]{1,0:T(8,128)(2,1)S(1)}, u32[]{:S(2)}, u32[]{:S(2)}) collective-permute-start(s16[528,128]{1,0:T(8,128)(2,1)S(1)} %add_pair.3.one), channel_id=1, source_target_pairs={{0,24},{8,16},{16,8},{24,0},{1,25},{9,17},{17,9},{25,1},{2,26},{10... | collective-permute-start | bytes 405512 | tf_op jit(solution)/shard_map/ppermute | solution.py:254
  52.2 3.6 %collective-permute-done.12.other = s16[528,128]{1,0:T(8,128)(2,1)S(1)} collective-permute-done((s16[528,128]{1,0:T(8,128)(2,1)S(1)}, s16[528,128]{1,0:T(8,128)(2,1)S(1)}, u32[]{:S(2)}, u32[]{:S(2)}) %collective-permute-start.12) | collective-permute-done | bytes 135200 | tf_op jit(solution)/shard_map/ppermute | solution.py:254
  56.1 1.7 %collective-permute-done.13.refs_2_ = s16[528,128]{1,0:T(8,128)(2,1)S(1)} collective-permute-done((s16[528,128]{1,0:T(8,128)(2,1)S(1)}, s16[528,128]{1,0:T(8,128)(2,1)S(1)}, u32[]{:S(2)}, u32[]{:S(2)}) %collective-permute-start.13) | collective-permute-done | bytes 135200 | tf_op jit(solution)/shard_map/ppermute | solution.py:254
  57.8 3.2 %collective-permute-done.14.refs_3_ = s16[528,128]{1,0:T(8,128)(2,1)S(1)} collective-permute-done((s16[528,128]{1,0:T(8,128)(2,1)S(1)}, s16[528,128]{1,0:T(8,128)(2,1)S(1)}, u32[]{:S(2)}, u32[]{:S(2)}) %collective-permute-start.14) | collective-permute-done | bytes 135200 | tf_op jit(solution)/shard_map/ppermute | solution.py:254
  61.1 1.4 %h1_update.1 = (f32[512,512]{1,0:T(8,128)}, bf16[512,512]{1,0:T(8,128)(2,1)S(1)}, f32[512,512]{1,0:T(8,128)S(1)}) custom-call(s32[1]{0:T(128)} %bitcast.2.flag, s16[528,128]{1,0:T(8,128)(2,1)S(1)} %get-tuple-element.95.refs_0_, s16[528,128]{1,0:T(8,128)(2,1)S(1)} %add_cross.3.refs_1_, s16[528,128]{1,0:T(8,128)(2,1)S(1)} %collective-permute-done.13.refs_2_, ...), custom_call_target="tpu_custom_call" | custom-call | tf_op jit(solution)/shard_map/h1_update/pallas_call | solution.py:248
  63.0 3.1 %layer_two.1 = (f32[64,512]{1,0:T(8,128)}, f32[80,512]{1,0:T(8,128)S(1)}, s16[512,512]{1,0:T(8,128)(2,1)S(1)}) custom-call(f32[512,512]{1,0:T(8,128)S(1)} %get-tuple-element.99.h1_ref, f32[64,512]{1,0:T(8,128)S(1)} %bitcast.9, f32[64,512]{1,0:T(8,128)S(1)} %copy-done.3, s16[512,512]{1,0:T(8,128)(2,1)} %get-tuple-element.85.refs_0_.v), custom_call_target="tpu_custom_call" | custom-call | tf_op jit(solution)/shard_map/layer_two/pallas_call | solution.py:434
  66.7 2.5 %second_products.3 = (s16[272,512]{1,0:T(8,128)(2,1)}, s16[272,512]{1,0:T(8,128)(2,1)}) custom-call(bf16[512,512]{1,0:T(8,128)(2,1)S(1)} %get-tuple-element.101.ha, bf16[512,512]{1,0:T(8,128)(2,1)S(1)} %collective-permute-done.16.hb, bf16[256,512]{1,0:T(8,128)(2,1)S(1)} %collective-permute-done.3.refs_0_, ...), custom_call_target="tpu_custom_call" | custom-call | flops 1610612736 | bytes 1572864 | tf_op jit(solution)/shard_map/second_products/pallas_call | solution.py:216
  69.2 1.6 %collective-permute-start.18 = (f32[40,512]{1,0:T(8,128)S(1)}, f32[40,512]{1,0:T(8,128)S(1)}, u32[]{:S(2)}, u32[]{:S(2)}) collective-permute-start(f32[40,512]{1,0:T(8,128)S(1)} %half_sum.1.a_ref), channel_id=1, source_target_pairs={{0,2},{1,3},{2,0},{3,1},{4,6},{5,7},{6,4},{7,5},{8,10},{9,11},{10,... | collective-permute-start | bytes 245768 | tf_op jit(solution)/shard_map/ppermute | solution.py:254
  70.8 1.5 %collective-permute-start.23 = (s16[272,512]{1,0:T(8,128)(2,1)}, s16[272,512]{1,0:T(8,128)(2,1)}, u32[]{:S(2)}, u32[]{:S(2)}) collective-permute-start(s16[272,512]{1,0:T(8,128)(2,1)} %get-tuple-element.117), channel_id=1, source_target_pairs={{0,4},{1,5},{2,6},{3,7},{4,0},{5,1},{6,2},{7,3},{8,12},{9,13},{10,... | collective-permute-start | bytes 835592 | tf_op jit(solution)/shard_map/ppermute | solution.py:254
  72.3 1.8 %collective-permute-done.18.b_ref = f32[40,512]{1,0:T(8,128)S(1)} collective-permute-done((f32[40,512]{1,0:T(8,128)S(1)}, f32[40,512]{1,0:T(8,128)S(1)}, u32[]{:S(2)}, u32[]{:S(2)}) %collective-permute-start.18) | collective-permute-done | bytes 81952 | tf_op jit(solution)/shard_map/ppermute | solution.py:254
  74.1 1.5 %collective-permute-start.24 = (s16[272,512]{1,0:T(8,128)(2,1)}, s16[272,512]{1,0:T(8,128)(2,1)}, u32[]{:S(2)}, u32[]{:S(2)}) collective-permute-start(s16[272,512]{1,0:T(8,128)(2,1)} %get-tuple-element.119), channel_id=1, source_target_pairs={{0,2},{1,3},{2,0},{3,1},{4,6},{5,7},{6,4},{7,5},{8,10},{9,11},{10,... | collective-permute-start | bytes 835592 | tf_op jit(solution)/shard_map/ppermute | solution.py:254
  75.6 1.6 %collective-permute-start.21 = (f32[40,512]{1,0:T(8,128)S(1)}, f32[40,512]{1,0:T(8,128)S(1)}, u32[]{:S(2)}, u32[]{:S(2)}) collective-permute-start(f32[40,512]{1,0:T(8,128)S(1)} %add_two.2.a_ref), channel_id=1, source_target_pairs={{0,4},{1,5},{2,6},{3,7},{4,0},{5,1},{6,2},{7,3},{8,12},{9,13},{10,... | collective-permute-start | bytes 245768 | tf_op jit(solution)/shard_map/ppermute | solution.py:254
  77.2 4.1 %second_products.4 = (f32[512,512]{1,0:T(8,128)S(1)}, f32[512,512]{1,0:T(8,128)S(1)}) custom-call(bf16[512,512]{1,0:T(8,128)(2,1)S(1)} %get-tuple-element.101.ha, bf16[512,512]{1,0:T(8,128)(2,1)S(1)} %collective-permute-done.16.hb, bf16[512,512]{1,0:T(8,128)(2,1)} %copy-done.5, s16[512,512]{1,0:T(8,128)(2,1)} %get-tuple-element.71.refs_1_, ...), custom_call_target="tpu_custom_call" | custom-call | flops 3221225472 | bytes 3145728 | tf_op jit(solution)/shard_map/second_products/pallas_call | solution.py:216
  81.3 2.6 %second_products.5.own = f32[512,512]{1,0:T(8,128)S(1)} custom-call(bf16[512,512]{1,0:T(8,128)(2,1)S(1)} %get-tuple-element.101.ha, bf16[512,512]{1,0:T(8,128)(2,1)S(1)} %collective-permute-done.16.hb, bf16[512,512]{1,0:T(8,128)(2,1)} %w_ref.1, s16[512,512]{1,0:T(8,128)(2,1)} %get-tuple-element.65.refs_1_, s16[512,512]{1,0:T(8,128)(2,1)S(1)} %collective-permute-done.22.refs_2_), custom_call_target="tpu_custom_call" | custom-call | flops 1610612736 | bytes 1572864 | tf_op jit(solution)/shard_map/second_products/pallas_call | solution.py:216
  84.0 1.9 %relay_add.1 = (s16[528,512]{1,0:T(8,128)(2,1)S(1)}, s16[528,512]{1,0:T(8,128)(2,1)S(1)}) custom-call(f32[512,512]{1,0:T(8,128)S(1)} %get-tuple-element.116.x, s16[272,512]{1,0:T(8,128)(2,1)} %collective-permute-done.23.x_in, f32[512,512]{1,0:T(8,128)S(1)} %get-tuple-element.118.y, s16[272,512]{1,0:T(8,128)(2,1)} %collective-permute-done.24.y_in), custom_call_target="tpu_custom_call" | custom-call | tf_op jit(solution)/shard_map/relay_add/pallas_call | solution.py:248
  88.3 12.3 %collective-permute-done.25.x = s16[528,512]{1,0:T(8,128)(2,1)S(1)} collective-permute-done((s16[528,512]{1,0:T(8,128)(2,1)S(1)}, s16[528,512]{1,0:T(8,128)(2,1)S(1)}, u32[]{:S(2)}, u32[]{:S(2)}) %collective-permute-start.25) | collective-permute-done | bytes 540704 | tf_op jit(solution)/shard_map/ppermute | solution.py:254
  101.9 1.3 %w1_update.1 = bf16[512,512]{1,0:T(8,128)(2,1)} custom-call(f32[512,512]{1,0:T(8,128)S(1)} %second_products.5.own, s16[528,512]{1,0:T(8,128)(2,1)S(1)} %collective-permute-done.25.x, s16[528,512]{1,0:T(8,128)(2,1)S(1)} %collective-permute-done.26.y, bf16[512,512]{1,0:T(8,128)(2,1)S(1)} %copy-done.2, f32[8,512]{1,0:T(8,128)S(1)} %slice.20.row_ref), custom_call_target="tpu_custom_call" | custom-call | tf_op jit(solution)/shard_map/w1_update/pallas_call | solution.py:248
  (71 shorter events, 12.3 us)
Async XLA Ops:
  0.6 11.9 %collective-permute-start.2 = (bf16[512,512]{1,0:T(8,128)(2,1)}, bf16[512,512]{1,0:T(8,128)(2,1)S(1)}, u32[]{:S(2)}, u32[]{:S(2)}) collective-permute-start(bf16[512,512]{1,0:T(8,128)(2,1)} %w_ref.1), channel_id=1, source_target_pairs={{0,1},{1,0},{2,3},{3,2},{4,5},{5,4},{6,7},{7,6},{8,9},{9,8},{10,11... | collective-permute-start | bytes 1572872 | tf_op jit(solution)/shard_map/ppermute | solution.py:254
  1.1 15.3 %collective-permute-start = (bf16[512,512]{1,0:T(8,128)(2,1)}, bf16[512,512]{1,0:T(8,128)(2,1)S(1)}, u32[]{:S(2)}, u32[]{:S(2)}) collective-permute-start(bf16[512,512]{1,0:T(8,128)(2,1)} %w_ref.1), channel_id=1, source_target_pairs={{0,2},{1,3},{2,0},{3,1},{4,6},{5,7},{6,4},{7,5},{8,10},{9,11},{10,... | collective-permute-start | bytes 1572872 | tf_op jit(solution)/shard_map/ppermute | solution.py:254
  3.7 14.3 %collective-permute-start.1 = (bf16[512,512]{1,0:T(8,128)(2,1)}, bf16[512,512]{1,0:T(8,128)(2,1)}, u32[]{:S(2)}, u32[]{:S(2)}) collective-permute-start(bf16[512,512]{1,0:T(8,128)(2,1)} %w_ref.1), channel_id=1, source_target_pairs={{0,4},{1,5},{2,6},{3,7},{4,0},{5,1},{6,2},{7,3},{8,12},{9,13},{10,... | collective-permute-start | bytes 1572872 | tf_op jit(solution)/shard_map/ppermute | solution.py:254
  18.0 3.6 %collective-permute-start.5 = (bf16[512,512]{1,0:T(8,128)(2,1)S(1)}, bf16[512,512]{1,0:T(8,128)(2,1)S(1)}, u32[]{:S(2)}, u32[]{:S(2)}) collective-permute-start(bf16[512,512]{1,0:T(8,128)(2,1)S(1)} %collective-permute-done.refs_0_), channel_id=1, source_target_pairs={{0,1},{1,0},{2,3},{3,2},{4,5},{5,4},{6,7},{7,6},{8,9},{9,8},{10,11... | collective-permute-start | bytes 1572872 | tf_op jit(solution)/shard_map/ppermute | solution.py:254
  18.0 3.6 %collective-permute-start.6 = (bf16[512,512]{1,0:T(8,128)(2,1)}, bf16[512,512]{1,0:T(8,128)(2,1)S(1)}, u32[]{:S(2)}, u32[]{:S(2)}) collective-permute-start(bf16[512,512]{1,0:T(8,128)(2,1)} %collective-permute-done.1.refs_2_.refs_3_), channel_id=1, source_target_pairs={{0,1},{1,0},{2,3},{3,2},{4,5},{5,4},{6,7},{7,6},{8,9},{9,8},{10,11... | collective-permute-start | bytes 1572872 | tf_op jit(solution)/shard_map/ppermute | solution.py:254
  19.5 8.3 %collective-permute-start.3 = (bf16[256,512]{1,0:T(8,128)(2,1)S(1)}, bf16[256,512]{1,0:T(8,128)(2,1)S(1)}, u32[]{:S(2)}, u32[]{:S(2)}) collective-permute-start(bf16[256,512]{1,0:T(8,128)(2,1)S(1)} %slice.15), channel_id=1, source_target_pairs={{0,2},{1,3},{2,0},{3,1},{4,6},{5,7},{6,4},{7,5},{8,10},{9,11},{10,... | collective-permute-start | bytes 786440 | tf_op jit(solution)/shard_map/ppermute | solution.py:254
  19.9 7.9 %collective-permute-start.4 = (bf16[256,512]{1,0:T(8,128)(2,1)S(1)}, bf16[256,512]{1,0:T(8,128)(2,1)S(1)}, u32[]{:S(2)}, u32[]{:S(2)}) collective-permute-start(bf16[256,512]{1,0:T(8,128)(2,1)S(1)} %slice.16), channel_id=1, source_target_pairs={{0,4},{1,5},{2,6},{3,7},{4,0},{5,1},{6,2},{7,3},{8,12},{9,13},{10,... | collective-permute-start | bytes 786440 | tf_op jit(solution)/shard_map/ppermute | solution.py:254
  26.1 34.9 %copy-start = (f32[512,512]{1,0:T(8,128)S(1)}, f32[512,512]{1,0:T(8,128)}, u32[]{:S(2)}) copy-start(f32[512,512]{1,0:T(8,128)} %refs_4_.1) | copy-start | bytes 3145732
  26.1 36.9 %copy-start.1 = (f32[512,64]{0,1:T(8,128)S(1)}, f32[512,64]{0,1:T(8,128)}, u32[]{:S(2)}) copy-start(f32[512,64]{0,1:T(8,128)} %param.8) | copy-start | bytes 393220
  26.2 36.9 %copy-start.3 = (f32[64,512]{1,0:T(8,128)S(1)}, f32[64,512]{1,0:T(8,128)}, u32[]{:S(2)}) copy-start(f32[64,512]{1,0:T(8,128)} %h2_ref.1) | copy-start | bytes 393220
  27.9 2.7 %collective-permute-start.7 = (bf16[256,512]{1,0:T(8,128)(2,1)S(1)}, bf16[256,512]{1,0:T(8,128)(2,1)}, u32[]{:S(2)}, u32[]{:S(2)}) collective-permute-start(bf16[256,512]{1,0:T(8,128)(2,1)S(1)} %collective-permute-done.3.refs_0_), channel_id=1, source_target_pairs={{0,1},{1,0},{2,3},{3,2},{4,5},{5,4},{6,7},{7,6},{8,9},{9,8},{10,11... | collective-permute-start | bytes 786440 | tf_op jit(solution)/shard_map/ppermute | solution.py:254
  27.9 2.7 %collective-permute-start.8 = (bf16[256,512]{1,0:T(8,128)(2,1)S(1)}, bf16[256,512]{1,0:T(8,128)(2,1)}, u32[]{:S(2)}, u32[]{:S(2)}) collective-permute-start(bf16[256,512]{1,0:T(8,128)(2,1)S(1)} %collective-permute-done.4.refs_1_), channel_id=1, source_target_pairs={{0,1},{1,0},{2,3},{3,2},{4,5},{5,4},{6,7},{7,6},{8,9},{9,8},{10,11... | collective-permute-start | bytes 786440 | tf_op jit(solution)/shard_map/ppermute | solution.py:254
  28.4 38.2 %copy-start.6 = (s16[512,512]{1,0:T(8,128)(2,1)S(1)}, s16[512,512]{1,0:T(8,128)(2,1)}, u32[]{:S(2)}) copy-start(s16[512,512]{1,0:T(8,128)(2,1)} %get-tuple-element.66.refs_3_) | copy-start | bytes 1572868
  32.8 5.6 %collective-permute-start.9 = (s16[528,128]{1,0:T(8,128)(2,1)S(1)}, s16[528,128]{1,0:T(8,128)(2,1)S(1)}, u32[]{:S(2)}, u32[]{:S(2)}) collective-permute-start(s16[528,128]{1,0:T(8,128)(2,1)S(1)} %get-tuple-element.94.refs_0_), channel_id=1, source_target_pairs={{0,8},{8,0},{16,24},{24,16},{1,9},{9,1},{17,25},{25,17},{2,10},{10... | collective-permute-start | bytes 405512 | tf_op jit(solution)/shard_map/ppermute | solution.py:254
  38.5 5.5 %collective-permute-start.11 = (s16[528,128]{1,0:T(8,128)(2,1)S(1)}, s16[528,128]{1,0:T(8,128)(2,1)S(1)}, u32[]{:S(2)}, u32[]{:S(2)}) collective-permute-start(s16[528,128]{1,0:T(8,128)(2,1)S(1)} %get-tuple-element.97), channel_id=1, source_target_pairs={{0,8},{8,0},{16,24},{24,16},{1,9},{9,1},{17,25},{25,17},{2,10},{10... | collective-permute-start | bytes 405512 | tf_op jit(solution)/shard_map/ppermute | solution.py:254
  40.3 11.6 %collective-permute-start.10 = (s16[528,128]{1,0:T(8,128)(2,1)S(1)}, s16[528,128]{1,0:T(8,128)(2,1)S(1)}, u32[]{:S(2)}, u32[]{:S(2)}) collective-permute-start(s16[528,128]{1,0:T(8,128)(2,1)S(1)} %add_pair.2.one), channel_id=1, source_target_pairs={{0,24},{8,16},{16,8},{24,0},{1,25},{9,17},{17,9},{25,1},{2,26},{10... | collective-permute-start | bytes 405512 | tf_op jit(solution)/shard_map/ppermute | solution.py:254
  44.2 11.6 %collective-permute-start.12 = (s16[528,128]{1,0:T(8,128)(2,1)S(1)}, s16[528,128]{1,0:T(8,128)(2,1)S(1)}, u32[]{:S(2)}, u32[]{:S(2)}) collective-permute-start(s16[528,128]{1,0:T(8,128)(2,1)S(1)} %add_pair.3.one), channel_id=1, source_target_pairs={{0,24},{8,16},{16,8},{24,0},{1,25},{9,17},{17,9},{25,1},{2,26},{10... | collective-permute-start | bytes 405512 | tf_op jit(solution)/shard_map/ppermute | solution.py:254
  52.1 5.7 %collective-permute-start.13 = (s16[528,128]{1,0:T(8,128)(2,1)S(1)}, s16[528,128]{1,0:T(8,128)(2,1)S(1)}, u32[]{:S(2)}, u32[]{:S(2)}) collective-permute-start(s16[528,128]{1,0:T(8,128)(2,1)S(1)} %get-tuple-element.95.refs_0_), channel_id=1, source_target_pairs={{0,8},{8,0},{16,24},{24,16},{1,9},{9,1},{17,25},{25,17},{2,10},{10... | collective-permute-start | bytes 405512 | tf_op jit(solution)/shard_map/ppermute | solution.py:254
  56.0 5.1 %collective-permute-start.14 = (s16[528,128]{1,0:T(8,128)(2,1)S(1)}, s16[528,128]{1,0:T(8,128)(2,1)S(1)}, u32[]{:S(2)}, u32[]{:S(2)}) collective-permute-start(s16[528,128]{1,0:T(8,128)(2,1)S(1)} %add_cross.3.refs_1_), channel_id=1, source_target_pairs={{0,8},{8,0},{16,24},{24,16},{1,9},{9,1},{17,25},{25,17},{2,10},{10... | collective-permute-start | bytes 405512 | tf_op jit(solution)/shard_map/ppermute | solution.py:254
  56.1 10.6 %collective-permute-start.17 = (s16[512,512]{1,0:T(8,128)(2,1)S(1)}, s16[512,512]{1,0:T(8,128)(2,1)S(1)}, u32[]{:S(2)}, u32[]{:S(2)}) collective-permute-start(s16[512,512]{1,0:T(8,128)(2,1)S(1)} %copy-done.4), channel_id=1, source_target_pairs={{0,1},{1,0},{2,3},{3,2},{4,5},{5,4},{6,7},{7,6},{8,9},{9,8},{10,11... | collective-permute-start | bytes 1572872 | tf_op jit(solution)/shard_map/ppermute | solution.py:254
  62.4 4.3 %collective-permute-start.16 = (bf16[512,512]{1,0:T(8,128)(2,1)S(1)}, bf16[512,512]{1,0:T(8,128)(2,1)S(1)}, u32[]{:S(2)}, u32[]{:S(2)}) collective-permute-start(bf16[512,512]{1,0:T(8,128)(2,1)S(1)} %get-tuple-element.101.ha), channel_id=1, source_target_pairs={{0,1},{1,0},{2,3},{3,2},{4,5},{5,4},{6,7},{7,6},{8,9},{9,8},{10,11... | collective-permute-start | bytes 1572872 | tf_op jit(solution)/shard_map/ppermute | solution.py:254
  62.5 13.1 %collective-permute-start.19 = (s16[512,512]{1,0:T(8,128)(2,1)S(1)}, s16[512,512]{1,0:T(8,128)(2,1)S(1)}, u32[]{:S(2)}, u32[]{:S(2)}) collective-permute-start(s16[512,512]{1,0:T(8,128)(2,1)S(1)} %copy-done.8), channel_id=1, source_target_pairs={{0,1},{1,0},{2,3},{3,2},{4,5},{5,4},{6,7},{7,6},{8,9},{9,8},{10,11... | collective-permute-start | bytes 1572872 | tf_op jit(solution)/shard_map/ppermute | solution.py:254
  63.0 14.2 %collective-permute-start.20 = (s16[512,512]{1,0:T(8,128)(2,1)S(1)}, s16[512,512]{1,0:T(8,128)(2,1)S(1)}, u32[]{:S(2)}, u32[]{:S(2)}) collective-permute-start(s16[512,512]{1,0:T(8,128)(2,1)S(1)} %copy-done.7), channel_id=1, source_target_pairs={{0,1},{1,0},{2,3},{3,2},{4,5},{5,4},{6,7},{7,6},{8,9},{9,8},{10,11... | collective-permute-start | bytes 1572872 | tf_op jit(solution)/shard_map/ppermute | solution.py:254
  66.1 3.1 %collective-permute-start.15 = (f32[80,512]{1,0:T(8,128)S(1)}, f32[80,512]{1,0:T(8,128)S(1)}, u32[]{:S(2)}, u32[]{:S(2)}) collective-permute-start(f32[80,512]{1,0:T(8,128)S(1)} %get-tuple-element.104.a_ref), channel_id=1, source_target_pairs={{0,1},{1,0},{2,3},{3,2},{4,5},{5,4},{6,7},{7,6},{8,9},{9,8},{10,11... | collective-permute-start | bytes 491528 | tf_op jit(solution)/shard_map/ppermute | solution.py:254
  66.6 14.6 %collective-permute-start.22 = (s16[512,512]{1,0:T(8,128)(2,1)S(1)}, s16[512,512]{1,0:T(8,128)(2,1)S(1)}, u32[]{:S(2)}, u32[]{:S(2)}) collective-permute-start(s16[512,512]{1,0:T(8,128)(2,1)S(1)} %copy-done.6), channel_id=1, source_target_pairs={{0,1},{1,0},{2,3},{3,2},{4,5},{5,4},{6,7},{7,6},{8,9},{9,8},{10,11... | collective-permute-start | bytes 1572872 | tf_op jit(solution)/shard_map/ppermute | solution.py:254
  69.2 4.8 %collective-permute-start.18 = (f32[40,512]{1,0:T(8,128)S(1)}, f32[40,512]{1,0:T(8,128)S(1)}, u32[]{:S(2)}, u32[]{:S(2)}) collective-permute-start(f32[40,512]{1,0:T(8,128)S(1)} %half_sum.1.a_ref), channel_id=1, source_target_pairs={{0,2},{1,3},{2,0},{3,1},{4,6},{5,7},{6,4},{7,5},{8,10},{9,11},{10,... | collective-permute-start | bytes 245768 | tf_op jit(solution)/shard_map/ppermute | solution.py:254
  70.8 13.2 %collective-permute-start.23 = (s16[272,512]{1,0:T(8,128)(2,1)}, s16[272,512]{1,0:T(8,128)(2,1)}, u32[]{:S(2)}, u32[]{:S(2)}) collective-permute-start(s16[272,512]{1,0:T(8,128)(2,1)} %get-tuple-element.117), channel_id=1, source_target_pairs={{0,4},{1,5},{2,6},{3,7},{4,0},{5,1},{6,2},{7,3},{8,12},{9,13},{10,... | collective-permute-start | bytes 835592 | tf_op jit(solution)/shard_map/ppermute | solution.py:254
  74.1 9.9 %collective-permute-start.24 = (s16[272,512]{1,0:T(8,128)(2,1)}, s16[272,512]{1,0:T(8,128)(2,1)}, u32[]{:S(2)}, u32[]{:S(2)}) collective-permute-start(s16[272,512]{1,0:T(8,128)(2,1)} %get-tuple-element.119), channel_id=1, source_target_pairs={{0,2},{1,3},{2,0},{3,1},{4,6},{5,7},{6,4},{7,5},{8,10},{9,11},{10,... | collective-permute-start | bytes 835592 | tf_op jit(solution)/shard_map/ppermute | solution.py:254
  75.6 8.3 %collective-permute-start.21 = (f32[40,512]{1,0:T(8,128)S(1)}, f32[40,512]{1,0:T(8,128)S(1)}, u32[]{:S(2)}, u32[]{:S(2)}) collective-permute-start(f32[40,512]{1,0:T(8,128)S(1)} %add_two.2.a_ref), channel_id=1, source_target_pairs={{0,4},{1,5},{2,6},{3,7},{4,0},{5,1},{6,2},{7,3},{8,12},{9,13},{10,... | collective-permute-start | bytes 245768 | tf_op jit(solution)/shard_map/ppermute | solution.py:254
  83.9 3.6 %collective-permute-start.27 = (f32[40,512]{1,0:T(8,128)S(1)}, f32[40,512]{1,0:T(8,128)S(1)}, u32[]{:S(2)}, u32[]{:S(2)}) collective-permute-start(f32[40,512]{1,0:T(8,128)S(1)} %add_two.3), channel_id=1, source_target_pairs={{0,1},{1,0},{2,3},{3,2},{4,5},{5,4},{6,7},{7,6},{8,9},{9,8},{10,11... | collective-permute-start | bytes 245768 | tf_op jit(solution)/shard_map/ppermute | solution.py:254
  85.9 14.7 %collective-permute-start.25 = (s16[528,512]{1,0:T(8,128)(2,1)S(1)}, s16[528,512]{1,0:T(8,128)(2,1)S(1)}, u32[]{:S(2)}, u32[]{:S(2)}) collective-permute-start(s16[528,512]{1,0:T(8,128)(2,1)S(1)} %get-tuple-element.120), channel_id=1, source_target_pairs={{0,2},{1,3},{2,0},{3,1},{4,6},{5,7},{6,4},{7,5},{8,10},{9,11},{10,... | collective-permute-start | bytes 1622024 | tf_op jit(solution)/shard_map/ppermute | solution.py:254
  86.5 14.4 %collective-permute-start.26 = (s16[528,512]{1,0:T(8,128)(2,1)S(1)}, s16[528,512]{1,0:T(8,128)(2,1)S(1)}, u32[]{:S(2)}, u32[]{:S(2)}) collective-permute-start(s16[528,512]{1,0:T(8,128)(2,1)S(1)} %get-tuple-element.121), channel_id=1, source_target_pairs={{0,4},{1,5},{2,6},{3,7},{4,0},{5,1},{6,2},{7,3},{8,12},{9,13},{10,... | collective-permute-start | bytes 1622024 | tf_op jit(solution)/shard_map/ppermute | solution.py:254
  (5 other events, 102.5 us)

commit v3 on v2

--- a/solution.py
+++ b/solution.py
@@ -21,34 +21,53 @@
     return lax.dot_general(a, b, ((dims[:1], dims[1:]), ((), ())), preferred_element_type=F32)
 
 
-def encode(x, out_ref, extra=None):
+def power_of(x):
+    return jnp.ceil(jnp.log2(jnp.maximum(x, 1e-30)))
+
+
+def encode(x, out_ref, extra=None, singles=(), at=0):
     rows, cols = x.shape
-    top = jnp.maximum(jnp.max(x, axis=0, keepdims=True), 1e-30)
-    power = jnp.ceil(jnp.log2(top))
+    power = power_of(jnp.max(x, axis=0, keepdims=True))
     q = jnp.minimum(x * (jnp.exp2(-power) * 65535.0) + 0.5, 65535.0)
-    out_ref[:rows, :] = (q.astype(jnp.int32) - 32768).astype(jnp.int16)
+    out_ref[at : at + rows, :] = (q.astype(jnp.int32) - 32768).astype(jnp.int16)
     lines = [power]
     if extra is not None:
         whole = jnp.floor(extra)
         for y in (whole, jnp.floor((extra - whole) * 32768.0 + 0.25)):
             lines += [y[:, i : i + cols] for i in range(0, y.shape[1], cols)]
+    for y in singles:
+        own = power_of(y)
+        y = y * (jnp.exp2(-own) * 32767.0)
+        whole = jnp.floor(y)
+        lines += [own, whole, jnp.floor((y - whole) * 32768.0)]
     lines.append(jnp.zeros((PAD - len(lines), cols), F32))
-    out_ref[rows:, :] = jnp.concatenate(lines, axis=0).astype(jnp.int32).astype(jnp.int16)
+    out_ref[at + rows : at + rows + PAD, :] = jnp.concatenate(lines, axis=0).astype(jnp.int32).astype(jnp.int16)
+
+
+def pad_rows(ref, end):
+    return ref[end - PAD : end, :].astype(jnp.int32).astype(F32)
 
 
 def decode_extra(ref, width):
-    rows, cols = ref.shape[0] - PAD, ref.shape[1]
-    n = width // cols
-    lines = ref[rows:, :].astype(jnp.int32).astype(F32)
+    n = width // ref.shape[1]
+    lines = pad_rows(ref, ref.shape[0])
     lines = [lines[1 + i : 2 + i] for i in range(2 * n)]
     return jnp.concatenate(lines[:n], axis=1) + jnp.concatenate(lines[n:], axis=1) * (1.0 / 32768.0)
 
 
-def decode(ref):
-    rows = ref.shape[0] - PAD
-    power = ref[rows:, :].astype(jnp.int32).astype(F32)[:1]
-    unit = jnp.exp2(power) * (1.0 / 65535.0)
-    return (ref[:rows, :].astype(jnp.int32) + 32768).astype(F32) * unit
+def decode_singles(ref, n, end):
+    lines = pad_rows(ref, end)
+    found = []
+    for i in range(1, 1 + 3 * n, 3):
+        unit = jnp.exp2(lines[i : i + 1]) * (1.0 / 32767.0)
+        found.append((lines[i + 1 : i + 2] + lines[i + 2 : i + 3] * (1.0 / 32768.0)) * unit)
+    return found
+
+
+def decode(ref, rows=None, at=0):
+    rows = ref.shape[0] - PAD if rows is None else rows
+    unit = jnp.exp2(pad_rows(ref, at + rows + PAD)[:1]) * (1.0 / 65535.0)
+    return (ref[at : at + rows, :].astype(jnp.int32) + 32768).astype(F32) * unit
 
 
 def coded(rows, cols):
@@ -299,25 +318,38 @@
     low_ref[...] = new.astype(BF16)
 
 
-def relay_add(x, x_in, y, y_in, x_ref, y_ref):
-    half = x.shape[0] // 2
-    encode(jnp.concatenate([x[:half, :], x[half:, :] + decode(x_in)], axis=0), x_ref)
-    encode(jnp.concatenate([y[:half, :] + decode(y_in), y[half:, :]], axis=0), y_ref)
-
-
-def half_sum(core, a_ref, b_ref, out_ref):
-    half = out_ref.shape[0]
-    total = a_ref[...] + b_ref[...]
-    out_ref[...] = jnp.where(core[0] == 0, total[:half], total[half:])
-
-
-def add_two(a_ref, b_ref, out_ref):
-    out_ref[...] = a_ref[...] + b_ref[...]
-
-
-def w1_update(own, x, y, w_ref, row_ref, out_ref):
-    total = own[...] + decode(x) + decode(y)
-    out_ref[...] = (w_ref[...].astype(F32) * total / row_ref[:1, :]).astype(BF16)
+def pack(k2, lo, hi, sums, sums_in, lo_ref, hi_ref):
+    total = sums[...] + sums_in[...]
+    t, half = lo.shape[0], k2 // 2
+    encode(lo[...], lo_ref)
+    encode(total[:half], lo_ref, singles=(total[k2 : k2 + 1], total[k2 + 8 : k2 + 9]), at=t + PAD)
+    encode(hi[...], hi_ref)
+    encode(total[half:k2], hi_ref, at=t + PAD)
+
+
+def relay_add(k2, x, x_in, y, y_in, lo, hi, x_ref, y_ref, x_sums, y_sums):
+    rows, half = x.shape[0], x.shape[0] // 2
+    encode(jnp.concatenate([x[:half, :], x[half:, :] + decode(x_in, half)], axis=0), x_ref)
+    encode(jnp.concatenate([y[:half, :] + decode(y_in, half), y[half:, :]], axis=0), y_ref)
+    at, few = half + PAD, k2 // 2
+    one = [a + b for a, b in zip(decode_singles(lo, 2, lo.shape[0]), decode_singles(y_in, 2, lo.shape[0]))]
+    encode(decode(lo, few, at) + decode(y_in, few, at), y_sums, singles=one)
+    encode(decode(hi, few, at) + decode(x_in, few, at), x_sums)
+    x_ref[rows + PAD :, :] = x_sums[...]
+    y_ref[rows + PAD :, :] = y_sums[...]
+
+
+def last_update(own, x, y, x_sums, y_sums, w_ref, w2t_ref, w1_ref, w2_ref):
+    rows, few = own.shape[0], x_sums.shape[0] - PAD
+    total = own[...] + decode(x, rows) + decode(y, rows)
+    singles = zip(decode_singles(y_sums, 2, few + PAD), decode_singles(y, 2, y.shape[0]))
+    row, h2_row = [a + b for a, b in singles]
+    w1_ref[...] = (w_ref[...].astype(F32) * total / row).astype(BF16)
+    h2_col = jnp.broadcast_to(h2_row, (8, h2_row.shape[1])).T[: 2 * few, :1]
+    at = rows + PAD
+    low = decode(y_sums, few) + decode(y, few, at)
+    high = decode(x_sums, few) + decode(x, few, at)
+    w2_ref[...] = w2t_ref[...] * jnp.concatenate([low, high], axis=0) / h2_col
 
 
 def parts(x):
@@ -447,28 +479,31 @@
     low2 = (h1_low2, h1_low2_other)
     if line:
         sums_in = cell(sums, bit=1)
-        d_lo, d_hi = second(((d_lo, d_hi, v_far, v_other[3]),), t, low2, True)
-        half = jax.ShapeDtypeStruct(((k2 + 16) // 2, k1), F32)
+        d_lo, d_hi = second(((d_lo, d_hi, v_far, v_other[3]),), t, low2, False)
         sums, sums_in, d_lo = after((sums, sums_in, d_lo))
-        part = plain(half_sum, half, sums, sums_in, flag=core.astype(jnp.int32)[None], name="half_sum")
-        part, d_lo, d_hi = after((part, d_lo, d_hi))
-        part_in = cell(part, bit=2)
+        few = k2 // 2 + PAD
+        with_sums = coded(t + few, k1)
+        d_lo, d_hi = plain(
+            functools.partial(pack, k2), (with_sums, with_sums), d_lo, d_hi, sums, sums_in, name="pack"
+        )
         y_in, x_in = cell(d_lo, bit=2), cell(d_hi, bit=4)
-        part = plain(add_two, half, part, part_in, name="add_two")
-        w_x, part = after((w_x, part))
-        part_in = cell(part, bit=4)
+        w_x, d_lo = after((w_x, d_lo))
         near = ((Later(w_x), on_mine[1], v_other[1]), (Later(w_y), on_mine[2], v_other[2]))
         x_num, y_num = second(near, rows, low2, False)
-        part, x_num = after((part, x_num))
-        w1_late, part = after((w1, part))
+        with_sums = coded(rows + few, k1)
+        sums_only = jax.ShapeDtypeStruct((few, k1), jnp.int16)
+        x_num, y_num, x_sums, y_sums = plain(
+            functools.partial(relay_add, k2), (with_sums, with_sums, sums_only, sums_only),
+            x_num, x_in, y_num, y_in, d_lo, d_hi, name="relay_add",
+        )
+        x_num_in, y_num_in = cell(x_num, bit=2), cell(y_num, bit=4)
+        w1_late, x_num = after((w1, x_num))
         (own,) = second(((Later(w1_late), on_mine[0], v_other[0]),), rows, low2, False)
-        piece = coded(rows, k1)
-        x_num, part_in, own = after((x_num, part_in, own))
-        x_num, y_num = plain(relay_add, (piece, piece), x_num, x_in, y_num, y_in, name="relay_add")
-        x_num_in, y_num_in = cell(x_num, bit=2), cell(y_num, bit=4)
-        part = plain(add_two, half, part, part_in, name="add_two")
-        rest = cell(part, bit=1)
-        sums = jnp.where(core == 0, jnp.concatenate([part, rest]), jnp.concatenate([rest, part]))
+        w1_new, w2_new = plain(
+            last_update, (jax.ShapeDtypeStruct((rows, k1), BF16), jax.ShapeDtypeStruct((k2, k1), F32)),
+            own, x_num_in, y_num_in, x_sums, y_sums, w1, w2t, name="last_update",
+        )
+        w2_new = w2_new.T
     else:
         found = []
         for i in range(0, chips, each):
@@ -478,14 +513,8 @@
             jnp.concatenate(found), "cell", scatter_dimension=0, tiled=True, axis_index_groups=groups
         )
         sums = lax.psum(sums, "cell")
-    w2_num, rowsum, h2_rows = sums[:k2], sums[k2 : k2 + 8], sums[k2 + 8, :k2]
-    w2_new = (w2t * w2_num / h2_rows[:, None]).T
-    if line:
-        w1_new = plain(
-            w1_update, jax.ShapeDtypeStruct((rows, k1), BF16), own, x_num_in, y_num_in, w1, rowsum, name="w1_update"
-        )
-    else:
-        w1_new = (w1.astype(F32) * w1_num / rowsum[:1]).astype(BF16)
+        w2_new = (w2t * sums[:k2] / sums[k2 + 8, :k2, None]).T
+        w1_new = (w1.astype(F32) * w1_num / sums[k2 : k2 + 1]).astype(BF16)
     return (w1_new, h1_new, w2_new, h2_new)
 
 

time: 104 us -> 98.3 us (0.945)
  starting transfers between devices: 30.9 us -> 28.1 us
    ppermute x28 -> x25, starting transfers between devices: 30.9 us -> 28.1 us  [flip(): return lax.ppermute(x, axis, [(i, i ^ bit) for i in range(size)])]
    pallas_call x7, Pallas kernels: 19.3 us -> 18 us  [products(): pl.pallas_call(functools.partial(body, sizes, later, len(fetch), flag), o...]
    pallas_call x11 -> x9, Pallas kernels: 5.48 us -> 5.9 us  [plain(): pl.pallas_call(body, out_shape=outs, in_specs=specs, out_specs=out_specs,...]
    ppermute x28 -> x25, waiting for transfers between devices: 32.1 us -> 32.5 us  [flip(): return lax.ppermute(x, axis, [(i, i ^ bit) for i in range(size)])]
  transfers between devices with their start and end apart: 28 -> 25, of which waited for: 12 -> 13; matrix products, arithmetic and copies ran while one was open for 3% -> 2% of each run, Pallas kernels for 31% -> 31%
where the time goes in v3:
time: 98.3 us; the launch traced here: 98 us
  Pallas kernels  34.2 us (35%)
  waiting for transfers between devices  32.5 us (33%)
  starting transfers between devices  28.1 us (29%)
  other arithmetic  1.37 us (1%)
  local copies, waits for them, and re-layouts  1.03 us (1%)
    ppermute x25, waiting for transfers between devices, flip(): return lax.ppermute(x, axis, [(i, i ^ bit) for i in range(size)])  32.5 us
    ppermute x25, starting transfers between devices, flip(): return lax.ppermute(x, axis, [(i, i ^ bit) for i in range(size)])  28.1 us
    pallas_call x7, Pallas kernels, products(): pl.pallas_call(functools.partial(body, sizes, later, len(fetch), flag), o...  18 us
    pallas_call x9, Pallas kernels, plain(): pl.pallas_call(body, out_shape=outs, in_specs=specs, out_specs=out_specs,...  5.9 us
    pallas_call x1, Pallas kernels, split_counts(): pl.pallas_call(functools.partial(counts_body, chips, rows), out_shape=(ou...  5.89 us
    pallas_call x1, Pallas kernels, on_device(): pl.pallas_call(layer_two, out_shape=(jax.ShapeDtypeStruct((k2, cells), F3...  3.07 us
  transfers between devices with their start and end apart: 25, of which 13 were waited for; matrix products, arithmetic and copies ran while one was open for 2% of the time, Pallas kernels for 31%

profile of v3, /device:TPU:0, one launch (start us, length us, event | category | flops | bytes accessed | tf_op | source)
XLA Modules:
  0.0 98.0 jit_solution(8102645502186032544)
XLA Ops:
  1.1 2.6 %collective-permute-start = (bf16[512,512]{1,0:T(8,128)(2,1)}, bf16[512,512]{1,0:T(8,128)(2,1)S(1)}, u32[]{:S(2)}, u32[]{:S(2)}) collective-permute-start(bf16[512,512]{1,0:T(8,128)(2,1)} %w_ref.1), channel_id=1, source_target_pairs={{0,2},{1,3},{2,0},{3,1},{4,6},{5,7},{6,4},{7,5},{8,10},{9,11},{10,... | collective-permute-start | bytes 1572872 | tf_op jit(solution)/shard_map/ppermute | solution.py:273
  3.7 1.5 %collective-permute-start.1 = (bf16[512,512]{1,0:T(8,128)(2,1)}, bf16[512,512]{1,0:T(8,128)(2,1)}, u32[]{:S(2)}, u32[]{:S(2)}) collective-permute-start(bf16[512,512]{1,0:T(8,128)(2,1)} %w_ref.1), channel_id=1, source_target_pairs={{0,4},{1,5},{2,6},{3,7},{4,0},{5,1},{6,2},{7,3},{8,12},{9,13},{10,... | collective-permute-start | bytes 1572872 | tf_op jit(solution)/shard_map/ppermute | solution.py:273
  5.2 1.3 %convert_element_type.3.h = bf16[512,512]{1,0:T(8,128)(2,1)S(1)} convert(f32[512,512]{1,0:T(8,128)} %refs_4_.1) | non-fusion elementwise | flops 262144 | bytes 1572864 | tf_op jit(solution)/shard_map/convert_element_type | solution.py:398
  6.6 5.9 %split_counts.1 = (s16[512,512]{1,0:T(8,128)(2,1)}, s16[512,512]{1,0:T(8,128)(2,1)}, s16[512,512]{1,0:T(8,128)(2,1)}, s16[512,512]{1,0:T(8,128)(2,1)}, s16[512,5...) custom-call(s32[2]{0:T(128)S(1)} %pad_add_fusion.at, s32[4096,512]{1,0:T(8,128)} %v.1), custom_call_target="tpu_custom_call" | custom-call | tf_op jit(solution)/shard_map/split_counts/pallas_call | solution.py:104
  12.5 3.0 %first_products.4 = (f32[512,512]{1,0:T(8,128)S(1)}, f32[8,512]{1,0:T(8,128)S(1)}) custom-call(bf16[512,512]{1,0:T(8,128)(2,1)S(1)} %convert_element_type.3.h, bf16[512,512]{1,0:T(8,128)(2,1)} %w_ref.1, s16[512,512]{1,0:T(8,128)(2,1)} %get-tuple-element.62.refs_1_, bf16[512,512]{1,0:T(8,128)(2,1)S(1)} %collective-permute-done.2.refs_2_, ...), custom_call_target="tpu_custom_call" | custom-call | flops 2147483648 | bytes 2097152 | tf_op jit(solution)/shard_map/first_products/pallas_call | solution.py:235
  16.4 1.6 %collective-permute-done.1.refs_2_.refs_3_ = bf16[512,512]{1,0:T(8,128)(2,1)} collective-permute-done((bf16[512,512]{1,0:T(8,128)(2,1)}, bf16[512,512]{1,0:T(8,128)(2,1)}, u32[]{:S(2)}, u32[]{:S(2)}) %collective-permute-start.1) | collective-permute-done | bytes 524320 | tf_op jit(solution)/shard_map/ppermute | solution.py:273
  19.9 1.7 %collective-permute-start.4 = (bf16[256,512]{1,0:T(8,128)(2,1)S(1)}, bf16[256,512]{1,0:T(8,128)(2,1)S(1)}, u32[]{:S(2)}, u32[]{:S(2)}) collective-permute-start(bf16[256,512]{1,0:T(8,128)(2,1)S(1)} %slice.7), channel_id=1, source_target_pairs={{0,4},{1,5},{2,6},{3,7},{4,0},{5,1},{6,2},{7,3},{8,12},{9,13},{10,... | collective-permute-start | bytes 786440 | tf_op jit(solution)/shard_map/ppermute | solution.py:273
  21.7 4.5 %first_products.5 = (f32[512,512]{1,0:T(8,128)S(1)}, f32[8,512]{1,0:T(8,128)S(1)}) custom-call(bf16[512,512]{1,0:T(8,128)(2,1)S(1)} %convert_element_type.3.h, bf16[512,512]{1,0:T(8,128)(2,1)} %copy-done.5, s16[512,512]{1,0:T(8,128)(2,1)} %get-tuple-element.68.refs_1_, ...), custom_call_target="tpu_custom_call", output_to_operand_aliasing={{0}: (9, {}), {1}: (10, {})} | custom-call | flops 4294967296 | bytes 4194304 | tf_op jit(solution)/shard_map/first_products/pallas_call | solution.py:235
  26.2 1.6 %collective-permute-done.3.refs_0_ = bf16[256,512]{1,0:T(8,128)(2,1)S(1)} collective-permute-done((bf16[256,512]{1,0:T(8,128)(2,1)S(1)}, bf16[256,512]{1,0:T(8,128)(2,1)S(1)}, u32[]{:S(2)}, u32[]{:S(2)}) %collective-permute-start.3) | collective-permute-done | bytes 262176 | tf_op jit(solution)/shard_map/ppermute | solution.py:273
  28.4 1.3 %fetch.1 = (s16[512,512]{1,0:T(8,128)(2,1)S(1)}, s16[512,512]{1,0:T(8,128)(2,1)S(1)}) custom-call(s16[512,512]{1,0:T(8,128)(2,1)} %get-tuple-element.82.refs_0_.v, s16[512,512]{1,0:T(8,128)(2,1)} %get-tuple-element.83.refs_1_), custom_call_target="tpu_custom_call" | custom-call | tf_op jit(solution)/shard_map/fetch/pallas_call | solution.py:164
  30.6 1.9 %first_products.7 = (f32[512,512]{1,0:T(8,128)S(1)}, f32[8,512]{1,0:T(8,128)S(1)}) custom-call(bf16[512,512]{1,0:T(8,128)(2,1)S(1)} %convert_element_type.3.h, bf16[256,512]{1,0:T(8,128)(2,1)} %collective-permute-done.7.refs_0_, bf16[256,512]{1,0:T(8,128)(2,1)} %collective-permute-done.8.refs_1_, ...), custom_call_target="tpu_custom_call", output_to_operand_aliasing={{0}: (4, {}), {1}: (5, {})} | custom-call | flops 1073741824 | bytes 1048576 | tf_op jit(solution)/shard_map/first_products/pallas_call | solution.py:235
  32.8 1.8 %collective-permute-start.9 = (s16[528,128]{1,0:T(8,128)(2,1)S(1)}, s16[528,128]{1,0:T(8,128)(2,1)S(1)}, u32[]{:S(2)}, u32[]{:S(2)}) collective-permute-start(s16[528,128]{1,0:T(8,128)(2,1)S(1)} %get-tuple-element.91.refs_0_), channel_id=1, source_target_pairs={{0,8},{8,0},{16,24},{24,16},{1,9},{9,1},{17,25},{25,17},{2,10},{10... | collective-permute-start | bytes 405512 | tf_op jit(solution)/shard_map/ppermute | solution.py:273
  34.7 3.7 %collective-permute-done.9.other = s16[528,128]{1,0:T(8,128)(2,1)S(1)} collective-permute-done((s16[528,128]{1,0:T(8,128)(2,1)S(1)}, s16[528,128]{1,0:T(8,128)(2,1)S(1)}, u32[]{:S(2)}, u32[]{:S(2)}) %collective-permute-start.9) | collective-permute-done | bytes 135200 | tf_op jit(solution)/shard_map/ppermute | solution.py:273
  38.6 1.8 %collective-permute-start.11 = (s16[528,128]{1,0:T(8,128)(2,1)S(1)}, s16[528,128]{1,0:T(8,128)(2,1)S(1)}, u32[]{:S(2)}, u32[]{:S(2)}) collective-permute-start(s16[528,128]{1,0:T(8,128)(2,1)S(1)} %get-tuple-element.94), channel_id=1, source_target_pairs={{0,8},{8,0},{16,24},{24,16},{1,9},{9,1},{17,25},{25,17},{2,10},{10... | collective-permute-start | bytes 405512 | tf_op jit(solution)/shard_map/ppermute | solution.py:273
  40.4 2.5 %collective-permute-start.10 = (s16[528,128]{1,0:T(8,128)(2,1)S(1)}, s16[528,128]{1,0:T(8,128)(2,1)S(1)}, u32[]{:S(2)}, u32[]{:S(2)}) collective-permute-start(s16[528,128]{1,0:T(8,128)(2,1)S(1)} %add_pair.2.one), channel_id=1, source_target_pairs={{0,24},{8,16},{16,8},{24,0},{1,25},{9,17},{17,9},{25,1},{2,26},{10... | collective-permute-start | bytes 405512 | tf_op jit(solution)/shard_map/ppermute | solution.py:273
  44.2 7.8 %collective-permute-start.12 = (s16[528,128]{1,0:T(8,128)(2,1)S(1)}, s16[528,128]{1,0:T(8,128)(2,1)S(1)}, u32[]{:S(2)}, u32[]{:S(2)}) collective-permute-start(s16[528,128]{1,0:T(8,128)(2,1)S(1)} %add_pair.3.one), channel_id=1, source_target_pairs={{0,24},{8,16},{16,8},{24,0},{1,25},{9,17},{17,9},{25,1},{2,26},{10... | collective-permute-start | bytes 405512 | tf_op jit(solution)/shard_map/ppermute | solution.py:273
  52.3 3.6 %collective-permute-done.12.other = s16[528,128]{1,0:T(8,128)(2,1)S(1)} collective-permute-done((s16[528,128]{1,0:T(8,128)(2,1)S(1)}, s16[528,128]{1,0:T(8,128)(2,1)S(1)}, u32[]{:S(2)}, u32[]{:S(2)}) %collective-permute-start.12) | collective-permute-done | bytes 135200 | tf_op jit(solution)/shard_map/ppermute | solution.py:273
  56.2 1.7 %collective-permute-done.13.refs_2_ = s16[528,128]{1,0:T(8,128)(2,1)S(1)} collective-permute-done((s16[528,128]{1,0:T(8,128)(2,1)S(1)}, s16[528,128]{1,0:T(8,128)(2,1)S(1)}, u32[]{:S(2)}, u32[]{:S(2)}) %collective-permute-start.13) | collective-permute-done | bytes 135200 | tf_op jit(solution)/shard_map/ppermute | solution.py:273
  57.9 3.2 %collective-permute-done.14.refs_3_ = s16[528,128]{1,0:T(8,128)(2,1)S(1)} collective-permute-done((s16[528,128]{1,0:T(8,128)(2,1)S(1)}, s16[528,128]{1,0:T(8,128)(2,1)S(1)}, u32[]{:S(2)}, u32[]{:S(2)}) %collective-permute-start.14) | collective-permute-done | bytes 135200 | tf_op jit(solution)/shard_map/ppermute | solution.py:273
  61.1 1.4 %h1_update.1 = (f32[512,512]{1,0:T(8,128)}, bf16[512,512]{1,0:T(8,128)(2,1)S(1)}, f32[512,512]{1,0:T(8,128)S(1)}) custom-call(s32[1]{0:T(128)} %bitcast.flag, s16[528,128]{1,0:T(8,128)(2,1)S(1)} %get-tuple-element.92.refs_0_, s16[528,128]{1,0:T(8,128)(2,1)S(1)} %add_cross.3.refs_1_, s16[528,128]{1,0:T(8,128)(2,1)S(1)} %collective-permute-done.13.refs_2_, ...), custom_call_target="tpu_custom_call" | custom-call | tf_op jit(solution)/shard_map/h1_update/pallas_call | solution.py:267
  63.1 3.1 %layer_two.1 = (f32[64,512]{1,0:T(8,128)}, f32[80,512]{1,0:T(8,128)S(1)}, s16[512,512]{1,0:T(8,128)(2,1)S(1)}) custom-call(f32[512,512]{1,0:T(8,128)S(1)} %get-tuple-element.97.h1_ref, f32[64,512]{1,0:T(8,128)S(1)} %bitcast.5, f32[64,512]{1,0:T(8,128)S(1)} %copy-done.3, s16[512,512]{1,0:T(8,128)(2,1)} %get-tuple-element.82.refs_0_.v), custom_call_target="tpu_custom_call" | custom-call | tf_op jit(solution)/shard_map/layer_two/pallas_call | solution.py:466
  66.6 1.2 %second_products.3 = (f32[256,512]{1,0:T(8,128)S(1)}, f32[256,512]{1,0:T(8,128)S(1)}) custom-call(bf16[512,512]{1,0:T(8,128)(2,1)S(1)} %get-tuple-element.96.ha, bf16[512,512]{1,0:T(8,128)(2,1)S(1)} %collective-permute-done.15.hb, bf16[256,512]{1,0:T(8,128)(2,1)S(1)} %collective-permute-done.3.refs_0_, bf16[256,512]{1,0:T(8,128)(2,1)S(1)} %collective-permute-done.4.refs_1_, ...), custom_call_target="tpu_custom_call" | custom-call | flops 1610612736 | bytes 1572864 | tf_op jit(solution)/shard_map/second_products/pallas_call | solution.py:235
  68.5 1.6 %collective-permute-start.20 = (s16[320,512]{1,0:T(8,128)(2,1)S(1)}, s16[320,512]{1,0:T(8,128)(2,1)S(1)}, u32[]{:S(2)}, u32[]{:S(2)}) collective-permute-start(s16[320,512]{1,0:T(8,128)(2,1)S(1)} %get-tuple-element.108.hi), channel_id=1, source_target_pairs={{0,4},{1,5},{2,6},{3,7},{4,0},{5,1},{6,2},{7,3},{8,12},{9,13},{10,... | collective-permute-start | bytes 983048 | tf_op jit(solution)/shard_map/ppermute | solution.py:273
  70.1 1.5 %collective-permute-start.21 = (s16[320,512]{1,0:T(8,128)(2,1)S(1)}, s16[320,512]{1,0:T(8,128)(2,1)S(1)}, u32[]{:S(2)}, u32[]{:S(2)}) collective-permute-start(s16[320,512]{1,0:T(8,128)(2,1)S(1)} %get-tuple-element.110.lo), channel_id=1, source_target_pairs={{0,2},{1,3},{2,0},{3,1},{4,6},{5,7},{6,4},{7,5},{8,10},{9,11},{10,... | collective-permute-start | bytes 983048 | tf_op jit(solution)/shard_map/ppermute | solution.py:273
  71.6 4.0 %second_products.4 = (f32[512,512]{1,0:T(8,128)S(1)}, f32[512,512]{1,0:T(8,128)S(1)}) custom-call(bf16[512,512]{1,0:T(8,128)(2,1)S(1)} %get-tuple-element.96.ha, bf16[512,512]{1,0:T(8,128)(2,1)S(1)} %collective-permute-done.15.hb, bf16[512,512]{1,0:T(8,128)(2,1)} %copy-done.5, s16[512,512]{1,0:T(8,128)(2,1)} %get-tuple-element.68.refs_1_, ...), custom_call_target="tpu_custom_call" | custom-call | flops 3221225472 | bytes 3145728 | tf_op jit(solution)/shard_map/second_products/pallas_call | solution.py:235
  75.6 2.7 %collective-permute-done.20.x_in = s16[320,512]{1,0:T(8,128)(2,1)S(1)} collective-permute-done((s16[320,512]{1,0:T(8,128)(2,1)S(1)}, s16[320,512]{1,0:T(8,128)(2,1)S(1)}, u32[]{:S(2)}, u32[]{:S(2)}) %collective-permute-start.20) | collective-permute-done | bytes 327712 | tf_op jit(solution)/shard_map/ppermute | solution.py:273
  78.3 1.2 %collective-permute-done.21.y_in = s16[320,512]{1,0:T(8,128)(2,1)S(1)} collective-permute-done((s16[320,512]{1,0:T(8,128)(2,1)S(1)}, s16[320,512]{1,0:T(8,128)(2,1)S(1)}, u32[]{:S(2)}, u32[]{:S(2)}) %collective-permute-start.21) | collective-permute-done | bytes 327712 | tf_op jit(solution)/shard_map/ppermute | solution.py:273
  80.7 1.6 %collective-permute-start.23 = (s16[576,512]{1,0:T(8,128)(2,1)S(1)}, s16[576,512]{1,0:T(8,128)(2,1)S(1)}, u32[]{:S(2)}, u32[]{:S(2)}) collective-permute-start(s16[576,512]{1,0:T(8,128)(2,1)S(1)} %get-tuple-element.111), channel_id=1, source_target_pairs={{0,2},{1,3},{2,0},{3,1},{4,6},{5,7},{6,4},{7,5},{8,10},{9,11},{10,... | collective-permute-start | bytes 1769480 | tf_op jit(solution)/shard_map/ppermute | solution.py:273
  82.8 2.5 %second_products.5.own = f32[512,512]{1,0:T(8,128)S(1)} custom-call(bf16[512,512]{1,0:T(8,128)(2,1)S(1)} %get-tuple-element.96.ha, bf16[512,512]{1,0:T(8,128)(2,1)S(1)} %collective-permute-done.15.hb, bf16[512,512]{1,0:T(8,128)(2,1)} %w_ref.1, s16[512,512]{1,0:T(8,128)(2,1)} %get-tuple-element.62.refs_1_, s16[512,512]{1,0:T(8,128)(2,1)S(1)} %collective-permute-done.22.refs_2_), custom_call_target="tpu_custom_call" | custom-call | flops 1610612736 | bytes 1572864 | tf_op jit(solution)/shard_map/second_products/pallas_call | solution.py:235
  85.3 9.6 %collective-permute-done.23.x = s16[576,512]{1,0:T(8,128)(2,1)S(1)} collective-permute-done((s16[576,512]{1,0:T(8,128)(2,1)S(1)}, s16[576,512]{1,0:T(8,128)(2,1)S(1)}, u32[]{:S(2)}, u32[]{:S(2)}) %collective-permute-start.23) | collective-permute-done | bytes 589856 | tf_op jit(solution)/shard_map/ppermute | solution.py:273
  95.0 1.2 %collective-permute-done.24.y = s16[576,512]{1,0:T(8,128)(2,1)S(1)} collective-permute-done((s16[576,512]{1,0:T(8,128)(2,1)S(1)}, s16[576,512]{1,0:T(8,128)(2,1)S(1)}, u32[]{:S(2)}, u32[]{:S(2)}) %collective-permute-start.24) | collective-permute-done | bytes 589856 | tf_op jit(solution)/shard_map/ppermute | solution.py:273
  96.2 1.8 %last_update.1 = (bf16[512,512]{1,0:T(8,128)(2,1)}, f32[64,512]{1,0:T(8,128)}) custom-call(f32[512,512]{1,0:T(8,128)S(1)} %second_products.5.own, s16[576,512]{1,0:T(8,128)(2,1)S(1)} %collective-permute-done.23.x, s16[576,512]{1,0:T(8,128)(2,1)S(1)} %collective-permute-done.24.y, s16[48,512]{1,0:T(8,128)(2,1)S(1)} %get-tuple-element.114.x_sums, ...), custom_call_target="tpu_custom_call" | custom-call | tf_op jit(solution)/shard_map/last_update/pallas_call | solution.py:267
  (59 shorter events, 10.6 us)
Async XLA Ops:
  0.6 11.9 %collective-permute-start.2 = (bf16[512,512]{1,0:T(8,128)(2,1)}, bf16[512,512]{1,0:T(8,128)(2,1)S(1)}, u32[]{:S(2)}, u32[]{:S(2)}) collective-permute-start(bf16[512,512]{1,0:T(8,128)(2,1)} %w_ref.1), channel_id=1, source_target_pairs={{0,1},{1,0},{2,3},{3,2},{4,5},{5,4},{6,7},{7,6},{8,9},{9,8},{10,11... | collective-permute-start | bytes 1572872 | tf_op jit(solution)/shard_map/ppermute | solution.py:273
  1.1 15.3 %collective-permute-start = (bf16[512,512]{1,0:T(8,128)(2,1)}, bf16[512,512]{1,0:T(8,128)(2,1)S(1)}, u32[]{:S(2)}, u32[]{:S(2)}) collective-permute-start(bf16[512,512]{1,0:T(8,128)(2,1)} %w_ref.1), channel_id=1, source_target_pairs={{0,2},{1,3},{2,0},{3,1},{4,6},{5,7},{6,4},{7,5},{8,10},{9,11},{10,... | collective-permute-start | bytes 1572872 | tf_op jit(solution)/shard_map/ppermute | solution.py:273
  3.7 14.3 %collective-permute-start.1 = (bf16[512,512]{1,0:T(8,128)(2,1)}, bf16[512,512]{1,0:T(8,128)(2,1)}, u32[]{:S(2)}, u32[]{:S(2)}) collective-permute-start(bf16[512,512]{1,0:T(8,128)(2,1)} %w_ref.1), channel_id=1, source_target_pairs={{0,4},{1,5},{2,6},{3,7},{4,0},{5,1},{6,2},{7,3},{8,12},{9,13},{10,... | collective-permute-start | bytes 1572872 | tf_op jit(solution)/shard_map/ppermute | solution.py:273
  18.0 3.6 %collective-permute-start.5 = (bf16[512,512]{1,0:T(8,128)(2,1)S(1)}, bf16[512,512]{1,0:T(8,128)(2,1)S(1)}, u32[]{:S(2)}, u32[]{:S(2)}) collective-permute-start(bf16[512,512]{1,0:T(8,128)(2,1)S(1)} %collective-permute-done.refs_0_), channel_id=1, source_target_pairs={{0,1},{1,0},{2,3},{3,2},{4,5},{5,4},{6,7},{7,6},{8,9},{9,8},{10,11... | collective-permute-start | bytes 1572872 | tf_op jit(solution)/shard_map/ppermute | solution.py:273
  18.0 3.6 %collective-permute-start.6 = (bf16[512,512]{1,0:T(8,128)(2,1)}, bf16[512,512]{1,0:T(8,128)(2,1)S(1)}, u32[]{:S(2)}, u32[]{:S(2)}) collective-permute-start(bf16[512,512]{1,0:T(8,128)(2,1)} %collective-permute-done.1.refs_2_.refs_3_), channel_id=1, source_target_pairs={{0,1},{1,0},{2,3},{3,2},{4,5},{5,4},{6,7},{7,6},{8,9},{9,8},{10,11... | collective-permute-start | bytes 1572872 | tf_op jit(solution)/shard_map/ppermute | solution.py:273
  19.5 8.3 %collective-permute-start.3 = (bf16[256,512]{1,0:T(8,128)(2,1)S(1)}, bf16[256,512]{1,0:T(8,128)(2,1)S(1)}, u32[]{:S(2)}, u32[]{:S(2)}) collective-permute-start(bf16[256,512]{1,0:T(8,128)(2,1)S(1)} %slice.6), channel_id=1, source_target_pairs={{0,2},{1,3},{2,0},{3,1},{4,6},{5,7},{6,4},{7,5},{8,10},{9,11},{10,... | collective-permute-start | bytes 786440 | tf_op jit(solution)/shard_map/ppermute | solution.py:273
  19.9 7.9 %collective-permute-start.4 = (bf16[256,512]{1,0:T(8,128)(2,1)S(1)}, bf16[256,512]{1,0:T(8,128)(2,1)S(1)}, u32[]{:S(2)}, u32[]{:S(2)}) collective-permute-start(bf16[256,512]{1,0:T(8,128)(2,1)S(1)} %slice.7), channel_id=1, source_target_pairs={{0,4},{1,5},{2,6},{3,7},{4,0},{5,1},{6,2},{7,3},{8,12},{9,13},{10,... | collective-permute-start | bytes 786440 | tf_op jit(solution)/shard_map/ppermute | solution.py:273
  26.1 34.9 %copy-start = (f32[512,512]{1,0:T(8,128)S(1)}, f32[512,512]{1,0:T(8,128)}, u32[]{:S(2)}) copy-start(f32[512,512]{1,0:T(8,128)} %refs_4_.1) | copy-start | bytes 3145732
  26.1 36.9 %copy-start.1 = (f32[512,64]{0,1:T(8,128)S(1)}, f32[512,64]{0,1:T(8,128)}, u32[]{:S(2)}) copy-start(f32[512,64]{0,1:T(8,128)} %param.8) | copy-start | bytes 393220
  26.2 36.9 %copy-start.3 = (f32[64,512]{1,0:T(8,128)S(1)}, f32[64,512]{1,0:T(8,128)}, u32[]{:S(2)}) copy-start(f32[64,512]{1,0:T(8,128)} %h2_ref.1) | copy-start | bytes 393220
  27.9 2.7 %collective-permute-start.7 = (bf16[256,512]{1,0:T(8,128)(2,1)S(1)}, bf16[256,512]{1,0:T(8,128)(2,1)}, u32[]{:S(2)}, u32[]{:S(2)}) collective-permute-start(bf16[256,512]{1,0:T(8,128)(2,1)S(1)} %collective-permute-done.3.refs_0_), channel_id=1, source_target_pairs={{0,1},{1,0},{2,3},{3,2},{4,5},{5,4},{6,7},{7,6},{8,9},{9,8},{10,11... | collective-permute-start | bytes 786440 | tf_op jit(solution)/shard_map/ppermute | solution.py:273
  27.9 2.7 %collective-permute-start.8 = (bf16[256,512]{1,0:T(8,128)(2,1)S(1)}, bf16[256,512]{1,0:T(8,128)(2,1)}, u32[]{:S(2)}, u32[]{:S(2)}) collective-permute-start(bf16[256,512]{1,0:T(8,128)(2,1)S(1)} %collective-permute-done.4.refs_1_), channel_id=1, source_target_pairs={{0,1},{1,0},{2,3},{3,2},{4,5},{5,4},{6,7},{7,6},{8,9},{9,8},{10,11... | collective-permute-start | bytes 786440 | tf_op jit(solution)/shard_map/ppermute | solution.py:273
  28.4 27.7 %copy-start.4 = (s16[512,512]{1,0:T(8,128)(2,1)S(1)}, s16[512,512]{1,0:T(8,128)(2,1)}, u32[]{:S(2)}) copy-start(s16[512,512]{1,0:T(8,128)(2,1)} %get-tuple-element.83.refs_1_) | copy-start | bytes 1572868
  28.4 34.1 %copy-start.8 = (s16[512,512]{1,0:T(8,128)(2,1)S(1)}, s16[512,512]{1,0:T(8,128)(2,1)}, u32[]{:S(2)}) copy-start(s16[512,512]{1,0:T(8,128)(2,1)} %get-tuple-element.70.refs_5_) | copy-start | bytes 1572868
  28.4 34.6 %copy-start.7 = (s16[512,512]{1,0:T(8,128)(2,1)S(1)}, s16[512,512]{1,0:T(8,128)(2,1)}, u32[]{:S(2)}) copy-start(s16[512,512]{1,0:T(8,128)(2,1)} %get-tuple-element.71.refs_7_) | copy-start | bytes 1572868
  30.6 41.0 %copy-start.6 = (s16[512,512]{1,0:T(8,128)(2,1)S(1)}, s16[512,512]{1,0:T(8,128)(2,1)}, u32[]{:S(2)}) copy-start(s16[512,512]{1,0:T(8,128)(2,1)} %get-tuple-element.63.refs_3_) | copy-start | bytes 1572868
  32.8 5.6 %collective-permute-start.9 = (s16[528,128]{1,0:T(8,128)(2,1)S(1)}, s16[528,128]{1,0:T(8,128)(2,1)S(1)}, u32[]{:S(2)}, u32[]{:S(2)}) collective-permute-start(s16[528,128]{1,0:T(8,128)(2,1)S(1)} %get-tuple-element.91.refs_0_), channel_id=1, source_target_pairs={{0,8},{8,0},{16,24},{24,16},{1,9},{9,1},{17,25},{25,17},{2,10},{10... | collective-permute-start | bytes 405512 | tf_op jit(solution)/shard_map/ppermute | solution.py:273
  38.6 5.5 %collective-permute-start.11 = (s16[528,128]{1,0:T(8,128)(2,1)S(1)}, s16[528,128]{1,0:T(8,128)(2,1)S(1)}, u32[]{:S(2)}, u32[]{:S(2)}) collective-permute-start(s16[528,128]{1,0:T(8,128)(2,1)S(1)} %get-tuple-element.94), channel_id=1, source_target_pairs={{0,8},{8,0},{16,24},{24,16},{1,9},{9,1},{17,25},{25,17},{2,10},{10... | collective-permute-start | bytes 405512 | tf_op jit(solution)/shard_map/ppermute | solution.py:273
  40.4 11.6 %collective-permute-start.10 = (s16[528,128]{1,0:T(8,128)(2,1)S(1)}, s16[528,128]{1,0:T(8,128)(2,1)S(1)}, u32[]{:S(2)}, u32[]{:S(2)}) collective-permute-start(s16[528,128]{1,0:T(8,128)(2,1)S(1)} %add_pair.2.one), channel_id=1, source_target_pairs={{0,24},{8,16},{16,8},{24,0},{1,25},{9,17},{17,9},{25,1},{2,26},{10... | collective-permute-start | bytes 405512 | tf_op jit(solution)/shard_map/ppermute | solution.py:273
  44.2 11.6 %collective-permute-start.12 = (s16[528,128]{1,0:T(8,128)(2,1)S(1)}, s16[528,128]{1,0:T(8,128)(2,1)S(1)}, u32[]{:S(2)}, u32[]{:S(2)}) collective-permute-start(s16[528,128]{1,0:T(8,128)(2,1)S(1)} %add_pair.3.one), channel_id=1, source_target_pairs={{0,24},{8,16},{16,8},{24,0},{1,25},{9,17},{17,9},{25,1},{2,26},{10... | collective-permute-start | bytes 405512 | tf_op jit(solution)/shard_map/ppermute | solution.py:273
  52.2 5.7 %collective-permute-start.13 = (s16[528,128]{1,0:T(8,128)(2,1)S(1)}, s16[528,128]{1,0:T(8,128)(2,1)S(1)}, u32[]{:S(2)}, u32[]{:S(2)}) collective-permute-start(s16[528,128]{1,0:T(8,128)(2,1)S(1)} %get-tuple-element.92.refs_0_), channel_id=1, source_target_pairs={{0,8},{8,0},{16,24},{24,16},{1,9},{9,1},{17,25},{25,17},{2,10},{10... | collective-permute-start | bytes 405512 | tf_op jit(solution)/shard_map/ppermute | solution.py:273
  56.0 5.1 %collective-permute-start.14 = (s16[528,128]{1,0:T(8,128)(2,1)S(1)}, s16[528,128]{1,0:T(8,128)(2,1)S(1)}, u32[]{:S(2)}, u32[]{:S(2)}) collective-permute-start(s16[528,128]{1,0:T(8,128)(2,1)S(1)} %add_cross.3.refs_1_), channel_id=1, source_target_pairs={{0,8},{8,0},{16,24},{24,16},{1,9},{9,1},{17,25},{25,17},{2,10},{10... | collective-permute-start | bytes 405512 | tf_op jit(solution)/shard_map/ppermute | solution.py:273
  56.1 10.6 %collective-permute-start.17 = (s16[512,512]{1,0:T(8,128)(2,1)S(1)}, s16[512,512]{1,0:T(8,128)(2,1)S(1)}, u32[]{:S(2)}, u32[]{:S(2)}) collective-permute-start(s16[512,512]{1,0:T(8,128)(2,1)S(1)} %copy-done.4), channel_id=1, source_target_pairs={{0,1},{1,0},{2,3},{3,2},{4,5},{5,4},{6,7},{7,6},{8,9},{9,8},{10,11... | collective-permute-start | bytes 1572872 | tf_op jit(solution)/shard_map/ppermute | solution.py:273
  62.5 4.2 %collective-permute-start.15 = (bf16[512,512]{1,0:T(8,128)(2,1)S(1)}, bf16[512,512]{1,0:T(8,128)(2,1)S(1)}, u32[]{:S(2)}, u32[]{:S(2)}) collective-permute-start(bf16[512,512]{1,0:T(8,128)(2,1)S(1)} %get-tuple-element.96.ha), channel_id=1, source_target_pairs={{0,1},{1,0},{2,3},{3,2},{4,5},{5,4},{6,7},{7,6},{8,9},{9,8},{10,11... | collective-permute-start | bytes 1572872 | tf_op jit(solution)/shard_map/ppermute | solution.py:273
  62.5 9.1 %collective-permute-start.18 = (s16[512,512]{1,0:T(8,128)(2,1)S(1)}, s16[512,512]{1,0:T(8,128)(2,1)S(1)}, u32[]{:S(2)}, u32[]{:S(2)}) collective-permute-start(s16[512,512]{1,0:T(8,128)(2,1)S(1)} %copy-done.8), channel_id=1, source_target_pairs={{0,1},{1,0},{2,3},{3,2},{4,5},{5,4},{6,7},{7,6},{8,9},{9,8},{10,11... | collective-permute-start | bytes 1572872 | tf_op jit(solution)/shard_map/ppermute | solution.py:273
  63.0 8.6 %collective-permute-start.19 = (s16[512,512]{1,0:T(8,128)(2,1)S(1)}, s16[512,512]{1,0:T(8,128)(2,1)S(1)}, u32[]{:S(2)}, u32[]{:S(2)}) collective-permute-start(s16[512,512]{1,0:T(8,128)(2,1)S(1)} %copy-done.7), channel_id=1, source_target_pairs={{0,1},{1,0},{2,3},{3,2},{4,5},{5,4},{6,7},{7,6},{8,9},{9,8},{10,11... | collective-permute-start | bytes 1572872 | tf_op jit(solution)/shard_map/ppermute | solution.py:273
  66.1 1.8 %collective-permute-start.16 = (f32[80,512]{1,0:T(8,128)S(1)}, f32[80,512]{1,0:T(8,128)S(1)}, u32[]{:S(2)}, u32[]{:S(2)}) collective-permute-start(f32[80,512]{1,0:T(8,128)S(1)} %get-tuple-element.103.sums), channel_id=1, source_target_pairs={{0,1},{1,0},{2,3},{3,2},{4,5},{5,4},{6,7},{7,6},{8,9},{9,8},{10,11... | collective-permute-start | bytes 491528 | tf_op jit(solution)/shard_map/ppermute | solution.py:273
  68.5 9.8 %collective-permute-start.20 = (s16[320,512]{1,0:T(8,128)(2,1)S(1)}, s16[320,512]{1,0:T(8,128)(2,1)S(1)}, u32[]{:S(2)}, u32[]{:S(2)}) collective-permute-start(s16[320,512]{1,0:T(8,128)(2,1)S(1)} %get-tuple-element.108.hi), channel_id=1, source_target_pairs={{0,4},{1,5},{2,6},{3,7},{4,0},{5,1},{6,2},{7,3},{8,12},{9,13},{10,... | collective-permute-start | bytes 983048 | tf_op jit(solution)/shard_map/ppermute | solution.py:273
  70.1 9.5 %collective-permute-start.21 = (s16[320,512]{1,0:T(8,128)(2,1)S(1)}, s16[320,512]{1,0:T(8,128)(2,1)S(1)}, u32[]{:S(2)}, u32[]{:S(2)}) collective-permute-start(s16[320,512]{1,0:T(8,128)(2,1)S(1)} %get-tuple-element.110.lo), channel_id=1, source_target_pairs={{0,2},{1,3},{2,0},{3,1},{4,6},{5,7},{6,4},{7,5},{8,10},{9,11},{10,... | collective-permute-start | bytes 983048 | tf_op jit(solution)/shard_map/ppermute | solution.py:273
  71.6 11.2 %collective-permute-start.22 = (s16[512,512]{1,0:T(8,128)(2,1)S(1)}, s16[512,512]{1,0:T(8,128)(2,1)S(1)}, u32[]{:S(2)}, u32[]{:S(2)}) collective-permute-start(s16[512,512]{1,0:T(8,128)(2,1)S(1)} %copy-done.6), channel_id=1, source_target_pairs={{0,1},{1,0},{2,3},{3,2},{4,5},{5,4},{6,7},{7,6},{8,9},{9,8},{10,11... | collective-permute-start | bytes 1572872 | tf_op jit(solution)/shard_map/ppermute | solution.py:273
  80.7 14.3 %collective-permute-start.23 = (s16[576,512]{1,0:T(8,128)(2,1)S(1)}, s16[576,512]{1,0:T(8,128)(2,1)S(1)}, u32[]{:S(2)}, u32[]{:S(2)}) collective-permute-start(s16[576,512]{1,0:T(8,128)(2,1)S(1)} %get-tuple-element.111), channel_id=1, source_target_pairs={{0,2},{1,3},{2,0},{3,1},{4,6},{5,7},{6,4},{7,5},{8,10},{9,11},{10,... | collective-permute-start | bytes 1769480 | tf_op jit(solution)/shard_map/ppermute | solution.py:273
  82.3 13.9 %collective-permute-start.24 = (s16[576,512]{1,0:T(8,128)(2,1)S(1)}, s16[576,512]{1,0:T(8,128)(2,1)S(1)}, u32[]{:S(2)}, u32[]{:S(2)}) collective-permute-start(s16[576,512]{1,0:T(8,128)(2,1)S(1)} %get-tuple-element.113), channel_id=1, source_target_pairs={{0,4},{1,5},{2,6},{3,7},{4,0},{5,1},{6,2},{7,3},{8,12},{9,13},{10,... | collective-permute-start | bytes 1769480 | tf_op jit(solution)/shard_map/ppermute | solution.py:273
  (2 other events, 31.4 us)

commit v4 on v3

--- a/solution.py
+++ b/solution.py
@@ -194,22 +194,23 @@
         copy.wait()
 
 
-def second_body(groups, later, n_ahead, code, ha, hb, *refs):
+def second_body(groups, later, n_ahead, codes, ha, hb, *refs):
     n, n_later = sum(groups) + 2 * len(groups), len(later)
     refs, scratch = (refs[:-n_later - 1], refs[-n_later - 1 :]) if later else (refs, ())
     operands, outs = fetching(refs[:n], later, scratch), refs[n:]
-    for n in groups:
+    for n, code in zip(groups, codes):
         pieces, v, operands = operands[:n], operands[n : n + 2], operands[n + 2 :]
-        w, t = joined(pieces), pieces[0][0].shape[0]
+        w = joined(pieces)
         total = 0.0
         for h, some in ((hb, v[1]), (ha, v[0])):
             low = h[...]
             approx = mm(w, low, (1, 0))
             total += mm(quotient(ready(some), approx), low, (1, 1))
-        for k in range(n):
+        t = w.shape[0] // len(code)
+        for k, coding in enumerate(code):
             out, outs = outs[0], outs[1:]
             part = total[k * t : (k + 1) * t]
-            if code:
+            if coding:
                 encode(part, out)
             else:
                 out[...] = part
@@ -251,11 +252,13 @@
     return products(first_body, bool(acc), outs, groups, (h,), acc, "first_products", fetch)
 
 
-def second(groups, t, h, code):
+def second(groups, rows, h, codes):
     k1 = h[0].shape[0]
-    out = coded(t, k1) if code else jax.ShapeDtypeStruct((t, k1), F32)
-    outs = (out,) * sum(len(g) - 2 for g in groups)
-    return products(second_body, code, outs, groups, h, (), "second_products")
+    outs = []
+    for code in codes:
+        t = rows // len(code)
+        outs += [coded(t, k1) if c else jax.ShapeDtypeStruct((t, k1), F32) for c in code]
+    return products(second_body, codes, tuple(outs), groups, h, (), "second_products")
 
 
 def plain(body, outs, *args, name, flag=None):
@@ -328,27 +331,28 @@
 
 
 def relay_add(k2, x, x_in, y, y_in, lo, hi, x_ref, y_ref, x_sums, y_sums):
-    rows, half = x.shape[0], x.shape[0] // 2
-    encode(jnp.concatenate([x[:half, :], x[half:, :] + decode(x_in, half)], axis=0), x_ref)
-    encode(jnp.concatenate([y[:half, :] + decode(y_in, half), y[half:, :]], axis=0), y_ref)
-    at, few = half + PAD, k2 // 2
+    rows = x.shape[0]
+    at, few = rows + PAD, k2 // 2
+    encode(x[...] + decode(x_in, rows), x_ref)
+    encode(y[...] + decode(y_in, rows), y_ref)
     one = [a + b for a, b in zip(decode_singles(lo, 2, lo.shape[0]), decode_singles(y_in, 2, lo.shape[0]))]
     encode(decode(lo, few, at) + decode(y_in, few, at), y_sums, singles=one)
     encode(decode(hi, few, at) + decode(x_in, few, at), x_sums)
-    x_ref[rows + PAD :, :] = x_sums[...]
-    y_ref[rows + PAD :, :] = y_sums[...]
-
-
-def last_update(own, x, y, x_sums, y_sums, w_ref, w2t_ref, w1_ref, w2_ref):
-    rows, few = own.shape[0], x_sums.shape[0] - PAD
-    total = own[...] + decode(x, rows) + decode(y, rows)
-    singles = zip(decode_singles(y_sums, 2, few + PAD), decode_singles(y, 2, y.shape[0]))
+    x_ref[at:, :] = x_sums[...]
+    y_ref[at:, :] = y_sums[...]
+
+
+def last_update(own, x_lo, x_hi, y_lo, y_hi, x_sums, y_sums, w_ref, w2t_ref, w1_ref, w2_ref):
+    t, few = x_lo.shape[0] - PAD, x_sums.shape[0] - PAD
+    singles = zip(decode_singles(y_sums, 2, few + PAD), decode_singles(y_lo, 2, y_lo.shape[0]))
     row, h2_row = [a + b for a, b in singles]
-    w1_ref[...] = (w_ref[...].astype(F32) * total / row).astype(BF16)
+    for at, x, y in ((0, x_lo, y_lo), (t, x_hi, y_hi)):
+        rows = slice(at, at + t)
+        total = own[rows, :] + decode(x, t) + decode(y, t)
+        w1_ref[rows, :] = (w_ref[rows, :].astype(F32) * total / row).astype(BF16)
     h2_col = jnp.broadcast_to(h2_row, (8, h2_row.shape[1])).T[: 2 * few, :1]
-    at = rows + PAD
-    low = decode(y_sums, few) + decode(y, few, at)
-    high = decode(x_sums, few) + decode(x, few, at)
+    low = decode(y_sums, few) + decode(y_lo, few, t + PAD)
+    high = decode(x_sums, few) + decode(x_hi, few, t + PAD)
     w2_ref[...] = w2t_ref[...] * jnp.concatenate([low, high], axis=0) / h2_col
 
 
@@ -479,7 +483,7 @@
     low2 = (h1_low2, h1_low2_other)
     if line:
         sums_in = cell(sums, bit=1)
-        d_lo, d_hi = second(((d_lo, d_hi, v_far, v_other[3]),), t, low2, False)
+        d_lo, d_hi = second(((d_lo, d_hi, v_far, v_other[3]),), rows, low2, ((False, False),))
         sums, sums_in, d_lo = after((sums, sums_in, d_lo))
         few = k2 // 2 + PAD
         with_sums = coded(t + few, k1)
@@ -489,26 +493,26 @@
         y_in, x_in = cell(d_lo, bit=2), cell(d_hi, bit=4)
         w_x, d_lo = after((w_x, d_lo))
         near = ((Later(w_x), on_mine[1], v_other[1]), (Later(w_y), on_mine[2], v_other[2]))
-        x_num, y_num = second(near, rows, low2, False)
-        with_sums = coded(rows + few, k1)
+        x_lo, x_hi, y_lo, y_hi = second(near, rows, low2, ((True, False), (False, True)))
+        x_lo_in, y_hi_in = cell(x_lo, bit=2), cell(y_hi, bit=4)
         sums_only = jax.ShapeDtypeStruct((few, k1), jnp.int16)
-        x_num, y_num, x_sums, y_sums = plain(
+        x_hi, y_lo, x_sums, y_sums = plain(
             functools.partial(relay_add, k2), (with_sums, with_sums, sums_only, sums_only),
-            x_num, x_in, y_num, y_in, d_lo, d_hi, name="relay_add",
+            x_hi, x_in, y_lo, y_in, d_lo, d_hi, name="relay_add",
         )
-        x_num_in, y_num_in = cell(x_num, bit=2), cell(y_num, bit=4)
-        w1_late, x_num = after((w1, x_num))
-        (own,) = second(((Later(w1_late), on_mine[0], v_other[0]),), rows, low2, False)
+        x_hi_in, y_lo_in = cell(x_hi, bit=2), cell(y_lo, bit=4)
+        w1_late, x_hi, x_lo_in, y_hi_in = after((w1, x_hi, x_lo_in, y_hi_in))
+        (own,) = second(((Later(w1_late), on_mine[0], v_other[0]),), rows, low2, ((False,),))
         w1_new, w2_new = plain(
             last_update, (jax.ShapeDtypeStruct((rows, k1), BF16), jax.ShapeDtypeStruct((k2, k1), F32)),
-            own, x_num_in, y_num_in, x_sums, y_sums, w1, w2t, name="last_update",
+            own, x_lo_in, x_hi_in, y_lo_in, y_hi_in, x_sums, y_sums, w1, w2t, name="last_update",
         )
         w2_new = w2_new.T
     else:
         found = []
         for i in range(0, chips, each):
             some = tuple((halves[0][j], v_mine[j], v_other[j]) for j in range(i, i + each))
-            found += second(some, rows, low2, False)
+            found += second(some, rows, low2, ((False,),) * each)
         w1_num = lax.psum_scatter(
             jnp.concatenate(found), "cell", scatter_dimension=0, tiled=True, axis_index_groups=groups
         )

time: 98.3 us -> 94.9 us (0.965)
  waiting for transfers between devices: 32.5 us -> 28.2 us
  starting transfers between devices: 28.1 us -> 29.3 us
    ppermute x25 -> x27, waiting for transfers between devices: 32.5 us -> 28.2 us  [flip(): return lax.ppermute(x, axis, [(i, i ^ bit) for i in range(size)])]
    ppermute x25 -> x27, starting transfers between devices: 28.1 us -> 29.3 us  [flip(): return lax.ppermute(x, axis, [(i, i ^ bit) for i in range(size)])]
  transfers between devices with their start and end apart: 25 -> 27, of which waited for: 13 -> 14; matrix products, arithmetic and copies ran while one was open for 2% -> 2% of each run, Pallas kernels for 31% -> 32%
where the time goes in v4:
time: 94.9 us; the launch traced here: 94.7 us
  Pallas kernels  33.9 us (36%)
  starting transfers between devices  29.3 us (31%)
  waiting for transfers between devices  28.2 us (30%)
  other arithmetic  1.37 us (1%)
  local copies, waits for them, and re-layouts  1.03 us (1%)
    ppermute x27, starting transfers between devices, flip(): return lax.ppermute(x, axis, [(i, i ^ bit) for i in range(size)])  29.3 us
    ppermute x27, waiting for transfers between devices, flip(): return lax.ppermute(x, axis, [(i, i ^ bit) for i in range(size)])  28.2 us
    pallas_call x7, Pallas kernels, products(): pl.pallas_call(functools.partial(body, sizes, later, len(fetch), flag), o...  18.1 us
    pallas_call x1, Pallas kernels, split_counts(): pl.pallas_call(functools.partial(counts_body, chips, rows), out_shape=(ou...  5.89 us
    pallas_call x9, Pallas kernels, plain(): pl.pallas_call(body, out_shape=outs, in_specs=specs, out_specs=out_specs,...  5.44 us
    pallas_call x1, Pallas kernels, on_device(): pl.pallas_call(layer_two, out_shape=(jax.ShapeDtypeStruct((k2, cells), F3...  3.07 us
  transfers between devices with their start and end apart: 27, of which 14 were waited for; matrix products, arithmetic and copies ran while one was open for 2% of the time, Pallas kernels for 32%

profile of v4, /device:TPU:0, one launch (start us, length us, event | category | flops | bytes accessed | tf_op | source)
XLA Modules:
  0.0 94.7 jit_solution(16116883552112390194)
XLA Ops:
  1.1 2.6 %collective-permute-start = (bf16[512,512]{1,0:T(8,128)(2,1)}, bf16[512,512]{1,0:T(8,128)(2,1)S(1)}, u32[]{:S(2)}, u32[]{:S(2)}) collective-permute-start(bf16[512,512]{1,0:T(8,128)(2,1)} %w_ref.1), channel_id=1, source_target_pairs={{0,2},{1,3},{2,0},{3,1},{4,6},{5,7},{6,4},{7,5},{8,10},{9,11},{10,... | collective-permute-start | bytes 1572872 | tf_op jit(solution)/shard_map/ppermute | solution.py:276
  3.7 1.5 %collective-permute-start.1 = (bf16[512,512]{1,0:T(8,128)(2,1)}, bf16[512,512]{1,0:T(8,128)(2,1)}, u32[]{:S(2)}, u32[]{:S(2)}) collective-permute-start(bf16[512,512]{1,0:T(8,128)(2,1)} %w_ref.1), channel_id=1, source_target_pairs={{0,4},{1,5},{2,6},{3,7},{4,0},{5,1},{6,2},{7,3},{8,12},{9,13},{10,... | collective-permute-start | bytes 1572872 | tf_op jit(solution)/shard_map/ppermute | solution.py:276
  5.2 1.3 %convert_element_type.3.h = bf16[512,512]{1,0:T(8,128)(2,1)S(1)} convert(f32[512,512]{1,0:T(8,128)} %refs_4_.1) | non-fusion elementwise | flops 262144 | bytes 1572864 | tf_op jit(solution)/shard_map/convert_element_type | solution.py:402
  6.6 5.9 %split_counts.1 = (s16[512,512]{1,0:T(8,128)(2,1)}, s16[512,512]{1,0:T(8,128)(2,1)}, s16[512,512]{1,0:T(8,128)(2,1)}, s16[512,512]{1,0:T(8,128)(2,1)}, s16[512,5...) custom-call(s32[2]{0:T(128)S(1)} %pad_add_fusion.at, s32[4096,512]{1,0:T(8,128)} %v.1), custom_call_target="tpu_custom_call" | custom-call | tf_op jit(solution)/shard_map/split_counts/pallas_call | solution.py:104
  12.5 3.0 %first_products.4 = (f32[512,512]{1,0:T(8,128)S(1)}, f32[8,512]{1,0:T(8,128)S(1)}) custom-call(bf16[512,512]{1,0:T(8,128)(2,1)S(1)} %convert_element_type.3.h, bf16[512,512]{1,0:T(8,128)(2,1)} %w_ref.1, s16[512,512]{1,0:T(8,128)(2,1)} %get-tuple-element.66.refs_1_, bf16[512,512]{1,0:T(8,128)(2,1)S(1)} %collective-permute-done.2.refs_2_, ...), custom_call_target="tpu_custom_call" | custom-call | flops 2147483648 | bytes 2097152 | tf_op jit(solution)/shard_map/first_products/pallas_call | solution.py:236
  16.4 1.6 %collective-permute-done.1.refs_2_.refs_3_ = bf16[512,512]{1,0:T(8,128)(2,1)} collective-permute-done((bf16[512,512]{1,0:T(8,128)(2,1)}, bf16[512,512]{1,0:T(8,128)(2,1)}, u32[]{:S(2)}, u32[]{:S(2)}) %collective-permute-start.1) | collective-permute-done | bytes 524320 | tf_op jit(solution)/shard_map/ppermute | solution.py:276
  19.9 1.7 %collective-permute-start.4 = (bf16[256,512]{1,0:T(8,128)(2,1)S(1)}, bf16[256,512]{1,0:T(8,128)(2,1)S(1)}, u32[]{:S(2)}, u32[]{:S(2)}) collective-permute-start(bf16[256,512]{1,0:T(8,128)(2,1)S(1)} %slice.7), channel_id=1, source_target_pairs={{0,4},{1,5},{2,6},{3,7},{4,0},{5,1},{6,2},{7,3},{8,12},{9,13},{10,... | collective-permute-start | bytes 786440 | tf_op jit(solution)/shard_map/ppermute | solution.py:276
  21.7 4.5 %first_products.5 = (f32[512,512]{1,0:T(8,128)S(1)}, f32[8,512]{1,0:T(8,128)S(1)}) custom-call(bf16[512,512]{1,0:T(8,128)(2,1)S(1)} %convert_element_type.3.h, bf16[512,512]{1,0:T(8,128)(2,1)} %copy-done.5, s16[512,512]{1,0:T(8,128)(2,1)} %get-tuple-element.72.refs_1_, ...), custom_call_target="tpu_custom_call", output_to_operand_aliasing={{0}: (9, {}), {1}: (10, {})} | custom-call | flops 4294967296 | bytes 4194304 | tf_op jit(solution)/shard_map/first_products/pallas_call | solution.py:236
  26.2 1.6 %collective-permute-done.3.refs_0_ = bf16[256,512]{1,0:T(8,128)(2,1)S(1)} collective-permute-done((bf16[256,512]{1,0:T(8,128)(2,1)S(1)}, bf16[256,512]{1,0:T(8,128)(2,1)S(1)}, u32[]{:S(2)}, u32[]{:S(2)}) %collective-permute-start.3) | collective-permute-done | bytes 262176 | tf_op jit(solution)/shard_map/ppermute | solution.py:276
  28.4 1.4 %fetch.1 = (s16[512,512]{1,0:T(8,128)(2,1)S(1)}, s16[512,512]{1,0:T(8,128)(2,1)S(1)}) custom-call(s16[512,512]{1,0:T(8,128)(2,1)} %get-tuple-element.86.refs_0_.v, s16[512,512]{1,0:T(8,128)(2,1)} %get-tuple-element.87.refs_1_), custom_call_target="tpu_custom_call" | custom-call | tf_op jit(solution)/shard_map/fetch/pallas_call | solution.py:164
  30.6 1.9 %first_products.7 = (f32[512,512]{1,0:T(8,128)S(1)}, f32[8,512]{1,0:T(8,128)S(1)}) custom-call(bf16[512,512]{1,0:T(8,128)(2,1)S(1)} %convert_element_type.3.h, bf16[256,512]{1,0:T(8,128)(2,1)} %collective-permute-done.7.refs_0_, bf16[256,512]{1,0:T(8,128)(2,1)} %collective-permute-done.8.refs_1_, ...), custom_call_target="tpu_custom_call", output_to_operand_aliasing={{0}: (4, {}), {1}: (5, {})} | custom-call | flops 1073741824 | bytes 1048576 | tf_op jit(solution)/shard_map/first_products/pallas_call | solution.py:236
  32.8 1.8 %collective-permute-start.9 = (s16[528,128]{1,0:T(8,128)(2,1)S(1)}, s16[528,128]{1,0:T(8,128)(2,1)S(1)}, u32[]{:S(2)}, u32[]{:S(2)}) collective-permute-start(s16[528,128]{1,0:T(8,128)(2,1)S(1)} %get-tuple-element.95.refs_0_), channel_id=1, source_target_pairs={{0,8},{8,0},{16,24},{24,16},{1,9},{9,1},{17,25},{25,17},{2,10},{10... | collective-permute-start | bytes 405512 | tf_op jit(solution)/shard_map/ppermute | solution.py:276
  34.6 3.8 %collective-permute-done.9.other = s16[528,128]{1,0:T(8,128)(2,1)S(1)} collective-permute-done((s16[528,128]{1,0:T(8,128)(2,1)S(1)}, s16[528,128]{1,0:T(8,128)(2,1)S(1)}, u32[]{:S(2)}, u32[]{:S(2)}) %collective-permute-start.9) | collective-permute-done | bytes 135200 | tf_op jit(solution)/shard_map/ppermute | solution.py:276
  38.5 1.8 %collective-permute-start.11 = (s16[528,128]{1,0:T(8,128)(2,1)S(1)}, s16[528,128]{1,0:T(8,128)(2,1)S(1)}, u32[]{:S(2)}, u32[]{:S(2)}) collective-permute-start(s16[528,128]{1,0:T(8,128)(2,1)S(1)} %get-tuple-element.98), channel_id=1, source_target_pairs={{0,8},{8,0},{16,24},{24,16},{1,9},{9,1},{17,25},{25,17},{2,10},{10... | collective-permute-start | bytes 405512 | tf_op jit(solution)/shard_map/ppermute | solution.py:276
  40.3 2.5 %collective-permute-start.10 = (s16[528,128]{1,0:T(8,128)(2,1)S(1)}, s16[528,128]{1,0:T(8,128)(2,1)S(1)}, u32[]{:S(2)}, u32[]{:S(2)}) collective-permute-start(s16[528,128]{1,0:T(8,128)(2,1)S(1)} %add_pair.2.one), channel_id=1, source_target_pairs={{0,24},{8,16},{16,8},{24,0},{1,25},{9,17},{17,9},{25,1},{2,26},{10... | collective-permute-start | bytes 405512 | tf_op jit(solution)/shard_map/ppermute | solution.py:276
  44.2 7.7 %collective-permute-start.12 = (s16[528,128]{1,0:T(8,128)(2,1)S(1)}, s16[528,128]{1,0:T(8,128)(2,1)S(1)}, u32[]{:S(2)}, u32[]{:S(2)}) collective-permute-start(s16[528,128]{1,0:T(8,128)(2,1)S(1)} %add_pair.3.one), channel_id=1, source_target_pairs={{0,24},{8,16},{16,8},{24,0},{1,25},{9,17},{17,9},{25,1},{2,26},{10... | collective-permute-start | bytes 405512 | tf_op jit(solution)/shard_map/ppermute | solution.py:276
  52.2 3.6 %collective-permute-done.12.other = s16[528,128]{1,0:T(8,128)(2,1)S(1)} collective-permute-done((s16[528,128]{1,0:T(8,128)(2,1)S(1)}, s16[528,128]{1,0:T(8,128)(2,1)S(1)}, u32[]{:S(2)}, u32[]{:S(2)}) %collective-permute-start.12) | collective-permute-done | bytes 135200 | tf_op jit(solution)/shard_map/ppermute | solution.py:276
  56.1 1.7 %collective-permute-done.13.refs_2_ = s16[528,128]{1,0:T(8,128)(2,1)S(1)} collective-permute-done((s16[528,128]{1,0:T(8,128)(2,1)S(1)}, s16[528,128]{1,0:T(8,128)(2,1)S(1)}, u32[]{:S(2)}, u32[]{:S(2)}) %collective-permute-start.13) | collective-permute-done | bytes 135200 | tf_op jit(solution)/shard_map/ppermute | solution.py:276
  57.8 3.2 %collective-permute-done.14.refs_3_ = s16[528,128]{1,0:T(8,128)(2,1)S(1)} collective-permute-done((s16[528,128]{1,0:T(8,128)(2,1)S(1)}, s16[528,128]{1,0:T(8,128)(2,1)S(1)}, u32[]{:S(2)}, u32[]{:S(2)}) %collective-permute-start.14) | collective-permute-done | bytes 135200 | tf_op jit(solution)/shard_map/ppermute | solution.py:276
  61.1 1.4 %h1_update.1 = (f32[512,512]{1,0:T(8,128)}, bf16[512,512]{1,0:T(8,128)(2,1)S(1)}, f32[512,512]{1,0:T(8,128)S(1)}) custom-call(s32[1]{0:T(128)} %bitcast.flag, s16[528,128]{1,0:T(8,128)(2,1)S(1)} %get-tuple-element.96.refs_0_, s16[528,128]{1,0:T(8,128)(2,1)S(1)} %add_cross.3.refs_1_, s16[528,128]{1,0:T(8,128)(2,1)S(1)} %collective-permute-done.13.refs_2_, ...), custom_call_target="tpu_custom_call" | custom-call | tf_op jit(solution)/shard_map/h1_update/pallas_call | solution.py:270
  63.0 3.1 %layer_two.1 = (f32[64,512]{1,0:T(8,128)}, f32[80,512]{1,0:T(8,128)S(1)}, s16[512,512]{1,0:T(8,128)(2,1)S(1)}) custom-call(f32[512,512]{1,0:T(8,128)S(1)} %get-tuple-element.101.h1_ref, f32[64,512]{1,0:T(8,128)S(1)} %bitcast.5, f32[64,512]{1,0:T(8,128)S(1)} %copy-done.3, s16[512,512]{1,0:T(8,128)(2,1)} %get-tuple-element.86.refs_0_.v), custom_call_target="tpu_custom_call" | custom-call | tf_op jit(solution)/shard_map/layer_two/pallas_call | solution.py:470
  66.7 1.2 %second_products.3 = (f32[256,512]{1,0:T(8,128)S(1)}, f32[256,512]{1,0:T(8,128)S(1)}) custom-call(bf16[512,512]{1,0:T(8,128)(2,1)S(1)} %get-tuple-element.100.ha, bf16[512,512]{1,0:T(8,128)(2,1)S(1)} %collective-permute-done.15.hb, bf16[256,512]{1,0:T(8,128)(2,1)S(1)} %collective-permute-done.3.refs_0_, bf16[256,512]{1,0:T(8,128)(2,1)S(1)} %collective-permute-done.4.refs_1_, ...), custom_call_target="tpu_custom_call" | custom-call | flops 1610612736 | bytes 1572864 | tf_op jit(solution)/shard_map/second_products/pallas_call | solution.py:236
  68.6 1.6 %collective-permute-start.21 = (s16[320,512]{1,0:T(8,128)(2,1)S(1)}, s16[320,512]{1,0:T(8,128)(2,1)S(1)}, u32[]{:S(2)}, u32[]{:S(2)}) collective-permute-start(s16[320,512]{1,0:T(8,128)(2,1)S(1)} %get-tuple-element.114.lo), channel_id=1, source_target_pairs={{0,2},{1,3},{2,0},{3,1},{4,6},{5,7},{6,4},{7,5},{8,10},{9,11},{10,... | collective-permute-start | bytes 983048 | tf_op jit(solution)/shard_map/ppermute | solution.py:276
  70.2 1.5 %collective-permute-start.20 = (s16[320,512]{1,0:T(8,128)(2,1)S(1)}, s16[320,512]{1,0:T(8,128)(2,1)S(1)}, u32[]{:S(2)}, u32[]{:S(2)}) collective-permute-start(s16[320,512]{1,0:T(8,128)(2,1)S(1)} %get-tuple-element.112.hi), channel_id=1, source_target_pairs={{0,4},{1,5},{2,6},{3,7},{4,0},{5,1},{6,2},{7,3},{8,12},{9,13},{10,... | collective-permute-start | bytes 983048 | tf_op jit(solution)/shard_map/ppermute | solution.py:276
  71.7 4.2 %second_products.4 = (s16[272,512]{1,0:T(8,128)(2,1)S(1)}, f32[256,512]{1,0:T(8,128)S(1)}, f32[256,512]{1,0:T(8,128)S(1)}, s16[272,512]{1,0:T(8,128)(2,1)S(1)}) custom-call(bf16[512,512]{1,0:T(8,128)(2,1)S(1)} %get-tuple-element.100.ha, bf16[512,512]{1,0:T(8,128)(2,1)S(1)} %collective-permute-done.15.hb, bf16[512,512]{1,0:T(8,128)(2,1)} %copy-done.5, ...), custom_call_target="tpu_custom_call" | custom-call | flops 3221225472 | bytes 3145728 | tf_op jit(solution)/shard_map/second_products/pallas_call | solution.py:236
  77.0 3.7 %collective-permute-done.20.x_in = s16[320,512]{1,0:T(8,128)(2,1)S(1)} collective-permute-done((s16[320,512]{1,0:T(8,128)(2,1)S(1)}, s16[320,512]{1,0:T(8,128)(2,1)S(1)}, u32[]{:S(2)}, u32[]{:S(2)}) %collective-permute-start.20) | collective-permute-done | bytes 327712 | tf_op jit(solution)/shard_map/ppermute | solution.py:276
  81.6 2.0 %collective-permute-start.26 = (s16[320,512]{1,0:T(8,128)(2,1)S(1)}, s16[320,512]{1,0:T(8,128)(2,1)S(1)}, u32[]{:S(2)}, u32[]{:S(2)}) collective-permute-start(s16[320,512]{1,0:T(8,128)(2,1)S(1)} %get-tuple-element.120), channel_id=1, source_target_pairs={{0,4},{1,5},{2,6},{3,7},{4,0},{5,1},{6,2},{7,3},{8,12},{9,13},{10,... | collective-permute-start | bytes 983048 | tf_op jit(solution)/shard_map/ppermute | solution.py:276
  83.6 1.9 %collective-permute-done.22.x_lo = s16[272,512]{1,0:T(8,128)(2,1)S(1)} collective-permute-done((s16[272,512]{1,0:T(8,128)(2,1)S(1)}, s16[272,512]{1,0:T(8,128)(2,1)S(1)}, u32[]{:S(2)}, u32[]{:S(2)}) %collective-permute-start.22) | collective-permute-done | bytes 278560 | tf_op jit(solution)/shard_map/ppermute | solution.py:276
  86.7 2.5 %second_products.5.own = f32[512,512]{1,0:T(8,128)S(1)} custom-call(bf16[512,512]{1,0:T(8,128)(2,1)S(1)} %get-tuple-element.100.ha, bf16[512,512]{1,0:T(8,128)(2,1)S(1)} %collective-permute-done.15.hb, bf16[512,512]{1,0:T(8,128)(2,1)} %w_ref.1, s16[512,512]{1,0:T(8,128)(2,1)} %get-tuple-element.66.refs_1_, s16[512,512]{1,0:T(8,128)(2,1)S(1)} %collective-permute-done.24.refs_2_), custom_call_target="tpu_custom_call" | custom-call | flops 1610612736 | bytes 1572864 | tf_op jit(solution)/shard_map/second_products/pallas_call | solution.py:236
  89.2 2.5 %collective-permute-done.25.x_hi = s16[320,512]{1,0:T(8,128)(2,1)S(1)} collective-permute-done((s16[320,512]{1,0:T(8,128)(2,1)S(1)}, s16[320,512]{1,0:T(8,128)(2,1)S(1)}, u32[]{:S(2)}, u32[]{:S(2)}) %collective-permute-start.25) | collective-permute-done | bytes 327712 | tf_op jit(solution)/shard_map/ppermute | solution.py:276
  91.7 1.2 %collective-permute-done.26.y_lo = s16[320,512]{1,0:T(8,128)(2,1)S(1)} collective-permute-done((s16[320,512]{1,0:T(8,128)(2,1)S(1)}, s16[320,512]{1,0:T(8,128)(2,1)S(1)}, u32[]{:S(2)}, u32[]{:S(2)}) %collective-permute-start.26) | collective-permute-done | bytes 327712 | tf_op jit(solution)/shard_map/ppermute | solution.py:276
  92.9 1.7 %last_update.1 = (bf16[512,512]{1,0:T(8,128)(2,1)}, f32[64,512]{1,0:T(8,128)}) custom-call(f32[512,512]{1,0:T(8,128)S(1)} %second_products.5.own, s16[272,512]{1,0:T(8,128)(2,1)S(1)} %collective-permute-done.22.x_lo, s16[320,512]{1,0:T(8,128)(2,1)S(1)} %collective-permute-done.25.x_hi, s16[320,512]{1,0:T(8,128)(2,1)S(1)} %collective-permute-done.26.y_lo, ...), custom_call_target="tpu_custom_call" | custom-call | tf_op jit(solution)/shard_map/last_update/pallas_call | solution.py:270
  (63 shorter events, 12.2 us)
Async XLA Ops:
  0.6 11.9 %collective-permute-start.2 = (bf16[512,512]{1,0:T(8,128)(2,1)}, bf16[512,512]{1,0:T(8,128)(2,1)S(1)}, u32[]{:S(2)}, u32[]{:S(2)}) collective-permute-start(bf16[512,512]{1,0:T(8,128)(2,1)} %w_ref.1), channel_id=1, source_target_pairs={{0,1},{1,0},{2,3},{3,2},{4,5},{5,4},{6,7},{7,6},{8,9},{9,8},{10,11... | collective-permute-start | bytes 1572872 | tf_op jit(solution)/shard_map/ppermute | solution.py:276
  1.1 15.3 %collective-permute-start = (bf16[512,512]{1,0:T(8,128)(2,1)}, bf16[512,512]{1,0:T(8,128)(2,1)S(1)}, u32[]{:S(2)}, u32[]{:S(2)}) collective-permute-start(bf16[512,512]{1,0:T(8,128)(2,1)} %w_ref.1), channel_id=1, source_target_pairs={{0,2},{1,3},{2,0},{3,1},{4,6},{5,7},{6,4},{7,5},{8,10},{9,11},{10,... | collective-permute-start | bytes 1572872 | tf_op jit(solution)/shard_map/ppermute | solution.py:276
  3.7 14.3 %collective-permute-start.1 = (bf16[512,512]{1,0:T(8,128)(2,1)}, bf16[512,512]{1,0:T(8,128)(2,1)}, u32[]{:S(2)}, u32[]{:S(2)}) collective-permute-start(bf16[512,512]{1,0:T(8,128)(2,1)} %w_ref.1), channel_id=1, source_target_pairs={{0,4},{1,5},{2,6},{3,7},{4,0},{5,1},{6,2},{7,3},{8,12},{9,13},{10,... | collective-permute-start | bytes 1572872 | tf_op jit(solution)/shard_map/ppermute | solution.py:276
  18.0 3.6 %collective-permute-start.5 = (bf16[512,512]{1,0:T(8,128)(2,1)S(1)}, bf16[512,512]{1,0:T(8,128)(2,1)S(1)}, u32[]{:S(2)}, u32[]{:S(2)}) collective-permute-start(bf16[512,512]{1,0:T(8,128)(2,1)S(1)} %collective-permute-done.refs_0_), channel_id=1, source_target_pairs={{0,1},{1,0},{2,3},{3,2},{4,5},{5,4},{6,7},{7,6},{8,9},{9,8},{10,11... | collective-permute-start | bytes 1572872 | tf_op jit(solution)/shard_map/ppermute | solution.py:276
  18.0 3.6 %collective-permute-start.6 = (bf16[512,512]{1,0:T(8,128)(2,1)}, bf16[512,512]{1,0:T(8,128)(2,1)S(1)}, u32[]{:S(2)}, u32[]{:S(2)}) collective-permute-start(bf16[512,512]{1,0:T(8,128)(2,1)} %collective-permute-done.1.refs_2_.refs_3_), channel_id=1, source_target_pairs={{0,1},{1,0},{2,3},{3,2},{4,5},{5,4},{6,7},{7,6},{8,9},{9,8},{10,11... | collective-permute-start | bytes 1572872 | tf_op jit(solution)/shard_map/ppermute | solution.py:276
  19.5 8.3 %collective-permute-start.3 = (bf16[256,512]{1,0:T(8,128)(2,1)S(1)}, bf16[256,512]{1,0:T(8,128)(2,1)S(1)}, u32[]{:S(2)}, u32[]{:S(2)}) collective-permute-start(bf16[256,512]{1,0:T(8,128)(2,1)S(1)} %slice.6), channel_id=1, source_target_pairs={{0,2},{1,3},{2,0},{3,1},{4,6},{5,7},{6,4},{7,5},{8,10},{9,11},{10,... | collective-permute-start | bytes 786440 | tf_op jit(solution)/shard_map/ppermute | solution.py:276
  19.9 7.9 %collective-permute-start.4 = (bf16[256,512]{1,0:T(8,128)(2,1)S(1)}, bf16[256,512]{1,0:T(8,128)(2,1)S(1)}, u32[]{:S(2)}, u32[]{:S(2)}) collective-permute-start(bf16[256,512]{1,0:T(8,128)(2,1)S(1)} %slice.7), channel_id=1, source_target_pairs={{0,4},{1,5},{2,6},{3,7},{4,0},{5,1},{6,2},{7,3},{8,12},{9,13},{10,... | collective-permute-start | bytes 786440 | tf_op jit(solution)/shard_map/ppermute | solution.py:276
  26.1 34.9 %copy-start = (f32[512,512]{1,0:T(8,128)S(1)}, f32[512,512]{1,0:T(8,128)}, u32[]{:S(2)}) copy-start(f32[512,512]{1,0:T(8,128)} %refs_4_.1) | copy-start | bytes 3145732
  26.1 36.9 %copy-start.1 = (f32[512,64]{0,1:T(8,128)S(1)}, f32[512,64]{0,1:T(8,128)}, u32[]{:S(2)}) copy-start(f32[512,64]{0,1:T(8,128)} %param.8) | copy-start | bytes 393220
  26.2 36.9 %copy-start.3 = (f32[64,512]{1,0:T(8,128)S(1)}, f32[64,512]{1,0:T(8,128)}, u32[]{:S(2)}) copy-start(f32[64,512]{1,0:T(8,128)} %h2_ref.1) | copy-start | bytes 393220
  27.9 2.7 %collective-permute-start.7 = (bf16[256,512]{1,0:T(8,128)(2,1)S(1)}, bf16[256,512]{1,0:T(8,128)(2,1)}, u32[]{:S(2)}, u32[]{:S(2)}) collective-permute-start(bf16[256,512]{1,0:T(8,128)(2,1)S(1)} %collective-permute-done.3.refs_0_), channel_id=1, source_target_pairs={{0,1},{1,0},{2,3},{3,2},{4,5},{5,4},{6,7},{7,6},{8,9},{9,8},{10,11... | collective-permute-start | bytes 786440 | tf_op jit(solution)/shard_map/ppermute | solution.py:276
  27.9 2.7 %collective-permute-start.8 = (bf16[256,512]{1,0:T(8,128)(2,1)S(1)}, bf16[256,512]{1,0:T(8,128)(2,1)}, u32[]{:S(2)}, u32[]{:S(2)}) collective-permute-start(bf16[256,512]{1,0:T(8,128)(2,1)S(1)} %collective-permute-done.4.refs_1_), channel_id=1, source_target_pairs={{0,1},{1,0},{2,3},{3,2},{4,5},{5,4},{6,7},{7,6},{8,9},{9,8},{10,11... | collective-permute-start | bytes 786440 | tf_op jit(solution)/shard_map/ppermute | solution.py:276
  28.4 34.6 %copy-start.7 = (s16[512,512]{1,0:T(8,128)(2,1)S(1)}, s16[512,512]{1,0:T(8,128)(2,1)}, u32[]{:S(2)}) copy-start(s16[512,512]{1,0:T(8,128)(2,1)} %get-tuple-element.75.refs_7_) | copy-start | bytes 1572868
  28.4 38.2 %copy-start.6 = (s16[512,512]{1,0:T(8,128)(2,1)S(1)}, s16[512,512]{1,0:T(8,128)(2,1)}, u32[]{:S(2)}) copy-start(s16[512,512]{1,0:T(8,128)(2,1)} %get-tuple-element.67.refs_3_) | copy-start | bytes 1572868
  32.8 5.6 %collective-permute-start.9 = (s16[528,128]{1,0:T(8,128)(2,1)S(1)}, s16[528,128]{1,0:T(8,128)(2,1)S(1)}, u32[]{:S(2)}, u32[]{:S(2)}) collective-permute-start(s16[528,128]{1,0:T(8,128)(2,1)S(1)} %get-tuple-element.95.refs_0_), channel_id=1, source_target_pairs={{0,8},{8,0},{16,24},{24,16},{1,9},{9,1},{17,25},{25,17},{2,10},{10... | collective-permute-start | bytes 405512 | tf_op jit(solution)/shard_map/ppermute | solution.py:276
  38.5 5.5 %collective-permute-start.11 = (s16[528,128]{1,0:T(8,128)(2,1)S(1)}, s16[528,128]{1,0:T(8,128)(2,1)S(1)}, u32[]{:S(2)}, u32[]{:S(2)}) collective-permute-start(s16[528,128]{1,0:T(8,128)(2,1)S(1)} %get-tuple-element.98), channel_id=1, source_target_pairs={{0,8},{8,0},{16,24},{24,16},{1,9},{9,1},{17,25},{25,17},{2,10},{10... | collective-permute-start | bytes 405512 | tf_op jit(solution)/shard_map/ppermute | solution.py:276
  40.3 11.6 %collective-permute-start.10 = (s16[528,128]{1,0:T(8,128)(2,1)S(1)}, s16[528,128]{1,0:T(8,128)(2,1)S(1)}, u32[]{:S(2)}, u32[]{:S(2)}) collective-permute-start(s16[528,128]{1,0:T(8,128)(2,1)S(1)} %add_pair.2.one), channel_id=1, source_target_pairs={{0,24},{8,16},{16,8},{24,0},{1,25},{9,17},{17,9},{25,1},{2,26},{10... | collective-permute-start | bytes 405512 | tf_op jit(solution)/shard_map/ppermute | solution.py:276
  44.2 11.6 %collective-permute-start.12 = (s16[528,128]{1,0:T(8,128)(2,1)S(1)}, s16[528,128]{1,0:T(8,128)(2,1)S(1)}, u32[]{:S(2)}, u32[]{:S(2)}) collective-permute-start(s16[528,128]{1,0:T(8,128)(2,1)S(1)} %add_pair.3.one), channel_id=1, source_target_pairs={{0,24},{8,16},{16,8},{24,0},{1,25},{9,17},{17,9},{25,1},{2,26},{10... | collective-permute-start | bytes 405512 | tf_op jit(solution)/shard_map/ppermute | solution.py:276
  52.1 5.7 %collective-permute-start.13 = (s16[528,128]{1,0:T(8,128)(2,1)S(1)}, s16[528,128]{1,0:T(8,128)(2,1)S(1)}, u32[]{:S(2)}, u32[]{:S(2)}) collective-permute-start(s16[528,128]{1,0:T(8,128)(2,1)S(1)} %get-tuple-element.96.refs_0_), channel_id=1, source_target_pairs={{0,8},{8,0},{16,24},{24,16},{1,9},{9,1},{17,25},{25,17},{2,10},{10... | collective-permute-start | bytes 405512 | tf_op jit(solution)/shard_map/ppermute | solution.py:276
  56.0 5.1 %collective-permute-start.14 = (s16[528,128]{1,0:T(8,128)(2,1)S(1)}, s16[528,128]{1,0:T(8,128)(2,1)S(1)}, u32[]{:S(2)}, u32[]{:S(2)}) collective-permute-start(s16[528,128]{1,0:T(8,128)(2,1)S(1)} %add_cross.3.refs_1_), channel_id=1, source_target_pairs={{0,8},{8,0},{16,24},{24,16},{1,9},{9,1},{17,25},{25,17},{2,10},{10... | collective-permute-start | bytes 405512 | tf_op jit(solution)/shard_map/ppermute | solution.py:276
  56.1 10.6 %collective-permute-start.17 = (s16[512,512]{1,0:T(8,128)(2,1)S(1)}, s16[512,512]{1,0:T(8,128)(2,1)S(1)}, u32[]{:S(2)}, u32[]{:S(2)}) collective-permute-start(s16[512,512]{1,0:T(8,128)(2,1)S(1)} %copy-done.4), channel_id=1, source_target_pairs={{0,1},{1,0},{2,3},{3,2},{4,5},{5,4},{6,7},{7,6},{8,9},{9,8},{10,11... | collective-permute-start | bytes 1572872 | tf_op jit(solution)/shard_map/ppermute | solution.py:276
  62.4 4.3 %collective-permute-start.15 = (bf16[512,512]{1,0:T(8,128)(2,1)S(1)}, bf16[512,512]{1,0:T(8,128)(2,1)S(1)}, u32[]{:S(2)}, u32[]{:S(2)}) collective-permute-start(bf16[512,512]{1,0:T(8,128)(2,1)S(1)} %get-tuple-element.100.ha), channel_id=1, source_target_pairs={{0,1},{1,0},{2,3},{3,2},{4,5},{5,4},{6,7},{7,6},{8,9},{9,8},{10,11... | collective-permute-start | bytes 1572872 | tf_op jit(solution)/shard_map/ppermute | solution.py:276
  62.5 9.2 %collective-permute-start.18 = (s16[512,512]{1,0:T(8,128)(2,1)S(1)}, s16[512,512]{1,0:T(8,128)(2,1)S(1)}, u32[]{:S(2)}, u32[]{:S(2)}) collective-permute-start(s16[512,512]{1,0:T(8,128)(2,1)S(1)} %copy-done.8), channel_id=1, source_target_pairs={{0,1},{1,0},{2,3},{3,2},{4,5},{5,4},{6,7},{7,6},{8,9},{9,8},{10,11... | collective-permute-start | bytes 1572872 | tf_op jit(solution)/shard_map/ppermute | solution.py:276
  63.0 8.7 %collective-permute-start.19 = (s16[512,512]{1,0:T(8,128)(2,1)S(1)}, s16[512,512]{1,0:T(8,128)(2,1)S(1)}, u32[]{:S(2)}, u32[]{:S(2)}) collective-permute-start(s16[512,512]{1,0:T(8,128)(2,1)S(1)} %copy-done.7), channel_id=1, source_target_pairs={{0,1},{1,0},{2,3},{3,2},{4,5},{5,4},{6,7},{7,6},{8,9},{9,8},{10,11... | collective-permute-start | bytes 1572872 | tf_op jit(solution)/shard_map/ppermute | solution.py:276
  66.1 1.9 %collective-permute-start.16 = (f32[80,512]{1,0:T(8,128)S(1)}, f32[80,512]{1,0:T(8,128)S(1)}, u32[]{:S(2)}, u32[]{:S(2)}) collective-permute-start(f32[80,512]{1,0:T(8,128)S(1)} %get-tuple-element.107.sums), channel_id=1, source_target_pairs={{0,1},{1,0},{2,3},{3,2},{4,5},{5,4},{6,7},{7,6},{8,9},{9,8},{10,11... | collective-permute-start | bytes 491528 | tf_op jit(solution)/shard_map/ppermute | solution.py:276
  66.6 20.1 %collective-permute-start.24 = (s16[512,512]{1,0:T(8,128)(2,1)S(1)}, s16[512,512]{1,0:T(8,128)(2,1)S(1)}, u32[]{:S(2)}, u32[]{:S(2)}) collective-permute-start(s16[512,512]{1,0:T(8,128)(2,1)S(1)} %copy-done.6), channel_id=1, source_target_pairs={{0,1},{1,0},{2,3},{3,2},{4,5},{5,4},{6,7},{7,6},{8,9},{9,8},{10,11... | collective-permute-start | bytes 1572872 | tf_op jit(solution)/shard_map/ppermute | solution.py:276
  68.6 12.1 %collective-permute-start.21 = (s16[320,512]{1,0:T(8,128)(2,1)S(1)}, s16[320,512]{1,0:T(8,128)(2,1)S(1)}, u32[]{:S(2)}, u32[]{:S(2)}) collective-permute-start(s16[320,512]{1,0:T(8,128)(2,1)S(1)} %get-tuple-element.114.lo), channel_id=1, source_target_pairs={{0,2},{1,3},{2,0},{3,1},{4,6},{5,7},{6,4},{7,5},{8,10},{9,11},{10,... | collective-permute-start | bytes 983048 | tf_op jit(solution)/shard_map/ppermute | solution.py:276
  70.2 10.6 %collective-permute-start.20 = (s16[320,512]{1,0:T(8,128)(2,1)S(1)}, s16[320,512]{1,0:T(8,128)(2,1)S(1)}, u32[]{:S(2)}, u32[]{:S(2)}) collective-permute-start(s16[320,512]{1,0:T(8,128)(2,1)S(1)} %get-tuple-element.112.hi), channel_id=1, source_target_pairs={{0,4},{1,5},{2,6},{3,7},{4,0},{5,1},{6,2},{7,3},{8,12},{9,13},{10,... | collective-permute-start | bytes 983048 | tf_op jit(solution)/shard_map/ppermute | solution.py:276
  75.9 9.6 %collective-permute-start.22 = (s16[272,512]{1,0:T(8,128)(2,1)S(1)}, s16[272,512]{1,0:T(8,128)(2,1)S(1)}, u32[]{:S(2)}, u32[]{:S(2)}) collective-permute-start(s16[272,512]{1,0:T(8,128)(2,1)S(1)} %get-tuple-element.116), channel_id=1, source_target_pairs={{0,2},{1,3},{2,0},{3,1},{4,6},{5,7},{6,4},{7,5},{8,10},{9,11},{10,... | collective-permute-start | bytes 835592 | tf_op jit(solution)/shard_map/ppermute | solution.py:276
  76.5 10.1 %collective-permute-start.23 = (s16[272,512]{1,0:T(8,128)(2,1)S(1)}, s16[272,512]{1,0:T(8,128)(2,1)S(1)}, u32[]{:S(2)}, u32[]{:S(2)}) collective-permute-start(s16[272,512]{1,0:T(8,128)(2,1)S(1)} %get-tuple-element.117), channel_id=1, source_target_pairs={{0,4},{1,5},{2,6},{3,7},{4,0},{5,1},{6,2},{7,3},{8,12},{9,13},{10,... | collective-permute-start | bytes 835592 | tf_op jit(solution)/shard_map/ppermute | solution.py:276
  81.5 10.2 %collective-permute-start.25 = (s16[320,512]{1,0:T(8,128)(2,1)S(1)}, s16[320,512]{1,0:T(8,128)(2,1)S(1)}, u32[]{:S(2)}, u32[]{:S(2)}) collective-permute-start(s16[320,512]{1,0:T(8,128)(2,1)S(1)} %get-tuple-element.115), channel_id=1, source_target_pairs={{0,2},{1,3},{2,0},{3,1},{4,6},{5,7},{6,4},{7,5},{8,10},{9,11},{10,... | collective-permute-start | bytes 983048 | tf_op jit(solution)/shard_map/ppermute | solution.py:276
  81.6 11.3 %collective-permute-start.26 = (s16[320,512]{1,0:T(8,128)(2,1)S(1)}, s16[320,512]{1,0:T(8,128)(2,1)S(1)}, u32[]{:S(2)}, u32[]{:S(2)}) collective-permute-start(s16[320,512]{1,0:T(8,128)(2,1)S(1)} %get-tuple-element.120), channel_id=1, source_target_pairs={{0,4},{1,5},{2,6},{3,7},{4,0},{5,1},{6,2},{7,3},{8,12},{9,13},{10,... | collective-permute-start | bytes 983048 | tf_op jit(solution)/shard_map/ppermute | solution.py:276
  (4 other events, 89.7 us)

commit v5 on v4

--- a/solution.py
+++ b/solution.py
@@ -321,6 +321,12 @@
     low_ref[...] = new.astype(BF16)
 
 
+def cut_halves(a_ref, b_ref, lo_ref, hi_ref):
+    t = lo_ref.shape[0]
+    lo_ref[...] = a_ref[:t, :]
+    hi_ref[...] = b_ref[t:, :]
+
+
 def pack(k2, lo, hi, sums, sums_in, lo_ref, hi_ref):
     total = sums[...] + sums_in[...]
     t, half = lo.shape[0], k2 // 2
@@ -342,13 +348,19 @@
     y_ref[at:, :] = y_sums[...]
 
 
-def last_update(own, x_lo, x_hi, y_lo, y_hi, x_sums, y_sums, w_ref, w2t_ref, w1_ref, w2_ref):
-    t, few = x_lo.shape[0] - PAD, x_sums.shape[0] - PAD
+def early_sum(own, x_lo, y_hi, out_ref):
+    t = x_lo.shape[0] - PAD
+    out_ref[:t, :] = own[:t, :] + decode(x_lo)
+    out_ref[t:, :] = own[t:, :] + decode(y_hi)
+
+
+def last_update(base, x_hi, y_lo, x_sums, y_sums, w_ref, w2t_ref, w1_ref, w2_ref):
+    t, few = base.shape[0] // 2, x_sums.shape[0] - PAD
     singles = zip(decode_singles(y_sums, 2, few + PAD), decode_singles(y_lo, 2, y_lo.shape[0]))
     row, h2_row = [a + b for a, b in singles]
-    for at, x, y in ((0, x_lo, y_lo), (t, x_hi, y_hi)):
+    for at, late in ((0, y_lo), (t, x_hi)):
         rows = slice(at, at + t)
-        total = own[rows, :] + decode(x, t) + decode(y, t)
+        total = base[rows, :] + decode(late, t)
         w1_ref[rows, :] = (w_ref[rows, :].astype(F32) * total / row).astype(BF16)
     h2_col = jnp.broadcast_to(h2_row, (8, h2_row.shape[1])).T[: 2 * few, :1]
     low = decode(y_sums, few) + decode(y_lo, few, t + PAD)
@@ -363,12 +375,15 @@
 
 def mm3(a, b, dims):
     (ah, al), (bh, bl) = a, b
+    if ah.shape[dims[0]] <= 64:
+        one, other = (jnp.concatenate(x, axis=d) for x, d in (((ah, ah, al), dims[0]), ((bh, bl, bh), dims[1])))
+        return mm(one, other, dims)
     return mm(ah, bh, dims) + (mm(ah, bl, dims) + mm(al, bh, dims))
 
 
-def layer_two(h1_ref, w2t_ref, h2_ref, v, new_ref, sums_ref, v_out, sem):
-    copy = pltpu.make_async_copy(v, v_out, sem)
-    copy.start()
+def layer_two(n_ahead, h1_ref, w2t_ref, h2_ref, *refs):
+    new_ref, sums_ref = refs[n_ahead : n_ahead + 2]
+    copies = ahead(refs[:n_ahead], refs[n_ahead + 2 : -1], refs[-1])
     h1, w2t, h2 = h1_ref[...], w2t_ref[...], h2_ref[...]
     k2, k1 = w2t.shape
     w2p = parts(w2t)
@@ -383,7 +398,8 @@
     sums_ref[k2 : k2 + 8, :] = mm3(row, parts(h1), (1, 1))
     sums_ref[k2 + 8 :, :] = jnp.zeros((8, k1), F32)
     sums_ref[k2 + 8 :, :k2] = mm3(row, h2p, (1, 1))
-    copy.wait()
+    for copy in copies:
+        copy.wait()
 
 
 def on_device(n_gene, n_cell, counts, w1, h1, w2, h2):
@@ -411,16 +427,16 @@
         on_mine, on_theirs = ([Later(v) for v in some] for some in (v_mine, v_theirs))
         acc = first(((Later(w1), on_mine[0]), (w_0, on_theirs[0])), h1_low)
         w_x, w_y, *acc = after((w_x, w_y, *acc))
-        d_lo, d_hi = cell(w_y[:t], bit=2), cell(w_x[t:], bit=4)
+        half = jax.ShapeDtypeStruct((t, k1), BF16)
+        y_lo, x_hi = plain(cut_halves, (half, half), w_y, w_x, name="cut_halves")
+        d_lo, d_hi = cell(y_lo, bit=2), cell(x_hi, bit=4)
         x_0, y_0 = cell(w_x, bit=1), cell(w_y, bit=1)
-        near = ((Later(w_x), on_mine[1]), (Later(w_y), on_mine[2]), (x_0, on_theirs[1]), (y_0, on_theirs[2]))
+        near = ((w_x, on_mine[1]), (w_y, on_mine[2]), (x_0, on_theirs[1]), (y_0, on_theirs[2]))
         acc = first(near, h1_low, acc)
         d_lo, d_hi, *acc = after((d_lo, d_hi, *acc))
-        v_far = after((v_mine[3], v_theirs[3], *acc))[:2]
-        v_far = plain_fetch(v_far)
-        far = cell(d_lo, bit=1), cell(d_hi, bit=1)
-        acc = first(((d_lo, d_hi, v_far[0]),), h1_low, acc)
-        num, col = first(((*far, v_far[1]),), h1_low, acc)
+        far = [Later(cell(d, bit=1)) for d in (d_lo, d_hi)]
+        *v_far, own_lo, own_hi = plain_fetch(after((v_mine[3], v_theirs[3], d_lo, d_hi, *acc))[:4])
+        num, col = first(((own_lo, own_hi, v_far[0]), (*far, v_far[1])), h1_low, acc)
 
         z = lax.axis_index("gene")
         inner = jnp.where((z == 1) | (z == 2), 1, 0).astype(jnp.int32)[None]
@@ -467,22 +483,24 @@
 
     w2t = w2.T
     vmem, hbm = pl.BlockSpec(memory_space=pltpu.VMEM), pl.BlockSpec(memory_space=pltpu.HBM)
-    h2_new, sums, v_far = pl.pallas_call(
-        layer_two,
+    soon = [pltpu.with_memory_space_constraint(x, pltpu.HBM) for x in ((v_mine[3], d_lo, d_hi) if line else v_mine[:1])]
+    h2_new, sums, *soon = pl.pallas_call(
+        functools.partial(layer_two, len(soon)),
         out_shape=(
             jax.ShapeDtypeStruct((k2, cells), F32),
             jax.ShapeDtypeStruct((k2 + 16, k1), F32),
-            jax.ShapeDtypeStruct(v_mine[-1].shape, jnp.int16),
+            *(jax.ShapeDtypeStruct(x.shape, x.dtype) for x in soon),
         ),
-        in_specs=[vmem] * 3 + [hbm],
-        out_specs=[vmem] * 3,
-        scratch_shapes=[pltpu.SemaphoreType.DMA(())],
+        in_specs=[vmem] * 3 + [hbm] * len(soon),
+        out_specs=[vmem] * (2 + len(soon)),
+        scratch_shapes=[pltpu.SemaphoreType.DMA((len(soon),))],
         compiler_params=params(),
         name="layer_two",
-    )(h1_late, w2t, h2, pltpu.with_memory_space_constraint(v_mine[-1], pltpu.HBM))
+    )(h1_late, w2t, h2, *soon)
     low2 = (h1_low2, h1_low2_other)
     if line:
         sums_in = cell(sums, bit=1)
+        v_far, d_lo, d_hi = soon
         d_lo, d_hi = second(((d_lo, d_hi, v_far, v_other[3]),), rows, low2, ((False, False),))
         sums, sums_in, d_lo = after((sums, sums_in, d_lo))
         few = k2 // 2 + PAD
@@ -503,9 +521,12 @@
         x_hi_in, y_lo_in = cell(x_hi, bit=2), cell(y_lo, bit=4)
         w1_late, x_hi, x_lo_in, y_hi_in = after((w1, x_hi, x_lo_in, y_hi_in))
         (own,) = second(((Later(w1_late), on_mine[0], v_other[0]),), rows, low2, ((False,),))
+        base = plain(
+            early_sum, jax.ShapeDtypeStruct((rows, k1), F32), own, x_lo_in, y_hi_in, name="early_sum"
+        )
         w1_new, w2_new = plain(
             last_update, (jax.ShapeDtypeStruct((rows, k1), BF16), jax.ShapeDtypeStruct((k2, k1), F32)),
-            own, x_lo_in, x_hi_in, y_lo_in, y_hi_in, x_sums, y_sums, w1, w2t, name="last_update",
+            base, x_hi_in, y_lo_in, x_sums, y_sums, w1, w2t, name="last_update",
         )
         w2_new = w2_new.T
     else:

time: 94.9 us -> 93.1 us (0.981)
  Pallas kernels: 33.9 us -> 32.9 us
  local copies, waits for them, and re-layouts: 1.03 us -> 0.04 us
    slice x2 -> x0, local copies, waits for them, and re-layouts: 0.99 us -> none  [on_device(): d_lo, d_hi = (cell(w_y[:t], bit=2), cell(w_x[t:], bit=4))]
    pallas_call x7 -> x6, Pallas kernels: 18.1 us -> 17.8 us  [products(): pl.pallas_call(functools.partial(body, sizes, later, len(fetch), flag), o...]
    pallas_call x9 -> x11, Pallas kernels: 5.44 us -> 5.17 us  [plain(): pl.pallas_call(body, out_shape=outs, in_specs=specs, out_specs=out_specs,...]
  transfers between devices with their start and end apart: 27 -> 27, of which waited for: 14 -> 15; matrix products, arithmetic and copies ran while one was open for 2% -> 1% of each run, Pallas kernels for 32% -> 31%
where the time goes in v5:
time: 93.1 us; the launch traced here: 92.8 us
  Pallas kernels  32.9 us (35%)
  starting transfers between devices  29.3 us (31%)
  waiting for transfers between devices  28.3 us (30%)
  other arithmetic  1.37 us (1%)
    ppermute x27, starting transfers between devices, flip(): return lax.ppermute(x, axis, [(i, i ^ bit) for i in range(size)])  29.3 us
    ppermute x27, waiting for transfers between devices, flip(): return lax.ppermute(x, axis, [(i, i ^ bit) for i in range(size)])  28.3 us
    pallas_call x6, Pallas kernels, products(): pl.pallas_call(functools.partial(body, sizes, later, len(fetch), flag), o...  17.8 us
    pallas_call x1, Pallas kernels, split_counts(): pl.pallas_call(functools.partial(counts_body, chips, rows), out_shape=(ou...  5.92 us
    pallas_call x11, Pallas kernels, plain(): pl.pallas_call(body, out_shape=outs, in_specs=specs, out_specs=out_specs,...  5.17 us
    pallas_call x1, Pallas kernels, on_device(): pl.pallas_call(functools.partial(layer_two, len(soon)), out_shape=(jax.Sh...  2.59 us
  transfers between devices with their start and end apart: 27, of which 15 were waited for; matrix products, arithmetic and copies ran while one was open for 1% of the time, Pallas kernels for 31%

profile of v5, /device:TPU:0, one launch (start us, length us, event | category | flops | bytes accessed | tf_op | source)
XLA Modules:
  0.0 92.8 jit_solution(14184057471241155468)
XLA Ops:
  1.1 2.6 %collective-permute-start = (bf16[512,512]{1,0:T(8,128)(2,1)}, bf16[512,512]{1,0:T(8,128)(2,1)S(1)}, u32[]{:S(2)}, u32[]{:S(2)}) collective-permute-start(bf16[512,512]{1,0:T(8,128)(2,1)} %w_ref.1), channel_id=1, source_target_pairs={{0,2},{1,3},{2,0},{3,1},{4,6},{5,7},{6,4},{7,5},{8,10},{9,11},{10,... | collective-permute-start | bytes 1572872 | tf_op jit(solution)/shard_map/ppermute | solution.py:276
  3.7 1.5 %collective-permute-start.1 = (bf16[512,512]{1,0:T(8,128)(2,1)}, bf16[512,512]{1,0:T(8,128)(2,1)S(1)}, u32[]{:S(2)}, u32[]{:S(2)}) collective-permute-start(bf16[512,512]{1,0:T(8,128)(2,1)} %w_ref.1), channel_id=1, source_target_pairs={{0,4},{1,5},{2,6},{3,7},{4,0},{5,1},{6,2},{7,3},{8,12},{9,13},{10,... | collective-permute-start | bytes 1572872 | tf_op jit(solution)/shard_map/ppermute | solution.py:276
  5.2 1.3 %convert_element_type.3.h = bf16[512,512]{1,0:T(8,128)(2,1)S(1)} convert(f32[512,512]{1,0:T(8,128)} %refs_4_.1) | non-fusion elementwise | flops 262144 | bytes 1572864 | tf_op jit(solution)/shard_map/convert_element_type | solution.py:418
  6.6 5.9 %split_counts.1 = (s16[512,512]{1,0:T(8,128)(2,1)}, s16[512,512]{1,0:T(8,128)(2,1)}, s16[512,512]{1,0:T(8,128)(2,1)}, s16[512,512]{1,0:T(8,128)(2,1)}, s16[512,5...) custom-call(s32[2]{0:T(128)S(1)} %pad_add_fusion.at, s32[4096,512]{1,0:T(8,128)} %v.1), custom_call_target="tpu_custom_call" | custom-call | tf_op jit(solution)/shard_map/split_counts/pallas_call | solution.py:104
  12.6 2.9 %first_products.3 = (f32[512,512]{1,0:T(8,128)S(1)}, f32[8,512]{1,0:T(8,128)S(1)}) custom-call(bf16[512,512]{1,0:T(8,128)(2,1)S(1)} %convert_element_type.3.h, bf16[512,512]{1,0:T(8,128)(2,1)} %w_ref.1, s16[512,512]{1,0:T(8,128)(2,1)} %get-tuple-element.74.refs_1_, bf16[512,512]{1,0:T(8,128)(2,1)S(1)} %collective-permute-done.2.refs_2_, ...), custom_call_target="tpu_custom_call" | custom-call | flops 2147483648 | bytes 2097152 | tf_op jit(solution)/shard_map/first_products/pallas_call | solution.py:236
  16.4 1.5 %collective-permute-done.1.a_ref.refs_2_.refs_3_ = bf16[512,512]{1,0:T(8,128)(2,1)S(1)} collective-permute-done((bf16[512,512]{1,0:T(8,128)(2,1)}, bf16[512,512]{1,0:T(8,128)(2,1)S(1)}, u32[]{:S(2)}, u32[]{:S(2)}) %collective-permute-start.1) | collective-permute-done | bytes 524320 | tf_op jit(solution)/shard_map/ppermute | solution.py:276
  18.9 1.7 %collective-permute-start.4 = (bf16[256,512]{1,0:T(8,128)(2,1)S(1)}, bf16[256,512]{1,0:T(8,128)(2,1)}, u32[]{:S(2)}, u32[]{:S(2)}) collective-permute-start(bf16[256,512]{1,0:T(8,128)(2,1)S(1)} %get-tuple-element.81), channel_id=1, source_target_pairs={{0,4},{1,5},{2,6},{3,7},{4,0},{5,1},{6,2},{7,3},{8,12},{9,13},{10,... | collective-permute-start | bytes 786440 | tf_op jit(solution)/shard_map/ppermute | solution.py:276
  20.6 4.3 %first_products.4 = (f32[512,512]{1,0:T(8,128)S(1)}, f32[8,512]{1,0:T(8,128)S(1)}) custom-call(bf16[512,512]{1,0:T(8,128)(2,1)S(1)} %convert_element_type.3.h, bf16[512,512]{1,0:T(8,128)(2,1)S(1)} %collective-permute-done.b_ref.refs_0_, s16[512,512]{1,0:T(8,128)(2,1)} %get-tuple-element.82.refs_1_, ...), custom_call_target="tpu_custom_call", output_to_operand_aliasing={{0}: (9, {}), {1}: (10, {})} | custom-call | flops 4294967296 | bytes 4194304 | tf_op jit(solution)/shard_map/first_products/pallas_call | solution.py:236
  24.9 1.9 %collective-permute-done.3.refs_2_.refs_1_ = bf16[256,512]{1,0:T(8,128)(2,1)} collective-permute-done((bf16[256,512]{1,0:T(8,128)(2,1)S(1)}, bf16[256,512]{1,0:T(8,128)(2,1)}, u32[]{:S(2)}, u32[]{:S(2)}) %collective-permute-start.3) | collective-permute-done | bytes 262176 | tf_op jit(solution)/shard_map/ppermute | solution.py:276
  27.5 1.4 %fetch.1 = (s16[512,512]{1,0:T(8,128)(2,1)S(1)}, s16[512,512]{1,0:T(8,128)(2,1)S(1)}, bf16[256,512]{1,0:T(8,128)(2,1)S(1)}, bf16[256,512]{1,0:T(8,128)(2,1)S(1)}) custom-call(s16[512,512]{1,0:T(8,128)(2,1)} %get-tuple-element.94.refs_0_, s16[512,512]{1,0:T(8,128)(2,1)} %get-tuple-element.95.refs_1_, bf16[256,512]{1,0:T(8,128)(2,1)} %collective-permute-done.3.refs_2_.refs_1_, ...), custom_call_target="tpu_custom_call" | custom-call | tf_op jit(solution)/shard_map/fetch/pallas_call | solution.py:164
  29.2 2.3 %first_products.5 = (f32[512,512]{1,0:T(8,128)S(1)}, f32[8,512]{1,0:T(8,128)S(1)}) custom-call(bf16[512,512]{1,0:T(8,128)(2,1)S(1)} %convert_element_type.3.h, bf16[256,512]{1,0:T(8,128)(2,1)S(1)} %get-tuple-element.98.refs_0_, bf16[256,512]{1,0:T(8,128)(2,1)S(1)} %get-tuple-element.99.refs_1_, ...), custom_call_target="tpu_custom_call", output_to_operand_aliasing={{0}: (7, {}), {1}: (8, {})} | custom-call | flops 2147483648 | bytes 2097152 | tf_op jit(solution)/shard_map/first_products/pallas_call | solution.py:236
  31.9 1.8 %collective-permute-start.9 = (s16[528,128]{1,0:T(8,128)(2,1)S(1)}, s16[528,128]{1,0:T(8,128)(2,1)S(1)}, u32[]{:S(2)}, u32[]{:S(2)}) collective-permute-start(s16[528,128]{1,0:T(8,128)(2,1)S(1)} %get-tuple-element.105.refs_0_), channel_id=1, source_target_pairs={{0,8},{8,0},{16,24},{24,16},{1,9},{9,1},{17,25},{25,17},{2,10},{10... | collective-permute-start | bytes 405512 | tf_op jit(solution)/shard_map/ppermute | solution.py:276
  33.6 3.9 %collective-permute-done.9.other = s16[528,128]{1,0:T(8,128)(2,1)S(1)} collective-permute-done((s16[528,128]{1,0:T(8,128)(2,1)S(1)}, s16[528,128]{1,0:T(8,128)(2,1)S(1)}, u32[]{:S(2)}, u32[]{:S(2)}) %collective-permute-start.9) | collective-permute-done | bytes 135200 | tf_op jit(solution)/shard_map/ppermute | solution.py:276
  37.7 1.7 %collective-permute-start.11 = (s16[528,128]{1,0:T(8,128)(2,1)S(1)}, s16[528,128]{1,0:T(8,128)(2,1)S(1)}, u32[]{:S(2)}, u32[]{:S(2)}) collective-permute-start(s16[528,128]{1,0:T(8,128)(2,1)S(1)} %get-tuple-element.108), channel_id=1, source_target_pairs={{0,8},{8,0},{16,24},{24,16},{1,9},{9,1},{17,25},{25,17},{2,10},{10... | collective-permute-start | bytes 405512 | tf_op jit(solution)/shard_map/ppermute | solution.py:276
  39.5 2.5 %collective-permute-start.10 = (s16[528,128]{1,0:T(8,128)(2,1)S(1)}, s16[528,128]{1,0:T(8,128)(2,1)S(1)}, u32[]{:S(2)}, u32[]{:S(2)}) collective-permute-start(s16[528,128]{1,0:T(8,128)(2,1)S(1)} %add_pair.2.one), channel_id=1, source_target_pairs={{0,24},{8,16},{16,8},{24,0},{1,25},{9,17},{17,9},{25,1},{2,26},{10... | collective-permute-start | bytes 405512 | tf_op jit(solution)/shard_map/ppermute | solution.py:276
  43.1 7.9 %collective-permute-start.12 = (s16[528,128]{1,0:T(8,128)(2,1)S(1)}, s16[528,128]{1,0:T(8,128)(2,1)S(1)}, u32[]{:S(2)}, u32[]{:S(2)}) collective-permute-start(s16[528,128]{1,0:T(8,128)(2,1)S(1)} %add_pair.3.one), channel_id=1, source_target_pairs={{0,24},{8,16},{16,8},{24,0},{1,25},{9,17},{17,9},{25,1},{2,26},{10... | collective-permute-start | bytes 405512 | tf_op jit(solution)/shard_map/ppermute | solution.py:276
  51.3 3.6 %collective-permute-done.12.other = s16[528,128]{1,0:T(8,128)(2,1)S(1)} collective-permute-done((s16[528,128]{1,0:T(8,128)(2,1)S(1)}, s16[528,128]{1,0:T(8,128)(2,1)S(1)}, u32[]{:S(2)}, u32[]{:S(2)}) %collective-permute-start.12) | collective-permute-done | bytes 135200 | tf_op jit(solution)/shard_map/ppermute | solution.py:276
  55.3 1.7 %collective-permute-done.13.refs_2_ = s16[528,128]{1,0:T(8,128)(2,1)S(1)} collective-permute-done((s16[528,128]{1,0:T(8,128)(2,1)S(1)}, s16[528,128]{1,0:T(8,128)(2,1)S(1)}, u32[]{:S(2)}, u32[]{:S(2)}) %collective-permute-start.13) | collective-permute-done | bytes 135200 | tf_op jit(solution)/shard_map/ppermute | solution.py:276
  56.9 3.2 %collective-permute-done.14.refs_3_ = s16[528,128]{1,0:T(8,128)(2,1)S(1)} collective-permute-done((s16[528,128]{1,0:T(8,128)(2,1)S(1)}, s16[528,128]{1,0:T(8,128)(2,1)S(1)}, u32[]{:S(2)}, u32[]{:S(2)}) %collective-permute-start.14) | collective-permute-done | bytes 135200 | tf_op jit(solution)/shard_map/ppermute | solution.py:276
  60.2 1.4 %h1_update.1 = (f32[512,512]{1,0:T(8,128)}, bf16[512,512]{1,0:T(8,128)(2,1)S(1)}, f32[512,512]{1,0:T(8,128)S(1)}) custom-call(s32[1]{0:T(128)} %bitcast.flag, s16[528,128]{1,0:T(8,128)(2,1)S(1)} %get-tuple-element.106.refs_0_, s16[528,128]{1,0:T(8,128)(2,1)S(1)} %add_cross.3.refs_1_, s16[528,128]{1,0:T(8,128)(2,1)S(1)} %collective-permute-done.13.refs_2_, ...), custom_call_target="tpu_custom_call" | custom-call | tf_op jit(solution)/shard_map/h1_update/pallas_call | solution.py:270
  62.1 2.6 %layer_two.1 = (f32[64,512]{1,0:T(8,128)}, f32[80,512]{1,0:T(8,128)S(1)}, s16[512,512]{1,0:T(8,128)(2,1)S(1)}, bf16[256,512]{1,0:T(8,128)(2,1)S(1)}, bf16[256,512]{1,0:T(8,128)(2,1)S(1)}) custom-call(f32[512,512]{1,0:T(8,128)S(1)} %get-tuple-element.111.h1_ref, f32[64,512]{1,0:T(8,128)S(1)} %bitcast.5, f32[64,512]{1,0:T(8,128)S(1)} %copy-done.5, ...), custom_call_target="tpu_custom_call" | custom-call | tf_op jit(solution)/shard_map/layer_two/pallas_call | solution.py:487
  65.4 1.2 %second_products.3 = (f32[256,512]{1,0:T(8,128)S(1)}, f32[256,512]{1,0:T(8,128)S(1)}) custom-call(bf16[512,512]{1,0:T(8,128)(2,1)S(1)} %get-tuple-element.110.ha, bf16[512,512]{1,0:T(8,128)(2,1)S(1)} %collective-permute-done.15.hb, bf16[256,512]{1,0:T(8,128)(2,1)S(1)} %get-tuple-element.113.refs_0_, bf16[256,512]{1,0:T(8,128)(2,1)S(1)} %get-tuple-element.114.refs_1_, ...), custom_call_target="tpu_custom_call" | custom-call | flops 1610612736 | bytes 1572864 | tf_op jit(solution)/shard_map/second_products/pallas_call | solution.py:236
  67.0 1.6 %collective-permute-start.21 = (s16[320,512]{1,0:T(8,128)(2,1)S(1)}, s16[320,512]{1,0:T(8,128)(2,1)S(1)}, u32[]{:S(2)}, u32[]{:S(2)}) collective-permute-start(s16[320,512]{1,0:T(8,128)(2,1)S(1)} %get-tuple-element.126.lo), channel_id=1, source_target_pairs={{0,2},{1,3},{2,0},{3,1},{4,6},{5,7},{6,4},{7,5},{8,10},{9,11},{10,... | collective-permute-start | bytes 983048 | tf_op jit(solution)/shard_map/ppermute | solution.py:276
  68.6 1.5 %collective-permute-start.20 = (s16[320,512]{1,0:T(8,128)(2,1)S(1)}, s16[320,512]{1,0:T(8,128)(2,1)S(1)}, u32[]{:S(2)}, u32[]{:S(2)}) collective-permute-start(s16[320,512]{1,0:T(8,128)(2,1)S(1)} %get-tuple-element.124.hi), channel_id=1, source_target_pairs={{0,4},{1,5},{2,6},{3,7},{4,0},{5,1},{6,2},{7,3},{8,12},{9,13},{10,... | collective-permute-start | bytes 983048 | tf_op jit(solution)/shard_map/ppermute | solution.py:276
  70.1 4.4 %second_products.4 = (s16[272,512]{1,0:T(8,128)(2,1)S(1)}, f32[256,512]{1,0:T(8,128)S(1)}, f32[256,512]{1,0:T(8,128)S(1)}, s16[272,512]{1,0:T(8,128)(2,1)S(1)}) custom-call(bf16[512,512]{1,0:T(8,128)(2,1)S(1)} %get-tuple-element.110.ha, bf16[512,512]{1,0:T(8,128)(2,1)S(1)} %collective-permute-done.15.hb, bf16[512,512]{1,0:T(8,128)(2,1)} %copy-done.3, ...), custom_call_target="tpu_custom_call" | custom-call | flops 3221225472 | bytes 3145728 | tf_op jit(solution)/shard_map/second_products/pallas_call | solution.py:236
  75.7 3.5 %collective-permute-done.20.x_in = s16[320,512]{1,0:T(8,128)(2,1)S(1)} collective-permute-done((s16[320,512]{1,0:T(8,128)(2,1)S(1)}, s16[320,512]{1,0:T(8,128)(2,1)S(1)}, u32[]{:S(2)}, u32[]{:S(2)}) %collective-permute-start.20) | collective-permute-done | bytes 327712 | tf_op jit(solution)/shard_map/ppermute | solution.py:276
  80.1 2.0 %collective-permute-start.26 = (s16[320,512]{1,0:T(8,128)(2,1)S(1)}, s16[320,512]{1,0:T(8,128)(2,1)S(1)}, u32[]{:S(2)}, u32[]{:S(2)}) collective-permute-start(s16[320,512]{1,0:T(8,128)(2,1)S(1)} %get-tuple-element.133), channel_id=1, source_target_pairs={{0,4},{1,5},{2,6},{3,7},{4,0},{5,1},{6,2},{7,3},{8,12},{9,13},{10,... | collective-permute-start | bytes 983048 | tf_op jit(solution)/shard_map/ppermute | solution.py:276
  82.1 2.1 %collective-permute-done.22.x_lo = s16[272,512]{1,0:T(8,128)(2,1)S(1)} collective-permute-done((s16[272,512]{1,0:T(8,128)(2,1)S(1)}, s16[272,512]{1,0:T(8,128)(2,1)S(1)}, u32[]{:S(2)}, u32[]{:S(2)}) %collective-permute-start.22) | collective-permute-done | bytes 278560 | tf_op jit(solution)/shard_map/ppermute | solution.py:276
  85.2 2.5 %second_products.5.own = f32[512,512]{1,0:T(8,128)S(1)} custom-call(bf16[512,512]{1,0:T(8,128)(2,1)S(1)} %get-tuple-element.110.ha, bf16[512,512]{1,0:T(8,128)(2,1)S(1)} %collective-permute-done.15.hb, bf16[512,512]{1,0:T(8,128)(2,1)} %w_ref.1, s16[512,512]{1,0:T(8,128)(2,1)} %get-tuple-element.74.refs_1_, s16[512,512]{1,0:T(8,128)(2,1)S(1)} %collective-permute-done.24.refs_2_), custom_call_target="tpu_custom_call" | custom-call | flops 1610612736 | bytes 1572864 | tf_op jit(solution)/shard_map/second_products/pallas_call | solution.py:236
  87.9 2.3 %collective-permute-done.25.x_hi = s16[320,512]{1,0:T(8,128)(2,1)S(1)} collective-permute-done((s16[320,512]{1,0:T(8,128)(2,1)S(1)}, s16[320,512]{1,0:T(8,128)(2,1)S(1)}, u32[]{:S(2)}, u32[]{:S(2)}) %collective-permute-start.25) | collective-permute-done | bytes 327712 | tf_op jit(solution)/shard_map/ppermute | solution.py:276
  90.2 1.2 %collective-permute-done.26.y_lo = s16[320,512]{1,0:T(8,128)(2,1)S(1)} collective-permute-done((s16[320,512]{1,0:T(8,128)(2,1)S(1)}, s16[320,512]{1,0:T(8,128)(2,1)S(1)}, u32[]{:S(2)}, u32[]{:S(2)}) %collective-permute-start.26) | collective-permute-done | bytes 327712 | tf_op jit(solution)/shard_map/ppermute | solution.py:276
  91.4 1.4 %last_update.1 = (bf16[512,512]{1,0:T(8,128)(2,1)}, f32[64,512]{1,0:T(8,128)}) custom-call(f32[512,512]{1,0:T(8,128)S(1)} %early_sum.1.base, s16[320,512]{1,0:T(8,128)(2,1)S(1)} %collective-permute-done.25.x_hi, s16[320,512]{1,0:T(8,128)(2,1)S(1)} %collective-permute-done.26.y_lo, s16[48,512]{1,0:T(8,128)(2,1)S(1)} %get-tuple-element.134.x_sums, ...), custom_call_target="tpu_custom_call" | custom-call | tf_op jit(solution)/shard_map/last_update/pallas_call | solution.py:270
  (58 shorter events, 10.3 us)
Async XLA Ops:
  0.6 11.9 %collective-permute-start.2 = (bf16[512,512]{1,0:T(8,128)(2,1)}, bf16[512,512]{1,0:T(8,128)(2,1)S(1)}, u32[]{:S(2)}, u32[]{:S(2)}) collective-permute-start(bf16[512,512]{1,0:T(8,128)(2,1)} %w_ref.1), channel_id=1, source_target_pairs={{0,1},{1,0},{2,3},{3,2},{4,5},{5,4},{6,7},{7,6},{8,9},{9,8},{10,11... | collective-permute-start | bytes 1572872 | tf_op jit(solution)/shard_map/ppermute | solution.py:276
  1.1 15.3 %collective-permute-start = (bf16[512,512]{1,0:T(8,128)(2,1)}, bf16[512,512]{1,0:T(8,128)(2,1)S(1)}, u32[]{:S(2)}, u32[]{:S(2)}) collective-permute-start(bf16[512,512]{1,0:T(8,128)(2,1)} %w_ref.1), channel_id=1, source_target_pairs={{0,2},{1,3},{2,0},{3,1},{4,6},{5,7},{6,4},{7,5},{8,10},{9,11},{10,... | collective-permute-start | bytes 1572872 | tf_op jit(solution)/shard_map/ppermute | solution.py:276
  3.7 14.2 %collective-permute-start.1 = (bf16[512,512]{1,0:T(8,128)(2,1)}, bf16[512,512]{1,0:T(8,128)(2,1)S(1)}, u32[]{:S(2)}, u32[]{:S(2)}) collective-permute-start(bf16[512,512]{1,0:T(8,128)(2,1)} %w_ref.1), channel_id=1, source_target_pairs={{0,4},{1,5},{2,6},{3,7},{4,0},{5,1},{6,2},{7,3},{8,12},{9,13},{10,... | collective-permute-start | bytes 1572872 | tf_op jit(solution)/shard_map/ppermute | solution.py:276
  17.9 2.7 %collective-permute-start.5 = (bf16[512,512]{1,0:T(8,128)(2,1)S(1)}, bf16[512,512]{1,0:T(8,128)(2,1)S(1)}, u32[]{:S(2)}, u32[]{:S(2)}) collective-permute-start(bf16[512,512]{1,0:T(8,128)(2,1)S(1)} %collective-permute-done.b_ref.refs_0_), channel_id=1, source_target_pairs={{0,1},{1,0},{2,3},{3,2},{4,5},{5,4},{6,7},{7,6},{8,9},{9,8},{10,11... | collective-permute-start | bytes 1572872 | tf_op jit(solution)/shard_map/ppermute | solution.py:276
  17.9 2.7 %collective-permute-start.6 = (bf16[512,512]{1,0:T(8,128)(2,1)S(1)}, bf16[512,512]{1,0:T(8,128)(2,1)S(1)}, u32[]{:S(2)}, u32[]{:S(2)}) collective-permute-start(bf16[512,512]{1,0:T(8,128)(2,1)S(1)} %collective-permute-done.1.a_ref.refs_2_.refs_3_), channel_id=1, source_target_pairs={{0,1},{1,0},{2,3},{3,2},{4,5},{5,4},{6,7},{7,6},{8,9},{9,8},{10,11... | collective-permute-start | bytes 1572872 | tf_op jit(solution)/shard_map/ppermute | solution.py:276
  18.5 8.4 %collective-permute-start.3 = (bf16[256,512]{1,0:T(8,128)(2,1)S(1)}, bf16[256,512]{1,0:T(8,128)(2,1)}, u32[]{:S(2)}, u32[]{:S(2)}) collective-permute-start(bf16[256,512]{1,0:T(8,128)(2,1)S(1)} %get-tuple-element.80), channel_id=1, source_target_pairs={{0,2},{1,3},{2,0},{3,1},{4,6},{5,7},{6,4},{7,5},{8,10},{9,11},{10,... | collective-permute-start | bytes 786440 | tf_op jit(solution)/shard_map/ppermute | solution.py:276
  18.9 8.1 %collective-permute-start.4 = (bf16[256,512]{1,0:T(8,128)(2,1)S(1)}, bf16[256,512]{1,0:T(8,128)(2,1)}, u32[]{:S(2)}, u32[]{:S(2)}) collective-permute-start(bf16[256,512]{1,0:T(8,128)(2,1)S(1)} %get-tuple-element.81), channel_id=1, source_target_pairs={{0,4},{1,5},{2,6},{3,7},{4,0},{5,1},{6,2},{7,3},{8,12},{9,13},{10,... | collective-permute-start | bytes 786440 | tf_op jit(solution)/shard_map/ppermute | solution.py:276
  24.9 35.3 %copy-start = (f32[512,512]{1,0:T(8,128)S(1)}, f32[512,512]{1,0:T(8,128)}, u32[]{:S(2)}) copy-start(f32[512,512]{1,0:T(8,128)} %refs_4_.1) | copy-start | bytes 3145732
  24.9 37.2 %copy-start.2 = (f32[512,64]{0,1:T(8,128)S(1)}, f32[512,64]{0,1:T(8,128)}, u32[]{:S(2)}) copy-start(f32[512,64]{0,1:T(8,128)} %param.8) | copy-start | bytes 393220
  24.9 37.2 %copy-start.5 = (f32[64,512]{1,0:T(8,128)S(1)}, f32[64,512]{1,0:T(8,128)}, u32[]{:S(2)}) copy-start(f32[64,512]{1,0:T(8,128)} %h2_ref.1) | copy-start | bytes 393220
  27.0 2.0 %collective-permute-start.7 = (bf16[256,512]{1,0:T(8,128)(2,1)}, bf16[256,512]{1,0:T(8,128)(2,1)}, u32[]{:S(2)}, u32[]{:S(2)}) collective-permute-start(bf16[256,512]{1,0:T(8,128)(2,1)} %collective-permute-done.3.refs_2_.refs_1_), channel_id=1, source_target_pairs={{0,1},{1,0},{2,3},{3,2},{4,5},{5,4},{6,7},{7,6},{8,9},{9,8},{10,11... | collective-permute-start | bytes 786440 | tf_op jit(solution)/shard_map/ppermute | solution.py:276
  27.0 2.2 %collective-permute-start.8 = (bf16[256,512]{1,0:T(8,128)(2,1)}, bf16[256,512]{1,0:T(8,128)(2,1)}, u32[]{:S(2)}, u32[]{:S(2)}) collective-permute-start(bf16[256,512]{1,0:T(8,128)(2,1)} %collective-permute-done.4.refs_3_.refs_2_), channel_id=1, source_target_pairs={{0,1},{1,0},{2,3},{3,2},{4,5},{5,4},{6,7},{7,6},{8,9},{9,8},{10,11... | collective-permute-start | bytes 786440 | tf_op jit(solution)/shard_map/ppermute | solution.py:276
  27.5 37.8 %copy-start.6 = (s16[512,512]{1,0:T(8,128)(2,1)S(1)}, s16[512,512]{1,0:T(8,128)(2,1)}, u32[]{:S(2)}) copy-start(s16[512,512]{1,0:T(8,128)(2,1)} %get-tuple-element.75.refs_3_) | copy-start | bytes 1572868
  31.9 5.7 %collective-permute-start.9 = (s16[528,128]{1,0:T(8,128)(2,1)S(1)}, s16[528,128]{1,0:T(8,128)(2,1)S(1)}, u32[]{:S(2)}, u32[]{:S(2)}) collective-permute-start(s16[528,128]{1,0:T(8,128)(2,1)S(1)} %get-tuple-element.105.refs_0_), channel_id=1, source_target_pairs={{0,8},{8,0},{16,24},{24,16},{1,9},{9,1},{17,25},{25,17},{2,10},{10... | collective-permute-start | bytes 405512 | tf_op jit(solution)/shard_map/ppermute | solution.py:276
  37.7 5.3 %collective-permute-start.11 = (s16[528,128]{1,0:T(8,128)(2,1)S(1)}, s16[528,128]{1,0:T(8,128)(2,1)S(1)}, u32[]{:S(2)}, u32[]{:S(2)}) collective-permute-start(s16[528,128]{1,0:T(8,128)(2,1)S(1)} %get-tuple-element.108), channel_id=1, source_target_pairs={{0,8},{8,0},{16,24},{24,16},{1,9},{9,1},{17,25},{25,17},{2,10},{10... | collective-permute-start | bytes 405512 | tf_op jit(solution)/shard_map/ppermute | solution.py:276
  39.5 11.6 %collective-permute-start.10 = (s16[528,128]{1,0:T(8,128)(2,1)S(1)}, s16[528,128]{1,0:T(8,128)(2,1)S(1)}, u32[]{:S(2)}, u32[]{:S(2)}) collective-permute-start(s16[528,128]{1,0:T(8,128)(2,1)S(1)} %add_pair.2.one), channel_id=1, source_target_pairs={{0,24},{8,16},{16,8},{24,0},{1,25},{9,17},{17,9},{25,1},{2,26},{10... | collective-permute-start | bytes 405512 | tf_op jit(solution)/shard_map/ppermute | solution.py:276
  43.1 11.8 %collective-permute-start.12 = (s16[528,128]{1,0:T(8,128)(2,1)S(1)}, s16[528,128]{1,0:T(8,128)(2,1)S(1)}, u32[]{:S(2)}, u32[]{:S(2)}) collective-permute-start(s16[528,128]{1,0:T(8,128)(2,1)S(1)} %add_pair.3.one), channel_id=1, source_target_pairs={{0,24},{8,16},{16,8},{24,0},{1,25},{9,17},{17,9},{25,1},{2,26},{10... | collective-permute-start | bytes 405512 | tf_op jit(solution)/shard_map/ppermute | solution.py:276
  51.3 5.7 %collective-permute-start.13 = (s16[528,128]{1,0:T(8,128)(2,1)S(1)}, s16[528,128]{1,0:T(8,128)(2,1)S(1)}, u32[]{:S(2)}, u32[]{:S(2)}) collective-permute-start(s16[528,128]{1,0:T(8,128)(2,1)S(1)} %get-tuple-element.106.refs_0_), channel_id=1, source_target_pairs={{0,8},{8,0},{16,24},{24,16},{1,9},{9,1},{17,25},{25,17},{2,10},{10... | collective-permute-start | bytes 405512 | tf_op jit(solution)/shard_map/ppermute | solution.py:276
  55.1 5.1 %collective-permute-start.14 = (s16[528,128]{1,0:T(8,128)(2,1)S(1)}, s16[528,128]{1,0:T(8,128)(2,1)S(1)}, u32[]{:S(2)}, u32[]{:S(2)}) collective-permute-start(s16[528,128]{1,0:T(8,128)(2,1)S(1)} %add_cross.3.refs_1_), channel_id=1, source_target_pairs={{0,8},{8,0},{16,24},{24,16},{1,9},{9,1},{17,25},{25,17},{2,10},{10... | collective-permute-start | bytes 405512 | tf_op jit(solution)/shard_map/ppermute | solution.py:276
  55.2 10.1 %collective-permute-start.17 = (s16[512,512]{1,0:T(8,128)(2,1)}, s16[512,512]{1,0:T(8,128)(2,1)S(1)}, u32[]{:S(2)}, u32[]{:S(2)}) collective-permute-start(s16[512,512]{1,0:T(8,128)(2,1)} %get-tuple-element.95.refs_1_), channel_id=1, source_target_pairs={{0,1},{1,0},{2,3},{3,2},{4,5},{5,4},{6,7},{7,6},{8,9},{9,8},{10,11... | collective-permute-start | bytes 1572872 | tf_op jit(solution)/shard_map/ppermute | solution.py:276
  61.6 3.8 %collective-permute-start.15 = (bf16[512,512]{1,0:T(8,128)(2,1)S(1)}, bf16[512,512]{1,0:T(8,128)(2,1)S(1)}, u32[]{:S(2)}, u32[]{:S(2)}) collective-permute-start(bf16[512,512]{1,0:T(8,128)(2,1)S(1)} %get-tuple-element.110.ha), channel_id=1, source_target_pairs={{0,1},{1,0},{2,3},{3,2},{4,5},{5,4},{6,7},{7,6},{8,9},{9,8},{10,11... | collective-permute-start | bytes 1572872 | tf_op jit(solution)/shard_map/ppermute | solution.py:276
  61.6 8.6 %collective-permute-start.18 = (s16[512,512]{1,0:T(8,128)(2,1)}, s16[512,512]{1,0:T(8,128)(2,1)S(1)}, u32[]{:S(2)}, u32[]{:S(2)}) collective-permute-start(s16[512,512]{1,0:T(8,128)(2,1)} %get-tuple-element.84.refs_5_), channel_id=1, source_target_pairs={{0,1},{1,0},{2,3},{3,2},{4,5},{5,4},{6,7},{7,6},{8,9},{9,8},{10,11... | collective-permute-start | bytes 1572872 | tf_op jit(solution)/shard_map/ppermute | solution.py:276
  62.1 8.1 %collective-permute-start.19 = (s16[512,512]{1,0:T(8,128)(2,1)}, s16[512,512]{1,0:T(8,128)(2,1)S(1)}, u32[]{:S(2)}, u32[]{:S(2)}) collective-permute-start(s16[512,512]{1,0:T(8,128)(2,1)} %get-tuple-element.85.refs_7_), channel_id=1, source_target_pairs={{0,1},{1,0},{2,3},{3,2},{4,5},{5,4},{6,7},{7,6},{8,9},{9,8},{10,11... | collective-permute-start | bytes 1572872 | tf_op jit(solution)/shard_map/ppermute | solution.py:276
  64.7 1.9 %collective-permute-start.16 = (f32[80,512]{1,0:T(8,128)S(1)}, f32[80,512]{1,0:T(8,128)S(1)}, u32[]{:S(2)}, u32[]{:S(2)}) collective-permute-start(f32[80,512]{1,0:T(8,128)S(1)} %get-tuple-element.119.sums), channel_id=1, source_target_pairs={{0,1},{1,0},{2,3},{3,2},{4,5},{5,4},{6,7},{7,6},{8,9},{9,8},{10,11... | collective-permute-start | bytes 491528 | tf_op jit(solution)/shard_map/ppermute | solution.py:276
  65.3 19.9 %collective-permute-start.24 = (s16[512,512]{1,0:T(8,128)(2,1)S(1)}, s16[512,512]{1,0:T(8,128)(2,1)S(1)}, u32[]{:S(2)}, u32[]{:S(2)}) collective-permute-start(s16[512,512]{1,0:T(8,128)(2,1)S(1)} %copy-done.6), channel_id=1, source_target_pairs={{0,1},{1,0},{2,3},{3,2},{4,5},{5,4},{6,7},{7,6},{8,9},{9,8},{10,11... | collective-permute-start | bytes 1572872 | tf_op jit(solution)/shard_map/ppermute | solution.py:276
  67.0 12.1 %collective-permute-start.21 = (s16[320,512]{1,0:T(8,128)(2,1)S(1)}, s16[320,512]{1,0:T(8,128)(2,1)S(1)}, u32[]{:S(2)}, u32[]{:S(2)}) collective-permute-start(s16[320,512]{1,0:T(8,128)(2,1)S(1)} %get-tuple-element.126.lo), channel_id=1, source_target_pairs={{0,2},{1,3},{2,0},{3,1},{4,6},{5,7},{6,4},{7,5},{8,10},{9,11},{10,... | collective-permute-start | bytes 983048 | tf_op jit(solution)/shard_map/ppermute | solution.py:276
  68.6 10.6 %collective-permute-start.20 = (s16[320,512]{1,0:T(8,128)(2,1)S(1)}, s16[320,512]{1,0:T(8,128)(2,1)S(1)}, u32[]{:S(2)}, u32[]{:S(2)}) collective-permute-start(s16[320,512]{1,0:T(8,128)(2,1)S(1)} %get-tuple-element.124.hi), channel_id=1, source_target_pairs={{0,4},{1,5},{2,6},{3,7},{4,0},{5,1},{6,2},{7,3},{8,12},{9,13},{10,... | collective-permute-start | bytes 983048 | tf_op jit(solution)/shard_map/ppermute | solution.py:276
  74.6 16.8 %copy-start.1 = (bf16[512,512]{1,0:T(8,128)(2,1)S(1)}, bf16[512,512]{1,0:T(8,128)(2,1)}, u32[]{:S(2)}) copy-start(bf16[512,512]{1,0:T(8,128)(2,1)} %w_ref.1) | copy-start | bytes 1572868
  74.6 9.6 %collective-permute-start.22 = (s16[272,512]{1,0:T(8,128)(2,1)S(1)}, s16[272,512]{1,0:T(8,128)(2,1)S(1)}, u32[]{:S(2)}, u32[]{:S(2)}) collective-permute-start(s16[272,512]{1,0:T(8,128)(2,1)S(1)} %get-tuple-element.128), channel_id=1, source_target_pairs={{0,2},{1,3},{2,0},{3,1},{4,6},{5,7},{6,4},{7,5},{8,10},{9,11},{10,... | collective-permute-start | bytes 835592 | tf_op jit(solution)/shard_map/ppermute | solution.py:276
  75.2 10.0 %collective-permute-start.23 = (s16[272,512]{1,0:T(8,128)(2,1)S(1)}, s16[272,512]{1,0:T(8,128)(2,1)S(1)}, u32[]{:S(2)}, u32[]{:S(2)}) collective-permute-start(s16[272,512]{1,0:T(8,128)(2,1)S(1)} %get-tuple-element.129), channel_id=1, source_target_pairs={{0,4},{1,5},{2,6},{3,7},{4,0},{5,1},{6,2},{7,3},{8,12},{9,13},{10,... | collective-permute-start | bytes 835592 | tf_op jit(solution)/shard_map/ppermute | solution.py:276
  80.0 10.2 %collective-permute-start.25 = (s16[320,512]{1,0:T(8,128)(2,1)S(1)}, s16[320,512]{1,0:T(8,128)(2,1)S(1)}, u32[]{:S(2)}, u32[]{:S(2)}) collective-permute-start(s16[320,512]{1,0:T(8,128)(2,1)S(1)} %get-tuple-element.127), channel_id=1, source_target_pairs={{0,2},{1,3},{2,0},{3,1},{4,6},{5,7},{6,4},{7,5},{8,10},{9,11},{10,... | collective-permute-start | bytes 983048 | tf_op jit(solution)/shard_map/ppermute | solution.py:276
  80.1 11.3 %collective-permute-start.26 = (s16[320,512]{1,0:T(8,128)(2,1)S(1)}, s16[320,512]{1,0:T(8,128)(2,1)S(1)}, u32[]{:S(2)}, u32[]{:S(2)}) collective-permute-start(s16[320,512]{1,0:T(8,128)(2,1)S(1)} %get-tuple-element.133), channel_id=1, source_target_pairs={{0,4},{1,5},{2,6},{3,7},{4,0},{5,1},{6,2},{7,3},{8,12},{9,13},{10,... | collective-permute-start | bytes 983048 | tf_op jit(solution)/shard_map/ppermute | solution.py:276
  (2 other events, 11.1 us)

commit v6 on v5

--- a/solution.py
+++ b/solution.py
@@ -301,7 +301,7 @@
 
 
 def h1_update(n, flag, *refs):
-    mine, theirs, (h1_ref, col_ref, new_ref, low_ref, late_ref) = refs[:n], refs[n : 2 * n], refs[2 * n :]
+    mine, theirs, (h1_ref, col_ref, low_ref, late_ref) = refs[:n], refs[n : 2 * n], refs[2 * n :]
     inner = flag[0] == 1
     half = h1_ref.shape[1] // 2
     width = half // n
@@ -310,7 +310,6 @@
         a, b = decode(mine[i]), decode(theirs[i])
         for at, num in ((i * width, jnp.where(inner, b, a)), (half + i * width, jnp.where(inner, a, b))):
             new = h1_ref[:, at : at + width] * num / col
-            new_ref[:, at : at + width] = new
             late_ref[:, at : at + width] = new
             low_ref[:, at : at + width] = new.astype(BF16)
 
@@ -348,7 +347,8 @@
     y_ref[at:, :] = y_sums[...]
 
 
-def early_sum(own, x_lo, y_hi, out_ref):
+def early_sum(own, x_lo, y_hi, w_ref, w2t_ref, out_ref, w_out, w2t_out):
+    w_out[...], w2t_out[...] = w_ref[...], w2t_ref[...]
     t = x_lo.shape[0] - PAD
     out_ref[:t, :] = own[:t, :] + decode(x_lo)
     out_ref[t:, :] = own[t:, :] + decode(y_hi)
@@ -378,12 +378,16 @@
     if ah.shape[dims[0]] <= 64:
         one, other = (jnp.concatenate(x, axis=d) for x, d in (((ah, ah, al), dims[0]), ((bh, bl, bh), dims[1])))
         return mm(one, other, dims)
+    m = ah.shape[1 - dims[0]]
+    if m <= 64:
+        both = mm(jnp.concatenate((ah, al), axis=1 - dims[0]), bh, dims)
+        return both[:m] + (both[m:] + mm(ah, bl, dims))
     return mm(ah, bh, dims) + (mm(ah, bl, dims) + mm(al, bh, dims))
 
 
 def layer_two(n_ahead, h1_ref, w2t_ref, h2_ref, *refs):
     new_ref, sums_ref = refs[n_ahead : n_ahead + 2]
-    copies = ahead(refs[:n_ahead], refs[n_ahead + 2 : -1], refs[-1])
+    copies = ahead((*refs[:n_ahead], h1_ref), refs[n_ahead + 2 : -1], refs[-1])
     h1, w2t, h2 = h1_ref[...], w2t_ref[...], h2_ref[...]
     k2, k1 = w2t.shape
     w2p = parts(w2t)
@@ -394,10 +398,10 @@
     ratio4 = h1 / mm3(w2p, h2p, (0, 0))
     sums_ref[:k2, :] = mm3(h2p, parts(ratio4), (1, 1))
     cells = h1.shape[1]
-    row = (jnp.ones((8, cells), BF16), jnp.zeros((8, cells), BF16))
-    sums_ref[k2 : k2 + 8, :] = mm3(row, parts(h1), (1, 1))
+    row = jnp.ones((8, cells), BF16)
+    sums_ref[k2 : k2 + 8, :] = sum(mm(row, x, (1, 1)) for x in parts(h1))
     sums_ref[k2 + 8 :, :] = jnp.zeros((8, k1), F32)
-    sums_ref[k2 + 8 :, :k2] = mm3(row, h2p, (1, 1))
+    sums_ref[k2 + 8 :, :k2] = sum(mm(row, x, (1, 1)) for x in h2p)
     for copy in copies:
         copy.wait()
 
@@ -459,8 +463,8 @@
         (first_mine, col), *mine = mine
         mine = [first_mine, *mine]
         theirs = [gene(x, bit=1) for x in mine]
-        h1_new, h1_low2, h1_late = plain(
-            functools.partial(h1_update, CHUNKS), new_shapes + new_shapes[:1], *mine, *theirs, h1, col,
+        h1_low2, h1_late = plain(
+            functools.partial(h1_update, CHUNKS), new_shapes[::-1], *mine, *theirs, h1, col,
             flag=inner, name="h1_update",
         )
         h1_low2_other = cell(h1_low2, bit=1)
@@ -484,16 +488,17 @@
     w2t = w2.T
     vmem, hbm = pl.BlockSpec(memory_space=pltpu.VMEM), pl.BlockSpec(memory_space=pltpu.HBM)
     soon = [pltpu.with_memory_space_constraint(x, pltpu.HBM) for x in ((v_mine[3], d_lo, d_hi) if line else v_mine[:1])]
-    h2_new, sums, *soon = pl.pallas_call(
+    h2_new, sums, *soon, h1_new = pl.pallas_call(
         functools.partial(layer_two, len(soon)),
         out_shape=(
             jax.ShapeDtypeStruct((k2, cells), F32),
             jax.ShapeDtypeStruct((k2 + 16, k1), F32),
             *(jax.ShapeDtypeStruct(x.shape, x.dtype) for x in soon),
+            pltpu.HBM(h1.shape, F32),
         ),
         in_specs=[vmem] * 3 + [hbm] * len(soon),
-        out_specs=[vmem] * (2 + len(soon)),
-        scratch_shapes=[pltpu.SemaphoreType.DMA((len(soon),))],
+        out_specs=[vmem] * (2 + len(soon)) + [hbm],
+        scratch_shapes=[pltpu.SemaphoreType.DMA((len(soon) + 1,))],
         compiler_params=params(),
         name="layer_two",
     )(h1_late, w2t, h2, *soon)
@@ -521,12 +526,13 @@
         x_hi_in, y_lo_in = cell(x_hi, bit=2), cell(y_lo, bit=4)
         w1_late, x_hi, x_lo_in, y_hi_in = after((w1, x_hi, x_lo_in, y_hi_in))
         (own,) = second(((Later(w1_late), on_mine[0], v_other[0]),), rows, low2, ((False,),))
-        base = plain(
-            early_sum, jax.ShapeDtypeStruct((rows, k1), F32), own, x_lo_in, y_hi_in, name="early_sum"
+        base, w1_late, w2t = plain(
+            early_sum, tuple(jax.ShapeDtypeStruct(*x) for x in (((rows, k1), F32), (w1.shape, BF16), (w2t.shape, F32))),
+            own, x_lo_in, y_hi_in, w1, w2t, name="early_sum",
         )
         w1_new, w2_new = plain(
             last_update, (jax.ShapeDtypeStruct((rows, k1), BF16), jax.ShapeDtypeStruct((k2, k1), F32)),
-            base, x_hi_in, y_lo_in, x_sums, y_sums, w1, w2t, name="last_update",
+            base, x_hi_in, y_lo_in, x_sums, y_sums, w1_late, w2t, name="last_update",
         )
         w2_new = w2_new.T
     else:

time: 93.1 us -> 91.9 us (0.987)
  Pallas kernels: 32.9 us -> 31.6 us
    pallas_call x11, Pallas kernels: 5.17 us -> 4.22 us  [plain(): pl.pallas_call(body, out_shape=outs, in_specs=specs, out_specs=out_specs,...]
  transfers between devices with their start and end apart: 27 -> 27, of which waited for: 15 -> 15; matrix products, arithmetic and copies ran while one was open for 1% -> 1% of each run, Pallas kernels for 31% -> 30%
where the time goes in v6:
time: 91.9 us; the launch traced here: 91.6 us
  Pallas kernels  31.6 us (34%)
  starting transfers between devices  29.4 us (32%)
  waiting for transfers between devices  28.2 us (31%)
  other arithmetic  1.37 us (1%)
    ppermute x27, starting transfers between devices, flip(): return lax.ppermute(x, axis, [(i, i ^ bit) for i in range(size)])  29.4 us
    ppermute x27, waiting for transfers between devices, flip(): return lax.ppermute(x, axis, [(i, i ^ bit) for i in range(size)])  28.2 us
    pallas_call x6, Pallas kernels, products(): pl.pallas_call(functools.partial(body, sizes, later, len(fetch), flag), o...  17.8 us
    pallas_call x1, Pallas kernels, split_counts(): pl.pallas_call(functools.partial(counts_body, chips, rows), out_shape=(ou...  5.92 us
    pallas_call x11, Pallas kernels, plain(): pl.pallas_call(body, out_shape=outs, in_specs=specs, out_specs=out_specs,...  4.22 us
    pallas_call x1, Pallas kernels, on_device(): pl.pallas_call(functools.partial(layer_two, len(soon)), out_shape=(jax.Sh...  2.27 us
  transfers between devices with their start and end apart: 27, of which 15 were waited for; matrix products, arithmetic and copies ran while one was open for 1% of the time, Pallas kernels for 30%

profile of v6, /device:TPU:0, one launch (start us, length us, event | category | flops | bytes accessed | tf_op | source)
XLA Modules:
  0.0 91.6 jit_solution(14919776803418907044)
XLA Ops:
  1.1 2.6 %collective-permute-start = (bf16[512,512]{1,0:T(8,128)(2,1)}, bf16[512,512]{1,0:T(8,128)(2,1)S(1)}, u32[]{:S(2)}, u32[]{:S(2)}) collective-permute-start(bf16[512,512]{1,0:T(8,128)(2,1)} %w_ref.1), channel_id=1, source_target_pairs={{0,2},{1,3},{2,0},{3,1},{4,6},{5,7},{6,4},{7,5},{8,10},{9,11},{10,... | collective-permute-start | bytes 1572872 | tf_op jit(solution)/shard_map/ppermute | solution.py:276
  3.7 1.5 %collective-permute-start.1 = (bf16[512,512]{1,0:T(8,128)(2,1)}, bf16[512,512]{1,0:T(8,128)(2,1)S(1)}, u32[]{:S(2)}, u32[]{:S(2)}) collective-permute-start(bf16[512,512]{1,0:T(8,128)(2,1)} %w_ref.1), channel_id=1, source_target_pairs={{0,4},{1,5},{2,6},{3,7},{4,0},{5,1},{6,2},{7,3},{8,12},{9,13},{10,... | collective-permute-start | bytes 1572872 | tf_op jit(solution)/shard_map/ppermute | solution.py:276
  5.2 1.3 %convert_element_type.3.h = bf16[512,512]{1,0:T(8,128)(2,1)S(1)} convert(f32[512,512]{1,0:T(8,128)} %refs_4_.1) | non-fusion elementwise | flops 262144 | bytes 1572864 | tf_op jit(solution)/shard_map/convert_element_type | solution.py:422
  6.6 5.9 %split_counts.1 = (s16[512,512]{1,0:T(8,128)(2,1)}, s16[512,512]{1,0:T(8,128)(2,1)}, s16[512,512]{1,0:T(8,128)(2,1)}, s16[512,512]{1,0:T(8,128)(2,1)}, s16[512,5...) custom-call(s32[2]{0:T(128)S(1)} %pad_add_fusion.at, s32[4096,512]{1,0:T(8,128)} %v.1), custom_call_target="tpu_custom_call" | custom-call | tf_op jit(solution)/shard_map/split_counts/pallas_call | solution.py:104
  12.6 3.0 %first_products.3 = (f32[512,512]{1,0:T(8,128)S(1)}, f32[8,512]{1,0:T(8,128)S(1)}) custom-call(bf16[512,512]{1,0:T(8,128)(2,1)S(1)} %convert_element_type.3.h, bf16[512,512]{1,0:T(8,128)(2,1)} %w_ref.1, s16[512,512]{1,0:T(8,128)(2,1)} %get-tuple-element.77.refs_1_, bf16[512,512]{1,0:T(8,128)(2,1)S(1)} %collective-permute-done.2.refs_2_, ...), custom_call_target="tpu_custom_call" | custom-call | flops 2147483648 | bytes 2097152 | tf_op jit(solution)/shard_map/first_products/pallas_call | solution.py:236
  16.4 1.5 %collective-permute-done.1.a_ref.refs_2_.refs_3_ = bf16[512,512]{1,0:T(8,128)(2,1)S(1)} collective-permute-done((bf16[512,512]{1,0:T(8,128)(2,1)}, bf16[512,512]{1,0:T(8,128)(2,1)S(1)}, u32[]{:S(2)}, u32[]{:S(2)}) %collective-permute-start.1) | collective-permute-done | bytes 524320 | tf_op jit(solution)/shard_map/ppermute | solution.py:276
  18.9 1.7 %collective-permute-start.4 = (bf16[256,512]{1,0:T(8,128)(2,1)S(1)}, bf16[256,512]{1,0:T(8,128)(2,1)}, u32[]{:S(2)}, u32[]{:S(2)}) collective-permute-start(bf16[256,512]{1,0:T(8,128)(2,1)S(1)} %get-tuple-element.84), channel_id=1, source_target_pairs={{0,4},{1,5},{2,6},{3,7},{4,0},{5,1},{6,2},{7,3},{8,12},{9,13},{10,... | collective-permute-start | bytes 786440 | tf_op jit(solution)/shard_map/ppermute | solution.py:276
  20.6 4.3 %first_products.4 = (f32[512,512]{1,0:T(8,128)S(1)}, f32[8,512]{1,0:T(8,128)S(1)}) custom-call(bf16[512,512]{1,0:T(8,128)(2,1)S(1)} %convert_element_type.3.h, bf16[512,512]{1,0:T(8,128)(2,1)S(1)} %collective-permute-done.b_ref.refs_0_, s16[512,512]{1,0:T(8,128)(2,1)} %get-tuple-element.85.refs_1_, ...), custom_call_target="tpu_custom_call", output_to_operand_aliasing={{0}: (9, {}), {1}: (10, {})} | custom-call | flops 4294967296 | bytes 4194304 | tf_op jit(solution)/shard_map/first_products/pallas_call | solution.py:236
  24.9 1.9 %collective-permute-done.3.refs_2_.refs_1_ = bf16[256,512]{1,0:T(8,128)(2,1)} collective-permute-done((bf16[256,512]{1,0:T(8,128)(2,1)S(1)}, bf16[256,512]{1,0:T(8,128)(2,1)}, u32[]{:S(2)}, u32[]{:S(2)}) %collective-permute-start.3) | collective-permute-done | bytes 262176 | tf_op jit(solution)/shard_map/ppermute | solution.py:276
  27.5 1.4 %fetch.1 = (s16[512,512]{1,0:T(8,128)(2,1)S(1)}, s16[512,512]{1,0:T(8,128)(2,1)S(1)}, bf16[256,512]{1,0:T(8,128)(2,1)S(1)}, bf16[256,512]{1,0:T(8,128)(2,1)S(1)}) custom-call(s16[512,512]{1,0:T(8,128)(2,1)} %get-tuple-element.97.refs_0_, s16[512,512]{1,0:T(8,128)(2,1)} %get-tuple-element.98.refs_1_, bf16[256,512]{1,0:T(8,128)(2,1)} %collective-permute-done.3.refs_2_.refs_1_, ...), custom_call_target="tpu_custom_call" | custom-call | tf_op jit(solution)/shard_map/fetch/pallas_call | solution.py:164
  29.2 2.3 %first_products.5 = (f32[512,512]{1,0:T(8,128)S(1)}, f32[8,512]{1,0:T(8,128)S(1)}) custom-call(bf16[512,512]{1,0:T(8,128)(2,1)S(1)} %convert_element_type.3.h, bf16[256,512]{1,0:T(8,128)(2,1)S(1)} %get-tuple-element.101.refs_0_, bf16[256,512]{1,0:T(8,128)(2,1)S(1)} %get-tuple-element.102.refs_1_, ...), custom_call_target="tpu_custom_call", output_to_operand_aliasing={{0}: (7, {}), {1}: (8, {})} | custom-call | flops 2147483648 | bytes 2097152 | tf_op jit(solution)/shard_map/first_products/pallas_call | solution.py:236
  31.9 1.8 %collective-permute-start.9 = (s16[528,128]{1,0:T(8,128)(2,1)S(1)}, s16[528,128]{1,0:T(8,128)(2,1)S(1)}, u32[]{:S(2)}, u32[]{:S(2)}) collective-permute-start(s16[528,128]{1,0:T(8,128)(2,1)S(1)} %get-tuple-element.108.refs_0_), channel_id=1, source_target_pairs={{0,8},{8,0},{16,24},{24,16},{1,9},{9,1},{17,25},{25,17},{2,10},{10... | collective-permute-start | bytes 405512 | tf_op jit(solution)/shard_map/ppermute | solution.py:276
  33.6 3.9 %collective-permute-done.9.other = s16[528,128]{1,0:T(8,128)(2,1)S(1)} collective-permute-done((s16[528,128]{1,0:T(8,128)(2,1)S(1)}, s16[528,128]{1,0:T(8,128)(2,1)S(1)}, u32[]{:S(2)}, u32[]{:S(2)}) %collective-permute-start.9) | collective-permute-done | bytes 135200 | tf_op jit(solution)/shard_map/ppermute | solution.py:276
  37.7 1.7 %collective-permute-start.11 = (s16[528,128]{1,0:T(8,128)(2,1)S(1)}, s16[528,128]{1,0:T(8,128)(2,1)S(1)}, u32[]{:S(2)}, u32[]{:S(2)}) collective-permute-start(s16[528,128]{1,0:T(8,128)(2,1)S(1)} %get-tuple-element.111), channel_id=1, source_target_pairs={{0,8},{8,0},{16,24},{24,16},{1,9},{9,1},{17,25},{25,17},{2,10},{10... | collective-permute-start | bytes 405512 | tf_op jit(solution)/shard_map/ppermute | solution.py:276
  39.5 2.5 %collective-permute-start.10 = (s16[528,128]{1,0:T(8,128)(2,1)S(1)}, s16[528,128]{1,0:T(8,128)(2,1)S(1)}, u32[]{:S(2)}, u32[]{:S(2)}) collective-permute-start(s16[528,128]{1,0:T(8,128)(2,1)S(1)} %add_pair.2.one), channel_id=1, source_target_pairs={{0,24},{8,16},{16,8},{24,0},{1,25},{9,17},{17,9},{25,1},{2,26},{10... | collective-permute-start | bytes 405512 | tf_op jit(solution)/shard_map/ppermute | solution.py:276
  41.9 1.0 %collective-permute-done.11.other = s16[528,128]{1,0:T(8,128)(2,1)S(1)} collective-permute-done((s16[528,128]{1,0:T(8,128)(2,1)S(1)}, s16[528,128]{1,0:T(8,128)(2,1)S(1)}, u32[]{:S(2)}, u32[]{:S(2)}) %collective-permute-start.11) | collective-permute-done | bytes 135200 | tf_op jit(solution)/shard_map/ppermute | solution.py:276
  43.1 7.9 %collective-permute-start.12 = (s16[528,128]{1,0:T(8,128)(2,1)S(1)}, s16[528,128]{1,0:T(8,128)(2,1)S(1)}, u32[]{:S(2)}, u32[]{:S(2)}) collective-permute-start(s16[528,128]{1,0:T(8,128)(2,1)S(1)} %add_pair.3.one), channel_id=1, source_target_pairs={{0,24},{8,16},{16,8},{24,0},{1,25},{9,17},{17,9},{25,1},{2,26},{10... | collective-permute-start | bytes 405512 | tf_op jit(solution)/shard_map/ppermute | solution.py:276
  51.3 3.6 %collective-permute-done.12.other = s16[528,128]{1,0:T(8,128)(2,1)S(1)} collective-permute-done((s16[528,128]{1,0:T(8,128)(2,1)S(1)}, s16[528,128]{1,0:T(8,128)(2,1)S(1)}, u32[]{:S(2)}, u32[]{:S(2)}) %collective-permute-start.12) | collective-permute-done | bytes 135200 | tf_op jit(solution)/shard_map/ppermute | solution.py:276
  55.3 1.7 %collective-permute-done.13.refs_2_ = s16[528,128]{1,0:T(8,128)(2,1)S(1)} collective-permute-done((s16[528,128]{1,0:T(8,128)(2,1)S(1)}, s16[528,128]{1,0:T(8,128)(2,1)S(1)}, u32[]{:S(2)}, u32[]{:S(2)}) %collective-permute-start.13) | collective-permute-done | bytes 135200 | tf_op jit(solution)/shard_map/ppermute | solution.py:276
  56.9 3.2 %collective-permute-done.14.refs_3_ = s16[528,128]{1,0:T(8,128)(2,1)S(1)} collective-permute-done((s16[528,128]{1,0:T(8,128)(2,1)S(1)}, s16[528,128]{1,0:T(8,128)(2,1)S(1)}, u32[]{:S(2)}, u32[]{:S(2)}) %collective-permute-start.14) | collective-permute-done | bytes 135200 | tf_op jit(solution)/shard_map/ppermute | solution.py:276
  61.2 2.3 %layer_two.1 = (f32[64,512]{1,0:T(8,128)}, f32[80,512]{1,0:T(8,128)S(1)}, s16[512,512]{1,0:T(8,128)(2,1)S(1)}, bf16[256,512]{1,0:T(8,128)(2,1)S(1)}, bf16[256,512]{1,0:T(8,128)(2,1)S(1)}, /*index=5*/f32[512,512]{1,0:T(8,128)}) custom-call(f32[512,512]{1,0:T(8,128)S(1)} %get-tuple-element.114.h1_ref, f32[64,512]{1,0:T(8,128)S(1)} %bitcast.5, ...), custom_call_target="tpu_custom_call" | custom-call | tf_op jit(solution)/shard_map/layer_two/pallas_call | solution.py:491
  64.1 1.2 %second_products.3 = (f32[256,512]{1,0:T(8,128)S(1)}, f32[256,512]{1,0:T(8,128)S(1)}) custom-call(bf16[512,512]{1,0:T(8,128)(2,1)S(1)} %get-tuple-element.113.ha, bf16[512,512]{1,0:T(8,128)(2,1)S(1)} %collective-permute-done.15.hb, bf16[256,512]{1,0:T(8,128)(2,1)S(1)} %get-tuple-element.116.refs_0_, bf16[256,512]{1,0:T(8,128)(2,1)S(1)} %get-tuple-element.117.refs_1_, ...), custom_call_target="tpu_custom_call" | custom-call | flops 1610612736 | bytes 1572864 | tf_op jit(solution)/shard_map/second_products/pallas_call | solution.py:236
  65.8 1.6 %collective-permute-start.21 = (s16[320,512]{1,0:T(8,128)(2,1)S(1)}, s16[320,512]{1,0:T(8,128)(2,1)S(1)}, u32[]{:S(2)}, u32[]{:S(2)}) collective-permute-start(s16[320,512]{1,0:T(8,128)(2,1)S(1)} %get-tuple-element.129.lo), channel_id=1, source_target_pairs={{0,2},{1,3},{2,0},{3,1},{4,6},{5,7},{6,4},{7,5},{8,10},{9,11},{10,... | collective-permute-start | bytes 983048 | tf_op jit(solution)/shard_map/ppermute | solution.py:276
  67.4 1.5 %collective-permute-start.20 = (s16[320,512]{1,0:T(8,128)(2,1)S(1)}, s16[320,512]{1,0:T(8,128)(2,1)S(1)}, u32[]{:S(2)}, u32[]{:S(2)}) collective-permute-start(s16[320,512]{1,0:T(8,128)(2,1)S(1)} %get-tuple-element.127.hi), channel_id=1, source_target_pairs={{0,4},{1,5},{2,6},{3,7},{4,0},{5,1},{6,2},{7,3},{8,12},{9,13},{10,... | collective-permute-start | bytes 983048 | tf_op jit(solution)/shard_map/ppermute | solution.py:276
  68.9 4.4 %second_products.4 = (s16[272,512]{1,0:T(8,128)(2,1)S(1)}, f32[256,512]{1,0:T(8,128)S(1)}, f32[256,512]{1,0:T(8,128)S(1)}, s16[272,512]{1,0:T(8,128)(2,1)S(1)}) custom-call(bf16[512,512]{1,0:T(8,128)(2,1)S(1)} %get-tuple-element.113.ha, bf16[512,512]{1,0:T(8,128)(2,1)S(1)} %collective-permute-done.15.hb, bf16[512,512]{1,0:T(8,128)(2,1)} %copy-done.3, ...), custom_call_target="tpu_custom_call" | custom-call | flops 3221225472 | bytes 3145728 | tf_op jit(solution)/shard_map/second_products/pallas_call | solution.py:236
  74.5 3.5 %collective-permute-done.20.x_in = s16[320,512]{1,0:T(8,128)(2,1)S(1)} collective-permute-done((s16[320,512]{1,0:T(8,128)(2,1)S(1)}, s16[320,512]{1,0:T(8,128)(2,1)S(1)}, u32[]{:S(2)}, u32[]{:S(2)}) %collective-permute-start.20) | collective-permute-done | bytes 327712 | tf_op jit(solution)/shard_map/ppermute | solution.py:276
  78.8 2.0 %collective-permute-start.26 = (s16[320,512]{1,0:T(8,128)(2,1)S(1)}, s16[320,512]{1,0:T(8,128)(2,1)S(1)}, u32[]{:S(2)}, u32[]{:S(2)}) collective-permute-start(s16[320,512]{1,0:T(8,128)(2,1)S(1)} %get-tuple-element.137), channel_id=1, source_target_pairs={{0,4},{1,5},{2,6},{3,7},{4,0},{5,1},{6,2},{7,3},{8,12},{9,13},{10,... | collective-permute-start | bytes 983048 | tf_op jit(solution)/shard_map/ppermute | solution.py:276
  80.9 2.1 %collective-permute-done.22.x_lo = s16[272,512]{1,0:T(8,128)(2,1)S(1)} collective-permute-done((s16[272,512]{1,0:T(8,128)(2,1)S(1)}, s16[272,512]{1,0:T(8,128)(2,1)S(1)}, u32[]{:S(2)}, u32[]{:S(2)}) %collective-permute-start.22) | collective-permute-done | bytes 278560 | tf_op jit(solution)/shard_map/ppermute | solution.py:276
  83.9 2.5 %second_products.5.own = f32[512,512]{1,0:T(8,128)S(1)} custom-call(bf16[512,512]{1,0:T(8,128)(2,1)S(1)} %get-tuple-element.113.ha, bf16[512,512]{1,0:T(8,128)(2,1)S(1)} %collective-permute-done.15.hb, bf16[512,512]{1,0:T(8,128)(2,1)} %w_ref.1, s16[512,512]{1,0:T(8,128)(2,1)} %get-tuple-element.77.refs_1_, s16[512,512]{1,0:T(8,128)(2,1)S(1)} %collective-permute-done.24.refs_2_), custom_call_target="tpu_custom_call" | custom-call | flops 1610612736 | bytes 1572864 | tf_op jit(solution)/shard_map/second_products/pallas_call | solution.py:236
  86.7 2.2 %collective-permute-done.25.x_hi = s16[320,512]{1,0:T(8,128)(2,1)S(1)} collective-permute-done((s16[320,512]{1,0:T(8,128)(2,1)S(1)}, s16[320,512]{1,0:T(8,128)(2,1)S(1)}, u32[]{:S(2)}, u32[]{:S(2)}) %collective-permute-start.25) | collective-permute-done | bytes 327712 | tf_op jit(solution)/shard_map/ppermute | solution.py:276
  88.9 1.2 %collective-permute-done.26.y_lo = s16[320,512]{1,0:T(8,128)(2,1)S(1)} collective-permute-done((s16[320,512]{1,0:T(8,128)(2,1)S(1)}, s16[320,512]{1,0:T(8,128)(2,1)S(1)}, u32[]{:S(2)}, u32[]{:S(2)}) %collective-permute-start.26) | collective-permute-done | bytes 327712 | tf_op jit(solution)/shard_map/ppermute | solution.py:276
  90.1 1.4 %last_update.1 = (bf16[512,512]{1,0:T(8,128)(2,1)}, f32[64,512]{1,0:T(8,128)}) custom-call(f32[512,512]{1,0:T(8,128)S(1)} %get-tuple-element.136.base, s16[320,512]{1,0:T(8,128)(2,1)S(1)} %collective-permute-done.25.x_hi, s16[320,512]{1,0:T(8,128)(2,1)S(1)} %collective-permute-done.26.y_lo, s16[48,512]{1,0:T(8,128)(2,1)S(1)} %get-tuple-element.138.x_sums, ...), custom_call_target="tpu_custom_call" | custom-call | tf_op jit(solution)/shard_map/last_update/pallas_call | solution.py:270
  (58 shorter events, 9.8 us)
Async XLA Ops:
  0.6 11.9 %collective-permute-start.2 = (bf16[512,512]{1,0:T(8,128)(2,1)}, bf16[512,512]{1,0:T(8,128)(2,1)S(1)}, u32[]{:S(2)}, u32[]{:S(2)}) collective-permute-start(bf16[512,512]{1,0:T(8,128)(2,1)} %w_ref.1), channel_id=1, source_target_pairs={{0,1},{1,0},{2,3},{3,2},{4,5},{5,4},{6,7},{7,6},{8,9},{9,8},{10,11... | collective-permute-start | bytes 1572872 | tf_op jit(solution)/shard_map/ppermute | solution.py:276
  1.1 15.3 %collective-permute-start = (bf16[512,512]{1,0:T(8,128)(2,1)}, bf16[512,512]{1,0:T(8,128)(2,1)S(1)}, u32[]{:S(2)}, u32[]{:S(2)}) collective-permute-start(bf16[512,512]{1,0:T(8,128)(2,1)} %w_ref.1), channel_id=1, source_target_pairs={{0,2},{1,3},{2,0},{3,1},{4,6},{5,7},{6,4},{7,5},{8,10},{9,11},{10,... | collective-permute-start | bytes 1572872 | tf_op jit(solution)/shard_map/ppermute | solution.py:276
  3.7 14.2 %collective-permute-start.1 = (bf16[512,512]{1,0:T(8,128)(2,1)}, bf16[512,512]{1,0:T(8,128)(2,1)S(1)}, u32[]{:S(2)}, u32[]{:S(2)}) collective-permute-start(bf16[512,512]{1,0:T(8,128)(2,1)} %w_ref.1), channel_id=1, source_target_pairs={{0,4},{1,5},{2,6},{3,7},{4,0},{5,1},{6,2},{7,3},{8,12},{9,13},{10,... | collective-permute-start | bytes 1572872 | tf_op jit(solution)/shard_map/ppermute | solution.py:276
  17.9 2.7 %collective-permute-start.5 = (bf16[512,512]{1,0:T(8,128)(2,1)S(1)}, bf16[512,512]{1,0:T(8,128)(2,1)S(1)}, u32[]{:S(2)}, u32[]{:S(2)}) collective-permute-start(bf16[512,512]{1,0:T(8,128)(2,1)S(1)} %collective-permute-done.b_ref.refs_0_), channel_id=1, source_target_pairs={{0,1},{1,0},{2,3},{3,2},{4,5},{5,4},{6,7},{7,6},{8,9},{9,8},{10,11... | collective-permute-start | bytes 1572872 | tf_op jit(solution)/shard_map/ppermute | solution.py:276
  17.9 2.7 %collective-permute-start.6 = (bf16[512,512]{1,0:T(8,128)(2,1)S(1)}, bf16[512,512]{1,0:T(8,128)(2,1)S(1)}, u32[]{:S(2)}, u32[]{:S(2)}) collective-permute-start(bf16[512,512]{1,0:T(8,128)(2,1)S(1)} %collective-permute-done.1.a_ref.refs_2_.refs_3_), channel_id=1, source_target_pairs={{0,1},{1,0},{2,3},{3,2},{4,5},{5,4},{6,7},{7,6},{8,9},{9,8},{10,11... | collective-permute-start | bytes 1572872 | tf_op jit(solution)/shard_map/ppermute | solution.py:276
  18.5 8.4 %collective-permute-start.3 = (bf16[256,512]{1,0:T(8,128)(2,1)S(1)}, bf16[256,512]{1,0:T(8,128)(2,1)}, u32[]{:S(2)}, u32[]{:S(2)}) collective-permute-start(bf16[256,512]{1,0:T(8,128)(2,1)S(1)} %get-tuple-element.83), channel_id=1, source_target_pairs={{0,2},{1,3},{2,0},{3,1},{4,6},{5,7},{6,4},{7,5},{8,10},{9,11},{10,... | collective-permute-start | bytes 786440 | tf_op jit(solution)/shard_map/ppermute | solution.py:276
  18.9 8.1 %collective-permute-start.4 = (bf16[256,512]{1,0:T(8,128)(2,1)S(1)}, bf16[256,512]{1,0:T(8,128)(2,1)}, u32[]{:S(2)}, u32[]{:S(2)}) collective-permute-start(bf16[256,512]{1,0:T(8,128)(2,1)S(1)} %get-tuple-element.84), channel_id=1, source_target_pairs={{0,4},{1,5},{2,6},{3,7},{4,0},{5,1},{6,2},{7,3},{8,12},{9,13},{10,... | collective-permute-start | bytes 786440 | tf_op jit(solution)/shard_map/ppermute | solution.py:276
  24.9 35.3 %copy-start = (f32[512,512]{1,0:T(8,128)S(1)}, f32[512,512]{1,0:T(8,128)}, u32[]{:S(2)}) copy-start(f32[512,512]{1,0:T(8,128)} %refs_4_.1) | copy-start | bytes 3145732
  24.9 36.3 %copy-start.2 = (f32[512,64]{0,1:T(8,128)S(1)}, f32[512,64]{0,1:T(8,128)}, u32[]{:S(2)}) copy-start(f32[512,64]{0,1:T(8,128)} %param.8) | copy-start | bytes 393220
  24.9 36.3 %copy-start.5 = (f32[64,512]{1,0:T(8,128)S(1)}, f32[64,512]{1,0:T(8,128)}, u32[]{:S(2)}) copy-start(f32[64,512]{1,0:T(8,128)} %h2_ref.1) | copy-start | bytes 393220
  27.0 2.0 %collective-permute-start.7 = (bf16[256,512]{1,0:T(8,128)(2,1)}, bf16[256,512]{1,0:T(8,128)(2,1)}, u32[]{:S(2)}, u32[]{:S(2)}) collective-permute-start(bf16[256,512]{1,0:T(8,128)(2,1)} %collective-permute-done.3.refs_2_.refs_1_), channel_id=1, source_target_pairs={{0,1},{1,0},{2,3},{3,2},{4,5},{5,4},{6,7},{7,6},{8,9},{9,8},{10,11... | collective-permute-start | bytes 786440 | tf_op jit(solution)/shard_map/ppermute | solution.py:276
  27.0 2.2 %collective-permute-start.8 = (bf16[256,512]{1,0:T(8,128)(2,1)}, bf16[256,512]{1,0:T(8,128)(2,1)}, u32[]{:S(2)}, u32[]{:S(2)}) collective-permute-start(bf16[256,512]{1,0:T(8,128)(2,1)} %collective-permute-done.4.refs_3_.refs_2_), channel_id=1, source_target_pairs={{0,1},{1,0},{2,3},{3,2},{4,5},{5,4},{6,7},{7,6},{8,9},{9,8},{10,11... | collective-permute-start | bytes 786440 | tf_op jit(solution)/shard_map/ppermute | solution.py:276
  27.5 36.5 %copy-start.6 = (s16[512,512]{1,0:T(8,128)(2,1)S(1)}, s16[512,512]{1,0:T(8,128)(2,1)}, u32[]{:S(2)}) copy-start(s16[512,512]{1,0:T(8,128)(2,1)} %get-tuple-element.78.refs_3_) | copy-start | bytes 1572868
  31.9 5.7 %collective-permute-start.9 = (s16[528,128]{1,0:T(8,128)(2,1)S(1)}, s16[528,128]{1,0:T(8,128)(2,1)S(1)}, u32[]{:S(2)}, u32[]{:S(2)}) collective-permute-start(s16[528,128]{1,0:T(8,128)(2,1)S(1)} %get-tuple-element.108.refs_0_), channel_id=1, source_target_pairs={{0,8},{8,0},{16,24},{24,16},{1,9},{9,1},{17,25},{25,17},{2,10},{10... | collective-permute-start | bytes 405512 | tf_op jit(solution)/shard_map/ppermute | solution.py:276
  37.7 5.3 %collective-permute-start.11 = (s16[528,128]{1,0:T(8,128)(2,1)S(1)}, s16[528,128]{1,0:T(8,128)(2,1)S(1)}, u32[]{:S(2)}, u32[]{:S(2)}) collective-permute-start(s16[528,128]{1,0:T(8,128)(2,1)S(1)} %get-tuple-element.111), channel_id=1, source_target_pairs={{0,8},{8,0},{16,24},{24,16},{1,9},{9,1},{17,25},{25,17},{2,10},{10... | collective-permute-start | bytes 405512 | tf_op jit(solution)/shard_map/ppermute | solution.py:276
  39.5 11.6 %collective-permute-start.10 = (s16[528,128]{1,0:T(8,128)(2,1)S(1)}, s16[528,128]{1,0:T(8,128)(2,1)S(1)}, u32[]{:S(2)}, u32[]{:S(2)}) collective-permute-start(s16[528,128]{1,0:T(8,128)(2,1)S(1)} %add_pair.2.one), channel_id=1, source_target_pairs={{0,24},{8,16},{16,8},{24,0},{1,25},{9,17},{17,9},{25,1},{2,26},{10... | collective-permute-start | bytes 405512 | tf_op jit(solution)/shard_map/ppermute | solution.py:276
  43.1 11.8 %collective-permute-start.12 = (s16[528,128]{1,0:T(8,128)(2,1)S(1)}, s16[528,128]{1,0:T(8,128)(2,1)S(1)}, u32[]{:S(2)}, u32[]{:S(2)}) collective-permute-start(s16[528,128]{1,0:T(8,128)(2,1)S(1)} %add_pair.3.one), channel_id=1, source_target_pairs={{0,24},{8,16},{16,8},{24,0},{1,25},{9,17},{17,9},{25,1},{2,26},{10... | collective-permute-start | bytes 405512 | tf_op jit(solution)/shard_map/ppermute | solution.py:276
  51.3 5.7 %collective-permute-start.13 = (s16[528,128]{1,0:T(8,128)(2,1)S(1)}, s16[528,128]{1,0:T(8,128)(2,1)S(1)}, u32[]{:S(2)}, u32[]{:S(2)}) collective-permute-start(s16[528,128]{1,0:T(8,128)(2,1)S(1)} %get-tuple-element.109.refs_0_), channel_id=1, source_target_pairs={{0,8},{8,0},{16,24},{24,16},{1,9},{9,1},{17,25},{25,17},{2,10},{10... | collective-permute-start | bytes 405512 | tf_op jit(solution)/shard_map/ppermute | solution.py:276
  55.1 5.1 %collective-permute-start.14 = (s16[528,128]{1,0:T(8,128)(2,1)S(1)}, s16[528,128]{1,0:T(8,128)(2,1)S(1)}, u32[]{:S(2)}, u32[]{:S(2)}) collective-permute-start(s16[528,128]{1,0:T(8,128)(2,1)S(1)} %add_cross.3.refs_1_), channel_id=1, source_target_pairs={{0,8},{8,0},{16,24},{24,16},{1,9},{9,1},{17,25},{25,17},{2,10},{10... | collective-permute-start | bytes 405512 | tf_op jit(solution)/shard_map/ppermute | solution.py:276
  55.2 8.8 %collective-permute-start.17 = (s16[512,512]{1,0:T(8,128)(2,1)}, s16[512,512]{1,0:T(8,128)(2,1)S(1)}, u32[]{:S(2)}, u32[]{:S(2)}) collective-permute-start(s16[512,512]{1,0:T(8,128)(2,1)} %get-tuple-element.98.refs_1_), channel_id=1, source_target_pairs={{0,1},{1,0},{2,3},{3,2},{4,5},{5,4},{6,7},{7,6},{8,9},{9,8},{10,11... | collective-permute-start | bytes 1572872 | tf_op jit(solution)/shard_map/ppermute | solution.py:276
  60.6 3.5 %collective-permute-start.15 = (bf16[512,512]{1,0:T(8,128)(2,1)S(1)}, bf16[512,512]{1,0:T(8,128)(2,1)S(1)}, u32[]{:S(2)}, u32[]{:S(2)}) collective-permute-start(bf16[512,512]{1,0:T(8,128)(2,1)S(1)} %get-tuple-element.113.ha), channel_id=1, source_target_pairs={{0,1},{1,0},{2,3},{3,2},{4,5},{5,4},{6,7},{7,6},{8,9},{9,8},{10,11... | collective-permute-start | bytes 1572872 | tf_op jit(solution)/shard_map/ppermute | solution.py:276
  60.7 8.2 %collective-permute-start.18 = (s16[512,512]{1,0:T(8,128)(2,1)}, s16[512,512]{1,0:T(8,128)(2,1)S(1)}, u32[]{:S(2)}, u32[]{:S(2)}) collective-permute-start(s16[512,512]{1,0:T(8,128)(2,1)} %get-tuple-element.87.refs_5_), channel_id=1, source_target_pairs={{0,1},{1,0},{2,3},{3,2},{4,5},{5,4},{6,7},{7,6},{8,9},{9,8},{10,11... | collective-permute-start | bytes 1572872 | tf_op jit(solution)/shard_map/ppermute | solution.py:276
  61.2 7.7 %collective-permute-start.19 = (s16[512,512]{1,0:T(8,128)(2,1)}, s16[512,512]{1,0:T(8,128)(2,1)S(1)}, u32[]{:S(2)}, u32[]{:S(2)}) collective-permute-start(s16[512,512]{1,0:T(8,128)(2,1)} %get-tuple-element.88.refs_7_), channel_id=1, source_target_pairs={{0,1},{1,0},{2,3},{3,2},{4,5},{5,4},{6,7},{7,6},{8,9},{9,8},{10,11... | collective-permute-start | bytes 1572872 | tf_op jit(solution)/shard_map/ppermute | solution.py:276
  63.5 1.9 %collective-permute-start.16 = (f32[80,512]{1,0:T(8,128)S(1)}, f32[80,512]{1,0:T(8,128)S(1)}, u32[]{:S(2)}, u32[]{:S(2)}) collective-permute-start(f32[80,512]{1,0:T(8,128)S(1)} %get-tuple-element.122.sums), channel_id=1, source_target_pairs={{0,1},{1,0},{2,3},{3,2},{4,5},{5,4},{6,7},{7,6},{8,9},{9,8},{10,11... | collective-permute-start | bytes 491528 | tf_op jit(solution)/shard_map/ppermute | solution.py:276
  64.0 19.9 %collective-permute-start.24 = (s16[512,512]{1,0:T(8,128)(2,1)S(1)}, s16[512,512]{1,0:T(8,128)(2,1)S(1)}, u32[]{:S(2)}, u32[]{:S(2)}) collective-permute-start(s16[512,512]{1,0:T(8,128)(2,1)S(1)} %copy-done.6), channel_id=1, source_target_pairs={{0,1},{1,0},{2,3},{3,2},{4,5},{5,4},{6,7},{7,6},{8,9},{9,8},{10,11... | collective-permute-start | bytes 1572872 | tf_op jit(solution)/shard_map/ppermute | solution.py:276
  65.8 12.1 %collective-permute-start.21 = (s16[320,512]{1,0:T(8,128)(2,1)S(1)}, s16[320,512]{1,0:T(8,128)(2,1)S(1)}, u32[]{:S(2)}, u32[]{:S(2)}) collective-permute-start(s16[320,512]{1,0:T(8,128)(2,1)S(1)} %get-tuple-element.129.lo), channel_id=1, source_target_pairs={{0,2},{1,3},{2,0},{3,1},{4,6},{5,7},{6,4},{7,5},{8,10},{9,11},{10,... | collective-permute-start | bytes 983048 | tf_op jit(solution)/shard_map/ppermute | solution.py:276
  67.4 19.1 %copy-start.1 = (bf16[512,512]{1,0:T(8,128)(2,1)S(1)}, bf16[512,512]{1,0:T(8,128)(2,1)}, u32[]{:S(2)}) copy-start(bf16[512,512]{1,0:T(8,128)(2,1)} %w_ref.1) | copy-start | bytes 1572868
  67.4 10.6 %collective-permute-start.20 = (s16[320,512]{1,0:T(8,128)(2,1)S(1)}, s16[320,512]{1,0:T(8,128)(2,1)S(1)}, u32[]{:S(2)}, u32[]{:S(2)}) collective-permute-start(s16[320,512]{1,0:T(8,128)(2,1)S(1)} %get-tuple-element.127.hi), channel_id=1, source_target_pairs={{0,4},{1,5},{2,6},{3,7},{4,0},{5,1},{6,2},{7,3},{8,12},{9,13},{10,... | collective-permute-start | bytes 983048 | tf_op jit(solution)/shard_map/ppermute | solution.py:276
  73.3 9.6 %collective-permute-start.22 = (s16[272,512]{1,0:T(8,128)(2,1)S(1)}, s16[272,512]{1,0:T(8,128)(2,1)S(1)}, u32[]{:S(2)}, u32[]{:S(2)}) collective-permute-start(s16[272,512]{1,0:T(8,128)(2,1)S(1)} %get-tuple-element.131), channel_id=1, source_target_pairs={{0,2},{1,3},{2,0},{3,1},{4,6},{5,7},{6,4},{7,5},{8,10},{9,11},{10,... | collective-permute-start | bytes 835592 | tf_op jit(solution)/shard_map/ppermute | solution.py:276
  74.0 10.0 %collective-permute-start.23 = (s16[272,512]{1,0:T(8,128)(2,1)S(1)}, s16[272,512]{1,0:T(8,128)(2,1)S(1)}, u32[]{:S(2)}, u32[]{:S(2)}) collective-permute-start(s16[272,512]{1,0:T(8,128)(2,1)S(1)} %get-tuple-element.132), channel_id=1, source_target_pairs={{0,4},{1,5},{2,6},{3,7},{4,0},{5,1},{6,2},{7,3},{8,12},{9,13},{10,... | collective-permute-start | bytes 835592 | tf_op jit(solution)/shard_map/ppermute | solution.py:276
  78.8 10.2 %collective-permute-start.25 = (s16[320,512]{1,0:T(8,128)(2,1)S(1)}, s16[320,512]{1,0:T(8,128)(2,1)S(1)}, u32[]{:S(2)}, u32[]{:S(2)}) collective-permute-start(s16[320,512]{1,0:T(8,128)(2,1)S(1)} %get-tuple-element.130), channel_id=1, source_target_pairs={{0,2},{1,3},{2,0},{3,1},{4,6},{5,7},{6,4},{7,5},{8,10},{9,11},{10,... | collective-permute-start | bytes 983048 | tf_op jit(solution)/shard_map/ppermute | solution.py:276
  78.8 11.3 %collective-permute-start.26 = (s16[320,512]{1,0:T(8,128)(2,1)S(1)}, s16[320,512]{1,0:T(8,128)(2,1)S(1)}, u32[]{:S(2)}, u32[]{:S(2)}) collective-permute-start(s16[320,512]{1,0:T(8,128)(2,1)S(1)} %get-tuple-element.137), channel_id=1, source_target_pairs={{0,4},{1,5},{2,6},{3,7},{4,0},{5,1},{6,2},{7,3},{8,12},{9,13},{10,... | collective-permute-start | bytes 983048 | tf_op jit(solution)/shard_map/ppermute | solution.py:276
  (2 other events, 11.1 us)

commit v7 on v6

--- a/solution.py
+++ b/solution.py
@@ -453,7 +453,7 @@
 
         pair = []
         for i, x in enumerate(sent):
-            got = gene(after((x, *pair))[0], bit=1)
+            got = gene(x, bit=1)
             extra = () if i else (x,)
             pair.append(plain(functools.partial(add_kept, i), piece, keep, got, *extra, name="add_pair"))
         mine = []

time: 91.9 us -> 89.2 us (0.971)
  waiting for transfers between devices: 28.2 us -> 24.7 us
    ppermute x27, waiting for transfers between devices: 28.2 us -> 24.7 us  [flip(): return lax.ppermute(x, axis, [(i, i ^ bit) for i in range(size)])]
  transfers between devices with their start and end apart: 27 -> 27, of which waited for: 15 -> 14; matrix products, arithmetic and copies ran while one was open for 1% -> 2% of each run, Pallas kernels for 30% -> 31%
where the time goes in v7:
time: 89.2 us; the launch traced here: 88.9 us
  Pallas kernels  31.6 us (35%)
  starting transfers between devices  30.2 us (34%)
  waiting for transfers between devices  24.7 us (28%)
  other arithmetic  1.37 us (2%)
    ppermute x27, starting transfers between devices, flip(): return lax.ppermute(x, axis, [(i, i ^ bit) for i in range(size)])  30.2 us
    ppermute x27, waiting for transfers between devices, flip(): return lax.ppermute(x, axis, [(i, i ^ bit) for i in range(size)])  24.7 us
    pallas_call x6, Pallas kernels, products(): pl.pallas_call(functools.partial(body, sizes, later, len(fetch), flag), o...  17.8 us
    pallas_call x1, Pallas kernels, split_counts(): pl.pallas_call(functools.partial(counts_body, chips, rows), out_shape=(ou...  5.92 us
    pallas_call x11, Pallas kernels, plain(): pl.pallas_call(body, out_shape=outs, in_specs=specs, out_specs=out_specs,...  4.22 us
    pallas_call x1, Pallas kernels, on_device(): pl.pallas_call(functools.partial(layer_two, len(soon)), out_shape=(jax.Sh...  2.27 us
  transfers between devices with their start and end apart: 27, of which 14 were waited for; matrix products, arithmetic and copies ran while one was open for 2% of the time, Pallas kernels for 31%

profile of v7, /device:TPU:0, one launch (start us, length us, event | category | flops | bytes accessed | tf_op | source)
XLA Modules:
  0.0 88.9 jit_solution(16811568553151037573)
XLA Ops:
  1.1 2.6 %collective-permute-start = (bf16[512,512]{1,0:T(8,128)(2,1)}, bf16[512,512]{1,0:T(8,128)(2,1)S(1)}, u32[]{:S(2)}, u32[]{:S(2)}) collective-permute-start(bf16[512,512]{1,0:T(8,128)(2,1)} %w_ref.1), channel_id=1, source_target_pairs={{0,2},{1,3},{2,0},{3,1},{4,6},{5,7},{6,4},{7,5},{8,10},{9,11},{10,... | collective-permute-start | bytes 1572872 | tf_op jit(solution)/shard_map/ppermute | solution.py:276
  3.7 1.5 %collective-permute-start.1 = (bf16[512,512]{1,0:T(8,128)(2,1)}, bf16[512,512]{1,0:T(8,128)(2,1)S(1)}, u32[]{:S(2)}, u32[]{:S(2)}) collective-permute-start(bf16[512,512]{1,0:T(8,128)(2,1)} %w_ref.1), channel_id=1, source_target_pairs={{0,4},{1,5},{2,6},{3,7},{4,0},{5,1},{6,2},{7,3},{8,12},{9,13},{10,... | collective-permute-start | bytes 1572872 | tf_op jit(solution)/shard_map/ppermute | solution.py:276
  5.2 1.3 %convert_element_type.3.h = bf16[512,512]{1,0:T(8,128)(2,1)S(1)} convert(f32[512,512]{1,0:T(8,128)} %refs_4_.1) | non-fusion elementwise | flops 262144 | bytes 1572864 | tf_op jit(solution)/shard_map/convert_element_type | solution.py:422
  6.6 5.9 %split_counts.1 = (s16[512,512]{1,0:T(8,128)(2,1)}, s16[512,512]{1,0:T(8,128)(2,1)}, s16[512,512]{1,0:T(8,128)(2,1)}, s16[512,512]{1,0:T(8,128)(2,1)}, s16[512,5...) custom-call(s32[2]{0:T(128)S(1)} %pad_add_fusion.at, s32[4096,512]{1,0:T(8,128)} %v.1), custom_call_target="tpu_custom_call" | custom-call | tf_op jit(solution)/shard_map/split_counts/pallas_call | solution.py:104
  12.6 3.0 %first_products.3 = (f32[512,512]{1,0:T(8,128)S(1)}, f32[8,512]{1,0:T(8,128)S(1)}) custom-call(bf16[512,512]{1,0:T(8,128)(2,1)S(1)} %convert_element_type.3.h, bf16[512,512]{1,0:T(8,128)(2,1)} %w_ref.1, s16[512,512]{1,0:T(8,128)(2,1)} %get-tuple-element.76.refs_1_, bf16[512,512]{1,0:T(8,128)(2,1)S(1)} %collective-permute-done.2.refs_2_, ...), custom_call_target="tpu_custom_call" | custom-call | flops 2147483648 | bytes 2097152 | tf_op jit(solution)/shard_map/first_products/pallas_call | solution.py:236
  16.4 1.5 %collective-permute-done.1.a_ref.refs_2_.refs_3_ = bf16[512,512]{1,0:T(8,128)(2,1)S(1)} collective-permute-done((bf16[512,512]{1,0:T(8,128)(2,1)}, bf16[512,512]{1,0:T(8,128)(2,1)S(1)}, u32[]{:S(2)}, u32[]{:S(2)}) %collective-permute-start.1) | collective-permute-done | bytes 524320 | tf_op jit(solution)/shard_map/ppermute | solution.py:276
  18.9 1.7 %collective-permute-start.4 = (bf16[256,512]{1,0:T(8,128)(2,1)S(1)}, bf16[256,512]{1,0:T(8,128)(2,1)}, u32[]{:S(2)}, u32[]{:S(2)}) collective-permute-start(bf16[256,512]{1,0:T(8,128)(2,1)S(1)} %get-tuple-element.83), channel_id=1, source_target_pairs={{0,4},{1,5},{2,6},{3,7},{4,0},{5,1},{6,2},{7,3},{8,12},{9,13},{10,... | collective-permute-start | bytes 786440 | tf_op jit(solution)/shard_map/ppermute | solution.py:276
  20.6 4.3 %first_products.4 = (f32[512,512]{1,0:T(8,128)S(1)}, f32[8,512]{1,0:T(8,128)S(1)}) custom-call(bf16[512,512]{1,0:T(8,128)(2,1)S(1)} %convert_element_type.3.h, bf16[512,512]{1,0:T(8,128)(2,1)S(1)} %collective-permute-done.b_ref.refs_0_, s16[512,512]{1,0:T(8,128)(2,1)} %get-tuple-element.84.refs_1_, ...), custom_call_target="tpu_custom_call", output_to_operand_aliasing={{0}: (9, {}), {1}: (10, {})} | custom-call | flops 4294967296 | bytes 4194304 | tf_op jit(solution)/shard_map/first_products/pallas_call | solution.py:236
  24.9 1.9 %collective-permute-done.3.refs_2_.refs_1_ = bf16[256,512]{1,0:T(8,128)(2,1)} collective-permute-done((bf16[256,512]{1,0:T(8,128)(2,1)S(1)}, bf16[256,512]{1,0:T(8,128)(2,1)}, u32[]{:S(2)}, u32[]{:S(2)}) %collective-permute-start.3) | collective-permute-done | bytes 262176 | tf_op jit(solution)/shard_map/ppermute | solution.py:276
  27.5 1.4 %fetch.1 = (s16[512,512]{1,0:T(8,128)(2,1)S(1)}, s16[512,512]{1,0:T(8,128)(2,1)S(1)}, bf16[256,512]{1,0:T(8,128)(2,1)S(1)}, bf16[256,512]{1,0:T(8,128)(2,1)S(1)}) custom-call(s16[512,512]{1,0:T(8,128)(2,1)} %get-tuple-element.96.refs_0_, s16[512,512]{1,0:T(8,128)(2,1)} %get-tuple-element.97.refs_1_, bf16[256,512]{1,0:T(8,128)(2,1)} %collective-permute-done.3.refs_2_.refs_1_, ...), custom_call_target="tpu_custom_call" | custom-call | tf_op jit(solution)/shard_map/fetch/pallas_call | solution.py:164
  29.2 2.3 %first_products.5 = (f32[512,512]{1,0:T(8,128)S(1)}, f32[8,512]{1,0:T(8,128)S(1)}) custom-call(bf16[512,512]{1,0:T(8,128)(2,1)S(1)} %convert_element_type.3.h, bf16[256,512]{1,0:T(8,128)(2,1)S(1)} %get-tuple-element.100.refs_0_, bf16[256,512]{1,0:T(8,128)(2,1)S(1)} %get-tuple-element.101.refs_1_, ...), custom_call_target="tpu_custom_call", output_to_operand_aliasing={{0}: (7, {}), {1}: (8, {})} | custom-call | flops 2147483648 | bytes 2097152 | tf_op jit(solution)/shard_map/first_products/pallas_call | solution.py:236
  31.9 1.8 %collective-permute-start.11 = (s16[528,128]{1,0:T(8,128)(2,1)S(1)}, s16[528,128]{1,0:T(8,128)(2,1)S(1)}, u32[]{:S(2)}, u32[]{:S(2)}) collective-permute-start(s16[528,128]{1,0:T(8,128)(2,1)S(1)} %get-tuple-element.109), channel_id=1, source_target_pairs={{0,8},{8,0},{16,24},{24,16},{1,9},{9,1},{17,25},{25,17},{2,10},{10... | collective-permute-start | bytes 405512 | tf_op jit(solution)/shard_map/ppermute | solution.py:276
  34.0 4.4 %collective-permute-done.11.other = s16[528,128]{1,0:T(8,128)(2,1)S(1)} collective-permute-done((s16[528,128]{1,0:T(8,128)(2,1)S(1)}, s16[528,128]{1,0:T(8,128)(2,1)S(1)}, u32[]{:S(2)}, u32[]{:S(2)}) %collective-permute-start.11) | collective-permute-done | bytes 135200 | tf_op jit(solution)/shard_map/ppermute | solution.py:276
  38.5 3.8 %collective-permute-start.12 = (s16[528,128]{1,0:T(8,128)(2,1)S(1)}, s16[528,128]{1,0:T(8,128)(2,1)S(1)}, u32[]{:S(2)}, u32[]{:S(2)}) collective-permute-start(s16[528,128]{1,0:T(8,128)(2,1)S(1)} %add_pair.3.one), channel_id=1, source_target_pairs={{0,24},{8,16},{16,8},{24,0},{1,25},{9,17},{17,9},{25,1},{2,26},{10... | collective-permute-start | bytes 405512 | tf_op jit(solution)/shard_map/ppermute | solution.py:276
  42.4 1.9 %collective-permute-start.10 = (s16[528,128]{1,0:T(8,128)(2,1)S(1)}, s16[528,128]{1,0:T(8,128)(2,1)S(1)}, u32[]{:S(2)}, u32[]{:S(2)}) collective-permute-start(s16[528,128]{1,0:T(8,128)(2,1)S(1)} %add_pair.2.one), channel_id=1, source_target_pairs={{0,24},{8,16},{16,8},{24,0},{1,25},{9,17},{17,9},{25,1},{2,26},{10... | collective-permute-start | bytes 405512 | tf_op jit(solution)/shard_map/ppermute | solution.py:276
  44.4 1.6 %collective-permute-done.12.other = s16[528,128]{1,0:T(8,128)(2,1)S(1)} collective-permute-done((s16[528,128]{1,0:T(8,128)(2,1)S(1)}, s16[528,128]{1,0:T(8,128)(2,1)S(1)}, u32[]{:S(2)}, u32[]{:S(2)}) %collective-permute-start.12) | collective-permute-done | bytes 135200 | tf_op jit(solution)/shard_map/ppermute | solution.py:276
  46.2 5.7 %collective-permute-start.14 = (s16[528,128]{1,0:T(8,128)(2,1)S(1)}, s16[528,128]{1,0:T(8,128)(2,1)S(1)}, u32[]{:S(2)}, u32[]{:S(2)}) collective-permute-start(s16[528,128]{1,0:T(8,128)(2,1)S(1)} %add_cross.3.refs_1_), channel_id=1, source_target_pairs={{0,8},{8,0},{16,24},{24,16},{1,9},{9,1},{17,25},{25,17},{2,10},{10... | collective-permute-start | bytes 405512 | tf_op jit(solution)/shard_map/ppermute | solution.py:276
  52.1 1.4 %collective-permute-start.13 = (s16[528,128]{1,0:T(8,128)(2,1)S(1)}, s16[528,128]{1,0:T(8,128)(2,1)S(1)}, u32[]{:S(2)}, u32[]{:S(2)}) collective-permute-start(s16[528,128]{1,0:T(8,128)(2,1)S(1)} %get-tuple-element.108.refs_0_), channel_id=1, source_target_pairs={{0,8},{8,0},{16,24},{24,16},{1,9},{9,1},{17,25},{25,17},{2,10},{10... | collective-permute-start | bytes 405512 | tf_op jit(solution)/shard_map/ppermute | solution.py:276
  53.5 2.6 %collective-permute-done.14.refs_3_ = s16[528,128]{1,0:T(8,128)(2,1)S(1)} collective-permute-done((s16[528,128]{1,0:T(8,128)(2,1)S(1)}, s16[528,128]{1,0:T(8,128)(2,1)S(1)}, u32[]{:S(2)}, u32[]{:S(2)}) %collective-permute-start.14) | collective-permute-done | bytes 135200 | tf_op jit(solution)/shard_map/ppermute | solution.py:276
  56.1 1.4 %collective-permute-done.13.refs_2_ = s16[528,128]{1,0:T(8,128)(2,1)S(1)} collective-permute-done((s16[528,128]{1,0:T(8,128)(2,1)S(1)}, s16[528,128]{1,0:T(8,128)(2,1)S(1)}, u32[]{:S(2)}, u32[]{:S(2)}) %collective-permute-start.13) | collective-permute-done | bytes 135200 | tf_op jit(solution)/shard_map/ppermute | solution.py:276
  58.6 2.3 %layer_two.1 = (f32[64,512]{1,0:T(8,128)}, f32[80,512]{1,0:T(8,128)S(1)}, s16[512,512]{1,0:T(8,128)(2,1)S(1)}, bf16[256,512]{1,0:T(8,128)(2,1)S(1)}, bf16[256,512]{1,0:T(8,128)(2,1)S(1)}, /*index=5*/f32[512,512]{1,0:T(8,128)}) custom-call(f32[512,512]{1,0:T(8,128)S(1)} %get-tuple-element.112.h1_ref, f32[64,512]{1,0:T(8,128)S(1)} %bitcast.5, ...), custom_call_target="tpu_custom_call" | custom-call | tf_op jit(solution)/shard_map/layer_two/pallas_call | solution.py:491
  61.5 1.2 %second_products.3 = (f32[256,512]{1,0:T(8,128)S(1)}, f32[256,512]{1,0:T(8,128)S(1)}) custom-call(bf16[512,512]{1,0:T(8,128)(2,1)S(1)} %get-tuple-element.111.ha, bf16[512,512]{1,0:T(8,128)(2,1)S(1)} %collective-permute-done.15.hb, bf16[256,512]{1,0:T(8,128)(2,1)S(1)} %get-tuple-element.114.refs_0_, bf16[256,512]{1,0:T(8,128)(2,1)S(1)} %get-tuple-element.115.refs_1_, ...), custom_call_target="tpu_custom_call" | custom-call | flops 1610612736 | bytes 1572864 | tf_op jit(solution)/shard_map/second_products/pallas_call | solution.py:236
  63.1 1.6 %collective-permute-start.21 = (s16[320,512]{1,0:T(8,128)(2,1)S(1)}, s16[320,512]{1,0:T(8,128)(2,1)S(1)}, u32[]{:S(2)}, u32[]{:S(2)}) collective-permute-start(s16[320,512]{1,0:T(8,128)(2,1)S(1)} %get-tuple-element.127.lo), channel_id=1, source_target_pairs={{0,2},{1,3},{2,0},{3,1},{4,6},{5,7},{6,4},{7,5},{8,10},{9,11},{10,... | collective-permute-start | bytes 983048 | tf_op jit(solution)/shard_map/ppermute | solution.py:276
  64.7 1.5 %collective-permute-start.20 = (s16[320,512]{1,0:T(8,128)(2,1)S(1)}, s16[320,512]{1,0:T(8,128)(2,1)S(1)}, u32[]{:S(2)}, u32[]{:S(2)}) collective-permute-start(s16[320,512]{1,0:T(8,128)(2,1)S(1)} %get-tuple-element.125.hi), channel_id=1, source_target_pairs={{0,4},{1,5},{2,6},{3,7},{4,0},{5,1},{6,2},{7,3},{8,12},{9,13},{10,... | collective-permute-start | bytes 983048 | tf_op jit(solution)/shard_map/ppermute | solution.py:276
  66.2 4.4 %second_products.4 = (s16[272,512]{1,0:T(8,128)(2,1)S(1)}, f32[256,512]{1,0:T(8,128)S(1)}, f32[256,512]{1,0:T(8,128)S(1)}, s16[272,512]{1,0:T(8,128)(2,1)S(1)}) custom-call(bf16[512,512]{1,0:T(8,128)(2,1)S(1)} %get-tuple-element.111.ha, bf16[512,512]{1,0:T(8,128)(2,1)S(1)} %collective-permute-done.15.hb, bf16[512,512]{1,0:T(8,128)(2,1)} %copy-done.3, ...), custom_call_target="tpu_custom_call" | custom-call | flops 3221225472 | bytes 3145728 | tf_op jit(solution)/shard_map/second_products/pallas_call | solution.py:236
  71.8 3.5 %collective-permute-done.20.x_in = s16[320,512]{1,0:T(8,128)(2,1)S(1)} collective-permute-done((s16[320,512]{1,0:T(8,128)(2,1)S(1)}, s16[320,512]{1,0:T(8,128)(2,1)S(1)}, u32[]{:S(2)}, u32[]{:S(2)}) %collective-permute-start.20) | collective-permute-done | bytes 327712 | tf_op jit(solution)/shard_map/ppermute | solution.py:276
  76.1 2.0 %collective-permute-start.26 = (s16[320,512]{1,0:T(8,128)(2,1)S(1)}, s16[320,512]{1,0:T(8,128)(2,1)S(1)}, u32[]{:S(2)}, u32[]{:S(2)}) collective-permute-start(s16[320,512]{1,0:T(8,128)(2,1)S(1)} %get-tuple-element.135), channel_id=1, source_target_pairs={{0,4},{1,5},{2,6},{3,7},{4,0},{5,1},{6,2},{7,3},{8,12},{9,13},{10,... | collective-permute-start | bytes 983048 | tf_op jit(solution)/shard_map/ppermute | solution.py:276
  78.2 2.1 %collective-permute-done.22.x_lo = s16[272,512]{1,0:T(8,128)(2,1)S(1)} collective-permute-done((s16[272,512]{1,0:T(8,128)(2,1)S(1)}, s16[272,512]{1,0:T(8,128)(2,1)S(1)}, u32[]{:S(2)}, u32[]{:S(2)}) %collective-permute-start.22) | collective-permute-done | bytes 278560 | tf_op jit(solution)/shard_map/ppermute | solution.py:276
  81.2 2.5 %second_products.5.own = f32[512,512]{1,0:T(8,128)S(1)} custom-call(bf16[512,512]{1,0:T(8,128)(2,1)S(1)} %get-tuple-element.111.ha, bf16[512,512]{1,0:T(8,128)(2,1)S(1)} %collective-permute-done.15.hb, bf16[512,512]{1,0:T(8,128)(2,1)} %w_ref.1, s16[512,512]{1,0:T(8,128)(2,1)} %get-tuple-element.76.refs_1_, s16[512,512]{1,0:T(8,128)(2,1)S(1)} %collective-permute-done.24.refs_2_), custom_call_target="tpu_custom_call" | custom-call | flops 1610612736 | bytes 1572864 | tf_op jit(solution)/shard_map/second_products/pallas_call | solution.py:236
  84.0 2.2 %collective-permute-done.25.x_hi = s16[320,512]{1,0:T(8,128)(2,1)S(1)} collective-permute-done((s16[320,512]{1,0:T(8,128)(2,1)S(1)}, s16[320,512]{1,0:T(8,128)(2,1)S(1)}, u32[]{:S(2)}, u32[]{:S(2)}) %collective-permute-start.25) | collective-permute-done | bytes 327712 | tf_op jit(solution)/shard_map/ppermute | solution.py:276
  86.2 1.2 %collective-permute-done.26.y_lo = s16[320,512]{1,0:T(8,128)(2,1)S(1)} collective-permute-done((s16[320,512]{1,0:T(8,128)(2,1)S(1)}, s16[320,512]{1,0:T(8,128)(2,1)S(1)}, u32[]{:S(2)}, u32[]{:S(2)}) %collective-permute-start.26) | collective-permute-done | bytes 327712 | tf_op jit(solution)/shard_map/ppermute | solution.py:276
  87.4 1.4 %last_update.1 = (bf16[512,512]{1,0:T(8,128)(2,1)}, f32[64,512]{1,0:T(8,128)}) custom-call(f32[512,512]{1,0:T(8,128)S(1)} %get-tuple-element.134.base, s16[320,512]{1,0:T(8,128)(2,1)S(1)} %collective-permute-done.25.x_hi, s16[320,512]{1,0:T(8,128)(2,1)S(1)} %collective-permute-done.26.y_lo, s16[48,512]{1,0:T(8,128)(2,1)S(1)} %get-tuple-element.136.x_sums, ...), custom_call_target="tpu_custom_call" | custom-call | tf_op jit(solution)/shard_map/last_update/pallas_call | solution.py:270
  (58 shorter events, 9.9 us)
Async XLA Ops:
  0.6 11.9 %collective-permute-start.2 = (bf16[512,512]{1,0:T(8,128)(2,1)}, bf16[512,512]{1,0:T(8,128)(2,1)S(1)}, u32[]{:S(2)}, u32[]{:S(2)}) collective-permute-start(bf16[512,512]{1,0:T(8,128)(2,1)} %w_ref.1), channel_id=1, source_target_pairs={{0,1},{1,0},{2,3},{3,2},{4,5},{5,4},{6,7},{7,6},{8,9},{9,8},{10,11... | collective-permute-start | bytes 1572872 | tf_op jit(solution)/shard_map/ppermute | solution.py:276
  1.1 15.3 %collective-permute-start = (bf16[512,512]{1,0:T(8,128)(2,1)}, bf16[512,512]{1,0:T(8,128)(2,1)S(1)}, u32[]{:S(2)}, u32[]{:S(2)}) collective-permute-start(bf16[512,512]{1,0:T(8,128)(2,1)} %w_ref.1), channel_id=1, source_target_pairs={{0,2},{1,3},{2,0},{3,1},{4,6},{5,7},{6,4},{7,5},{8,10},{9,11},{10,... | collective-permute-start | bytes 1572872 | tf_op jit(solution)/shard_map/ppermute | solution.py:276
  3.7 14.2 %collective-permute-start.1 = (bf16[512,512]{1,0:T(8,128)(2,1)}, bf16[512,512]{1,0:T(8,128)(2,1)S(1)}, u32[]{:S(2)}, u32[]{:S(2)}) collective-permute-start(bf16[512,512]{1,0:T(8,128)(2,1)} %w_ref.1), channel_id=1, source_target_pairs={{0,4},{1,5},{2,6},{3,7},{4,0},{5,1},{6,2},{7,3},{8,12},{9,13},{10,... | collective-permute-start | bytes 1572872 | tf_op jit(solution)/shard_map/ppermute | solution.py:276
  17.9 2.7 %collective-permute-start.5 = (bf16[512,512]{1,0:T(8,128)(2,1)S(1)}, bf16[512,512]{1,0:T(8,128)(2,1)S(1)}, u32[]{:S(2)}, u32[]{:S(2)}) collective-permute-start(bf16[512,512]{1,0:T(8,128)(2,1)S(1)} %collective-permute-done.b_ref.refs_0_), channel_id=1, source_target_pairs={{0,1},{1,0},{2,3},{3,2},{4,5},{5,4},{6,7},{7,6},{8,9},{9,8},{10,11... | collective-permute-start | bytes 1572872 | tf_op jit(solution)/shard_map/ppermute | solution.py:276
  17.9 2.7 %collective-permute-start.6 = (bf16[512,512]{1,0:T(8,128)(2,1)S(1)}, bf16[512,512]{1,0:T(8,128)(2,1)S(1)}, u32[]{:S(2)}, u32[]{:S(2)}) collective-permute-start(bf16[512,512]{1,0:T(8,128)(2,1)S(1)} %collective-permute-done.1.a_ref.refs_2_.refs_3_), channel_id=1, source_target_pairs={{0,1},{1,0},{2,3},{3,2},{4,5},{5,4},{6,7},{7,6},{8,9},{9,8},{10,11... | collective-permute-start | bytes 1572872 | tf_op jit(solution)/shard_map/ppermute | solution.py:276
  18.5 8.4 %collective-permute-start.3 = (bf16[256,512]{1,0:T(8,128)(2,1)S(1)}, bf16[256,512]{1,0:T(8,128)(2,1)}, u32[]{:S(2)}, u32[]{:S(2)}) collective-permute-start(bf16[256,512]{1,0:T(8,128)(2,1)S(1)} %get-tuple-element.82), channel_id=1, source_target_pairs={{0,2},{1,3},{2,0},{3,1},{4,6},{5,7},{6,4},{7,5},{8,10},{9,11},{10,... | collective-permute-start | bytes 786440 | tf_op jit(solution)/shard_map/ppermute | solution.py:276
  18.9 8.1 %collective-permute-start.4 = (bf16[256,512]{1,0:T(8,128)(2,1)S(1)}, bf16[256,512]{1,0:T(8,128)(2,1)}, u32[]{:S(2)}, u32[]{:S(2)}) collective-permute-start(bf16[256,512]{1,0:T(8,128)(2,1)S(1)} %get-tuple-element.83), channel_id=1, source_target_pairs={{0,4},{1,5},{2,6},{3,7},{4,0},{5,1},{6,2},{7,3},{8,12},{9,13},{10,... | collective-permute-start | bytes 786440 | tf_op jit(solution)/shard_map/ppermute | solution.py:276
  24.9 32.6 %copy-start = (f32[512,512]{1,0:T(8,128)S(1)}, f32[512,512]{1,0:T(8,128)}, u32[]{:S(2)}) copy-start(f32[512,512]{1,0:T(8,128)} %refs_4_.1) | copy-start | bytes 3145732
  24.9 33.7 %copy-start.2 = (f32[512,64]{0,1:T(8,128)S(1)}, f32[512,64]{0,1:T(8,128)}, u32[]{:S(2)}) copy-start(f32[512,64]{0,1:T(8,128)} %param.8) | copy-start | bytes 393220
  24.9 33.7 %copy-start.5 = (f32[64,512]{1,0:T(8,128)S(1)}, f32[64,512]{1,0:T(8,128)}, u32[]{:S(2)}) copy-start(f32[64,512]{1,0:T(8,128)} %h2_ref.1) | copy-start | bytes 393220
  27.0 2.0 %collective-permute-start.7 = (bf16[256,512]{1,0:T(8,128)(2,1)}, bf16[256,512]{1,0:T(8,128)(2,1)}, u32[]{:S(2)}, u32[]{:S(2)}) collective-permute-start(bf16[256,512]{1,0:T(8,128)(2,1)} %collective-permute-done.3.refs_2_.refs_1_), channel_id=1, source_target_pairs={{0,1},{1,0},{2,3},{3,2},{4,5},{5,4},{6,7},{7,6},{8,9},{9,8},{10,11... | collective-permute-start | bytes 786440 | tf_op jit(solution)/shard_map/ppermute | solution.py:276
  27.0 2.2 %collective-permute-start.8 = (bf16[256,512]{1,0:T(8,128)(2,1)}, bf16[256,512]{1,0:T(8,128)(2,1)}, u32[]{:S(2)}, u32[]{:S(2)}) collective-permute-start(bf16[256,512]{1,0:T(8,128)(2,1)} %collective-permute-done.4.refs_3_.refs_2_), channel_id=1, source_target_pairs={{0,1},{1,0},{2,3},{3,2},{4,5},{5,4},{6,7},{7,6},{8,9},{9,8},{10,11... | collective-permute-start | bytes 786440 | tf_op jit(solution)/shard_map/ppermute | solution.py:276
  27.5 33.8 %copy-start.6 = (s16[512,512]{1,0:T(8,128)(2,1)S(1)}, s16[512,512]{1,0:T(8,128)(2,1)}, u32[]{:S(2)}) copy-start(s16[512,512]{1,0:T(8,128)(2,1)} %get-tuple-element.77.refs_3_) | copy-start | bytes 1572868
  31.9 6.5 %collective-permute-start.11 = (s16[528,128]{1,0:T(8,128)(2,1)S(1)}, s16[528,128]{1,0:T(8,128)(2,1)S(1)}, u32[]{:S(2)}, u32[]{:S(2)}) collective-permute-start(s16[528,128]{1,0:T(8,128)(2,1)S(1)} %get-tuple-element.109), channel_id=1, source_target_pairs={{0,8},{8,0},{16,24},{24,16},{1,9},{9,1},{17,25},{25,17},{2,10},{10... | collective-permute-start | bytes 405512 | tf_op jit(solution)/shard_map/ppermute | solution.py:276
  33.6 8.7 %collective-permute-start.9 = (s16[528,128]{1,0:T(8,128)(2,1)S(1)}, s16[528,128]{1,0:T(8,128)(2,1)S(1)}, u32[]{:S(2)}, u32[]{:S(2)}) collective-permute-start(s16[528,128]{1,0:T(8,128)(2,1)S(1)} %get-tuple-element.107.refs_0_), channel_id=1, source_target_pairs={{0,8},{8,0},{16,24},{24,16},{1,9},{9,1},{17,25},{25,17},{2,10},{10... | collective-permute-start | bytes 405512 | tf_op jit(solution)/shard_map/ppermute | solution.py:276
  38.5 7.5 %collective-permute-start.12 = (s16[528,128]{1,0:T(8,128)(2,1)S(1)}, s16[528,128]{1,0:T(8,128)(2,1)S(1)}, u32[]{:S(2)}, u32[]{:S(2)}) collective-permute-start(s16[528,128]{1,0:T(8,128)(2,1)S(1)} %add_pair.3.one), channel_id=1, source_target_pairs={{0,24},{8,16},{16,8},{24,0},{1,25},{9,17},{17,9},{25,1},{2,26},{10... | collective-permute-start | bytes 405512 | tf_op jit(solution)/shard_map/ppermute | solution.py:276
  42.4 9.4 %collective-permute-start.10 = (s16[528,128]{1,0:T(8,128)(2,1)S(1)}, s16[528,128]{1,0:T(8,128)(2,1)S(1)}, u32[]{:S(2)}, u32[]{:S(2)}) collective-permute-start(s16[528,128]{1,0:T(8,128)(2,1)S(1)} %add_pair.2.one), channel_id=1, source_target_pairs={{0,24},{8,16},{16,8},{24,0},{1,25},{9,17},{17,9},{25,1},{2,26},{10... | collective-permute-start | bytes 405512 | tf_op jit(solution)/shard_map/ppermute | solution.py:276
  46.2 9.9 %collective-permute-start.14 = (s16[528,128]{1,0:T(8,128)(2,1)S(1)}, s16[528,128]{1,0:T(8,128)(2,1)S(1)}, u32[]{:S(2)}, u32[]{:S(2)}) collective-permute-start(s16[528,128]{1,0:T(8,128)(2,1)S(1)} %add_cross.3.refs_1_), channel_id=1, source_target_pairs={{0,8},{8,0},{16,24},{24,16},{1,9},{9,1},{17,25},{25,17},{2,10},{10... | collective-permute-start | bytes 405512 | tf_op jit(solution)/shard_map/ppermute | solution.py:276
  52.1 5.4 %collective-permute-start.13 = (s16[528,128]{1,0:T(8,128)(2,1)S(1)}, s16[528,128]{1,0:T(8,128)(2,1)S(1)}, u32[]{:S(2)}, u32[]{:S(2)}) collective-permute-start(s16[528,128]{1,0:T(8,128)(2,1)S(1)} %get-tuple-element.108.refs_0_), channel_id=1, source_target_pairs={{0,8},{8,0},{16,24},{24,16},{1,9},{9,1},{17,25},{25,17},{2,10},{10... | collective-permute-start | bytes 405512 | tf_op jit(solution)/shard_map/ppermute | solution.py:276
  53.5 7.9 %collective-permute-start.17 = (s16[512,512]{1,0:T(8,128)(2,1)}, s16[512,512]{1,0:T(8,128)(2,1)S(1)}, u32[]{:S(2)}, u32[]{:S(2)}) collective-permute-start(s16[512,512]{1,0:T(8,128)(2,1)} %get-tuple-element.97.refs_1_), channel_id=1, source_target_pairs={{0,1},{1,0},{2,3},{3,2},{4,5},{5,4},{6,7},{7,6},{8,9},{9,8},{10,11... | collective-permute-start | bytes 1572872 | tf_op jit(solution)/shard_map/ppermute | solution.py:276
  57.9 3.5 %collective-permute-start.15 = (bf16[512,512]{1,0:T(8,128)(2,1)S(1)}, bf16[512,512]{1,0:T(8,128)(2,1)S(1)}, u32[]{:S(2)}, u32[]{:S(2)}) collective-permute-start(bf16[512,512]{1,0:T(8,128)(2,1)S(1)} %get-tuple-element.111.ha), channel_id=1, source_target_pairs={{0,1},{1,0},{2,3},{3,2},{4,5},{5,4},{6,7},{7,6},{8,9},{9,8},{10,11... | collective-permute-start | bytes 1572872 | tf_op jit(solution)/shard_map/ppermute | solution.py:276
  58.0 8.2 %collective-permute-start.18 = (s16[512,512]{1,0:T(8,128)(2,1)}, s16[512,512]{1,0:T(8,128)(2,1)S(1)}, u32[]{:S(2)}, u32[]{:S(2)}) collective-permute-start(s16[512,512]{1,0:T(8,128)(2,1)} %get-tuple-element.86.refs_5_), channel_id=1, source_target_pairs={{0,1},{1,0},{2,3},{3,2},{4,5},{5,4},{6,7},{7,6},{8,9},{9,8},{10,11... | collective-permute-start | bytes 1572872 | tf_op jit(solution)/shard_map/ppermute | solution.py:276
  58.5 7.7 %collective-permute-start.19 = (s16[512,512]{1,0:T(8,128)(2,1)}, s16[512,512]{1,0:T(8,128)(2,1)S(1)}, u32[]{:S(2)}, u32[]{:S(2)}) collective-permute-start(s16[512,512]{1,0:T(8,128)(2,1)} %get-tuple-element.87.refs_7_), channel_id=1, source_target_pairs={{0,1},{1,0},{2,3},{3,2},{4,5},{5,4},{6,7},{7,6},{8,9},{9,8},{10,11... | collective-permute-start | bytes 1572872 | tf_op jit(solution)/shard_map/ppermute | solution.py:276
  60.9 1.9 %collective-permute-start.16 = (f32[80,512]{1,0:T(8,128)S(1)}, f32[80,512]{1,0:T(8,128)S(1)}, u32[]{:S(2)}, u32[]{:S(2)}) collective-permute-start(f32[80,512]{1,0:T(8,128)S(1)} %get-tuple-element.120.sums), channel_id=1, source_target_pairs={{0,1},{1,0},{2,3},{3,2},{4,5},{5,4},{6,7},{7,6},{8,9},{9,8},{10,11... | collective-permute-start | bytes 491528 | tf_op jit(solution)/shard_map/ppermute | solution.py:276
  61.4 19.9 %collective-permute-start.24 = (s16[512,512]{1,0:T(8,128)(2,1)S(1)}, s16[512,512]{1,0:T(8,128)(2,1)S(1)}, u32[]{:S(2)}, u32[]{:S(2)}) collective-permute-start(s16[512,512]{1,0:T(8,128)(2,1)S(1)} %copy-done.6), channel_id=1, source_target_pairs={{0,1},{1,0},{2,3},{3,2},{4,5},{5,4},{6,7},{7,6},{8,9},{9,8},{10,11... | collective-permute-start | bytes 1572872 | tf_op jit(solution)/shard_map/ppermute | solution.py:276
  63.1 12.1 %collective-permute-start.21 = (s16[320,512]{1,0:T(8,128)(2,1)S(1)}, s16[320,512]{1,0:T(8,128)(2,1)S(1)}, u32[]{:S(2)}, u32[]{:S(2)}) collective-permute-start(s16[320,512]{1,0:T(8,128)(2,1)S(1)} %get-tuple-element.127.lo), channel_id=1, source_target_pairs={{0,2},{1,3},{2,0},{3,1},{4,6},{5,7},{6,4},{7,5},{8,10},{9,11},{10,... | collective-permute-start | bytes 983048 | tf_op jit(solution)/shard_map/ppermute | solution.py:276
  64.7 19.1 %copy-start.1 = (bf16[512,512]{1,0:T(8,128)(2,1)S(1)}, bf16[512,512]{1,0:T(8,128)(2,1)}, u32[]{:S(2)}) copy-start(bf16[512,512]{1,0:T(8,128)(2,1)} %w_ref.1) | copy-start | bytes 1572868
  64.7 10.6 %collective-permute-start.20 = (s16[320,512]{1,0:T(8,128)(2,1)S(1)}, s16[320,512]{1,0:T(8,128)(2,1)S(1)}, u32[]{:S(2)}, u32[]{:S(2)}) collective-permute-start(s16[320,512]{1,0:T(8,128)(2,1)S(1)} %get-tuple-element.125.hi), channel_id=1, source_target_pairs={{0,4},{1,5},{2,6},{3,7},{4,0},{5,1},{6,2},{7,3},{8,12},{9,13},{10,... | collective-permute-start | bytes 983048 | tf_op jit(solution)/shard_map/ppermute | solution.py:276
  70.7 9.6 %collective-permute-start.22 = (s16[272,512]{1,0:T(8,128)(2,1)S(1)}, s16[272,512]{1,0:T(8,128)(2,1)S(1)}, u32[]{:S(2)}, u32[]{:S(2)}) collective-permute-start(s16[272,512]{1,0:T(8,128)(2,1)S(1)} %get-tuple-element.129), channel_id=1, source_target_pairs={{0,2},{1,3},{2,0},{3,1},{4,6},{5,7},{6,4},{7,5},{8,10},{9,11},{10,... | collective-permute-start | bytes 835592 | tf_op jit(solution)/shard_map/ppermute | solution.py:276
  71.3 9.9 %collective-permute-start.23 = (s16[272,512]{1,0:T(8,128)(2,1)S(1)}, s16[272,512]{1,0:T(8,128)(2,1)S(1)}, u32[]{:S(2)}, u32[]{:S(2)}) collective-permute-start(s16[272,512]{1,0:T(8,128)(2,1)S(1)} %get-tuple-element.130), channel_id=1, source_target_pairs={{0,4},{1,5},{2,6},{3,7},{4,0},{5,1},{6,2},{7,3},{8,12},{9,13},{10,... | collective-permute-start | bytes 835592 | tf_op jit(solution)/shard_map/ppermute | solution.py:276
  76.0 10.2 %collective-permute-start.25 = (s16[320,512]{1,0:T(8,128)(2,1)S(1)}, s16[320,512]{1,0:T(8,128)(2,1)S(1)}, u32[]{:S(2)}, u32[]{:S(2)}) collective-permute-start(s16[320,512]{1,0:T(8,128)(2,1)S(1)} %get-tuple-element.128), channel_id=1, source_target_pairs={{0,2},{1,3},{2,0},{3,1},{4,6},{5,7},{6,4},{7,5},{8,10},{9,11},{10,... | collective-permute-start | bytes 983048 | tf_op jit(solution)/shard_map/ppermute | solution.py:276
  76.1 11.3 %collective-permute-start.26 = (s16[320,512]{1,0:T(8,128)(2,1)S(1)}, s16[320,512]{1,0:T(8,128)(2,1)S(1)}, u32[]{:S(2)}, u32[]{:S(2)}) collective-permute-start(s16[320,512]{1,0:T(8,128)(2,1)S(1)} %get-tuple-element.135), channel_id=1, source_target_pairs={{0,4},{1,5},{2,6},{3,7},{4,0},{5,1},{6,2},{7,3},{8,12},{9,13},{10,... | collective-permute-start | bytes 983048 | tf_op jit(solution)/shard_map/ppermute | solution.py:276
  (2 other events, 11.1 us)

commit v8 on v7

--- a/solution.py
+++ b/solution.py
@@ -287,6 +287,37 @@
         encode(jnp.where(inner, lo, hi), send, None if i else col[:1, :])
 
 
+def first_and_split(groups, h, acc, flag, outs):
+    sizes = tuple(len(g) - 1 for g in groups)
+    flat = [x for g in groups for x in g]
+    later = tuple(i for i, x in enumerate(flat) if isinstance(x, Later))
+    n, n_outs, n_later = len(flat), len(outs), len(later)
+    flat = [pltpu.with_memory_space_constraint(x.array, pltpu.HBM) if isinstance(x, Later) else x for x in flat]
+    vmem, hbm = pl.BlockSpec(memory_space=pltpu.VMEM), pl.BlockSpec(memory_space=pltpu.HBM)
+
+    def body(flag_ref, h_ref, *refs):
+        inputs, out_refs, scratch = refs[: n + 2], refs[n + 2 : n + 2 + n_outs], refs[n + 2 + n_outs :]
+        num, col = scratch[-2:]
+        first_body(sizes, later, 0, True, h_ref, *inputs, num, col, *scratch[:-2])
+        split_num(flag_ref, num, col, *out_refs)
+
+    scratch = [pltpu.VMEM(flat[i].shape, flat[i].dtype) for i in later]
+    if later:
+        scratch.append(pltpu.SemaphoreType.DMA((n_later,)))
+    return pl.pallas_call(
+        body,
+        out_shape=outs,
+        in_specs=[pl.BlockSpec(memory_space=pltpu.SMEM), vmem] + [hbm if i in later else vmem for i in range(n)] + [vmem] * 2,
+        out_specs=[vmem] * n_outs,
+        scratch_shapes=scratch + [pltpu.VMEM(x.shape, x.dtype) for x in acc],
+        compiler_params=params(),
+        cost_estimate=pl.CostEstimate(
+            flops=8 * flat[0].shape[0] * h.shape[0] * h.shape[1], bytes_accessed=4 * h.size, transcendentals=0
+        ),
+        name="first_and_split",
+    )(flag, h, *flat, *acc)
+
+
 def add_kept(i, keep, other, *refs):
     width, k1 = other.shape[1], keep.shape[0]
     extra = None if i else decode_extra(refs[0], k1) + decode_extra(other, k1)
@@ -434,23 +465,21 @@
         half = jax.ShapeDtypeStruct((t, k1), BF16)
         y_lo, x_hi = plain(cut_halves, (half, half), w_y, w_x, name="cut_halves")
         d_lo, d_hi = cell(y_lo, bit=2), cell(x_hi, bit=4)
+        w_x, w_y, x_hi, y_lo = after((w_x, w_y, x_hi, y_lo))
         x_0, y_0 = cell(w_x, bit=1), cell(w_y, bit=1)
         near = ((w_x, on_mine[1]), (w_y, on_mine[2]), (x_0, on_theirs[1]), (y_0, on_theirs[2]))
         acc = first(near, h1_low, acc)
         d_lo, d_hi, *acc = after((d_lo, d_hi, *acc))
-        far = [Later(cell(d, bit=1)) for d in (d_lo, d_hi)]
+        far = [cell(d, bit=1) for d in (d_lo, d_hi)]
         *v_far, own_lo, own_hi = plain_fetch(after((v_mine[3], v_theirs[3], d_lo, d_hi, *acc))[:4])
-        num, col = first(((own_lo, own_hi, v_far[0]), (*far, v_far[1])), h1_low, acc)
-
         z = lax.axis_index("gene")
         inner = jnp.where((z == 1) | (z == 2), 1, 0).astype(jnp.int32)[None]
         chunks = tuple(range(CHUNKS))
         piece = coded(k1, cells // 2 // CHUNKS)
-        keep, *sent = plain(
-            split_num, (jax.ShapeDtypeStruct((k1, cells // 2), F32),) + (piece,) * CHUNKS,
-            num, col, flag=inner, name="split_num",
-        )
-
+        keep, *sent = first_and_split(
+            ((own_lo, own_hi, v_far[0]), (*far, v_far[1])), h1_low, acc, inner,
+            (jax.ShapeDtypeStruct((k1, cells // 2), F32),) + (piece,) * CHUNKS,
+        )
         pair = []
         for i, x in enumerate(sent):
             got = gene(x, bit=1)

time: 89.2 us -> 88.2 us (0.989)
  waiting for transfers between devices: 24.7 us -> 21.8 us
  local copies, waits for them, and re-layouts: 0.03 us -> 2.9 us
  Pallas kernels: 31.6 us -> 30.6 us
    ppermute x27, waiting for transfers between devices: 24.7 us -> 21.8 us  [flip(): return lax.ppermute(x, axis, [(i, i ^ bit) for i in range(size)])]
    unnamed x14 -> x24, local copies, waits for them, and re-layouts: 0.03 us -> 2.9 us
    pallas_call x6 -> x5, Pallas kernels: 17.8 us -> 15.4 us  [products(): pl.pallas_call(functools.partial(body, sizes, later, len(fetch), flag), o...]
    pallas_call x0 -> x1, Pallas kernels: none -> 1.6 us  [first_and_split(): pl.pallas_call(body, out_shape=outs, in_specs=[pl.BlockSpec(memory_space=...]
    pallas_call x11 -> x10, Pallas kernels: 4.22 us -> 3.95 us  [plain(): pl.pallas_call(body, out_shape=outs, in_specs=specs, out_specs=out_specs,...]
where the time goes in v8:
time: 88.2 us; the launch traced here: 87.8 us
  Pallas kernels  30.6 us (35%)
  starting transfers between devices  30.2 us (34%)
  waiting for transfers between devices  21.8 us (25%)
  local copies, waits for them, and re-layouts  2.9 us (3%)
  other arithmetic  1.37 us (2%)
  between operations  0.92 us (1%)
    ppermute x27, starting transfers between devices, flip(): return lax.ppermute(x, axis, [(i, i ^ bit) for i in range(size)])  30.2 us
    ppermute x27, waiting for transfers between devices, flip(): return lax.ppermute(x, axis, [(i, i ^ bit) for i in range(size)])  21.8 us
    pallas_call x5, Pallas kernels, products(): pl.pallas_call(functools.partial(body, sizes, later, len(fetch), flag), o...  15.4 us
    pallas_call x1, Pallas kernels, split_counts(): pl.pallas_call(functools.partial(counts_body, chips, rows), out_shape=(ou...  5.88 us
    pallas_call x10, Pallas kernels, plain(): pl.pallas_call(body, out_shape=outs, in_specs=specs, out_specs=out_specs,...  3.95 us
    unnamed x24, local copies, waits for them, and re-layouts  2.9 us
    pallas_call x1, Pallas kernels, on_device(): pl.pallas_call(functools.partial(layer_two, len(soon)), out_shape=(jax.Sh...  2.27 us
  transfers between devices with their start and end apart: 27, of which 14 were waited for; matrix products, arithmetic and copies ran while one was open for 2% of the time, Pallas kernels for 31%

profile of v8, /device:TPU:0, one launch (start us, length us, event | category | flops | bytes accessed | tf_op | source)
XLA Modules:
  0.0 87.8 jit_solution(16138223606684958843)
XLA Ops:
  1.1 2.6 %collective-permute-start = (bf16[512,512]{1,0:T(8,128)(2,1)}, bf16[512,512]{1,0:T(8,128)(2,1)S(1)}, u32[]{:S(2)}, u32[]{:S(2)}) collective-permute-start(bf16[512,512]{1,0:T(8,128)(2,1)} %w_ref.1), channel_id=1, source_target_pairs={{0,2},{1,3},{2,0},{3,1},{4,6},{5,7},{6,4},{7,5},{8,10},{9,11},{10,... | collective-permute-start | bytes 1572872 | tf_op jit(solution)/shard_map/ppermute | solution.py:276
  3.7 1.5 %collective-permute-start.1 = (bf16[512,512]{1,0:T(8,128)(2,1)}, bf16[512,512]{1,0:T(8,128)(2,1)S(1)}, u32[]{:S(2)}, u32[]{:S(2)}) collective-permute-start(bf16[512,512]{1,0:T(8,128)(2,1)} %w_ref.1), channel_id=1, source_target_pairs={{0,4},{1,5},{2,6},{3,7},{4,0},{5,1},{6,2},{7,3},{8,12},{9,13},{10,... | collective-permute-start | bytes 1572872 | tf_op jit(solution)/shard_map/ppermute | solution.py:276
  5.2 1.3 %convert_element_type.3.h.h_ref = bf16[512,512]{1,0:T(8,128)(2,1)S(1)} convert(f32[512,512]{1,0:T(8,128)} %refs_4_.1) | non-fusion elementwise | flops 262144 | bytes 1572864 | tf_op jit(solution)/shard_map/convert_element_type | solution.py:453
  6.6 5.9 %split_counts.1 = (s16[512,512]{1,0:T(8,128)(2,1)}, s16[512,512]{1,0:T(8,128)(2,1)}, s16[512,512]{1,0:T(8,128)(2,1)}, s16[512,512]{1,0:T(8,128)(2,1)}, s16[512,5...) custom-call(s32[2]{0:T(128)S(1)} %pad_add_fusion.at, s32[4096,512]{1,0:T(8,128)} %v.1), custom_call_target="tpu_custom_call" | custom-call | tf_op jit(solution)/shard_map/split_counts/pallas_call | solution.py:104
  13.3 1.0 %copy-done.8 = bf16[512,512]{1,0:T(8,128)(2,1)S(1)} copy-done((bf16[512,512]{1,0:T(8,128)(2,1)S(1)}, bf16[512,512]{1,0:T(8,128)(2,1)}, u32[]{:S(2)}) %copy-start.8) | copy-done | bytes 524312
  14.3 3.0 %first_products.2 = (f32[512,512]{1,0:T(8,128)S(1)}, f32[8,512]{1,0:T(8,128)S(1)}) custom-call(bf16[512,512]{1,0:T(8,128)(2,1)S(1)} %convert_element_type.3.h.h_ref, bf16[512,512]{1,0:T(8,128)(2,1)} %w_ref.1, s16[512,512]{1,0:T(8,128)(2,1)} %get-tuple-element.76.refs_1_, bf16[512,512]{1,0:T(8,128)(2,1)S(1)} %copy-done.8, ...), custom_call_target="tpu_custom_call" | custom-call | flops 2147483648 | bytes 2097152 | tf_op jit(solution)/shard_map/first_products/pallas_call | solution.py:236
  18.9 1.7 %collective-permute-start.4 = (bf16[256,512]{1,0:T(8,128)(2,1)S(1)}, bf16[256,512]{1,0:T(8,128)(2,1)}, u32[]{:S(2)}, u32[]{:S(2)}) collective-permute-start(bf16[256,512]{1,0:T(8,128)(2,1)S(1)} %get-tuple-element.83), channel_id=1, source_target_pairs={{0,4},{1,5},{2,6},{3,7},{4,0},{5,1},{6,2},{7,3},{8,12},{9,13},{10,... | collective-permute-start | bytes 786440 | tf_op jit(solution)/shard_map/ppermute | solution.py:276
  20.7 1.0 %copy-done.5 = bf16[512,512]{1,0:T(8,128)(2,1)S(1)} copy-done((bf16[512,512]{1,0:T(8,128)(2,1)S(1)}, bf16[512,512]{1,0:T(8,128)(2,1)}, u32[]{:S(2)}) %copy-start.5) | copy-done | bytes 524312
  21.7 4.3 %first_products.3 = (f32[512,512]{1,0:T(8,128)S(1)}, f32[8,512]{1,0:T(8,128)S(1)}) custom-call(bf16[512,512]{1,0:T(8,128)(2,1)S(1)} %convert_element_type.3.h.h_ref, bf16[512,512]{1,0:T(8,128)(2,1)S(1)} %collective-permute-done.b_ref.refs_0_, s16[512,512]{1,0:T(8,128)(2,1)} %get-tuple-element.85.refs_1_, ...), custom_call_target="tpu_custom_call", output_to_operand_aliasing={{0}: (9, {}), {1}: (10, {})} | custom-call | flops 4294967296 | bytes 4194304 | tf_op jit(solution)/shard_map/first_products/pallas_call | solution.py:236
  27.5 1.5 %fetch.1 = (s16[512,512]{1,0:T(8,128)(2,1)S(1)}, s16[512,512]{1,0:T(8,128)(2,1)S(1)}, bf16[256,512]{1,0:T(8,128)(2,1)S(1)}, bf16[256,512]{1,0:T(8,128)(2,1)S(1)}) custom-call(s16[512,512]{1,0:T(8,128)(2,1)} %get-tuple-element.98.refs_0_, s16[512,512]{1,0:T(8,128)(2,1)} %get-tuple-element.99.refs_1_, bf16[256,512]{1,0:T(8,128)(2,1)} %collective-permute-done.3.refs_2_.refs_1_, ...), custom_call_target="tpu_custom_call" | custom-call | tf_op jit(solution)/shard_map/fetch/pallas_call | solution.py:164
  29.1 1.6 %first_and_split.1 = (f32[512,256]{1,0:T(8,128)S(1)}, s16[528,128]{1,0:T(8,128)(2,1)S(1)}, s16[528,128]{1,0:T(8,128)(2,1)S(1)}) custom-call(s32[1]{0:T(128)} %bitcast.flag_ref.flag, bf16[512,512]{1,0:T(8,128)(2,1)S(1)} %convert_element_type.3.h.h_ref, bf16[256,512]{1,0:T(8,128)(2,1)S(1)} %get-tuple-element.102.refs_0_, ...), custom_call_target="tpu_custom_call" | custom-call | flops 536870912 | bytes 1048576 | tf_op jit(solution)/shard_map/first_and_split/pallas_call | solution.py:307
  30.7 1.8 %collective-permute-start.11 = (s16[528,128]{1,0:T(8,128)(2,1)S(1)}, s16[528,128]{1,0:T(8,128)(2,1)S(1)}, u32[]{:S(2)}, u32[]{:S(2)}) collective-permute-start(s16[528,128]{1,0:T(8,128)(2,1)S(1)} %get-tuple-element.109), channel_id=1, source_target_pairs={{0,8},{8,0},{16,24},{24,16},{1,9},{9,1},{17,25},{25,17},{2,10},{10... | collective-permute-start | bytes 405512 | tf_op jit(solution)/shard_map/ppermute | solution.py:276
  32.8 4.4 %collective-permute-done.11.other = s16[528,128]{1,0:T(8,128)(2,1)S(1)} collective-permute-done((s16[528,128]{1,0:T(8,128)(2,1)S(1)}, s16[528,128]{1,0:T(8,128)(2,1)S(1)}, u32[]{:S(2)}, u32[]{:S(2)}) %collective-permute-start.11) | collective-permute-done | bytes 135200 | tf_op jit(solution)/shard_map/ppermute | solution.py:276
  37.4 3.9 %collective-permute-start.12 = (s16[528,128]{1,0:T(8,128)(2,1)S(1)}, s16[528,128]{1,0:T(8,128)(2,1)S(1)}, u32[]{:S(2)}, u32[]{:S(2)}) collective-permute-start(s16[528,128]{1,0:T(8,128)(2,1)S(1)} %add_pair.3.one), channel_id=1, source_target_pairs={{0,24},{8,16},{16,8},{24,0},{1,25},{9,17},{17,9},{25,1},{2,26},{10... | collective-permute-start | bytes 405512 | tf_op jit(solution)/shard_map/ppermute | solution.py:276
  41.4 1.9 %collective-permute-start.10 = (s16[528,128]{1,0:T(8,128)(2,1)S(1)}, s16[528,128]{1,0:T(8,128)(2,1)S(1)}, u32[]{:S(2)}, u32[]{:S(2)}) collective-permute-start(s16[528,128]{1,0:T(8,128)(2,1)S(1)} %add_pair.2.one), channel_id=1, source_target_pairs={{0,24},{8,16},{16,8},{24,0},{1,25},{9,17},{17,9},{25,1},{2,26},{10... | collective-permute-start | bytes 405512 | tf_op jit(solution)/shard_map/ppermute | solution.py:276
  43.3 1.6 %collective-permute-done.12.other = s16[528,128]{1,0:T(8,128)(2,1)S(1)} collective-permute-done((s16[528,128]{1,0:T(8,128)(2,1)S(1)}, s16[528,128]{1,0:T(8,128)(2,1)S(1)}, u32[]{:S(2)}, u32[]{:S(2)}) %collective-permute-start.12) | collective-permute-done | bytes 135200 | tf_op jit(solution)/shard_map/ppermute | solution.py:276
  45.1 5.7 %collective-permute-start.14 = (s16[528,128]{1,0:T(8,128)(2,1)S(1)}, s16[528,128]{1,0:T(8,128)(2,1)S(1)}, u32[]{:S(2)}, u32[]{:S(2)}) collective-permute-start(s16[528,128]{1,0:T(8,128)(2,1)S(1)} %add_cross.3.refs_1_), channel_id=1, source_target_pairs={{0,8},{8,0},{16,24},{24,16},{1,9},{9,1},{17,25},{25,17},{2,10},{10... | collective-permute-start | bytes 405512 | tf_op jit(solution)/shard_map/ppermute | solution.py:276
  51.0 1.4 %collective-permute-start.13 = (s16[528,128]{1,0:T(8,128)(2,1)S(1)}, s16[528,128]{1,0:T(8,128)(2,1)S(1)}, u32[]{:S(2)}, u32[]{:S(2)}) collective-permute-start(s16[528,128]{1,0:T(8,128)(2,1)S(1)} %get-tuple-element.108.refs_0_), channel_id=1, source_target_pairs={{0,8},{8,0},{16,24},{24,16},{1,9},{9,1},{17,25},{25,17},{2,10},{10... | collective-permute-start | bytes 405512 | tf_op jit(solution)/shard_map/ppermute | solution.py:276
  52.4 2.6 %collective-permute-done.14.refs_3_ = s16[528,128]{1,0:T(8,128)(2,1)S(1)} collective-permute-done((s16[528,128]{1,0:T(8,128)(2,1)S(1)}, s16[528,128]{1,0:T(8,128)(2,1)S(1)}, u32[]{:S(2)}, u32[]{:S(2)}) %collective-permute-start.14) | collective-permute-done | bytes 135200 | tf_op jit(solution)/shard_map/ppermute | solution.py:276
  55.0 1.4 %collective-permute-done.13.refs_2_ = s16[528,128]{1,0:T(8,128)(2,1)S(1)} collective-permute-done((s16[528,128]{1,0:T(8,128)(2,1)S(1)}, s16[528,128]{1,0:T(8,128)(2,1)S(1)}, u32[]{:S(2)}, u32[]{:S(2)}) %collective-permute-start.13) | collective-permute-done | bytes 135200 | tf_op jit(solution)/shard_map/ppermute | solution.py:276
  57.5 2.3 %layer_two.1 = (f32[64,512]{1,0:T(8,128)}, f32[80,512]{1,0:T(8,128)S(1)}, s16[512,512]{1,0:T(8,128)(2,1)S(1)}, bf16[256,512]{1,0:T(8,128)(2,1)S(1)}, bf16[256,512]{1,0:T(8,128)(2,1)S(1)}, /*index=5*/f32[512,512]{1,0:T(8,128)}) custom-call(f32[512,512]{1,0:T(8,128)S(1)} %get-tuple-element.112.h1_ref, f32[64,512]{1,0:T(8,128)S(1)} %bitcast.5, ...), custom_call_target="tpu_custom_call" | custom-call | tf_op jit(solution)/shard_map/layer_two/pallas_call | solution.py:520
  60.4 1.2 %second_products.3 = (f32[256,512]{1,0:T(8,128)S(1)}, f32[256,512]{1,0:T(8,128)S(1)}) custom-call(bf16[512,512]{1,0:T(8,128)(2,1)S(1)} %get-tuple-element.111.ha, bf16[512,512]{1,0:T(8,128)(2,1)S(1)} %collective-permute-done.15.hb, bf16[256,512]{1,0:T(8,128)(2,1)S(1)} %get-tuple-element.114.refs_0_, bf16[256,512]{1,0:T(8,128)(2,1)S(1)} %get-tuple-element.115.refs_1_, ...), custom_call_target="tpu_custom_call" | custom-call | flops 1610612736 | bytes 1572864 | tf_op jit(solution)/shard_map/second_products/pallas_call | solution.py:236
  62.1 1.6 %collective-permute-start.21 = (s16[320,512]{1,0:T(8,128)(2,1)S(1)}, s16[320,512]{1,0:T(8,128)(2,1)S(1)}, u32[]{:S(2)}, u32[]{:S(2)}) collective-permute-start(s16[320,512]{1,0:T(8,128)(2,1)S(1)} %get-tuple-element.127.lo), channel_id=1, source_target_pairs={{0,2},{1,3},{2,0},{3,1},{4,6},{5,7},{6,4},{7,5},{8,10},{9,11},{10,... | collective-permute-start | bytes 983048 | tf_op jit(solution)/shard_map/ppermute | solution.py:276
  63.6 1.5 %collective-permute-start.20 = (s16[320,512]{1,0:T(8,128)(2,1)S(1)}, s16[320,512]{1,0:T(8,128)(2,1)S(1)}, u32[]{:S(2)}, u32[]{:S(2)}) collective-permute-start(s16[320,512]{1,0:T(8,128)(2,1)S(1)} %get-tuple-element.125.hi), channel_id=1, source_target_pairs={{0,4},{1,5},{2,6},{3,7},{4,0},{5,1},{6,2},{7,3},{8,12},{9,13},{10,... | collective-permute-start | bytes 983048 | tf_op jit(solution)/shard_map/ppermute | solution.py:276
  65.2 4.4 %second_products.4 = (s16[272,512]{1,0:T(8,128)(2,1)S(1)}, f32[256,512]{1,0:T(8,128)S(1)}, f32[256,512]{1,0:T(8,128)S(1)}, s16[272,512]{1,0:T(8,128)(2,1)S(1)}) custom-call(bf16[512,512]{1,0:T(8,128)(2,1)S(1)} %get-tuple-element.111.ha, bf16[512,512]{1,0:T(8,128)(2,1)S(1)} %collective-permute-done.15.hb, bf16[512,512]{1,0:T(8,128)(2,1)} %copy-done.3, ...), custom_call_target="tpu_custom_call" | custom-call | flops 3221225472 | bytes 3145728 | tf_op jit(solution)/shard_map/second_products/pallas_call | solution.py:236
  70.7 3.5 %collective-permute-done.20.x_in = s16[320,512]{1,0:T(8,128)(2,1)S(1)} collective-permute-done((s16[320,512]{1,0:T(8,128)(2,1)S(1)}, s16[320,512]{1,0:T(8,128)(2,1)S(1)}, u32[]{:S(2)}, u32[]{:S(2)}) %collective-permute-start.20) | collective-permute-done | bytes 327712 | tf_op jit(solution)/shard_map/ppermute | solution.py:276
  75.1 2.0 %collective-permute-start.26 = (s16[320,512]{1,0:T(8,128)(2,1)S(1)}, s16[320,512]{1,0:T(8,128)(2,1)S(1)}, u32[]{:S(2)}, u32[]{:S(2)}) collective-permute-start(s16[320,512]{1,0:T(8,128)(2,1)S(1)} %get-tuple-element.135), channel_id=1, source_target_pairs={{0,4},{1,5},{2,6},{3,7},{4,0},{5,1},{6,2},{7,3},{8,12},{9,13},{10,... | collective-permute-start | bytes 983048 | tf_op jit(solution)/shard_map/ppermute | solution.py:276
  77.1 2.1 %collective-permute-done.22.x_lo = s16[272,512]{1,0:T(8,128)(2,1)S(1)} collective-permute-done((s16[272,512]{1,0:T(8,128)(2,1)S(1)}, s16[272,512]{1,0:T(8,128)(2,1)S(1)}, u32[]{:S(2)}, u32[]{:S(2)}) %collective-permute-start.22) | collective-permute-done | bytes 278560 | tf_op jit(solution)/shard_map/ppermute | solution.py:276
  80.2 2.5 %second_products.5.own = f32[512,512]{1,0:T(8,128)S(1)} custom-call(bf16[512,512]{1,0:T(8,128)(2,1)S(1)} %get-tuple-element.111.ha, bf16[512,512]{1,0:T(8,128)(2,1)S(1)} %collective-permute-done.15.hb, bf16[512,512]{1,0:T(8,128)(2,1)} %w_ref.1, s16[512,512]{1,0:T(8,128)(2,1)} %get-tuple-element.76.refs_1_, s16[512,512]{1,0:T(8,128)(2,1)S(1)} %collective-permute-done.24.refs_2_), custom_call_target="tpu_custom_call" | custom-call | flops 1610612736 | bytes 1572864 | tf_op jit(solution)/shard_map/second_products/pallas_call | solution.py:236
  82.9 2.2 %collective-permute-done.25.x_hi = s16[320,512]{1,0:T(8,128)(2,1)S(1)} collective-permute-done((s16[320,512]{1,0:T(8,128)(2,1)S(1)}, s16[320,512]{1,0:T(8,128)(2,1)S(1)}, u32[]{:S(2)}, u32[]{:S(2)}) %collective-permute-start.25) | collective-permute-done | bytes 327712 | tf_op jit(solution)/shard_map/ppermute | solution.py:276
  85.2 1.2 %collective-permute-done.26.y_lo = s16[320,512]{1,0:T(8,128)(2,1)S(1)} collective-permute-done((s16[320,512]{1,0:T(8,128)(2,1)S(1)}, s16[320,512]{1,0:T(8,128)(2,1)S(1)}, u32[]{:S(2)}, u32[]{:S(2)}) %collective-permute-start.26) | collective-permute-done | bytes 327712 | tf_op jit(solution)/shard_map/ppermute | solution.py:276
  86.4 1.4 %last_update.1 = (bf16[512,512]{1,0:T(8,128)(2,1)}, f32[64,512]{1,0:T(8,128)}) custom-call(f32[512,512]{1,0:T(8,128)S(1)} %get-tuple-element.134.base, s16[320,512]{1,0:T(8,128)(2,1)S(1)} %collective-permute-done.25.x_hi, s16[320,512]{1,0:T(8,128)(2,1)S(1)} %collective-permute-done.26.y_lo, s16[48,512]{1,0:T(8,128)(2,1)S(1)} %get-tuple-element.136.x_sums, ...), custom_call_target="tpu_custom_call" | custom-call | tf_op jit(solution)/shard_map/last_update/pallas_call | solution.py:270
  (67 shorter events, 10.7 us)
Async XLA Ops:
  0.6 11.9 %collective-permute-start.2 = (bf16[512,512]{1,0:T(8,128)(2,1)}, bf16[512,512]{1,0:T(8,128)(2,1)S(1)}, u32[]{:S(2)}, u32[]{:S(2)}) collective-permute-start(bf16[512,512]{1,0:T(8,128)(2,1)} %w_ref.1), channel_id=1, source_target_pairs={{0,1},{1,0},{2,3},{3,2},{4,5},{5,4},{6,7},{7,6},{8,9},{9,8},{10,11... | collective-permute-start | bytes 1572872 | tf_op jit(solution)/shard_map/ppermute | solution.py:276
  1.1 16.2 %collective-permute-start = (bf16[512,512]{1,0:T(8,128)(2,1)}, bf16[512,512]{1,0:T(8,128)(2,1)S(1)}, u32[]{:S(2)}, u32[]{:S(2)}) collective-permute-start(bf16[512,512]{1,0:T(8,128)(2,1)} %w_ref.1), channel_id=1, source_target_pairs={{0,2},{1,3},{2,0},{3,1},{4,6},{5,7},{6,4},{7,5},{8,10},{9,11},{10,... | collective-permute-start | bytes 1572872 | tf_op jit(solution)/shard_map/ppermute | solution.py:276
  3.7 14.2 %collective-permute-start.1 = (bf16[512,512]{1,0:T(8,128)(2,1)}, bf16[512,512]{1,0:T(8,128)(2,1)S(1)}, u32[]{:S(2)}, u32[]{:S(2)}) collective-permute-start(bf16[512,512]{1,0:T(8,128)(2,1)} %w_ref.1), channel_id=1, source_target_pairs={{0,4},{1,5},{2,6},{3,7},{4,0},{5,1},{6,2},{7,3},{8,12},{9,13},{10,... | collective-permute-start | bytes 1572872 | tf_op jit(solution)/shard_map/ppermute | solution.py:276
  18.0 2.6 %collective-permute-start.5 = (bf16[512,512]{1,0:T(8,128)(2,1)S(1)}, bf16[512,512]{1,0:T(8,128)(2,1)S(1)}, u32[]{:S(2)}, u32[]{:S(2)}) collective-permute-start(bf16[512,512]{1,0:T(8,128)(2,1)S(1)} %collective-permute-done.b_ref.refs_0_), channel_id=1, source_target_pairs={{0,1},{1,0},{2,3},{3,2},{4,5},{5,4},{6,7},{7,6},{8,9},{9,8},{10,11... | collective-permute-start | bytes 1572872 | tf_op jit(solution)/shard_map/ppermute | solution.py:276
  18.0 2.6 %collective-permute-start.6 = (bf16[512,512]{1,0:T(8,128)(2,1)S(1)}, bf16[512,512]{1,0:T(8,128)(2,1)S(1)}, u32[]{:S(2)}, u32[]{:S(2)}) collective-permute-start(bf16[512,512]{1,0:T(8,128)(2,1)S(1)} %collective-permute-done.1.a_ref.refs_2_.refs_3_), channel_id=1, source_target_pairs={{0,1},{1,0},{2,3},{3,2},{4,5},{5,4},{6,7},{7,6},{8,9},{9,8},{10,11... | collective-permute-start | bytes 1572872 | tf_op jit(solution)/shard_map/ppermute | solution.py:276
  18.5 8.4 %collective-permute-start.3 = (bf16[256,512]{1,0:T(8,128)(2,1)S(1)}, bf16[256,512]{1,0:T(8,128)(2,1)}, u32[]{:S(2)}, u32[]{:S(2)}) collective-permute-start(bf16[256,512]{1,0:T(8,128)(2,1)S(1)} %get-tuple-element.82), channel_id=1, source_target_pairs={{0,2},{1,3},{2,0},{3,1},{4,6},{5,7},{6,4},{7,5},{8,10},{9,11},{10,... | collective-permute-start | bytes 786440 | tf_op jit(solution)/shard_map/ppermute | solution.py:276
  18.9 8.1 %collective-permute-start.4 = (bf16[256,512]{1,0:T(8,128)(2,1)S(1)}, bf16[256,512]{1,0:T(8,128)(2,1)}, u32[]{:S(2)}, u32[]{:S(2)}) collective-permute-start(bf16[256,512]{1,0:T(8,128)(2,1)S(1)} %get-tuple-element.83), channel_id=1, source_target_pairs={{0,4},{1,5},{2,6},{3,7},{4,0},{5,1},{6,2},{7,3},{8,12},{9,13},{10,... | collective-permute-start | bytes 786440 | tf_op jit(solution)/shard_map/ppermute | solution.py:276
  21.7 34.7 %copy-start = (f32[512,512]{1,0:T(8,128)S(1)}, f32[512,512]{1,0:T(8,128)}, u32[]{:S(2)}) copy-start(f32[512,512]{1,0:T(8,128)} %refs_4_.1) | copy-start | bytes 3145732
  26.0 31.5 %copy-start.2 = (f32[512,64]{0,1:T(8,128)S(1)}, f32[512,64]{0,1:T(8,128)}, u32[]{:S(2)}) copy-start(f32[512,64]{0,1:T(8,128)} %param.8) | copy-start | bytes 393220
  26.1 31.5 %copy-start.6 = (f32[64,512]{1,0:T(8,128)S(1)}, f32[64,512]{1,0:T(8,128)}, u32[]{:S(2)}) copy-start(f32[64,512]{1,0:T(8,128)} %h2_ref.1) | copy-start | bytes 393220
  27.0 2.0 %collective-permute-start.7 = (bf16[256,512]{1,0:T(8,128)(2,1)}, bf16[256,512]{1,0:T(8,128)(2,1)S(1)}, u32[]{:S(2)}, u32[]{:S(2)}) collective-permute-start(bf16[256,512]{1,0:T(8,128)(2,1)} %collective-permute-done.3.refs_2_.refs_1_), channel_id=1, source_target_pairs={{0,1},{1,0},{2,3},{3,2},{4,5},{5,4},{6,7},{7,6},{8,9},{9,8},{10,11... | collective-permute-start | bytes 786440 | tf_op jit(solution)/shard_map/ppermute | solution.py:276
  27.0 2.1 %collective-permute-start.8 = (bf16[256,512]{1,0:T(8,128)(2,1)}, bf16[256,512]{1,0:T(8,128)(2,1)S(1)}, u32[]{:S(2)}, u32[]{:S(2)}) collective-permute-start(bf16[256,512]{1,0:T(8,128)(2,1)} %collective-permute-done.4.refs_3_.refs_2_), channel_id=1, source_target_pairs={{0,1},{1,0},{2,3},{3,2},{4,5},{5,4},{6,7},{7,6},{8,9},{9,8},{10,11... | collective-permute-start | bytes 786440 | tf_op jit(solution)/shard_map/ppermute | solution.py:276
  27.5 29.9 %copy-start.10 = (s16[512,512]{1,0:T(8,128)(2,1)S(1)}, s16[512,512]{1,0:T(8,128)(2,1)}, u32[]{:S(2)}) copy-start(s16[512,512]{1,0:T(8,128)(2,1)} %get-tuple-element.89.refs_7_) | copy-start | bytes 1572868
  27.5 32.8 %copy-start.9 = (s16[512,512]{1,0:T(8,128)(2,1)S(1)}, s16[512,512]{1,0:T(8,128)(2,1)}, u32[]{:S(2)}) copy-start(s16[512,512]{1,0:T(8,128)(2,1)} %get-tuple-element.77.refs_3_) | copy-start | bytes 1572868
  30.7 6.5 %collective-permute-start.11 = (s16[528,128]{1,0:T(8,128)(2,1)S(1)}, s16[528,128]{1,0:T(8,128)(2,1)S(1)}, u32[]{:S(2)}, u32[]{:S(2)}) collective-permute-start(s16[528,128]{1,0:T(8,128)(2,1)S(1)} %get-tuple-element.109), channel_id=1, source_target_pairs={{0,8},{8,0},{16,24},{24,16},{1,9},{9,1},{17,25},{25,17},{2,10},{10... | collective-permute-start | bytes 405512 | tf_op jit(solution)/shard_map/ppermute | solution.py:276
  32.6 8.7 %collective-permute-start.9 = (s16[528,128]{1,0:T(8,128)(2,1)S(1)}, s16[528,128]{1,0:T(8,128)(2,1)S(1)}, u32[]{:S(2)}, u32[]{:S(2)}) collective-permute-start(s16[528,128]{1,0:T(8,128)(2,1)S(1)} %get-tuple-element.107.refs_0_), channel_id=1, source_target_pairs={{0,8},{8,0},{16,24},{24,16},{1,9},{9,1},{17,25},{25,17},{2,10},{10... | collective-permute-start | bytes 405512 | tf_op jit(solution)/shard_map/ppermute | solution.py:276
  37.4 7.6 %collective-permute-start.12 = (s16[528,128]{1,0:T(8,128)(2,1)S(1)}, s16[528,128]{1,0:T(8,128)(2,1)S(1)}, u32[]{:S(2)}, u32[]{:S(2)}) collective-permute-start(s16[528,128]{1,0:T(8,128)(2,1)S(1)} %add_pair.3.one), channel_id=1, source_target_pairs={{0,24},{8,16},{16,8},{24,0},{1,25},{9,17},{17,9},{25,1},{2,26},{10... | collective-permute-start | bytes 405512 | tf_op jit(solution)/shard_map/ppermute | solution.py:276
  41.4 9.4 %collective-permute-start.10 = (s16[528,128]{1,0:T(8,128)(2,1)S(1)}, s16[528,128]{1,0:T(8,128)(2,1)S(1)}, u32[]{:S(2)}, u32[]{:S(2)}) collective-permute-start(s16[528,128]{1,0:T(8,128)(2,1)S(1)} %add_pair.2.one), channel_id=1, source_target_pairs={{0,24},{8,16},{16,8},{24,0},{1,25},{9,17},{17,9},{25,1},{2,26},{10... | collective-permute-start | bytes 405512 | tf_op jit(solution)/shard_map/ppermute | solution.py:276
  45.1 9.9 %collective-permute-start.14 = (s16[528,128]{1,0:T(8,128)(2,1)S(1)}, s16[528,128]{1,0:T(8,128)(2,1)S(1)}, u32[]{:S(2)}, u32[]{:S(2)}) collective-permute-start(s16[528,128]{1,0:T(8,128)(2,1)S(1)} %add_cross.3.refs_1_), channel_id=1, source_target_pairs={{0,8},{8,0},{16,24},{24,16},{1,9},{9,1},{17,25},{25,17},{2,10},{10... | collective-permute-start | bytes 405512 | tf_op jit(solution)/shard_map/ppermute | solution.py:276
  51.0 5.4 %collective-permute-start.13 = (s16[528,128]{1,0:T(8,128)(2,1)S(1)}, s16[528,128]{1,0:T(8,128)(2,1)S(1)}, u32[]{:S(2)}, u32[]{:S(2)}) collective-permute-start(s16[528,128]{1,0:T(8,128)(2,1)S(1)} %get-tuple-element.108.refs_0_), channel_id=1, source_target_pairs={{0,8},{8,0},{16,24},{24,16},{1,9},{9,1},{17,25},{25,17},{2,10},{10... | collective-permute-start | bytes 405512 | tf_op jit(solution)/shard_map/ppermute | solution.py:276
  52.4 7.9 %collective-permute-start.17 = (s16[512,512]{1,0:T(8,128)(2,1)}, s16[512,512]{1,0:T(8,128)(2,1)S(1)}, u32[]{:S(2)}, u32[]{:S(2)}) collective-permute-start(s16[512,512]{1,0:T(8,128)(2,1)} %get-tuple-element.99.refs_1_), channel_id=1, source_target_pairs={{0,1},{1,0},{2,3},{3,2},{4,5},{5,4},{6,7},{7,6},{8,9},{9,8},{10,11... | collective-permute-start | bytes 1572872 | tf_op jit(solution)/shard_map/ppermute | solution.py:276
  56.9 3.5 %collective-permute-start.15 = (bf16[512,512]{1,0:T(8,128)(2,1)S(1)}, bf16[512,512]{1,0:T(8,128)(2,1)S(1)}, u32[]{:S(2)}, u32[]{:S(2)}) collective-permute-start(bf16[512,512]{1,0:T(8,128)(2,1)S(1)} %get-tuple-element.111.ha), channel_id=1, source_target_pairs={{0,1},{1,0},{2,3},{3,2},{4,5},{5,4},{6,7},{7,6},{8,9},{9,8},{10,11... | collective-permute-start | bytes 1572872 | tf_op jit(solution)/shard_map/ppermute | solution.py:276
  56.9 8.2 %collective-permute-start.18 = (s16[512,512]{1,0:T(8,128)(2,1)S(1)}, s16[512,512]{1,0:T(8,128)(2,1)S(1)}, u32[]{:S(2)}, u32[]{:S(2)}) collective-permute-start(s16[512,512]{1,0:T(8,128)(2,1)S(1)} %copy-done.11), channel_id=1, source_target_pairs={{0,1},{1,0},{2,3},{3,2},{4,5},{5,4},{6,7},{7,6},{8,9},{9,8},{10,11... | collective-permute-start | bytes 1572872 | tf_op jit(solution)/shard_map/ppermute | solution.py:276
  57.4 7.7 %collective-permute-start.19 = (s16[512,512]{1,0:T(8,128)(2,1)S(1)}, s16[512,512]{1,0:T(8,128)(2,1)S(1)}, u32[]{:S(2)}, u32[]{:S(2)}) collective-permute-start(s16[512,512]{1,0:T(8,128)(2,1)S(1)} %copy-done.10), channel_id=1, source_target_pairs={{0,1},{1,0},{2,3},{3,2},{4,5},{5,4},{6,7},{7,6},{8,9},{9,8},{10,11... | collective-permute-start | bytes 1572872 | tf_op jit(solution)/shard_map/ppermute | solution.py:276
  59.8 1.8 %collective-permute-start.16 = (f32[80,512]{1,0:T(8,128)S(1)}, f32[80,512]{1,0:T(8,128)S(1)}, u32[]{:S(2)}, u32[]{:S(2)}) collective-permute-start(f32[80,512]{1,0:T(8,128)S(1)} %get-tuple-element.120.sums), channel_id=1, source_target_pairs={{0,1},{1,0},{2,3},{3,2},{4,5},{5,4},{6,7},{7,6},{8,9},{9,8},{10,11... | collective-permute-start | bytes 491528 | tf_op jit(solution)/shard_map/ppermute | solution.py:276
  60.3 19.9 %collective-permute-start.24 = (s16[512,512]{1,0:T(8,128)(2,1)S(1)}, s16[512,512]{1,0:T(8,128)(2,1)S(1)}, u32[]{:S(2)}, u32[]{:S(2)}) collective-permute-start(s16[512,512]{1,0:T(8,128)(2,1)S(1)} %copy-done.9), channel_id=1, source_target_pairs={{0,1},{1,0},{2,3},{3,2},{4,5},{5,4},{6,7},{7,6},{8,9},{9,8},{10,11... | collective-permute-start | bytes 1572872 | tf_op jit(solution)/shard_map/ppermute | solution.py:276
  62.1 12.1 %collective-permute-start.21 = (s16[320,512]{1,0:T(8,128)(2,1)S(1)}, s16[320,512]{1,0:T(8,128)(2,1)S(1)}, u32[]{:S(2)}, u32[]{:S(2)}) collective-permute-start(s16[320,512]{1,0:T(8,128)(2,1)S(1)} %get-tuple-element.127.lo), channel_id=1, source_target_pairs={{0,2},{1,3},{2,0},{3,1},{4,6},{5,7},{6,4},{7,5},{8,10},{9,11},{10,... | collective-permute-start | bytes 983048 | tf_op jit(solution)/shard_map/ppermute | solution.py:276
  63.6 10.6 %collective-permute-start.20 = (s16[320,512]{1,0:T(8,128)(2,1)S(1)}, s16[320,512]{1,0:T(8,128)(2,1)S(1)}, u32[]{:S(2)}, u32[]{:S(2)}) collective-permute-start(s16[320,512]{1,0:T(8,128)(2,1)S(1)} %get-tuple-element.125.hi), channel_id=1, source_target_pairs={{0,4},{1,5},{2,6},{3,7},{4,0},{5,1},{6,2},{7,3},{8,12},{9,13},{10,... | collective-permute-start | bytes 983048 | tf_op jit(solution)/shard_map/ppermute | solution.py:276
  69.6 9.6 %collective-permute-start.22 = (s16[272,512]{1,0:T(8,128)(2,1)S(1)}, s16[272,512]{1,0:T(8,128)(2,1)S(1)}, u32[]{:S(2)}, u32[]{:S(2)}) collective-permute-start(s16[272,512]{1,0:T(8,128)(2,1)S(1)} %get-tuple-element.129), channel_id=1, source_target_pairs={{0,2},{1,3},{2,0},{3,1},{4,6},{5,7},{6,4},{7,5},{8,10},{9,11},{10,... | collective-permute-start | bytes 835592 | tf_op jit(solution)/shard_map/ppermute | solution.py:276
  70.2 10.0 %collective-permute-start.23 = (s16[272,512]{1,0:T(8,128)(2,1)S(1)}, s16[272,512]{1,0:T(8,128)(2,1)S(1)}, u32[]{:S(2)}, u32[]{:S(2)}) collective-permute-start(s16[272,512]{1,0:T(8,128)(2,1)S(1)} %get-tuple-element.130), channel_id=1, source_target_pairs={{0,4},{1,5},{2,6},{3,7},{4,0},{5,1},{6,2},{7,3},{8,12},{9,13},{10,... | collective-permute-start | bytes 835592 | tf_op jit(solution)/shard_map/ppermute | solution.py:276
  75.0 10.2 %collective-permute-start.25 = (s16[320,512]{1,0:T(8,128)(2,1)S(1)}, s16[320,512]{1,0:T(8,128)(2,1)S(1)}, u32[]{:S(2)}, u32[]{:S(2)}) collective-permute-start(s16[320,512]{1,0:T(8,128)(2,1)S(1)} %get-tuple-element.128), channel_id=1, source_target_pairs={{0,2},{1,3},{2,0},{3,1},{4,6},{5,7},{6,4},{7,5},{8,10},{9,11},{10,... | collective-permute-start | bytes 983048 | tf_op jit(solution)/shard_map/ppermute | solution.py:276
  75.1 11.3 %collective-permute-start.26 = (s16[320,512]{1,0:T(8,128)(2,1)S(1)}, s16[320,512]{1,0:T(8,128)(2,1)S(1)}, u32[]{:S(2)}, u32[]{:S(2)}) collective-permute-start(s16[320,512]{1,0:T(8,128)(2,1)S(1)} %get-tuple-element.135), channel_id=1, source_target_pairs={{0,4},{1,5},{2,6},{3,7},{4,0},{5,1},{6,2},{7,3},{8,12},{9,13},{10,... | collective-permute-start | bytes 983048 | tf_op jit(solution)/shard_map/ppermute | solution.py:276
  (7 other events, 62.9 us)

commit v9 on v8

--- a/solution.py
+++ b/solution.py
@@ -465,7 +465,6 @@
         half = jax.ShapeDtypeStruct((t, k1), BF16)
         y_lo, x_hi = plain(cut_halves, (half, half), w_y, w_x, name="cut_halves")
         d_lo, d_hi = cell(y_lo, bit=2), cell(x_hi, bit=4)
-        w_x, w_y, x_hi, y_lo = after((w_x, w_y, x_hi, y_lo))
         x_0, y_0 = cell(w_x, bit=1), cell(w_y, bit=1)
         near = ((w_x, on_mine[1]), (w_y, on_mine[2]), (x_0, on_theirs[1]), (y_0, on_theirs[2]))
         acc = first(near, h1_low, acc)

time: 88.2 us -> 88.1 us (level)
  transfers between devices with their start and end apart: 27 -> 27, of which waited for: 14 -> 13; matrix products, arithmetic and copies ran while one was open for 2% -> 2% of each run, Pallas kernels for 31% -> 31%
where the time goes in v9:
time: 88.1 us; the launch traced here: 87.8 us
  Pallas kernels  30.7 us (35%)
  starting transfers between devices  30.1 us (34%)
  waiting for transfers between devices  21.8 us (25%)
  local copies, waits for them, and re-layouts  2.89 us (3%)
  other arithmetic  1.37 us (2%)
  between operations  0.92 us (1%)
    ppermute x27, starting transfers between devices, flip(): return lax.ppermute(x, axis, [(i, i ^ bit) for i in range(size)])  30.1 us
    ppermute x27, waiting for transfers between devices, flip(): return lax.ppermute(x, axis, [(i, i ^ bit) for i in range(size)])  21.8 us
    pallas_call x5, Pallas kernels, products(): pl.pallas_call(functools.partial(body, sizes, later, len(fetch), flag), o...  15.5 us
    pallas_call x1, Pallas kernels, split_counts(): pl.pallas_call(functools.partial(counts_body, chips, rows), out_shape=(ou...  5.88 us
    pallas_call x10, Pallas kernels, plain(): pl.pallas_call(body, out_shape=outs, in_specs=specs, out_specs=out_specs,...  3.95 us
    unnamed x24, local copies, waits for them, and re-layouts  2.89 us
    pallas_call x1, Pallas kernels, on_device(): pl.pallas_call(functools.partial(layer_two, len(soon)), out_shape=(jax.Sh...  2.27 us
  transfers between devices with their start and end apart: 27, of which 13 were waited for; matrix products, arithmetic and copies ran while one was open for 2% of the time, Pallas kernels for 31%

profile of v9, /device:TPU:0, one launch (start us, length us, event | category | flops | bytes accessed | tf_op | source)
XLA Modules:
  0.0 87.8 jit_solution(3405973730941504313)
XLA Ops:
  1.1 2.6 %collective-permute-start = (bf16[512,512]{1,0:T(8,128)(2,1)}, bf16[512,512]{1,0:T(8,128)(2,1)S(1)}, u32[]{:S(2)}, u32[]{:S(2)}) collective-permute-start(bf16[512,512]{1,0:T(8,128)(2,1)} %w_ref.1), channel_id=1, source_target_pairs={{0,2},{1,3},{2,0},{3,1},{4,6},{5,7},{6,4},{7,5},{8,10},{9,11},{10,... | collective-permute-start | bytes 1572872 | tf_op jit(solution)/shard_map/ppermute | solution.py:276
  3.7 1.5 %collective-permute-start.1 = (bf16[512,512]{1,0:T(8,128)(2,1)}, bf16[512,512]{1,0:T(8,128)(2,1)S(1)}, u32[]{:S(2)}, u32[]{:S(2)}) collective-permute-start(bf16[512,512]{1,0:T(8,128)(2,1)} %w_ref.1), channel_id=1, source_target_pairs={{0,4},{1,5},{2,6},{3,7},{4,0},{5,1},{6,2},{7,3},{8,12},{9,13},{10,... | collective-permute-start | bytes 1572872 | tf_op jit(solution)/shard_map/ppermute | solution.py:276
  5.2 1.3 %convert_element_type.3.h.h_ref = bf16[512,512]{1,0:T(8,128)(2,1)S(1)} convert(f32[512,512]{1,0:T(8,128)} %refs_4_.1) | non-fusion elementwise | flops 262144 | bytes 1572864 | tf_op jit(solution)/shard_map/convert_element_type | solution.py:453
  6.6 5.9 %split_counts.1 = (s16[512,512]{1,0:T(8,128)(2,1)}, s16[512,512]{1,0:T(8,128)(2,1)}, s16[512,512]{1,0:T(8,128)(2,1)}, s16[512,512]{1,0:T(8,128)(2,1)}, s16[512,5...) custom-call(s32[2]{0:T(128)S(1)} %pad_add_fusion.at, s32[4096,512]{1,0:T(8,128)} %v.1), custom_call_target="tpu_custom_call" | custom-call | tf_op jit(solution)/shard_map/split_counts/pallas_call | solution.py:104
  13.3 1.0 %copy-done.8 = bf16[512,512]{1,0:T(8,128)(2,1)S(1)} copy-done((bf16[512,512]{1,0:T(8,128)(2,1)S(1)}, bf16[512,512]{1,0:T(8,128)(2,1)}, u32[]{:S(2)}) %copy-start.8) | copy-done | bytes 524312
  14.3 3.0 %first_products.2 = (f32[512,512]{1,0:T(8,128)S(1)}, f32[8,512]{1,0:T(8,128)S(1)}) custom-call(bf16[512,512]{1,0:T(8,128)(2,1)S(1)} %convert_element_type.3.h.h_ref, bf16[512,512]{1,0:T(8,128)(2,1)} %w_ref.1, s16[512,512]{1,0:T(8,128)(2,1)} %get-tuple-element.74.refs_1_, bf16[512,512]{1,0:T(8,128)(2,1)S(1)} %copy-done.8, ...), custom_call_target="tpu_custom_call" | custom-call | flops 2147483648 | bytes 2097152 | tf_op jit(solution)/shard_map/first_products/pallas_call | solution.py:236
  18.9 1.7 %collective-permute-start.4 = (bf16[256,512]{1,0:T(8,128)(2,1)S(1)}, bf16[256,512]{1,0:T(8,128)(2,1)}, u32[]{:S(2)}, u32[]{:S(2)}) collective-permute-start(bf16[256,512]{1,0:T(8,128)(2,1)S(1)} %get-tuple-element.81), channel_id=1, source_target_pairs={{0,4},{1,5},{2,6},{3,7},{4,0},{5,1},{6,2},{7,3},{8,12},{9,13},{10,... | collective-permute-start | bytes 786440 | tf_op jit(solution)/shard_map/ppermute | solution.py:276
  20.6 1.0 %copy-done.5 = bf16[512,512]{1,0:T(8,128)(2,1)S(1)} copy-done((bf16[512,512]{1,0:T(8,128)(2,1)S(1)}, bf16[512,512]{1,0:T(8,128)(2,1)}, u32[]{:S(2)}) %copy-start.5) | copy-done | bytes 524312
  21.6 4.3 %first_products.3 = (f32[512,512]{1,0:T(8,128)S(1)}, f32[8,512]{1,0:T(8,128)S(1)}) custom-call(bf16[512,512]{1,0:T(8,128)(2,1)S(1)} %convert_element_type.3.h.h_ref, bf16[512,512]{1,0:T(8,128)(2,1)S(1)} %collective-permute-done.b_ref.refs_0_, s16[512,512]{1,0:T(8,128)(2,1)} %get-tuple-element.82.refs_1_, ...), custom_call_target="tpu_custom_call", output_to_operand_aliasing={{0}: (9, {}), {1}: (10, {})} | custom-call | flops 4294967296 | bytes 4194304 | tf_op jit(solution)/shard_map/first_products/pallas_call | solution.py:236
  27.5 1.5 %fetch.1 = (s16[512,512]{1,0:T(8,128)(2,1)S(1)}, s16[512,512]{1,0:T(8,128)(2,1)S(1)}, bf16[256,512]{1,0:T(8,128)(2,1)S(1)}, bf16[256,512]{1,0:T(8,128)(2,1)S(1)}) custom-call(s16[512,512]{1,0:T(8,128)(2,1)} %get-tuple-element.94.refs_0_, s16[512,512]{1,0:T(8,128)(2,1)} %get-tuple-element.95.refs_1_, bf16[256,512]{1,0:T(8,128)(2,1)} %collective-permute-done.3.refs_2_.refs_1_, ...), custom_call_target="tpu_custom_call" | custom-call | tf_op jit(solution)/shard_map/fetch/pallas_call | solution.py:164
  29.1 1.6 %first_and_split.1 = (f32[512,256]{1,0:T(8,128)S(1)}, s16[528,128]{1,0:T(8,128)(2,1)S(1)}, s16[528,128]{1,0:T(8,128)(2,1)S(1)}) custom-call(s32[1]{0:T(128)} %bitcast.flag_ref.flag, bf16[512,512]{1,0:T(8,128)(2,1)S(1)} %convert_element_type.3.h.h_ref, bf16[256,512]{1,0:T(8,128)(2,1)S(1)} %get-tuple-element.98.refs_0_, ...), custom_call_target="tpu_custom_call" | custom-call | flops 536870912 | bytes 1048576 | tf_op jit(solution)/shard_map/first_and_split/pallas_call | solution.py:307
  30.7 1.8 %collective-permute-start.11 = (s16[528,128]{1,0:T(8,128)(2,1)S(1)}, s16[528,128]{1,0:T(8,128)(2,1)S(1)}, u32[]{:S(2)}, u32[]{:S(2)}) collective-permute-start(s16[528,128]{1,0:T(8,128)(2,1)S(1)} %get-tuple-element.105), channel_id=1, source_target_pairs={{0,8},{8,0},{16,24},{24,16},{1,9},{9,1},{17,25},{25,17},{2,10},{10... | collective-permute-start | bytes 405512 | tf_op jit(solution)/shard_map/ppermute | solution.py:276
  32.8 4.4 %collective-permute-done.11.other = s16[528,128]{1,0:T(8,128)(2,1)S(1)} collective-permute-done((s16[528,128]{1,0:T(8,128)(2,1)S(1)}, s16[528,128]{1,0:T(8,128)(2,1)S(1)}, u32[]{:S(2)}, u32[]{:S(2)}) %collective-permute-start.11) | collective-permute-done | bytes 135200 | tf_op jit(solution)/shard_map/ppermute | solution.py:276
  37.4 3.8 %collective-permute-start.12 = (s16[528,128]{1,0:T(8,128)(2,1)S(1)}, s16[528,128]{1,0:T(8,128)(2,1)S(1)}, u32[]{:S(2)}, u32[]{:S(2)}) collective-permute-start(s16[528,128]{1,0:T(8,128)(2,1)S(1)} %add_pair.3.one), channel_id=1, source_target_pairs={{0,24},{8,16},{16,8},{24,0},{1,25},{9,17},{17,9},{25,1},{2,26},{10... | collective-permute-start | bytes 405512 | tf_op jit(solution)/shard_map/ppermute | solution.py:276
  41.3 1.9 %collective-permute-start.10 = (s16[528,128]{1,0:T(8,128)(2,1)S(1)}, s16[528,128]{1,0:T(8,128)(2,1)S(1)}, u32[]{:S(2)}, u32[]{:S(2)}) collective-permute-start(s16[528,128]{1,0:T(8,128)(2,1)S(1)} %add_pair.2.one), channel_id=1, source_target_pairs={{0,24},{8,16},{16,8},{24,0},{1,25},{9,17},{17,9},{25,1},{2,26},{10... | collective-permute-start | bytes 405512 | tf_op jit(solution)/shard_map/ppermute | solution.py:276
  43.2 1.6 %collective-permute-done.12.other = s16[528,128]{1,0:T(8,128)(2,1)S(1)} collective-permute-done((s16[528,128]{1,0:T(8,128)(2,1)S(1)}, s16[528,128]{1,0:T(8,128)(2,1)S(1)}, u32[]{:S(2)}, u32[]{:S(2)}) %collective-permute-start.12) | collective-permute-done | bytes 135200 | tf_op jit(solution)/shard_map/ppermute | solution.py:276
  45.1 5.7 %collective-permute-start.14 = (s16[528,128]{1,0:T(8,128)(2,1)S(1)}, s16[528,128]{1,0:T(8,128)(2,1)S(1)}, u32[]{:S(2)}, u32[]{:S(2)}) collective-permute-start(s16[528,128]{1,0:T(8,128)(2,1)S(1)} %add_cross.3.refs_1_), channel_id=1, source_target_pairs={{0,8},{8,0},{16,24},{24,16},{1,9},{9,1},{17,25},{25,17},{2,10},{10... | collective-permute-start | bytes 405512 | tf_op jit(solution)/shard_map/ppermute | solution.py:276
  50.9 1.4 %collective-permute-start.13 = (s16[528,128]{1,0:T(8,128)(2,1)S(1)}, s16[528,128]{1,0:T(8,128)(2,1)S(1)}, u32[]{:S(2)}, u32[]{:S(2)}) collective-permute-start(s16[528,128]{1,0:T(8,128)(2,1)S(1)} %get-tuple-element.104.refs_0_), channel_id=1, source_target_pairs={{0,8},{8,0},{16,24},{24,16},{1,9},{9,1},{17,25},{25,17},{2,10},{10... | collective-permute-start | bytes 405512 | tf_op jit(solution)/shard_map/ppermute | solution.py:276
  52.4 2.6 %collective-permute-done.14.refs_3_ = s16[528,128]{1,0:T(8,128)(2,1)S(1)} collective-permute-done((s16[528,128]{1,0:T(8,128)(2,1)S(1)}, s16[528,128]{1,0:T(8,128)(2,1)S(1)}, u32[]{:S(2)}, u32[]{:S(2)}) %collective-permute-start.14) | collective-permute-done | bytes 135200 | tf_op jit(solution)/shard_map/ppermute | solution.py:276
  54.9 1.4 %collective-permute-done.13.refs_2_ = s16[528,128]{1,0:T(8,128)(2,1)S(1)} collective-permute-done((s16[528,128]{1,0:T(8,128)(2,1)S(1)}, s16[528,128]{1,0:T(8,128)(2,1)S(1)}, u32[]{:S(2)}, u32[]{:S(2)}) %collective-permute-start.13) | collective-permute-done | bytes 135200 | tf_op jit(solution)/shard_map/ppermute | solution.py:276
  57.5 2.3 %layer_two.1 = (f32[64,512]{1,0:T(8,128)}, f32[80,512]{1,0:T(8,128)S(1)}, s16[512,512]{1,0:T(8,128)(2,1)S(1)}, bf16[256,512]{1,0:T(8,128)(2,1)S(1)}, bf16[256,512]{1,0:T(8,128)(2,1)S(1)}, /*index=5*/f32[512,512]{1,0:T(8,128)}) custom-call(f32[512,512]{1,0:T(8,128)S(1)} %get-tuple-element.108.h1_ref, f32[64,512]{1,0:T(8,128)S(1)} %bitcast.5, ...), custom_call_target="tpu_custom_call" | custom-call | tf_op jit(solution)/shard_map/layer_two/pallas_call | solution.py:519
  60.3 1.2 %second_products.3 = (f32[256,512]{1,0:T(8,128)S(1)}, f32[256,512]{1,0:T(8,128)S(1)}) custom-call(bf16[512,512]{1,0:T(8,128)(2,1)S(1)} %get-tuple-element.107.ha, bf16[512,512]{1,0:T(8,128)(2,1)S(1)} %collective-permute-done.15.hb, bf16[256,512]{1,0:T(8,128)(2,1)S(1)} %get-tuple-element.110.refs_0_, bf16[256,512]{1,0:T(8,128)(2,1)S(1)} %get-tuple-element.111.refs_1_, ...), custom_call_target="tpu_custom_call" | custom-call | flops 1610612736 | bytes 1572864 | tf_op jit(solution)/shard_map/second_products/pallas_call | solution.py:236
  62.0 1.6 %collective-permute-start.21 = (s16[320,512]{1,0:T(8,128)(2,1)S(1)}, s16[320,512]{1,0:T(8,128)(2,1)S(1)}, u32[]{:S(2)}, u32[]{:S(2)}) collective-permute-start(s16[320,512]{1,0:T(8,128)(2,1)S(1)} %get-tuple-element.123.lo), channel_id=1, source_target_pairs={{0,2},{1,3},{2,0},{3,1},{4,6},{5,7},{6,4},{7,5},{8,10},{9,11},{10,... | collective-permute-start | bytes 983048 | tf_op jit(solution)/shard_map/ppermute | solution.py:276
  63.6 1.5 %collective-permute-start.20 = (s16[320,512]{1,0:T(8,128)(2,1)S(1)}, s16[320,512]{1,0:T(8,128)(2,1)S(1)}, u32[]{:S(2)}, u32[]{:S(2)}) collective-permute-start(s16[320,512]{1,0:T(8,128)(2,1)S(1)} %get-tuple-element.121.hi), channel_id=1, source_target_pairs={{0,4},{1,5},{2,6},{3,7},{4,0},{5,1},{6,2},{7,3},{8,12},{9,13},{10,... | collective-permute-start | bytes 983048 | tf_op jit(solution)/shard_map/ppermute | solution.py:276
  65.1 4.4 %second_products.4 = (s16[272,512]{1,0:T(8,128)(2,1)S(1)}, f32[256,512]{1,0:T(8,128)S(1)}, f32[256,512]{1,0:T(8,128)S(1)}, s16[272,512]{1,0:T(8,128)(2,1)S(1)}) custom-call(bf16[512,512]{1,0:T(8,128)(2,1)S(1)} %get-tuple-element.107.ha, bf16[512,512]{1,0:T(8,128)(2,1)S(1)} %collective-permute-done.15.hb, bf16[512,512]{1,0:T(8,128)(2,1)} %copy-done.3, ...), custom_call_target="tpu_custom_call" | custom-call | flops 3221225472 | bytes 3145728 | tf_op jit(solution)/shard_map/second_products/pallas_call | solution.py:236
  70.6 3.5 %collective-permute-done.20.x_in = s16[320,512]{1,0:T(8,128)(2,1)S(1)} collective-permute-done((s16[320,512]{1,0:T(8,128)(2,1)S(1)}, s16[320,512]{1,0:T(8,128)(2,1)S(1)}, u32[]{:S(2)}, u32[]{:S(2)}) %collective-permute-start.20) | collective-permute-done | bytes 327712 | tf_op jit(solution)/shard_map/ppermute | solution.py:276
  75.0 2.0 %collective-permute-start.26 = (s16[320,512]{1,0:T(8,128)(2,1)S(1)}, s16[320,512]{1,0:T(8,128)(2,1)S(1)}, u32[]{:S(2)}, u32[]{:S(2)}) collective-permute-start(s16[320,512]{1,0:T(8,128)(2,1)S(1)} %get-tuple-element.131), channel_id=1, source_target_pairs={{0,4},{1,5},{2,6},{3,7},{4,0},{5,1},{6,2},{7,3},{8,12},{9,13},{10,... | collective-permute-start | bytes 983048 | tf_op jit(solution)/shard_map/ppermute | solution.py:276
  77.1 2.1 %collective-permute-done.22.x_lo = s16[272,512]{1,0:T(8,128)(2,1)S(1)} collective-permute-done((s16[272,512]{1,0:T(8,128)(2,1)S(1)}, s16[272,512]{1,0:T(8,128)(2,1)S(1)}, u32[]{:S(2)}, u32[]{:S(2)}) %collective-permute-start.22) | collective-permute-done | bytes 278560 | tf_op jit(solution)/shard_map/ppermute | solution.py:276
  80.1 2.5 %second_products.5.own = f32[512,512]{1,0:T(8,128)S(1)} custom-call(bf16[512,512]{1,0:T(8,128)(2,1)S(1)} %get-tuple-element.107.ha, bf16[512,512]{1,0:T(8,128)(2,1)S(1)} %collective-permute-done.15.hb, bf16[512,512]{1,0:T(8,128)(2,1)} %w_ref.1, s16[512,512]{1,0:T(8,128)(2,1)} %get-tuple-element.74.refs_1_, s16[512,512]{1,0:T(8,128)(2,1)S(1)} %collective-permute-done.24.refs_2_), custom_call_target="tpu_custom_call" | custom-call | flops 1610612736 | bytes 1572864 | tf_op jit(solution)/shard_map/second_products/pallas_call | solution.py:236
  82.9 2.2 %collective-permute-done.25.x_hi = s16[320,512]{1,0:T(8,128)(2,1)S(1)} collective-permute-done((s16[320,512]{1,0:T(8,128)(2,1)S(1)}, s16[320,512]{1,0:T(8,128)(2,1)S(1)}, u32[]{:S(2)}, u32[]{:S(2)}) %collective-permute-start.25) | collective-permute-done | bytes 327712 | tf_op jit(solution)/shard_map/ppermute | solution.py:276
  85.1 1.2 %collective-permute-done.26.y_lo = s16[320,512]{1,0:T(8,128)(2,1)S(1)} collective-permute-done((s16[320,512]{1,0:T(8,128)(2,1)S(1)}, s16[320,512]{1,0:T(8,128)(2,1)S(1)}, u32[]{:S(2)}, u32[]{:S(2)}) %collective-permute-start.26) | collective-permute-done | bytes 327712 | tf_op jit(solution)/shard_map/ppermute | solution.py:276
  86.3 1.4 %last_update.1 = (bf16[512,512]{1,0:T(8,128)(2,1)}, f32[64,512]{1,0:T(8,128)}) custom-call(f32[512,512]{1,0:T(8,128)S(1)} %get-tuple-element.130.base, s16[320,512]{1,0:T(8,128)(2,1)S(1)} %collective-permute-done.25.x_hi, s16[320,512]{1,0:T(8,128)(2,1)S(1)} %collective-permute-done.26.y_lo, s16[48,512]{1,0:T(8,128)(2,1)S(1)} %get-tuple-element.132.x_sums, ...), custom_call_target="tpu_custom_call" | custom-call | tf_op jit(solution)/shard_map/last_update/pallas_call | solution.py:270
  (67 shorter events, 10.8 us)
Async XLA Ops:
  0.6 11.9 %collective-permute-start.2 = (bf16[512,512]{1,0:T(8,128)(2,1)}, bf16[512,512]{1,0:T(8,128)(2,1)S(1)}, u32[]{:S(2)}, u32[]{:S(2)}) collective-permute-start(bf16[512,512]{1,0:T(8,128)(2,1)} %w_ref.1), channel_id=1, source_target_pairs={{0,1},{1,0},{2,3},{3,2},{4,5},{5,4},{6,7},{7,6},{8,9},{9,8},{10,11... | collective-permute-start | bytes 1572872 | tf_op jit(solution)/shard_map/ppermute | solution.py:276
  1.1 16.2 %collective-permute-start = (bf16[512,512]{1,0:T(8,128)(2,1)}, bf16[512,512]{1,0:T(8,128)(2,1)S(1)}, u32[]{:S(2)}, u32[]{:S(2)}) collective-permute-start(bf16[512,512]{1,0:T(8,128)(2,1)} %w_ref.1), channel_id=1, source_target_pairs={{0,2},{1,3},{2,0},{3,1},{4,6},{5,7},{6,4},{7,5},{8,10},{9,11},{10,... | collective-permute-start | bytes 1572872 | tf_op jit(solution)/shard_map/ppermute | solution.py:276
  3.7 14.2 %collective-permute-start.1 = (bf16[512,512]{1,0:T(8,128)(2,1)}, bf16[512,512]{1,0:T(8,128)(2,1)S(1)}, u32[]{:S(2)}, u32[]{:S(2)}) collective-permute-start(bf16[512,512]{1,0:T(8,128)(2,1)} %w_ref.1), channel_id=1, source_target_pairs={{0,4},{1,5},{2,6},{3,7},{4,0},{5,1},{6,2},{7,3},{8,12},{9,13},{10,... | collective-permute-start | bytes 1572872 | tf_op jit(solution)/shard_map/ppermute | solution.py:276
  17.9 2.7 %collective-permute-start.5 = (bf16[512,512]{1,0:T(8,128)(2,1)S(1)}, bf16[512,512]{1,0:T(8,128)(2,1)S(1)}, u32[]{:S(2)}, u32[]{:S(2)}) collective-permute-start(bf16[512,512]{1,0:T(8,128)(2,1)S(1)} %collective-permute-done.b_ref.refs_0_), channel_id=1, source_target_pairs={{0,1},{1,0},{2,3},{3,2},{4,5},{5,4},{6,7},{7,6},{8,9},{9,8},{10,11... | collective-permute-start | bytes 1572872 | tf_op jit(solution)/shard_map/ppermute | solution.py:276
  17.9 2.7 %collective-permute-start.6 = (bf16[512,512]{1,0:T(8,128)(2,1)S(1)}, bf16[512,512]{1,0:T(8,128)(2,1)S(1)}, u32[]{:S(2)}, u32[]{:S(2)}) collective-permute-start(bf16[512,512]{1,0:T(8,128)(2,1)S(1)} %collective-permute-done.1.a_ref.refs_2_.refs_3_), channel_id=1, source_target_pairs={{0,1},{1,0},{2,3},{3,2},{4,5},{5,4},{6,7},{7,6},{8,9},{9,8},{10,11... | collective-permute-start | bytes 1572872 | tf_op jit(solution)/shard_map/ppermute | solution.py:276
  18.5 8.4 %collective-permute-start.3 = (bf16[256,512]{1,0:T(8,128)(2,1)S(1)}, bf16[256,512]{1,0:T(8,128)(2,1)}, u32[]{:S(2)}, u32[]{:S(2)}) collective-permute-start(bf16[256,512]{1,0:T(8,128)(2,1)S(1)} %get-tuple-element.80), channel_id=1, source_target_pairs={{0,2},{1,3},{2,0},{3,1},{4,6},{5,7},{6,4},{7,5},{8,10},{9,11},{10,... | collective-permute-start | bytes 786440 | tf_op jit(solution)/shard_map/ppermute | solution.py:276
  18.9 8.1 %collective-permute-start.4 = (bf16[256,512]{1,0:T(8,128)(2,1)S(1)}, bf16[256,512]{1,0:T(8,128)(2,1)}, u32[]{:S(2)}, u32[]{:S(2)}) collective-permute-start(bf16[256,512]{1,0:T(8,128)(2,1)S(1)} %get-tuple-element.81), channel_id=1, source_target_pairs={{0,4},{1,5},{2,6},{3,7},{4,0},{5,1},{6,2},{7,3},{8,12},{9,13},{10,... | collective-permute-start | bytes 786440 | tf_op jit(solution)/shard_map/ppermute | solution.py:276
  21.6 34.7 %copy-start = (f32[512,512]{1,0:T(8,128)S(1)}, f32[512,512]{1,0:T(8,128)}, u32[]{:S(2)}) copy-start(f32[512,512]{1,0:T(8,128)} %refs_4_.1) | copy-start | bytes 3145732
  26.0 31.5 %copy-start.2 = (f32[512,64]{0,1:T(8,128)S(1)}, f32[512,64]{0,1:T(8,128)}, u32[]{:S(2)}) copy-start(f32[512,64]{0,1:T(8,128)} %param.8) | copy-start | bytes 393220
  26.0 31.5 %copy-start.6 = (f32[64,512]{1,0:T(8,128)S(1)}, f32[64,512]{1,0:T(8,128)}, u32[]{:S(2)}) copy-start(f32[64,512]{1,0:T(8,128)} %h2_ref.1) | copy-start | bytes 393220
  27.0 2.0 %collective-permute-start.7 = (bf16[256,512]{1,0:T(8,128)(2,1)}, bf16[256,512]{1,0:T(8,128)(2,1)S(1)}, u32[]{:S(2)}, u32[]{:S(2)}) collective-permute-start(bf16[256,512]{1,0:T(8,128)(2,1)} %collective-permute-done.3.refs_2_.refs_1_), channel_id=1, source_target_pairs={{0,1},{1,0},{2,3},{3,2},{4,5},{5,4},{6,7},{7,6},{8,9},{9,8},{10,11... | collective-permute-start | bytes 786440 | tf_op jit(solution)/shard_map/ppermute | solution.py:276
  27.0 2.1 %collective-permute-start.8 = (bf16[256,512]{1,0:T(8,128)(2,1)}, bf16[256,512]{1,0:T(8,128)(2,1)S(1)}, u32[]{:S(2)}, u32[]{:S(2)}) collective-permute-start(bf16[256,512]{1,0:T(8,128)(2,1)} %collective-permute-done.4.refs_3_.refs_2_), channel_id=1, source_target_pairs={{0,1},{1,0},{2,3},{3,2},{4,5},{5,4},{6,7},{7,6},{8,9},{9,8},{10,11... | collective-permute-start | bytes 786440 | tf_op jit(solution)/shard_map/ppermute | solution.py:276
  27.5 29.9 %copy-start.10 = (s16[512,512]{1,0:T(8,128)(2,1)S(1)}, s16[512,512]{1,0:T(8,128)(2,1)}, u32[]{:S(2)}) copy-start(s16[512,512]{1,0:T(8,128)(2,1)} %get-tuple-element.85.refs_7_) | copy-start | bytes 1572868
  27.5 32.7 %copy-start.9 = (s16[512,512]{1,0:T(8,128)(2,1)S(1)}, s16[512,512]{1,0:T(8,128)(2,1)}, u32[]{:S(2)}) copy-start(s16[512,512]{1,0:T(8,128)(2,1)} %get-tuple-element.75.refs_3_) | copy-start | bytes 1572868
  30.7 6.5 %collective-permute-start.11 = (s16[528,128]{1,0:T(8,128)(2,1)S(1)}, s16[528,128]{1,0:T(8,128)(2,1)S(1)}, u32[]{:S(2)}, u32[]{:S(2)}) collective-permute-start(s16[528,128]{1,0:T(8,128)(2,1)S(1)} %get-tuple-element.105), channel_id=1, source_target_pairs={{0,8},{8,0},{16,24},{24,16},{1,9},{9,1},{17,25},{25,17},{2,10},{10... | collective-permute-start | bytes 405512 | tf_op jit(solution)/shard_map/ppermute | solution.py:276
  32.5 8.7 %collective-permute-start.9 = (s16[528,128]{1,0:T(8,128)(2,1)S(1)}, s16[528,128]{1,0:T(8,128)(2,1)S(1)}, u32[]{:S(2)}, u32[]{:S(2)}) collective-permute-start(s16[528,128]{1,0:T(8,128)(2,1)S(1)} %get-tuple-element.103.refs_0_), channel_id=1, source_target_pairs={{0,8},{8,0},{16,24},{24,16},{1,9},{9,1},{17,25},{25,17},{2,10},{10... | collective-permute-start | bytes 405512 | tf_op jit(solution)/shard_map/ppermute | solution.py:276
  37.4 7.5 %collective-permute-start.12 = (s16[528,128]{1,0:T(8,128)(2,1)S(1)}, s16[528,128]{1,0:T(8,128)(2,1)S(1)}, u32[]{:S(2)}, u32[]{:S(2)}) collective-permute-start(s16[528,128]{1,0:T(8,128)(2,1)S(1)} %add_pair.3.one), channel_id=1, source_target_pairs={{0,24},{8,16},{16,8},{24,0},{1,25},{9,17},{17,9},{25,1},{2,26},{10... | collective-permute-start | bytes 405512 | tf_op jit(solution)/shard_map/ppermute | solution.py:276
  41.3 9.4 %collective-permute-start.10 = (s16[528,128]{1,0:T(8,128)(2,1)S(1)}, s16[528,128]{1,0:T(8,128)(2,1)S(1)}, u32[]{:S(2)}, u32[]{:S(2)}) collective-permute-start(s16[528,128]{1,0:T(8,128)(2,1)S(1)} %add_pair.2.one), channel_id=1, source_target_pairs={{0,24},{8,16},{16,8},{24,0},{1,25},{9,17},{17,9},{25,1},{2,26},{10... | collective-permute-start | bytes 405512 | tf_op jit(solution)/shard_map/ppermute | solution.py:276
  45.1 9.9 %collective-permute-start.14 = (s16[528,128]{1,0:T(8,128)(2,1)S(1)}, s16[528,128]{1,0:T(8,128)(2,1)S(1)}, u32[]{:S(2)}, u32[]{:S(2)}) collective-permute-start(s16[528,128]{1,0:T(8,128)(2,1)S(1)} %add_cross.3.refs_1_), channel_id=1, source_target_pairs={{0,8},{8,0},{16,24},{24,16},{1,9},{9,1},{17,25},{25,17},{2,10},{10... | collective-permute-start | bytes 405512 | tf_op jit(solution)/shard_map/ppermute | solution.py:276
  50.9 5.4 %collective-permute-start.13 = (s16[528,128]{1,0:T(8,128)(2,1)S(1)}, s16[528,128]{1,0:T(8,128)(2,1)S(1)}, u32[]{:S(2)}, u32[]{:S(2)}) collective-permute-start(s16[528,128]{1,0:T(8,128)(2,1)S(1)} %get-tuple-element.104.refs_0_), channel_id=1, source_target_pairs={{0,8},{8,0},{16,24},{24,16},{1,9},{9,1},{17,25},{25,17},{2,10},{10... | collective-permute-start | bytes 405512 | tf_op jit(solution)/shard_map/ppermute | solution.py:276
  52.3 7.9 %collective-permute-start.17 = (s16[512,512]{1,0:T(8,128)(2,1)}, s16[512,512]{1,0:T(8,128)(2,1)S(1)}, u32[]{:S(2)}, u32[]{:S(2)}) collective-permute-start(s16[512,512]{1,0:T(8,128)(2,1)} %get-tuple-element.95.refs_1_), channel_id=1, source_target_pairs={{0,1},{1,0},{2,3},{3,2},{4,5},{5,4},{6,7},{7,6},{8,9},{9,8},{10,11... | collective-permute-start | bytes 1572872 | tf_op jit(solution)/shard_map/ppermute | solution.py:276
  56.8 3.5 %collective-permute-start.15 = (bf16[512,512]{1,0:T(8,128)(2,1)S(1)}, bf16[512,512]{1,0:T(8,128)(2,1)S(1)}, u32[]{:S(2)}, u32[]{:S(2)}) collective-permute-start(bf16[512,512]{1,0:T(8,128)(2,1)S(1)} %get-tuple-element.107.ha), channel_id=1, source_target_pairs={{0,1},{1,0},{2,3},{3,2},{4,5},{5,4},{6,7},{7,6},{8,9},{9,8},{10,11... | collective-permute-start | bytes 1572872 | tf_op jit(solution)/shard_map/ppermute | solution.py:276
  56.9 8.2 %collective-permute-start.18 = (s16[512,512]{1,0:T(8,128)(2,1)S(1)}, s16[512,512]{1,0:T(8,128)(2,1)S(1)}, u32[]{:S(2)}, u32[]{:S(2)}) collective-permute-start(s16[512,512]{1,0:T(8,128)(2,1)S(1)} %copy-done.11), channel_id=1, source_target_pairs={{0,1},{1,0},{2,3},{3,2},{4,5},{5,4},{6,7},{7,6},{8,9},{9,8},{10,11... | collective-permute-start | bytes 1572872 | tf_op jit(solution)/shard_map/ppermute | solution.py:276
  57.4 7.7 %collective-permute-start.19 = (s16[512,512]{1,0:T(8,128)(2,1)S(1)}, s16[512,512]{1,0:T(8,128)(2,1)S(1)}, u32[]{:S(2)}, u32[]{:S(2)}) collective-permute-start(s16[512,512]{1,0:T(8,128)(2,1)S(1)} %copy-done.10), channel_id=1, source_target_pairs={{0,1},{1,0},{2,3},{3,2},{4,5},{5,4},{6,7},{7,6},{8,9},{9,8},{10,11... | collective-permute-start | bytes 1572872 | tf_op jit(solution)/shard_map/ppermute | solution.py:276
  59.7 1.8 %collective-permute-start.16 = (f32[80,512]{1,0:T(8,128)S(1)}, f32[80,512]{1,0:T(8,128)S(1)}, u32[]{:S(2)}, u32[]{:S(2)}) collective-permute-start(f32[80,512]{1,0:T(8,128)S(1)} %get-tuple-element.116.sums), channel_id=1, source_target_pairs={{0,1},{1,0},{2,3},{3,2},{4,5},{5,4},{6,7},{7,6},{8,9},{9,8},{10,11... | collective-permute-start | bytes 491528 | tf_op jit(solution)/shard_map/ppermute | solution.py:276
  60.2 19.9 %collective-permute-start.24 = (s16[512,512]{1,0:T(8,128)(2,1)S(1)}, s16[512,512]{1,0:T(8,128)(2,1)S(1)}, u32[]{:S(2)}, u32[]{:S(2)}) collective-permute-start(s16[512,512]{1,0:T(8,128)(2,1)S(1)} %copy-done.9), channel_id=1, source_target_pairs={{0,1},{1,0},{2,3},{3,2},{4,5},{5,4},{6,7},{7,6},{8,9},{9,8},{10,11... | collective-permute-start | bytes 1572872 | tf_op jit(solution)/shard_map/ppermute | solution.py:276
  62.0 12.1 %collective-permute-start.21 = (s16[320,512]{1,0:T(8,128)(2,1)S(1)}, s16[320,512]{1,0:T(8,128)(2,1)S(1)}, u32[]{:S(2)}, u32[]{:S(2)}) collective-permute-start(s16[320,512]{1,0:T(8,128)(2,1)S(1)} %get-tuple-element.123.lo), channel_id=1, source_target_pairs={{0,2},{1,3},{2,0},{3,1},{4,6},{5,7},{6,4},{7,5},{8,10},{9,11},{10,... | collective-permute-start | bytes 983048 | tf_op jit(solution)/shard_map/ppermute | solution.py:276
  63.6 10.6 %collective-permute-start.20 = (s16[320,512]{1,0:T(8,128)(2,1)S(1)}, s16[320,512]{1,0:T(8,128)(2,1)S(1)}, u32[]{:S(2)}, u32[]{:S(2)}) collective-permute-start(s16[320,512]{1,0:T(8,128)(2,1)S(1)} %get-tuple-element.121.hi), channel_id=1, source_target_pairs={{0,4},{1,5},{2,6},{3,7},{4,0},{5,1},{6,2},{7,3},{8,12},{9,13},{10,... | collective-permute-start | bytes 983048 | tf_op jit(solution)/shard_map/ppermute | solution.py:276
  69.5 9.6 %collective-permute-start.22 = (s16[272,512]{1,0:T(8,128)(2,1)S(1)}, s16[272,512]{1,0:T(8,128)(2,1)S(1)}, u32[]{:S(2)}, u32[]{:S(2)}) collective-permute-start(s16[272,512]{1,0:T(8,128)(2,1)S(1)} %get-tuple-element.125), channel_id=1, source_target_pairs={{0,2},{1,3},{2,0},{3,1},{4,6},{5,7},{6,4},{7,5},{8,10},{9,11},{10,... | collective-permute-start | bytes 835592 | tf_op jit(solution)/shard_map/ppermute | solution.py:276
  70.1 10.0 %collective-permute-start.23 = (s16[272,512]{1,0:T(8,128)(2,1)S(1)}, s16[272,512]{1,0:T(8,128)(2,1)S(1)}, u32[]{:S(2)}, u32[]{:S(2)}) collective-permute-start(s16[272,512]{1,0:T(8,128)(2,1)S(1)} %get-tuple-element.126), channel_id=1, source_target_pairs={{0,4},{1,5},{2,6},{3,7},{4,0},{5,1},{6,2},{7,3},{8,12},{9,13},{10,... | collective-permute-start | bytes 835592 | tf_op jit(solution)/shard_map/ppermute | solution.py:276
  74.9 10.2 %collective-permute-start.25 = (s16[320,512]{1,0:T(8,128)(2,1)S(1)}, s16[320,512]{1,0:T(8,128)(2,1)S(1)}, u32[]{:S(2)}, u32[]{:S(2)}) collective-permute-start(s16[320,512]{1,0:T(8,128)(2,1)S(1)} %get-tuple-element.124), channel_id=1, source_target_pairs={{0,2},{1,3},{2,0},{3,1},{4,6},{5,7},{6,4},{7,5},{8,10},{9,11},{10,... | collective-permute-start | bytes 983048 | tf_op jit(solution)/shard_map/ppermute | solution.py:276
  75.0 11.3 %collective-permute-start.26 = (s16[320,512]{1,0:T(8,128)(2,1)S(1)}, s16[320,512]{1,0:T(8,128)(2,1)S(1)}, u32[]{:S(2)}, u32[]{:S(2)}) collective-permute-start(s16[320,512]{1,0:T(8,128)(2,1)S(1)} %get-tuple-element.131), channel_id=1, source_target_pairs={{0,4},{1,5},{2,6},{3,7},{4,0},{5,1},{6,2},{7,3},{8,12},{9,13},{10,... | collective-permute-start | bytes 983048 | tf_op jit(solution)/shard_map/ppermute | solution.py:276
  (7 other events, 62.6 us)
